TPU v7x, 128 devices: a whole 4x4x4 slice. The times are simulated.
128 devices in a mesh: ctx: 64 (over x, y, z_hi, core), wa: 2 (over z_lo).
Axes of the slice: x: 4, y: 4, z: 4 (z_hi: 2, z_lo: 2; z = z_hi * 2 + z_lo), core: 2. Of those that a mesh axis runs over, the one named last changes fastest.
Arguments:
- tokens: bfloat16 [8192, 768], P('ctx'), may hold values from -6 to 6
- doc_start: int32 [8192], P('ctx'), may hold values from 0 to 8191, as said below
- exit_layer: int32 [8192], P('ctx'), may hold values from 1 to 12, as said below
- cotangent: bfloat16 [8192, 768], P('ctx'), may hold values from -6 to 6
- ln1_gain: float32 [768], replicated, may hold values from 0.25 to 1.75
- ln1_shift: float32 [768], replicated, may hold values from -1.5 to 1.5
- q_weight: bfloat16 [768, 768], P(None, 'wa'), may hold values from -0.3125 to 0.3125
- q_bias: float32 [768], P('wa'), may hold values from -1.5 to 1.5
- k_weight: bfloat16 [768, 768], P(None, 'wa'), may hold values from -0.3125 to 0.3125
- v_weight: bfloat16 [768, 768], P(None, 'wa'), may hold values from -0.21875 to 0.21875
- v_bias: float32 [768], P('wa'), may hold values from -1.5 to 1.5
- o_weight: bfloat16 [768, 768], P('wa'), may hold values from -1.75 to 1.75
- o_bias: float32 [768], replicated, may hold values from -1.5 to 1.5
- ln2_gain: float32 [768], replicated, may hold values from 0.25 to 1.75
- ln2_shift: float32 [768], replicated, may hold values from -1.5 to 1.5
- up_weight: bfloat16 [768, 3072], P(None, 'wa'), may hold values from -0.21875 to 0.21875
- up_bias: float32 [3072], P('wa'), may hold values from -1.5 to 1.5
- down_weight: bfloat16 [3072, 768], P('wa'), may hold values from -0.15625 to 0.15625
- down_bias: float32 [768], replicated, may hold values from -1.5 to 1.5
Outputs:
- output: bfloat16 [8192, 768], P('ctx')
- input_grad: float32 [8192, 768], P('ctx')
- ln1_gain_grad: float32 [768], replicated
- ln1_shift_grad: float32 [768], replicated
- q_weight_grad: float32 [768, 768], P('ctx', 'wa')
- q_bias_grad: float32 [768], P('wa')
- k_weight_grad: float32 [768, 768], P('ctx', 'wa')
- v_weight_grad: float32 [768, 768], P('ctx', 'wa')
- v_bias_grad: float32 [768], P('wa')
- o_weight_grad_t: float32 [768, 768], P('ctx', 'wa')
- o_bias_grad: float32 [768], replicated
- ln2_gain_grad: float32 [768], replicated
- ln2_shift_grad: float32 [768], replicated
- up_weight_grad: float32 [768, 3072], P('ctx', 'wa')
- up_bias_grad: float32 [3072], P('wa')
- down_weight_grad_t: float32 [768, 3072], P('ctx', 'wa')
- down_bias_grad: float32 [768], replicated
Inputs may be any that keep to these rules, and one draw needn't show every extreme that they name: doc_start(k) is the stream position at which the document holding place(k) begins; documents are contiguous runs of the stream of 1 to 4096 positions; one of exactly 4096 positions begins among the first 64 positions of the stream, and the stream's last position is a document of its own. `exit_layer`: within a document, exit layers never increase along the stream, and a document's first position has exit layer 12, so the active positions of each document form a non-empty prefix of it; every position of the document of 4096 positions that begins among the first 64 is active.
All inputs are finite; a program needn't handle non-finite values.
Results may differ from a plain program's by a relative error of at most 0.014.
The roundings to bfloat16 on the way count: a program that leaves them out, or rounds other values in their place, can miss the bound.
Values may be sent and summed in bfloat16 or wider, within the bound.
No kernel may reach another device: no remote copies, remote signals or barrier semaphores. Data moves between devices by JAX's collectives and lax.ppermute only.
A program may use at most 192 MiB of HBM per device.

v0:
```python
import math

import jax
import jax.numpy as jnp
from jax import lax
from jax.experimental import pallas as pl
from jax.experimental.pallas import tpu as pltpu
from jax.sharding import Mesh, PartitionSpec as P

HEAD_DIM = 64
LAYER = 6
CTX = ("x", "y", "zh", "core")
PLANE = ("x", "y")
SWAP = ((0, 1), (1, 0))
CROSS = ((0, 3), (1, 2), (2, 1), (3, 0))
HALF = 64
BLOCKS = 16
GROUP = 256
STREAM = 8192
ROWS = (BLOCKS + 1) * HALF
FF_TILE = 512
FAR = 1e9
SCALING = 1.0 / math.sqrt(HEAD_DIM)
EXP2_SCALE = SCALING / math.log(2.0)
VMEM_BYTES = 64 * 2**20


epsilon = 1e-05
trans_right = (((1,), (1,)), ((), ()))
trans_left = (((0,), (0,)), ((), ()))
cubic_coef = 0.044715


def gelu_pair(values):
    outer = math.sqrt(2.0 / math.pi)
    inner = outer * (values + cubic_coef * values * values * values)
    tangent = jnp.tanh(inner)
    result = 0.5 * values * (1.0 + tangent)
    gelu_slope = 0.5 * (1.0 + tangent) + 0.5 * values * (1.0 - tangent * tangent) * outer * (
        1.0 + 3.0 * cubic_coef * values * values
    )
    return (result, gelu_slope)


def norm_forward(values, gain_vec, shift_vec):
    average = jnp.mean(values, axis=-1, keepdims=True)
    centred = values - average
    inverse_std = lax.rsqrt(jnp.mean(centred * centred, axis=-1, keepdims=True) + epsilon)
    normed = centred * inverse_std
    return (normed * gain_vec + shift_vec, normed, inverse_std)


def norm_backward(grad_out, normed, inverse_std, gain_vec):
    scaled = grad_out * gain_vec
    return inverse_std * (
        scaled
        - jnp.mean(scaled, axis=-1, keepdims=True)
        - normed * jnp.mean(scaled * normed, axis=-1, keepdims=True)
    )


def swap_add(part, axis):
    other = lax.ppermute(part, axis, SWAP)
    return part.astype(jnp.float32) + other.astype(jnp.float32)


def whole(*shape, dtype=jnp.bfloat16):
    return jax.ShapeDtypeStruct(shape, dtype)


def head_place():
    upper = lax.axis_index("y") % 2
    sub = 2 * lax.axis_index("zh") + lax.axis_index("core")
    last = sub == 3
    return (
        upper,
        jnp.where(upper == 1, 3 - sub, sub),
        jnp.where((upper == 0) & last, 1, 0),
        jnp.where((upper == 1) & last, 1, 0),
    )


def call(kernel, name, ins, outs, scratch=(), lazy=()):
    copied_in = [at for at, (mode, _) in enumerate(ins) if mode == "d"]
    copied_out = [at for at, (mode, _) in enumerate(outs) if mode == "d"]

    def buffer(array):
        shape = array.shape if len(array.shape) > 1 else (1,) + tuple(array.shape)
        return pltpu.VMEM(shape, array.dtype)

    def body(*refs):
        given, rest = list(refs[: len(ins)]), refs[len(ins) :]
        results, rest = list(rest[: len(outs)]), rest[len(outs) :]
        in_buffers, rest = rest[: len(copied_in)], rest[len(copied_in) :]
        out_buffers, rest = rest[: len(copied_out)], rest[len(copied_out) :]
        in_sems, out_sems, rest = rest[0], rest[1], rest[2:]
        pending, flushing = [], []
        for slot, at in enumerate(copied_in):
            there = in_buffers[slot]
            into = there if len(ins[at][1].shape) > 1 else there.at[0]
            copy = pltpu.make_async_copy(given[at], into, in_sems.at[slot])
            copy.start()
            given[at] = there
            pending.append((there, at, copy))
        targets = []
        for slot, at in enumerate(copied_out):
            made = out_buffers[slot] if len(outs[at][1].shape) > 1 else out_buffers[slot].at[0]
            copy = pltpu.make_async_copy(made, results[at], out_sems.at[slot])
            results[at] = out_buffers[slot]
            targets.append((out_buffers[slot], copy))

        def wait(ref):
            for entry in list(pending):
                if entry[0] is ref:
                    entry[2].wait()
                    pending[:] = [other for other in pending if other is not entry]

        def flush(ref):
            for entry in list(targets):
                if entry[0] is ref:
                    entry[1].start()
                    flushing.append(entry[1])
                    targets[:] = [other for other in targets if other is not entry]

        for entry in list(pending):
            if entry[1] not in lazy:
                wait(entry[0])
        kernel(wait, flush, *given, *results, *rest)
        for entry in list(pending):
            wait(entry[0])
        for entry in list(targets):
            flush(entry[0])
        for copy in flushing:
            copy.wait()

    vmem, anywhere = pl.BlockSpec(memory_space=pltpu.VMEM), pl.BlockSpec(memory_space=pltpu.HBM)
    result = pl.pallas_call(
        body,
        out_shape=tuple(out for _, out in outs),
        in_specs=[anywhere if mode == "d" else vmem for mode, _ in ins],
        out_specs=tuple(anywhere if mode == "d" else vmem for mode, _ in outs),
        scratch_shapes=[buffer(ins[at][1]) for at in copied_in]
        + [buffer(outs[at][1]) for at in copied_out]
        + [
            pltpu.SemaphoreType.DMA((max(1, len(copied_in)),)),
            pltpu.SemaphoreType.DMA((max(1, len(copied_out)),)),
        ]
        + list(scratch),
        compiler_params=pltpu.CompilerParams(vmem_limit_bytes=VMEM_BYTES),
        name=name,
    )(*[array for _, array in ins])
    return result[0] if len(outs) == 1 else result


def lane_ids(rows, cols):
    return lax.broadcasted_iota(jnp.int32, (rows, cols), 1)


def row_ids_of(rows, cols):
    return lax.broadcasted_iota(jnp.int32, (rows, cols), 0)


def turn(values):
    return pltpu.roll(values, HALF, 1)


def unpack_low(packed):
    wide = packed.astype(jnp.float32)
    left = lane_ids(32, 128) < HALF
    both = jnp.concatenate([wide, turn(wide)], axis=0)
    return jnp.where(jnp.concatenate([left, left], axis=0), both, 0.0)


def unpack_high(packed):
    wide = packed.astype(jnp.float32)
    right = lane_ids(32, 128) >= HALF
    both = jnp.concatenate([turn(wide), wide], axis=0)
    return jnp.where(jnp.concatenate([right, right], axis=0), both, 0.0)


def pack_from_low(block):
    return jnp.where(lane_ids(32, 128) < HALF, block[:32], turn(block[32:]))


def pack_from_high(block):
    return jnp.where(lane_ids(32, 128) < HALF, turn(block[:32]), block[32:])


def key_places(scal, group):
    lane = lane_ids(8, GROUP)
    sub = (lane >> 6) ^ scal[1]
    return (scal[0] * (STREAM // 2) + GROUP * group + (sub << 6) + (lane & 63)).astype(
        jnp.float32
    )


def edge_places():
    return (STREAM // 2 + lane_ids(8, 128)).astype(jnp.float32)


def query_places(scal, block):
    row = row_ids_of(HALF, 128)
    return (
        scal[0] * (STREAM // 2) + GROUP * block + (scal[1] << 6) + row
    ).astype(jnp.float32)


def spread(rows, width):
    return jnp.concatenate([rows] * (width // 128), axis=1) if width > 128 else rows


def weights_of(scal, queries, starts, keys, places, group):
    scores = lax.dot_general(queries, keys, trans_right, preferred_element_type=jnp.float32)
    count = queries.shape[0]
    own = spread(query_places(scal, group), GROUP)
    limit = jnp.concatenate([own, jnp.full((count - HALF, GROUP), FAR, jnp.float32)], axis=0)
    seen = (spread(starts, GROUP) <= places[:1]) & (places[:1] <= limit)
    return jnp.where(seen, jnp.exp2(scores * EXP2_SCALE), 0.0)


def edge_weights(queries, starts, keys):
    scores = lax.dot_general(queries, keys, trans_right, preferred_element_type=jnp.float32)
    places = edge_places()[:1]
    limit = (STREAM // 2 + row_ids_of(HALF, 128)).astype(jnp.float32)
    return jnp.where(
        (starts <= places) & (places <= limit), jnp.exp2(scores * EXP2_SCALE), 0.0
    )


def attend_kernel(
    wait, flush, own_ref, one_ref, two_ref, three_ref, edge_ref,
    back_ref, kv_ref, q_ref, start_ref, full_ref,
    num_ref, den_ref,
):
    scal = head_place()
    upper = scal[0]
    diag = jnp.where(
        lane_ids(HALF, 128) == row_ids_of(HALF, 128),
        64.0,
        jnp.where(lane_ids(HALF, 128) == row_ids_of(HALF, 128) + HALF, 1.0, 0.0),
    )

    def starts(line, off):
        found = jnp.sum(line.astype(jnp.float32) * diag, axis=1, keepdims=True)
        return jnp.broadcast_to(jnp.where(off, FAR, found), (HALF, 128))

    for block in range(BLOCKS):
        place = jnp.where(upper == 1, BLOCKS - 1 - block, block)
        rows = slice(block * HALF, (block + 1) * HALF)
        mine = own_ref[pl.ds(place, 1)][0]
        kv_ref[block, 0:HALF] = mine[:HALF]
        kv_ref[block, HALF : 2 * HALF] = one_ref[pl.ds(place, 1)][0]
        kv_ref[block, 2 * HALF : 3 * HALF] = two_ref[pl.ds(place, 1)][0]
        kv_ref[block, 3 * HALF :] = three_ref[pl.ds(place, 1)][0]
        q_ref[rows] = unpack_low(mine[HALF : HALF + 32]).astype(jnp.bfloat16)
        off = (scal[3] == 1) if block == 0 else False
        start_ref[rows] = starts(mine[HALF + 32 : HALF + 33], off)
    kv_ref[BLOCKS] = jnp.zeros((GROUP, 128), jnp.bfloat16)
    kv_ref[BLOCKS, :HALF] = edge_ref[:HALF]
    q_ref[BLOCKS * HALF :] = unpack_low(edge_ref[HALF : HALF + 32]).astype(jnp.bfloat16)
    start_ref[BLOCKS * HALF :] = starts(edge_ref[HALF + 32 : HALF + 33], scal[2] == 0)
    flush(kv_ref)
    flush(q_ref)
    flush(start_ref)

    for group in range(BLOCKS + 1):
        rows = slice(group * HALF, ROWS)
        if group < BLOCKS:
            keys = kv_ref[group]
            weights = weights_of(
                scal, q_ref[rows], start_ref[rows], keys, key_places(scal, group), group
            )
            total = weights[:, :128] + weights[:, 128:]
        else:
            keys = kv_ref[group, :128]
            weights = total = edge_weights(q_ref[rows], start_ref[rows], keys)
        product = jnp.dot(weights.astype(jnp.bfloat16), keys, preferred_element_type=jnp.float32)
        if group == 0:
            num_ref[rows] = product
            den_ref[rows] = total
        else:
            num_ref[rows] += product
            den_ref[rows] += total

    for block in range(BLOCKS + 1):
        rows = slice(block * HALF, (block + 1) * HALF)
        den = jnp.sum(den_ref[rows], axis=1, keepdims=True)
        recip = jnp.broadcast_to(1.0 / jnp.where(den == 0.0, 1.0, den), (HALF, 128))
        full = num_ref[rows] * recip
        full_ref[rows] = jnp.where(lane_ids(HALF, 128) < HALF, recip, full)
        packed = pack_from_high(full).astype(jnp.bfloat16)
        if block < BLOCKS:
            place = jnp.where(upper == 1, BLOCKS - 1 - block, block)
            for copy in range(2):
                back_ref[pl.ds(2 * place + copy, 1), :32] = packed[None]
                back_ref[pl.ds(2 * place + copy, 1), 32:] = jnp.zeros((1, 32, 128), jnp.bfloat16)
        else:
            for copy in range(2):
                back_ref[2 * BLOCKS - 2 + copy, 32:] = packed


def attend_grad_kernel(
    wait, flush, kv_ref, q_ref, start_ref, full_ref, dh_in_ref,
    send_ref, keep_ref, dq_ref, edge_ref,
    dhn_ref, dot_ref, dq_acc,
):
    scal = head_place()
    upper = scal[0]
    left = lane_ids(HALF, 128) < HALF
    wait(full_ref)
    for block in range(BLOCKS + 1):
        rows = slice(block * HALF, (block + 1) * HALF)
        if block < BLOCKS:
            place = jnp.where(upper == 1, BLOCKS - 1 - block, block)
            packed = dh_in_ref[pl.ds(place, 1), :32][0]
        else:
            packed = dh_in_ref[BLOCKS - 1, 32:]
        full = full_ref[rows]
        scaled = unpack_high(packed) * jnp.where(left, full, turn(full))
        scaled = scaled.astype(jnp.bfloat16).astype(jnp.float32)
        dhn_ref[rows] = scaled.astype(jnp.bfloat16)
        dot_ref[rows] = jnp.broadcast_to(
            jnp.sum(jnp.where(left, 0.0, scaled * full), axis=1, keepdims=True), (HALF, 128)
        )
    wait(kv_ref)
    wait(q_ref)
    wait(start_ref)
    for group in range(BLOCKS + 1):
        rows = slice(group * HALF, ROWS)
        if group < BLOCKS:
            keys = kv_ref[group]
            weights = weights_of(
                scal, q_ref[rows], start_ref[rows], keys, key_places(scal, group), group
            )
        else:
            keys = kv_ref[group, :128]
            weights = edge_weights(q_ref[rows], start_ref[rows], keys)
        dprob = lax.dot_general(
            dhn_ref[rows], keys, trans_right, preferred_element_type=jnp.float32
        )
        dscore = (weights * (dprob - spread(dot_ref[rows], keys.shape[0]))).astype(jnp.bfloat16)
        dquery = jnp.dot(dscore, keys, preferred_element_type=jnp.float32)
        if group == 0:
            dq_acc[rows] = dquery
        else:
            dq_acc[rows] += dquery
        grads = lax.dot_general(
            dscore, q_ref[rows], trans_left, preferred_element_type=jnp.float32
        ) * SCALING + lax.dot_general(
            weights.astype(jnp.bfloat16),
            dhn_ref[rows],
            trans_left,
            preferred_element_type=jnp.float32,
        )
        low = grads.astype(jnp.bfloat16)
        if group < BLOCKS:
            place = jnp.where(upper == 1, BLOCKS - 1 - group, group)
            for quarter in range(4):
                out = send_ref if quarter % 2 else keep_ref
                out[pl.ds(quarter // 2 * BLOCKS + place, 1)] = low[
                    None, quarter * HALF : (quarter + 1) * HALF
                ]
        else:
            edge_ref[:HALF] = low[:HALF]

    for block in range(BLOCKS + 1):
        rows = slice(block * HALF, (block + 1) * HALF)
        packed = pack_from_low(dq_acc[rows] * SCALING).astype(jnp.bfloat16)
        if block < BLOCKS:
            place = jnp.where(upper == 1, BLOCKS - 1 - block, block)
            dq_ref[pl.ds(place, 1)] = packed[None]
        else:
            edge_ref[HALF:] = packed


def attend(own, one, two, three, edge):
    f32 = jnp.float32
    return call(
        attend_kernel, "attend",
        [("v", own), ("v", one), ("v", two), ("v", three), ("v", edge)],
        [
            ("d", whole(2 * BLOCKS, HALF, 128)),
            ("d", whole(BLOCKS + 1, GROUP, 128)),
            ("d", whole(ROWS, 128)),
            ("d", whole(ROWS, 128, dtype=f32)),
            ("d", whole(ROWS, 128, dtype=f32)),
        ],
        [pltpu.VMEM((ROWS, 128), f32), pltpu.VMEM((ROWS, 128), f32)],
    )


def attend_grad(kv, q, start, full, dh):
    f32 = jnp.float32
    return call(
        attend_grad_kernel, "attend_grad",
        [("d", kv), ("d", q), ("d", start), ("d", full), ("v", dh)],
        [
            ("v", whole(2 * BLOCKS, HALF, 128)),
            ("v", whole(2 * BLOCKS, HALF, 128)),
            ("v", whole(BLOCKS, 32, 128)),
            ("v", whole(96, 128)),
        ],
        [
            pltpu.VMEM((ROWS, 128), jnp.bfloat16),
            pltpu.VMEM((ROWS, 128), f32),
            pltpu.VMEM((ROWS, 128), f32),
        ],
        lazy=(0, 1, 2, 3),
    )


def column(line):
    return jnp.sum(
        jnp.where(lane_ids(128, 128) == row_ids_of(128, 128), line, 0.0), axis=1, keepdims=True
    )


def pairs_low(even, odd):
    left = lane_ids(32, 128) < HALF
    return jnp.concatenate(
        [jnp.where(left, even, turn(odd)), jnp.where(left, turn(even), odd)], axis=0
    )


def project_kernel(
    wait, flush,
    tokens_ref, start_ref, gain_ref, shift_ref, q_bias_ref, v_bias_ref, q_ref, k_ref, v_ref,
    pay_ref, low_ref,
):
    normed, _, _ = norm_forward(tokens_ref[...].astype(jnp.float32), gain_ref[...], shift_ref[...])
    low = normed.astype(jnp.bfloat16)
    low_ref[...] = low
    flush(low_ref)
    starts = start_ref[...]
    high_part = (starts >> 6).astype(jnp.float32)
    low_part = (starts & 63).astype(jnp.float32)
    left = lane_ids(1, 128) < HALF
    lines = (
        jnp.where(left, high_part, turn(low_part)),
        jnp.where(left, turn(high_part), low_part),
    )
    lines = [jnp.broadcast_to(line, (16, 128)).astype(jnp.bfloat16) for line in lines]
    wide = lane_ids(HALF, 128) < HALF
    for ref in (q_ref, k_ref, v_ref):
        wait(ref)
    for pair in range(3):
        columns = slice(pair * 128, (pair + 1) * 128)
        queries = (
            jnp.dot(low, q_ref[:, columns], preferred_element_type=jnp.float32)
            + q_bias_ref[:, columns]
        )
        keyset = jnp.dot(low, k_ref[:, columns], preferred_element_type=jnp.float32)
        values = (
            jnp.dot(low, v_ref[:, columns], preferred_element_type=jnp.float32)
            + v_bias_ref[:, columns]
        )
        for half in range(2):
            rows = slice(half * HALF, (half + 1) * HALF)
            for odd in range(2):
                if odd:
                    both = jnp.where(wide, turn(keyset[rows]), values[rows])
                    packed = pack_from_high(queries[rows])
                else:
                    both = jnp.where(wide, keyset[rows], turn(values[rows]))
                    packed = pack_from_low(queries[rows])
                index = 4 * pair + 2 * odd + half
                pay_ref[index, :HALF] = both.astype(jnp.bfloat16)
                pay_ref[index, HALF : HALF + 32] = packed.astype(jnp.bfloat16)
                pay_ref[index, HALF + 32 :] = lines[half]
    pay_ref[12:] = jnp.zeros((4, HALF + 48, 128), jnp.bfloat16)


def prepare_kernel(wait, flush, low_ref, send_ref, order_ref, keep_ref):
    lane = lane_ids(8, 768)
    core = (lane >= 384).astype(jnp.int32)
    rest = lane - 384 * core
    plane = (rest * 171) >> 12
    within = rest - 24 * plane
    high = (within >= 12).astype(jnp.int32)
    source = (48 * plane + 12 * (2 * high + core) + (within - 12 * high))[:1]
    order = jnp.where(row_ids_of(768, 768) == source, 1.0, 0.0).astype(jnp.bfloat16)
    order_ref[...] = order
    flush(order_ref)
    ordered = jnp.dot(low_ref[...], order, preferred_element_type=jnp.float32).astype(jnp.bfloat16)
    first = lax.axis_index("core") == 0
    keep_ref[...] = jnp.where(first, ordered[:, :384], ordered[:, 384:])
    send_ref[...] = jnp.where(first, ordered[:, 384:], ordered[:, :384])


def attn_tile(got_ref, side, pair):
    parts = []
    for half in range(2):
        heads = []
        for odd in range(2):
            index = 4 * pair + 2 * odd
            lower = got_ref[pl.ds(2 * index + side, 1)][0].astype(jnp.float32)
            if half:
                higher = got_ref[pl.ds(2 * index + 2 + side, 1)][0].astype(jnp.float32)
                packed = higher[:32] + lower[32:]
            else:
                packed = lower[:32]
            heads.append(packed)
        parts.append(pairs_low(*heads))
    return jnp.concatenate(parts, axis=0).astype(jnp.bfloat16)


def middle_kernel(
    wait, flush, got_ref, tokens_ref, cot_ref, exit_ref, o_bias_ref, gain_ref, shift_ref,
    up_bias_ref, o_own_ref, o_other_ref, up_ref, down_ref,
    dn_ref, send_ref, keep_ref, mid_ref, ffn_ref, attn_ref, vec_ref,
    acc_ref,
):
    first = lax.axis_index("core") == 0
    side = lax.axis_index("wa")
    for pair in range(3):
        rows = slice(pair * 128, (pair + 1) * 128)
        attn_ref[:, rows] = attn_tile(got_ref, side, pair)
        acc_ref[:, rows] = attn_tile(got_ref, 1 - side, pair)
    flush(attn_ref)
    wait(o_own_ref)
    wait(o_other_ref)
    total = jnp.dot(
        attn_ref[...], o_own_ref[...], preferred_element_type=jnp.float32
    ) + jnp.dot(acc_ref[...], o_other_ref[...], preferred_element_type=jnp.float32)
    middle = tokens_ref[...].astype(jnp.float32) + (total + o_bias_ref[...])
    mid_ref[...] = middle
    flush(mid_ref)
    normed, _, _ = norm_forward(middle, gain_ref[...], shift_ref[...])
    low = normed.astype(jnp.bfloat16)
    active = column((exit_ref[...] > LAYER).astype(jnp.float32))
    branch = jnp.where(active > 0.0, cot_ref[...].astype(jnp.float32), 0.0)
    branch_low = branch.astype(jnp.bfloat16)
    keep_ref[:, :768] = jnp.where(first, low, branch_low)
    send_ref[:, :768] = jnp.where(first, branch_low, low)
    vec_ref[:, 1536:] = jnp.sum(branch, axis=0, keepdims=True)
    ffn = None
    dnormed = None
    wait(up_ref)
    wait(down_ref)
    for begin in range(0, 1536, FF_TILE):
        columns = slice(begin, begin + FF_TILE)
        outs = slice(768 + begin, 768 + begin + FF_TILE)
        pre_act = (
            jnp.dot(low, up_ref[:, columns], preferred_element_type=jnp.float32)
            + up_bias_ref[:, columns]
        )
        hidden_full, slope = gelu_pair(pre_act)
        hidden = hidden_full.astype(jnp.bfloat16)
        dhidden = lax.dot_general(
            branch_low, down_ref[columns], trans_right, preferred_element_type=jnp.float32
        )
        dpre = (dhidden * slope).astype(jnp.bfloat16)
        vec_ref[:, columns] = jnp.sum(dpre.astype(jnp.float32), axis=0, keepdims=True)
        keep_ref[:, outs] = jnp.where(first, dpre, hidden)
        send_ref[:, outs] = jnp.where(first, hidden, dpre)
        ffn_term = jnp.dot(hidden, down_ref[columns], preferred_element_type=jnp.float32)
        dn_term = lax.dot_general(
            dpre, up_ref[:, columns], trans_right, preferred_element_type=jnp.float32
        )
        ffn = ffn_term if ffn is None else ffn + ffn_term
        dnormed = dn_term if dnormed is None else dnormed + dn_term
    ffn_ref[...] = ffn.astype(jnp.bfloat16)
    dn_ref[...] = dnormed.astype(jnp.bfloat16)


def dheads_kernel(
    wait, flush, dn_ref, other_ref, mid_ref, cot_ref, exit_ref, gain_ref, o_ref, attn_ref, order_ref,
    pay_ref, send_ref, keep_ref, dmid_ref, vec_ref,
):
    middle = mid_ref[...]
    _, unit, inverse = norm_forward(middle, gain_ref[...], 0.0)
    dnormed = dn_ref[...].astype(jnp.float32) + other_ref[...].astype(jnp.float32)
    active = column((exit_ref[...] > LAYER).astype(jnp.float32))
    branch = jnp.where(active > 0.0, cot_ref[...].astype(jnp.float32), 0.0)
    dmiddle = branch + norm_backward(dnormed, unit, inverse, gain_ref[...])
    dmid_ref[...] = dmiddle
    flush(dmid_ref)
    low = dmiddle.astype(jnp.bfloat16)
    vec_ref[:, :768] = jnp.sum(dnormed * unit, axis=0, keepdims=True)
    vec_ref[:, 768:1536] = jnp.sum(dnormed, axis=0, keepdims=True)
    vec_ref[:, 1536:] = jnp.sum(low.astype(jnp.float32), axis=0, keepdims=True)
    wait(o_ref)
    for pair in range(3):
        dheads = lax.dot_general(
            low,
            o_ref[pair * 128 : (pair + 1) * 128],
            trans_right,
            preferred_element_type=jnp.float32,
        )
        for odd in range(2):
            pack = pack_from_high if odd else pack_from_low
            lower = pack(dheads[:HALF]).astype(jnp.bfloat16)
            higher = pack(dheads[HALF:]).astype(jnp.bfloat16)
            index = 4 * pair + 2 * odd
            pay_ref[index, :32] = lower
            pay_ref[index, 32:] = higher
            pay_ref[index + 1, :32] = higher
            pay_ref[index + 1, 32:] = higher
    pay_ref[12:] = jnp.zeros((4, HALF, 128), jnp.bfloat16)
    flush(pay_ref)
    wait(order_ref)
    ordered = jnp.dot(low, order_ref[...], preferred_element_type=jnp.float32).astype(jnp.bfloat16)
    first = lax.axis_index("core") == 0
    keep_ref[:, :384] = jnp.where(first, ordered[:, :384], ordered[:, 384:])
    send_ref[:, :384] = jnp.where(first, ordered[:, 384:], ordered[:, :384])
    keep_ref[:, 384:] = attn_ref[...]
    send_ref[:, 384:] = attn_ref[...]


def o_products_kernel(wait, flush, keep_ref, sent_ref, far_ref, near_ref):
    both = jnp.concatenate([keep_ref[...], sent_ref[...]], axis=0)
    low = lax.axis_index("zh") == 0
    product = lax.dot_general(
        both[:, :384], both[:, 384:], trans_left, preferred_element_type=jnp.float32
    )
    spare = jnp.zeros((4, 384), jnp.float32)
    for plane in range(16):
        one = jnp.concatenate([product[24 * plane : 24 * plane + 12], spare], axis=0)
        two = jnp.concatenate([product[24 * plane + 12 : 24 * plane + 24], spare], axis=0)
        near_ref[plane] = jnp.where(low, one, two)
        far_ref[plane] = jnp.where(low, two, one).astype(jnp.bfloat16)


def ffn_products_kernel(wait, flush, keep_ref, sent_ref, out_ref):
    for at in range(768, 2304, 384):
        columns = slice(at, at + 384)
        lefts = jnp.concatenate([keep_ref[:, :768], sent_ref[:, :768]], axis=0)
        rights = jnp.concatenate([keep_ref[:, columns], sent_ref[:, columns]], axis=0)
        out_ref[:, at - 768 : at - 384] = lax.dot_general(
            lefts, rights, trans_left, preferred_element_type=jnp.float32
        ).astype(jnp.bfloat16)


def dnormed_kernel(
    wait, flush, got_ref, tokens_ref, ffn_ref, two_ref, q_ref, k_ref, v_ref,
    grads_ref, vec_ref, dn_ref,
):
    wide = lane_ids(HALF, 128) < HALF
    for pair in range(3):
        columns = slice(pair * 128, (pair + 1) * 128)
        key_columns = slice(384 + pair * 128, 512 + pair * 128)
        value_columns = slice(768 + pair * 128, 896 + pair * 128)
        for half in range(2):
            rows = slice(half * HALF, (half + 1) * HALF)
            even = got_ref[4 * pair + half, :96].astype(jnp.float32)
            odd = got_ref[4 * pair + 2 + half, :96].astype(jnp.float32)
            grads_ref[rows, key_columns] = jnp.where(wide, even[:HALF], turn(odd[:HALF])).astype(
                jnp.bfloat16
            )
            grads_ref[rows, value_columns] = jnp.where(
                wide, turn(even[:HALF]), odd[:HALF]
            ).astype(jnp.bfloat16)
            grads_ref[rows, columns] = pairs_low(even[HALF:], odd[HALF:]).astype(jnp.bfloat16)
    for ref in (q_ref, k_ref, v_ref):
        wait(ref)
    dnormed = (
        lax.dot_general(
            grads_ref[:, :384], q_ref[...], trans_right, preferred_element_type=jnp.float32
        )
        + lax.dot_general(
            grads_ref[:, 384:768], k_ref[...], trans_right, preferred_element_type=jnp.float32
        )
        + lax.dot_general(
            grads_ref[:, 768:], v_ref[...], trans_right, preferred_element_type=jnp.float32
        )
    )
    dn_ref[...] = dnormed.astype(jnp.bfloat16)
    _, unit, _ = norm_forward(tokens_ref[...].astype(jnp.float32), 1.0, 0.0)
    total = jnp.sum(grads_ref[...].astype(jnp.float32), axis=0, keepdims=True)
    vec_ref[:, :768] = jnp.sum(dnormed, axis=0, keepdims=True)
    vec_ref[:, 768:1536] = jnp.sum(dnormed * unit, axis=0, keepdims=True)
    vec_ref[:, 1536:1920] = total[:, :384]
    vec_ref[:, 1920:2304] = total[:, 768:]
    vec_ref[:, 2304:4608] = ffn_ref[...]
    vec_ref[:, 4608:] = two_ref[...]


def input_grad_kernel(
    wait, flush, dn_ref, other_ref, tokens_ref, cot_ref, exit_ref, gain_ref, dmid_ref, out_ref
):
    _, unit, inverse = norm_forward(tokens_ref[...].astype(jnp.float32), 1.0, 0.0)
    dnormed = dn_ref[...].astype(jnp.float32) + other_ref[...].astype(jnp.float32)
    active = column((exit_ref[...] > LAYER).astype(jnp.float32))
    out_ref[...] = (
        dmid_ref[...]
        + norm_backward(dnormed, unit, inverse, gain_ref[...])
        + jnp.where(active > 0.0, 0.0, cot_ref[...].astype(jnp.float32))
    )


def far_kernel(wait, flush, kept_ref, taken_ref, far_ref):
    far_ref[...] = (
        kept_ref[BLOCKS:].astype(jnp.float32) + taken_ref[BLOCKS:].astype(jnp.float32)
    ).astype(jnp.bfloat16)


def merge_kernel(
    wait, flush, kept_ref, taken_ref, far_ref, dq_ref, edge_ref, o_near_ref, o_far_ref, out_ref
):
    for block in range(BLOCKS):
        pair = (
            kept_ref[block].astype(jnp.float32)
            + taken_ref[block].astype(jnp.float32)
            + far_ref[block].astype(jnp.float32)
        )
        query = dq_ref[block]
        if block == BLOCKS - 1:
            pair = pair + edge_ref[:HALF].astype(jnp.float32)
            query = (query.astype(jnp.float32) + edge_ref[HALF:].astype(jnp.float32)).astype(
                jnp.bfloat16
            )
        out_ref[block, :HALF] = pair.astype(jnp.bfloat16)
        out_ref[block, HALF:96] = query
        product = o_near_ref[block] + o_far_ref[block].astype(jnp.float32)
        for tile in range(3):
            out_ref[block, 96 + 16 * tile : 112 + 16 * tile] = product[
                :, 128 * tile : 128 * tile + 128
            ].astype(jnp.bfloat16)


def o_sums_kernel(wait, flush, got_ref, out_ref):
    for tile in range(3):
        rows = slice(96 + 16 * tile, 112 + 16 * tile)
        total = got_ref[0, rows].astype(jnp.float32)
        for source in range(1, 16):
            total = total + got_ref[source, rows].astype(jnp.float32)
        out_ref[:, 128 * tile : 128 * tile + 128] = total[:12]


def qkv_products_kernel(
    wait, flush, keep_ref, sent_ref, grads_ref, grads_sent_ref, vec_ref, vec_sent_ref, out_ref
):
    lefts = jnp.concatenate([keep_ref[...], sent_ref[...]], axis=0)
    vec = vec_ref[...] + vec_sent_ref[...]
    lines = jnp.concatenate(
        [vec[:, 1152 * row : 1152 * (row + 1)] for row in range(6)]
        + [jnp.zeros((2, 1152), jnp.float32)],
        axis=0,
    )
    for at in range(0, 1152, 384):
        columns = slice(at, at + 384)
        rights = jnp.concatenate([grads_ref[:, columns], grads_sent_ref[:, columns]], axis=0)
        product = lax.dot_general(lefts, rights, trans_left, preferred_element_type=jnp.float32)
        for plane in range(16):
            out_ref[plane, :, columns] = jnp.concatenate(
                [product[24 * plane : 24 * plane + 24], lines[:, columns]], axis=0
            ).astype(jnp.bfloat16)


def plane_sums_kernel(wait, flush, got_ref, far_ref, norm_ref, near_ref):
    total = got_ref[0].astype(jnp.float32)
    for source in range(1, 16):
        total = total + got_ref[source].astype(jnp.float32)
    low = lax.axis_index("zh") == 0
    spare = jnp.zeros((4, 1152), jnp.float32)
    one, two, vec = total[:12], total[12:24], total[24:32]
    near_ref[...] = jnp.concatenate([jnp.where(low, one, two), spare, vec], axis=0)
    far_ref[...] = jnp.concatenate([jnp.where(low, two, one), spare, vec], axis=0)
    norm_ref[...] = vec


def finish_kernel(
    wait, flush, near_ref, far_ref, wa_ref, cross_ref,
    q_ref, k_ref, v_ref, shift_out, gain_out, q_bias_out, v_bias_out,
    up_bias_out, down_bias_out, gain_two_out, shift_two_out, o_bias_out,
):
    both = near_ref[...] + far_ref[...]
    q_ref[...] = both[:12, :384]
    k_ref[...] = both[:12, 384:768]
    v_ref[...] = both[:12, 768:]
    vec = both[16:24]
    norms = vec + (wa_ref[...] + cross_ref[...])
    shift_out[...] = norms[0:1, :768]
    gain_out[:, :384] = norms[0:1, 768:]
    gain_out[:, 384:] = norms[1:2, :384]
    q_bias_out[...] = vec[1:2, 384:768]
    v_bias_out[...] = vec[1:2, 768:]
    up_bias_out[:, :1152] = vec[2:3]
    up_bias_out[:, 1152:] = vec[3:4, :384]
    down_bias_out[...] = vec[3:4, 384:]
    gain_two_out[...] = vec[4:5, :768]
    shift_two_out[:, :384] = vec[4:5, 768:]
    shift_two_out[:, 384:] = vec[5:6, :384]
    o_bias_out[...] = vec[5:6, 384:]


def sub_sums(summed):
    mine = summed.shape[0] // 4
    parts = summed.reshape(4, mine, summed.shape[1])
    me = lax.axis_index(("zh", "core"))

    def part(index):
        return lax.dynamic_index_in_dim(parts, index, 0, keepdims=False)

    here = part(me)
    core_way = lax.ppermute(part(jnp.bitwise_xor(me, 1)), "core", SWAP)
    z_way = lax.ppermute(part(jnp.bitwise_xor(me, 2)), "zh", SWAP)
    cross_way = lax.ppermute(part(jnp.bitwise_xor(me, 3)), ("zh", "core"), CROSS)
    mine_sum, other_sum = here + z_way, core_way + cross_way
    first = lax.axis_index("core") == 0
    return jnp.where(first, mine_sum, other_sum), jnp.where(first, other_sum, mine_sum)


def on_device(
    tokens,
    doc_start,
    exit_layer,
    cotangent,
    ln1_gain,
    ln1_shift,
    q_weight,
    q_bias,
    k_weight,
    v_weight,
    v_bias,
    o_weight,
    o_bias,
    ln2_gain,
    ln2_shift,
    up_weight,
    up_bias,
    down_weight,
    down_bias,
):
    f32 = jnp.float32

    def copied(*arrays):
        return [("d", array) for array in arrays]

    payload, low_one = call(
        project_kernel, "project",
        copied(
            tokens, doc_start, ln1_gain, ln1_shift, q_bias, v_bias, q_weight, k_weight, v_weight
        ),
        [("d", whole(16, HALF + 48, 128)), ("d", whole(128, 768))],
        lazy=(6, 7, 8),
    )
    own = lax.all_to_all(payload, PLANE, 0, 0, tiled=True)
    low_one, o_given = lax.optimization_barrier((low_one, o_weight))
    o_other = lax.ppermute(o_given, "wa", SWAP)
    x_send, order, x_keep = call(
        prepare_kernel, "prepare",
        copied(low_one),
        [("v", whole(128, 384)), ("d", whole(768, 768)), ("d", whole(128, 384))],
    )
    own, x_send, o_other = lax.optimization_barrier((own, x_send, o_other))
    pairs = own[:, :HALF]
    one = lax.ppermute(pairs, "core", SWAP)
    edge = lax.ppermute(own[BLOCKS - 1], "y", ((1, 0), (3, 2)))
    two = lax.ppermute(pairs, "zh", SWAP)
    two, edge = lax.optimization_barrier((two, edge))
    three = lax.ppermute(two, "core", SWAP)
    x_sent = lax.ppermute(x_send, "core", SWAP)
    back, kv, q_rows, start_rows, full_rows = attend(own, one, two, three, edge)
    got = lax.all_to_all(back, ("x", "y", "wa"), 0, 0, tiled=True)
    dn_two, send, keep, middle, ffn, attn_low, vec_ffn = call(
        middle_kernel, "middle",
        [("v", got)]
        + copied(
            tokens, cotangent, exit_layer, o_bias, ln2_gain, ln2_shift, up_bias, o_weight, o_other,
            up_weight, down_weight,
        ),
        [
            ("v", whole(128, 768)),
            ("v", whole(128, 2304)),
            ("v", whole(128, 2304)),
            ("d", whole(128, 768, dtype=f32)),
            ("d", whole(128, 768)),
            ("d", whole(128, 384)),
            ("d", whole(1, 2304, dtype=f32)),
        ],
        [pltpu.VMEM((128, 384), jnp.bfloat16)],
        lazy=(8, 9, 10, 11),
    )
    dn_two_other = lax.ppermute(dn_two, "wa", SWAP)
    sent = lax.ppermute(send, "core", SWAP)
    ffn_products = call(
        ffn_products_kernel, "ffn_products",
        [("v", keep), ("v", sent)],
        [("d", whole(768, 1536))],
    )
    dh_payload, o_send, o_keep, dmiddle, vec_two = call(
        dheads_kernel, "dheads",
        [("v", dn_two), ("v", dn_two_other)]
        + copied(middle, cotangent, exit_layer, ln2_gain, o_weight, attn_low, order),
        [
            ("d", whole(16, HALF, 128)),
            ("v", whole(128, 768)),
            ("v", whole(128, 768)),
            ("d", whole(128, 768, dtype=f32)),
            ("d", whole(1, 2304, dtype=f32)),
        ],
        lazy=(6, 8),
    )
    dh = lax.all_to_all(dh_payload, PLANE, 0, 0, tiled=True)
    o_sent = lax.ppermute(o_send, "core", SWAP)
    o_far, o_near = call(
        o_products_kernel, "o_products",
        [("v", o_keep), ("v", o_sent)],
        [("v", whole(16, 16, 384)), ("d", whole(16, 16, 384, dtype=f32))],
    )
    o_got = lax.ppermute(o_far, "zh", SWAP)
    dh, ffn_products, o_got = lax.optimization_barrier((dh, ffn_products, o_got))
    ffn_blocks = lax.all_to_all(
        ffn_products.reshape(16, 48, 1536), PLANE, 0, 0, tiled=True
    )
    given, kept, dq, edge_grad = attend_grad(kv, q_rows, start_rows, full_rows, dh)
    edge_got = lax.ppermute(edge_grad, "y", ((0, 1), (2, 3)))
    taken = lax.ppermute(given, "core", SWAP)
    far = call(far_kernel, "far", [("v", kept), ("v", taken)], [("v", whole(BLOCKS, HALF, 128))])
    far = lax.ppermute(far, "zh", SWAP)
    merged = call(
        merge_kernel, "merge",
        [("v", kept), ("v", taken), ("v", far), ("v", dq), ("v", edge_got)] + copied(o_near, o_got),
        [("d", whole(BLOCKS, 144, 128))],
    )
    merged, ffn_blocks, ffn = lax.optimization_barrier((merged, ffn_blocks, ffn))
    grads = lax.all_to_all(merged, PLANE, 0, 0, tiled=True)
    grads_rows, vec, dn_one = call(
        dnormed_kernel, "dnormed",
        [("v", grads)] + copied(tokens, vec_ffn, vec_two, q_weight, k_weight, v_weight),
        [("v", whole(128, 1152)), ("v", whole(1, 6912, dtype=f32)), ("v", whole(128, 768))],
        lazy=(4, 5, 6),
    )
    o_weight_grad_t = call(
        o_sums_kernel, "o_sums", [("v", grads)], [("d", whole(12, 384, dtype=f32))]
    )
    grads_sent = lax.ppermute(grads_rows, "core", SWAP)
    vec_sent = lax.ppermute(vec, "core", SWAP)
    products = call(
        qkv_products_kernel, "qkv_products",
        copied(x_keep, x_sent)
        + [("v", grads_rows), ("v", grads_sent), ("v", vec), ("v", vec_sent)],
        [("d", whole(16, 32, 1152))],
    )
    products = lax.all_to_all(products, PLANE, 0, 0, tiled=True)
    far_sums, norm_sums, near_sums = call(
        plane_sums_kernel, "plane_sums",
        [("v", products)],
        [
            ("v", whole(24, 1152, dtype=f32)),
            ("v", whole(8, 1152, dtype=f32)),
            ("v", whole(24, 1152, dtype=f32)),
        ],
    )
    far_sums = lax.ppermute(far_sums, "zh", SWAP)
    wa_sums = lax.ppermute(norm_sums, "wa", SWAP)
    cross_sums = lax.ppermute(norm_sums, ("zh", "wa"), CROSS)
    dn_one_other = lax.ppermute(dn_one, "wa", SWAP)
    up_weight_grad, down_weight_grad_t = sub_sums(jnp.sum(ffn_blocks.astype(f32), axis=0))
    ffn_out = ffn.astype(f32) + lax.ppermute(ffn, "wa", SWAP).astype(f32) + down_bias
    output = jnp.where(
        (exit_layer > LAYER)[:, None], middle + ffn_out, tokens.astype(f32)
    ).astype(jnp.bfloat16)
    input_grad = call(
        input_grad_kernel, "input_grad",
        [("v", dn_one), ("v", dn_one_other)]
        + copied(tokens, cotangent, exit_layer, ln1_gain, dmiddle),
        [("d", whole(128, 768, dtype=f32))],
    )
    (
        q_weight_grad, k_weight_grad, v_weight_grad,
        ln1_shift_grad, ln1_gain_grad, q_bias_grad, v_bias_grad,
        up_bias_grad, down_bias_grad, ln2_gain_grad, ln2_shift_grad, o_bias_grad,
    ) = call(
        finish_kernel, "finish",
        [("v", near_sums), ("v", far_sums), ("v", wa_sums), ("v", cross_sums)],
        [("d", whole(12, 384, dtype=f32)) for _ in range(3)]
        + [
            ("d", whole(count, dtype=f32))
            for count in (768, 768, 384, 384, 1536, 768, 768, 768, 768)
        ],
    )
    return (
        output,
        input_grad,
        ln1_gain_grad,
        ln1_shift_grad,
        q_weight_grad,
        q_bias_grad,
        k_weight_grad,
        v_weight_grad,
        v_bias_grad,
        o_weight_grad_t,
        o_bias_grad,
        ln2_gain_grad,
        ln2_shift_grad,
        up_weight_grad,
        up_bias_grad,
        down_weight_grad_t,
        down_bias_grad,
    )


def solution(mesh):
    fine = Mesh(mesh.devices.reshape(4, 4, 2, 2, 2), CTX + ("wa",))
    return jax.shard_map(
        on_device,
        mesh=fine,
        in_specs=(
            P(CTX, None),
            P(CTX),
            P(CTX),
            P(CTX, None),
            P(),
            P(),
            P(None, "wa"),
            P("wa"),
            P(None, "wa"),
            P(None, "wa"),
            P("wa"),
            P("wa", None),
            P(),
            P(),
            P(),
            P(None, "wa"),
            P("wa"),
            P("wa", None),
            P(),
        ),
        out_specs=(
            P(CTX, None),
            P(CTX, None),
            P(),
            P(),
            P(CTX, "wa"),
            P("wa"),
            P(CTX, "wa"),
            P(CTX, "wa"),
            P("wa"),
            P(CTX, "wa"),
            P(),
            P(),
            P(),
            P(CTX, "wa"),
            P("wa"),
            P(CTX, "wa"),
            P(),
        ),
        check_vma=False,
    )
```

profile of v0, /device:TPU:1, one launch (start us, length us, event | category | flops | bytes accessed | tf_op | source)
XLA Modules:
  0.0 204.7 jit_solution(12847137905541947953)
XLA Ops:
  0.7 3.2 %project.1 = (bf16[16,112,128]{2,1,0:T(8,128)(2,1)}, bf16[128,768]{1,0:T(8,128)(2,1)}) custom-call(bf16[128,768]{1,0:T(8,128)(2,1)} %refs_2_.5, s32[128]{0:T(128)} %refs_1_.3, f32[768]{0:T(1024)} %refs_5_.9, f32[768]{0:T(1024)} %refs_3_.4, f32[384]{0:T(512)} %refs_4_.5, f32[384]{0:T(512)} %refs_5_.5, bf16[768,384]{1,0:T(8,128)(2,1)} %refs_4_.8, ...), custom_call_target="tpu_custom_call" | custom-call | tf_op jit(solution)/shard_map/project/pallas_call | solution.py:137
  3.9 2.5 %collective-permute-start = (bf16[384,768]{1,0:T(8,128)(2,1)}, bf16[384,768]{1,0:T(8,128)(2,1)}, u32[]{:S(2)}, u32[]{:S(2)}) collective-permute-start(bf16[384,768]{1,0:T(8,128)(2,1)} %refs_6_.6), channel_id=1, source_target_pairs={{0,1},{1,0},{2,3},{3,2},{4,5},{5,4},{6,7},{7,6},{8,9},{9,8},{10,11... | collective-permute-start | bytes 1769480 | tf_op jit(solution)/shard_map/ppermute | solution.py:840
  6.4 6.8 %all-to-all-start = ((bf16[16,112,128]{2,1,0:T(8,128)(2,1)}), bf16[16,112,128]{2,1,0:T(8,128)(2,1)}, u32[]{:S(2)}, u32[]{:S(2)}) async-start(bf16[16,112,128]{2,1,0:T(8,128)(2,1)} %get-tuple-element.76), calls=%async_computation | async-start | bytes 917504 | tf_op jit(solution)/shard_map/all_to_all | solution.py:838
  13.2 3.0 %prepare.1 = (bf16[128,384]{1,0:T(8,128)(2,1)}, bf16[768,768]{1,0:T(8,128)(2,1)}, bf16[128,384]{1,0:T(8,128)(2,1)}) custom-call(bf16[128,768]{1,0:T(8,128)(2,1)} %get-tuple-element.78.refs_0_), custom_call_target="tpu_custom_call" | custom-call | tf_op jit(solution)/shard_map/prepare/pallas_call | solution.py:137
  16.2 5.7 %all-to-all-done.refs_0_ = bf16[16,112,128]{2,1,0:T(8,128)(2,1)} async-done(((bf16[16,112,128]{2,1,0:T(8,128)(2,1)}), bf16[16,112,128]{2,1,0:T(8,128)(2,1)}, u32[]{:S(2)}, u32[]{:S(2)}) %all-to-all-start) | async-done | bytes 458784 | tf_op jit(solution)/shard_map/all_to_all | solution.py:838
  22.8 3.4 %collective-permute-start.2 = (bf16[16,64,128]{2,1,0:T(8,128)(2,1)S(1)}, bf16[16,64,128]{2,1,0:T(8,128)(2,1)S(1)}, u32[]{:S(2)}, u32[]{:S(2)}) collective-permute-start(bf16[16,64,128]{2,1,0:T(8,128)(2,1)S(1)} %slice.6), channel_id=1, source_target_pairs={{0,4},{4,0},{1,5},{5,1},{2,6},{6,2},{3,7},{7,3},{8,12},{12,8},{9,1... | collective-permute-start | bytes 786440 | tf_op jit(solution)/shard_map/ppermute | solution.py:850
  28.3 3.5 %collective-permute-start.1 = (bf16[16,64,128]{2,1,0:T(8,128)(2,1)S(1)}, bf16[16,64,128]{2,1,0:T(8,128)(2,1)}, u32[]{:S(2)}, u32[]{:S(2)}) collective-permute-start(bf16[16,64,128]{2,1,0:T(8,128)(2,1)S(1)} %slice.6), channel_id=1, source_target_pairs={{0,2},{2,0},{1,3},{3,1},{4,6},{6,4},{5,7},{7,5},{8,10},{10,8},{9,1... | collective-permute-start | bytes 786440 | tf_op jit(solution)/shard_map/ppermute | solution.py:848
  32.6 4.3 %collective-permute-start.4 = (bf16[16,64,128]{2,1,0:T(8,128)(2,1)S(1)}, bf16[16,64,128]{2,1,0:T(8,128)(2,1)}, u32[]{:S(2)}, u32[]{:S(2)}) collective-permute-start(bf16[16,64,128]{2,1,0:T(8,128)(2,1)S(1)} %collective-permute-done.2.refs_2_), channel_id=1, source_target_pairs={{0,2},{2,0},{1,3},{3,1},{4,6},{6,4},{5,7},{7,5},{8,10},{10,8},{9,1... | collective-permute-start | bytes 786440 | tf_op jit(solution)/shard_map/ppermute | solution.py:852
  36.9 1.3 collective-permute-done.4.refs_3_
  38.2 6.3 %attend.1 = (bf16[32,64,128]{2,1,0:T(8,128)(2,1)}, bf16[17,256,128]{2,1,0:T(8,128)(2,1)}, bf16[1088,128]{1,0:T(8,128)(2,1)}, f32[1088,128]{1,0:T(8,128)}, f32[1088,128]{1,0:T(8,128)}) custom-call(bf16[16,112,128]{2,1,0:T(8,128)(2,1)} %all-to-all-done.refs_0_, bf16[16,64,128]{2,1,0:T(8,128)(2,1)} %collective-permute-done.1.refs_1_, ...), custom_call_target="tpu_custom_call" | custom-call | tf_op jit(solution)/shard_map/attend/pallas_call | solution.py:137
  44.5 15.9 %all_to_all.30.refs_0_ = bf16[32,64,128]{2,1,0:T(8,128)(2,1)} all-to-all(bf16[32,64,128]{2,1,0:T(8,128)(2,1)} %get-tuple-element.84), channel_id=1, replica_groups=mesh['x'=4,'y'=4,'zh'=2,'core'=2,'wa'=2] {'x','y','wa'}, dimensions={0} | all-to-all | bytes 1048576 | tf_op jit(solution)/shard_map/all_to_all | solution.py:855
  60.4 8.4 %middle.1 = (bf16[128,768]{1,0:T(8,128)(2,1)}, bf16[128,2304]{1,0:T(8,128)(2,1)}, bf16[128,2304]{1,0:T(8,128)(2,1)}, f32[128,768]{1,0:T(8,128)}, bf16[128,768]{1...) custom-call(bf16[32,64,128]{2,1,0:T(8,128)(2,1)} %all_to_all.30.refs_0_, bf16[128,768]{1,0:T(8,128)(2,1)} %refs_2_.5, ...), custom_call_target="tpu_custom_call" | custom-call | tf_op jit(solution)/shard_map/middle/pallas_call | solution.py:137
  69.2 1.9 collective-permute-start.6
  71.2 2.5 %collective-permute-done.5.refs_1_ = bf16[128,768]{1,0:T(8,128)(2,1)} collective-permute-done((bf16[128,768]{1,0:T(8,128)(2,1)}, bf16[128,768]{1,0:T(8,128)(2,1)}, u32[]{:S(2)}, u32[]{:S(2)}) %collective-permute-start.5) | collective-permute-done | bytes 196640 | tf_op jit(solution)/shard_map/ppermute | solution.py:875
  73.7 4.8 %dheads.1 = (bf16[16,64,128]{2,1,0:T(8,128)(2,1)}, bf16[128,768]{1,0:T(8,128)(2,1)}, bf16[128,768]{1,0:T(8,128)(2,1)}, f32[128,768]{1,0:T(8,128)}, f32[1,2304]{1,0:T(1,128)}) custom-call(bf16[128,768]{1,0:T(8,128)(2,1)} %get-tuple-element.91.refs_0_, bf16[128,768]{1,0:T(8,128)(2,1)} %collective-permute-done.5.refs_1_, f32[128,768]{1,0:T(8,128)} %get-tuple-element.86.refs_2_, ...), custom_call_target="tpu_custom_call" | custom-call | tf_op jit(solution)/shard_map/dheads/pallas_call | solution.py:137
  78.5 2.9 %collective-permute-start.7 = (bf16[128,768]{1,0:T(8,128)(2,1)}, bf16[128,768]{1,0:T(8,128)(2,1)}, u32[]{:S(2)}, u32[]{:S(2)}) collective-permute-start(bf16[128,768]{1,0:T(8,128)(2,1)} %get-tuple-element.98), channel_id=1, source_target_pairs={{0,2},{2,0},{1,3},{3,1},{4,6},{6,4},{5,7},{7,5},{8,10},{10,8},{9,1... | collective-permute-start | bytes 589832 | tf_op jit(solution)/shard_map/ppermute | solution.py:896
  81.4 4.2 %all-to-all-start.2 = ((bf16[16,64,128]{2,1,0:T(8,128)(2,1)}), bf16[16,64,128]{2,1,0:T(8,128)(2,1)}, u32[]{:S(2)}, u32[]{:S(2)}) async-start(bf16[16,64,128]{2,1,0:T(8,128)(2,1)} %get-tuple-element.94), calls=%async_computation.2 | async-start | bytes 524288 | tf_op jit(solution)/shard_map/all_to_all | solution.py:895
  85.6 2.8 %o_products.1 = (bf16[16,16,384]{2,1,0:T(8,128)(2,1)}, f32[16,16,384]{2,1,0:T(8,128)}) custom-call(bf16[128,768]{1,0:T(8,128)(2,1)} %get-tuple-element.97.refs_0_, bf16[128,768]{1,0:T(8,128)(2,1)} %collective-permute-done.7.refs_1_), custom_call_target="tpu_custom_call" | custom-call | tf_op jit(solution)/shard_map/o_products/pallas_call | solution.py:137
  88.4 1.9 collective-permute-start.8
  90.3 3.7 %ffn_products.1 = bf16[768,1536]{1,0:T(8,128)(2,1)} custom-call(bf16[128,2304]{1,0:T(8,128)(2,1)} %get-tuple-element.95.refs_0_, bf16[128,2304]{1,0:T(8,128)(2,1)} %collective-permute-done.6.refs_1_), custom_call_target="tpu_custom_call" | custom-call | tf_op jit(solution)/shard_map/ffn_products/pallas_call | solution.py:137
  94.0 3.0 %collective-permute-done.8.refs_6_ = bf16[16,16,384]{2,1,0:T(8,128)(2,1)} collective-permute-done((bf16[16,16,384]{2,1,0:T(8,128)(2,1)}, bf16[16,16,384]{2,1,0:T(8,128)(2,1)}, u32[]{:S(2)}, u32[]{:S(2)}) %collective-permute-start.8) | collective-permute-done | bytes 196640 | tf_op jit(solution)/shard_map/ppermute | solution.py:902
  97.0 6.3 %all-to-all-start.3 = ((bf16[16,48,1536]{2,1,0:T(8,128)(2,1)}), bf16[16,48,1536]{2,1,0:T(8,128)(2,1)}, u32[]{:S(2)}, u32[]{:S(2)}) async-start(bf16[16,48,1536]{2,1,0:T(8,128)(2,1)} %bitcast.15), calls=%async_computation.3 | async-start | bytes 4718592 | tf_op jit(solution)/shard_map/all_to_all | solution.py:904
  103.2 13.4 %attend_grad.1 = (bf16[32,64,128]{2,1,0:T(8,128)(2,1)}, bf16[32,64,128]{2,1,0:T(8,128)(2,1)}, bf16[16,32,128]{2,1,0:T(8,128)(2,1)}, bf16[96,128]{1,0:T(8,128)(2,1)}) custom-call(bf16[17,256,128]{2,1,0:T(8,128)(2,1)} %get-tuple-element.87.refs_0_, bf16[1088,128]{1,0:T(8,128)(2,1)} %get-tuple-element.88.refs_1_, f32[1088,128]{1,0:T(8,128)} %get-tuple-element.89.refs_2_, ...), custom_call_target="tpu_custom_call" | custom-call | tf_op jit(solution)/shard_map/attend_grad/pallas_call | solution.py:137
  116.6 1.5 collective-permute-start.9
  118.1 1.9 collective-permute-done.9.refs_1_
  120.0 2.0 far.1
  122.0 1.7 collective-permute-start.10
  123.7 4.1 %collective-permute-start.11 = (bf16[96,128]{1,0:T(8,128)(2,1)}, bf16[96,128]{1,0:T(8,128)(2,1)}, u32[]{:S(2)}, u32[]{:S(2)}) collective-permute-start(bf16[96,128]{1,0:T(8,128)(2,1)} %get-tuple-element.104), channel_id=1, source_target_pairs={{0,8},{16,24},{1,9},{17,25},{2,10},{18,26},{3,11},{19,27},{4,12},{... | collective-permute-start | bytes 73736 | tf_op jit(solution)/shard_map/ppermute | solution.py:908
  127.8 1.7 collective-permute-done.11.refs_4_
  129.5 1.9 collective-permute-done.10.refs_2_
  131.4 3.3 %merge.1 = bf16[16,144,128]{2,1,0:T(8,128)(2,1)} custom-call(bf16[32,64,128]{2,1,0:T(8,128)(2,1)} %get-tuple-element.101.refs_0_, bf16[32,64,128]{2,1,0:T(8,128)(2,1)} %collective-permute-done.9.refs_1_, bf16[16,64,128]{2,1,0:T(8,128)(2,1)} %collective-permute-done.10.refs_2_, bf16[16,32,128]{2,1,0:T(8,128)(2,1)} %get-tuple-element.103.refs_3_, ...), custom_call_target="tpu_custom_call" | custom-call | tf_op jit(solution)/shard_map/merge/pallas_call | solution.py:137
  134.8 20.8 %all_to_all.31.refs_0_ = bf16[16,144,128]{2,1,0:T(8,128)(2,1)} all-to-all(bf16[16,144,128]{2,1,0:T(8,128)(2,1)} %merge.1), channel_id=1, replica_groups=mesh['x'=4,'y'=4,'zh'=2,'core'=2,'wa'=2] {'x','y'}, dimensions={0} | all-to-all | bytes 1179648 | tf_op jit(solution)/shard_map/all_to_all | solution.py:918
  155.6 4.1 %dnormed.1 = (bf16[128,1152]{1,0:T(8,128)(2,1)}, f32[1,6912]{1,0:T(1,128)}, bf16[128,768]{1,0:T(8,128)(2,1)}) custom-call(bf16[16,144,128]{2,1,0:T(8,128)(2,1)} %all_to_all.31.refs_0_, bf16[128,768]{1,0:T(8,128)(2,1)} %refs_2_.5, f32[1,2304]{1,0:T(1,128)} %get-tuple-element.111.refs_2_, f32[1,2304]{1,0:T(1,128)} %get-tuple-element.112.refs_3_, ...), custom_call_target="tpu_custom_call" | custom-call | tf_op jit(solution)/shard_map/dnormed/pallas_call | solution.py:137
  159.7 1.8 collective-permute-start.15
  163.3 3.5 %qkv_products.1 = bf16[16,32,1152]{2,1,0:T(8,128)(2,1)} custom-call(bf16[128,384]{1,0:T(8,128)(2,1)} %get-tuple-element.115.refs_0_, bf16[128,384]{1,0:T(8,128)(2,1)} %collective-permute-done.14.refs_1_, bf16[128,1152]{1,0:T(8,128)(2,1)} %get-tuple-element.117.refs_2_, bf16[128,1152]{1,0:T(8,128)(2,1)} %collective-permute-done.15.refs_3_, ...), custom_call_target="tpu_custom_call" | custom-call | tf_op jit(solution)/shard_map/qkv_products/pallas_call | solution.py:137
  166.8 4.4 %all-to-all-start.5 = ((bf16[16,32,1152]{2,1,0:T(8,128)(2,1)}), bf16[16,32,1152]{2,1,0:T(8,128)(2,1)}, u32[]{:S(2)}, u32[]{:S(2)}) async-start(bf16[16,32,1152]{2,1,0:T(8,128)(2,1)} %qkv_products.1), calls=%async_computation.5 | async-start | bytes 2359296 | tf_op jit(solution)/shard_map/all_to_all | solution.py:936
  171.3 2.0 convert_reduce_fusion
  173.4 1.7 collective-permute-start.20
  177.7 1.4 collective-permute-done.20
  179.1 3.4 %collective-permute-done.22 = f32[12,1536]{1,0:T(8,128)S(1)} collective-permute-done((f32[12,1536]{1,0:T(8,128)S(1)}, f32[12,1536]{1,0:T(8,128)S(1)}, u32[]{:S(2)}, u32[]{:S(2)}) %collective-permute-start.22) | collective-permute-done | bytes 73760 | tf_op jit(solution)/shard_map/ppermute | solution.py:798
  183.7 6.5 %all-to-all-done.5.refs_0_ = bf16[16,32,1152]{2,1,0:T(8,128)(2,1)} async-done(((bf16[16,32,1152]{2,1,0:T(8,128)(2,1)}), bf16[16,32,1152]{2,1,0:T(8,128)(2,1)}, u32[]{:S(2)}, u32[]{:S(2)}) %all-to-all-start.5) | async-done | bytes 1179680 | tf_op jit(solution)/shard_map/all_to_all | solution.py:936
  190.2 2.1 %plane_sums.1 = (f32[24,1152]{1,0:T(8,128)}, f32[8,1152]{1,0:T(8,128)}, f32[24,1152]{1,0:T(8,128)}) custom-call(bf16[16,32,1152]{2,1,0:T(8,128)(2,1)} %all-to-all-done.5.refs_0_), custom_call_target="tpu_custom_call" | custom-call | tf_op jit(solution)/shard_map/plane_sums/pallas_call | solution.py:137
  192.8 1.6 collective-permute-start.19
  194.3 1.4 collective-permute-start.17
  195.7 2.0 select_convert_fusion
  197.7 1.7 o_sums.1
  199.4 3.4 %input_grad.1 = f32[128,768]{1,0:T(8,128)} custom-call(bf16[128,768]{1,0:T(8,128)(2,1)} %get-tuple-element.113.refs_0_, bf16[128,768]{1,0:T(8,128)(2,1)} %collective-permute-done.13.refs_1_, bf16[128,768]{1,0:T(8,128)(2,1)} %refs_2_.5, bf16[128,768]{1,0:T(8,128)(2,1)} %refs_3_.7, s32[128]{0:T(128)} %refs_4_.9, f32[768]{0:T(1024)} %refs_5_.9, ...), custom_call_target="tpu_custom_call" | custom-call | tf_op jit(solution)/shard_map/input_grad/pallas_call | solution.py:137
  202.9 1.7 finish.1
  (38 shorter events, 10.4 us)
Async XLA Ops:
  3.9 18.0 %collective-permute-start = (bf16[384,768]{1,0:T(8,128)(2,1)}, bf16[384,768]{1,0:T(8,128)(2,1)}, u32[]{:S(2)}, u32[]{:S(2)}) collective-permute-start(bf16[384,768]{1,0:T(8,128)(2,1)} %refs_6_.6), channel_id=1, source_target_pairs={{0,1},{1,0},{2,3},{3,2},{4,5},{5,4},{6,7},{7,6},{8,9},{9,8},{10,11... | collective-permute-start | bytes 1769480 | tf_op jit(solution)/shard_map/ppermute | solution.py:840
  6.4 15.5 %all-to-all-start = ((bf16[16,112,128]{2,1,0:T(8,128)(2,1)}), bf16[16,112,128]{2,1,0:T(8,128)(2,1)}, u32[]{:S(2)}, u32[]{:S(2)}) async-start(bf16[16,112,128]{2,1,0:T(8,128)(2,1)} %get-tuple-element.76), calls=%async_computation | async-start | bytes 917504 | tf_op jit(solution)/shard_map/all_to_all | solution.py:838
  22.8 9.0 %collective-permute-start.2 = (bf16[16,64,128]{2,1,0:T(8,128)(2,1)S(1)}, bf16[16,64,128]{2,1,0:T(8,128)(2,1)S(1)}, u32[]{:S(2)}, u32[]{:S(2)}) collective-permute-start(bf16[16,64,128]{2,1,0:T(8,128)(2,1)S(1)} %slice.6), channel_id=1, source_target_pairs={{0,4},{4,0},{1,5},{5,1},{2,6},{6,2},{3,7},{7,3},{8,12},{12,8},{9,1... | collective-permute-start | bytes 786440 | tf_op jit(solution)/shard_map/ppermute | solution.py:850
  27.0 4.9 %collective-permute-start.3 = (bf16[112,128]{1,0:T(8,128)(2,1)S(1)}, bf16[112,128]{1,0:T(8,128)(2,1)S(1)}, u32[]{:S(2)}, u32[]{:S(2)}) collective-permute-start(bf16[112,128]{1,0:T(8,128)(2,1)S(1)} %slice_bitcast_fusion), channel_id=1, source_target_pairs={{8,0},{24,16},{9,1},{25,17},{10,2},{26,18},{11,3},{27,19},{12,4},{... | collective-permute-start | bytes 86024 | tf_op jit(solution)/shard_map/ppermute | solution.py:849
  28.3 8.6 %collective-permute-start.1 = (bf16[16,64,128]{2,1,0:T(8,128)(2,1)S(1)}, bf16[16,64,128]{2,1,0:T(8,128)(2,1)}, u32[]{:S(2)}, u32[]{:S(2)}) collective-permute-start(bf16[16,64,128]{2,1,0:T(8,128)(2,1)S(1)} %slice.6), channel_id=1, source_target_pairs={{0,2},{2,0},{1,3},{3,1},{4,6},{6,4},{5,7},{7,5},{8,10},{10,8},{9,1... | collective-permute-start | bytes 786440 | tf_op jit(solution)/shard_map/ppermute | solution.py:848
  31.9 5.0 %copy-start.1 = (bf16[112,128]{1,0:T(8,128)(2,1)}, bf16[112,128]{1,0:T(8,128)(2,1)S(1)}, u32[]{:S(2)}) copy-start(bf16[112,128]{1,0:T(8,128)(2,1)S(1)} %collective-permute-done.3.refs_4_) | copy-start | bytes 86020
  31.9 0.7 copy-start
  32.6 5.6 %collective-permute-start.4 = (bf16[16,64,128]{2,1,0:T(8,128)(2,1)S(1)}, bf16[16,64,128]{2,1,0:T(8,128)(2,1)}, u32[]{:S(2)}, u32[]{:S(2)}) collective-permute-start(bf16[16,64,128]{2,1,0:T(8,128)(2,1)S(1)} %collective-permute-done.2.refs_2_), channel_id=1, source_target_pairs={{0,2},{2,0},{1,3},{3,1},{4,6},{6,4},{5,7},{7,5},{8,10},{10,8},{9,1... | collective-permute-start | bytes 786440 | tf_op jit(solution)/shard_map/ppermute | solution.py:852
  68.8 4.9 %collective-permute-start.5 = (bf16[128,768]{1,0:T(8,128)(2,1)}, bf16[128,768]{1,0:T(8,128)(2,1)}, u32[]{:S(2)}, u32[]{:S(2)}) collective-permute-start(bf16[128,768]{1,0:T(8,128)(2,1)} %get-tuple-element.91.refs_0_), channel_id=1, source_target_pairs={{0,1},{1,0},{2,3},{3,2},{4,5},{5,4},{6,7},{7,6},{8,9},{9,8},{10,11... | collective-permute-start | bytes 589832 | tf_op jit(solution)/shard_map/ppermute | solution.py:875
  69.2 21.0 %collective-permute-start.6 = (bf16[128,2304]{1,0:T(8,128)(2,1)}, bf16[128,2304]{1,0:T(8,128)(2,1)}, u32[]{:S(2)}, u32[]{:S(2)}) collective-permute-start(bf16[128,2304]{1,0:T(8,128)(2,1)} %get-tuple-element.96), channel_id=1, source_target_pairs={{0,2},{2,0},{1,3},{3,1},{4,6},{6,4},{5,7},{7,5},{8,10},{10,8},{9,1... | collective-permute-start | bytes 1769480 | tf_op jit(solution)/shard_map/ppermute | solution.py:876
  78.5 7.1 %collective-permute-start.7 = (bf16[128,768]{1,0:T(8,128)(2,1)}, bf16[128,768]{1,0:T(8,128)(2,1)}, u32[]{:S(2)}, u32[]{:S(2)}) collective-permute-start(bf16[128,768]{1,0:T(8,128)(2,1)} %get-tuple-element.98), channel_id=1, source_target_pairs={{0,2},{2,0},{1,3},{3,1},{4,6},{6,4},{5,7},{7,5},{8,10},{10,8},{9,1... | collective-permute-start | bytes 589832 | tf_op jit(solution)/shard_map/ppermute | solution.py:896
  81.4 12.6 %all-to-all-start.2 = ((bf16[16,64,128]{2,1,0:T(8,128)(2,1)}), bf16[16,64,128]{2,1,0:T(8,128)(2,1)}, u32[]{:S(2)}, u32[]{:S(2)}) async-start(bf16[16,64,128]{2,1,0:T(8,128)(2,1)} %get-tuple-element.94), calls=%async_computation.2 | async-start | bytes 524288 | tf_op jit(solution)/shard_map/all_to_all | solution.py:895
  88.4 8.6 %collective-permute-start.8 = (bf16[16,16,384]{2,1,0:T(8,128)(2,1)}, bf16[16,16,384]{2,1,0:T(8,128)(2,1)}, u32[]{:S(2)}, u32[]{:S(2)}) collective-permute-start(bf16[16,16,384]{2,1,0:T(8,128)(2,1)} %get-tuple-element.99), channel_id=1, source_target_pairs={{0,4},{4,0},{1,5},{5,1},{2,6},{6,2},{3,7},{7,3},{8,12},{12,8},{9,1... | collective-permute-start | bytes 589832 | tf_op jit(solution)/shard_map/ppermute | solution.py:902
  97.0 37.8 %all-to-all-start.3 = ((bf16[16,48,1536]{2,1,0:T(8,128)(2,1)}), bf16[16,48,1536]{2,1,0:T(8,128)(2,1)}, u32[]{:S(2)}, u32[]{:S(2)}) async-start(bf16[16,48,1536]{2,1,0:T(8,128)(2,1)} %bitcast.15), calls=%async_computation.3 | async-start | bytes 4718592 | tf_op jit(solution)/shard_map/all_to_all | solution.py:904
  116.6 3.4 %collective-permute-start.9 = (bf16[32,64,128]{2,1,0:T(8,128)(2,1)}, bf16[32,64,128]{2,1,0:T(8,128)(2,1)}, u32[]{:S(2)}, u32[]{:S(2)}) collective-permute-start(bf16[32,64,128]{2,1,0:T(8,128)(2,1)} %get-tuple-element.102), channel_id=1, source_target_pairs={{0,2},{2,0},{1,3},{3,1},{4,6},{6,4},{5,7},{7,5},{8,10},{10,8},{9,1... | collective-permute-start | bytes 1572872 | tf_op jit(solution)/shard_map/ppermute | solution.py:909
  122.0 9.4 %collective-permute-start.10 = (bf16[16,64,128]{2,1,0:T(8,128)(2,1)}, bf16[16,64,128]{2,1,0:T(8,128)(2,1)}, u32[]{:S(2)}, u32[]{:S(2)}) collective-permute-start(bf16[16,64,128]{2,1,0:T(8,128)(2,1)} %far.1), channel_id=1, source_target_pairs={{0,4},{4,0},{1,5},{5,1},{2,6},{6,2},{3,7},{7,3},{8,12},{12,8},{9,1... | collective-permute-start | bytes 786440 | tf_op jit(solution)/shard_map/ppermute | solution.py:911
  123.7 5.8 %collective-permute-start.11 = (bf16[96,128]{1,0:T(8,128)(2,1)}, bf16[96,128]{1,0:T(8,128)(2,1)}, u32[]{:S(2)}, u32[]{:S(2)}) collective-permute-start(bf16[96,128]{1,0:T(8,128)(2,1)} %get-tuple-element.104), channel_id=1, source_target_pairs={{0,8},{16,24},{1,9},{17,25},{2,10},{18,26},{3,11},{19,27},{4,12},{... | collective-permute-start | bytes 73736 | tf_op jit(solution)/shard_map/ppermute | solution.py:908
  159.7 3.6 %collective-permute-start.15 = (bf16[128,1152]{1,0:T(8,128)(2,1)}, bf16[128,1152]{1,0:T(8,128)(2,1)}, u32[]{:S(2)}, u32[]{:S(2)}) collective-permute-start(bf16[128,1152]{1,0:T(8,128)(2,1)} %get-tuple-element.117.refs_2_), channel_id=1, source_target_pairs={{0,2},{2,0},{1,3},{3,1},{4,6},{6,4},{5,7},{7,5},{8,10},{10,8},{9,1... | collective-permute-start | bytes 884744 | tf_op jit(solution)/shard_map/ppermute | solution.py:928
  161.4 1.7 collective-permute-start.14
  161.8 1.5 collective-permute-start.16
  166.8 23.3 %all-to-all-start.5 = ((bf16[16,32,1152]{2,1,0:T(8,128)(2,1)}), bf16[16,32,1152]{2,1,0:T(8,128)(2,1)}, u32[]{:S(2)}, u32[]{:S(2)}) async-start(bf16[16,32,1152]{2,1,0:T(8,128)(2,1)} %qkv_products.1), calls=%async_computation.5 | async-start | bytes 2359296 | tf_op jit(solution)/shard_map/all_to_all | solution.py:936
  171.2 5.6 %copy-start.2 = (s32[128]{0:T(128)S(1)}, s32[128]{0:T(128)}, u32[]{:S(2)}) copy-start(s32[128]{0:T(128)} %refs_4_.9) | copy-start | bytes 1540
  173.4 5.7 %collective-permute-start.20 = (f32[12,1536]{1,0:T(8,128)S(1)}, f32[12,1536]{1,0:T(8,128)S(1)}, u32[]{:S(2)}, u32[]{:S(2)}) collective-permute-start(f32[12,1536]{1,0:T(8,128)S(1)} %get-tuple-element.137), channel_id=1, source_target_pairs={{0,4},{4,0},{1,5},{5,1},{2,6},{6,2},{3,7},{7,3},{8,12},{12,8},{9,1... | collective-permute-start | bytes 221192 | tf_op jit(solution)/shard_map/ppermute | solution.py:797
  175.1 4.0 %collective-permute-start.21 = (f32[12,1536]{1,0:T(8,128)S(1)}, f32[12,1536]{1,0:T(8,128)S(1)}, u32[]{:S(2)}, u32[]{:S(2)}) collective-permute-start(f32[12,1536]{1,0:T(8,128)S(1)} %get-tuple-element.139), channel_id=1, source_target_pairs={{0,2},{2,0},{1,3},{3,1},{4,6},{6,4},{5,7},{7,5},{8,10},{10,8},{9,1... | collective-permute-start | bytes 221192 | tf_op jit(solution)/shard_map/ppermute | solution.py:796
  175.6 7.0 %collective-permute-start.22 = (f32[12,1536]{1,0:T(8,128)S(1)}, f32[12,1536]{1,0:T(8,128)S(1)}, u32[]{:S(2)}, u32[]{:S(2)}) collective-permute-start(f32[12,1536]{1,0:T(8,128)S(1)} %get-tuple-element.138), channel_id=1, source_target_pairs={{0,6},{2,4},{4,2},{6,0},{1,7},{3,5},{5,3},{7,1},{8,14},{10,12},{12... | collective-permute-start | bytes 221192 | tf_op jit(solution)/shard_map/ppermute | solution.py:798
  177.3 18.3 %collective-permute-start.12 = (bf16[128,768]{1,0:T(8,128)(2,1)}, bf16[128,768]{1,0:T(8,128)(2,1)}, u32[]{:S(2)}, u32[]{:S(2)}) collective-permute-start(bf16[128,768]{1,0:T(8,128)(2,1)} %get-tuple-element.109), channel_id=1, source_target_pairs={{0,1},{1,0},{2,3},{3,2},{4,5},{5,4},{6,7},{7,6},{8,9},{9,8},{10,11... | collective-permute-start | bytes 589832 | tf_op jit(solution)/shard_map/ppermute | solution.py:951
  183.2 16.2 %collective-permute-start.13 = (bf16[128,768]{1,0:T(8,128)(2,1)}, bf16[128,768]{1,0:T(8,128)(2,1)}, u32[]{:S(2)}, u32[]{:S(2)}) collective-permute-start(bf16[128,768]{1,0:T(8,128)(2,1)} %get-tuple-element.113.refs_0_), channel_id=1, source_target_pairs={{0,1},{1,0},{2,3},{3,2},{4,5},{5,4},{6,7},{7,6},{8,9},{9,8},{10,11... | collective-permute-start | bytes 589832 | tf_op jit(solution)/shard_map/ppermute | solution.py:949
  192.3 10.5 %collective-permute-start.18 = (f32[8,1152]{1,0:T(8,128)}, f32[8,1152]{1,0:T(8,128)}, u32[]{:S(2)}, u32[]{:S(2)}) collective-permute-start(f32[8,1152]{1,0:T(8,128)} %get-tuple-element.121), channel_id=1, source_target_pairs={{0,1},{1,0},{2,3},{3,2},{4,5},{5,4},{6,7},{7,6},{8,9},{9,8},{10,11... | collective-permute-start | bytes 110600 | tf_op jit(solution)/shard_map/ppermute | solution.py:947
  192.8 10.1 %collective-permute-start.19 = (f32[8,1152]{1,0:T(8,128)}, f32[8,1152]{1,0:T(8,128)}, u32[]{:S(2)}, u32[]{:S(2)}) collective-permute-start(f32[8,1152]{1,0:T(8,128)} %get-tuple-element.121), channel_id=1, source_target_pairs={{0,5},{1,4},{4,1},{5,0},{2,7},{3,6},{6,3},{7,2},{8,13},{9,12},{12,... | collective-permute-start | bytes 110600 | tf_op jit(solution)/shard_map/ppermute | solution.py:948
  194.3 8.5 %collective-permute-start.17 = (f32[24,1152]{1,0:T(8,128)}, f32[24,1152]{1,0:T(8,128)}, u32[]{:S(2)}, u32[]{:S(2)}) collective-permute-start(f32[24,1152]{1,0:T(8,128)} %get-tuple-element.120), channel_id=1, source_target_pairs={{0,4},{4,0},{1,5},{5,1},{2,6},{6,2},{3,7},{7,3},{8,12},{12,8},{9,1... | collective-permute-start | bytes 331784 | tf_op jit(solution)/shard_map/ppermute | solution.py:946
where the time goes:
time: 207 us; the launch traced here: 205 us
  Pallas kernels  67.4 us (33%)
  starting transfers between devices  60.9 us (29%)
  blocking collectives  36.7 us (18%)
  waiting for transfers between devices  30.9 us (15%)
  other arithmetic  5.22 us (3%)
  local copies, waits for them, and re-layouts  2.5 us (1%)
    pallas_call x16, Pallas kernels, call(): pl.pallas_call(body, out_shape=tuple((out for _, out in outs)), in_specs=...  67.4 us
    all_to_all x1, blocking collectives, on_device(): grads = lax.all_to_all(merged, PLANE, 0, 0, tiled=True)  20.8 us
    all_to_all x1, blocking collectives, on_device(): got = lax.all_to_all(back, ('x', 'y', 'wa'), 0, 0, tiled=True)  15.9 us
    all_to_all x1, starting transfers between devices, on_device(): own = lax.all_to_all(payload, PLANE, 0, 0, tiled=True)  6.8 us
    all_to_all x1, waiting for transfers between devices, on_device(): products = lax.all_to_all(products, PLANE, 0, 0, tiled=True)  6.52 us
    all_to_all x1, starting transfers between devices, on_device(): lax.all_to_all(ffn_products.reshape(16, 48, 1536), PLANE, 0, 0, tiled=True)  6.25 us
    all_to_all x1, waiting for transfers between devices, on_device(): own = lax.all_to_all(payload, PLANE, 0, 0, tiled=True)  5.66 us
    all_to_all x1, starting transfers between devices, on_device(): products = lax.all_to_all(products, PLANE, 0, 0, tiled=True)  4.39 us
  transfers between devices with their start and end apart: 27, of which 13 were waited for; matrix products, arithmetic and copies ran while one was open for 3% of the time, Pallas kernels for 20%

commit v1 on v0

--- a/solution.py
+++ b/solution.py
@@ -10,6 +10,7 @@
 HEAD_DIM = 64
 LAYER = 6
 CTX = ("x", "y", "zh", "core")
+CHIPS = ("x", "y", "zh")
 PLANE = ("x", "y")
 SWAP = ((0, 1), (1, 0))
 CROSS = ((0, 3), (1, 2), (2, 1), (3, 0))
@@ -80,7 +81,7 @@
     )
 
 
-def call(kernel, name, ins, outs, scratch=(), lazy=()):
+def call(kernel, name, ins, outs, scratch=(), lazy=(), cost=2):
     copied_in = [at for at, (mode, _) in enumerate(ins) if mode == "d"]
     copied_out = [at for at, (mode, _) in enumerate(outs) if mode == "d"]
 
@@ -147,6 +148,9 @@
         ]
         + list(scratch),
         compiler_params=pltpu.CompilerParams(vmem_limit_bytes=VMEM_BYTES),
+        cost_estimate=pl.CostEstimate(
+            flops=cost * 10**9, transcendentals=0, bytes_accessed=0
+        ),
         name=name,
     )(*[array for _, array in ins])
     return result[0] if len(outs) == 1 else result
@@ -386,6 +390,7 @@
             ("d", whole(ROWS, 128, dtype=f32)),
         ],
         [pltpu.VMEM((ROWS, 128), f32), pltpu.VMEM((ROWS, 128), f32)],
+        cost=3,
     )
 
 
@@ -406,6 +411,7 @@
             pltpu.VMEM((ROWS, 128), f32),
         ],
         lazy=(0, 1, 2, 3),
+        cost=40,
     )
 
 
@@ -470,21 +476,18 @@
     pay_ref[12:] = jnp.zeros((4, HALF + 48, 128), jnp.bfloat16)
 
 
-def prepare_kernel(wait, flush, low_ref, send_ref, order_ref, keep_ref):
-    lane = lane_ids(8, 768)
-    core = (lane >= 384).astype(jnp.int32)
-    rest = lane - 384 * core
-    plane = (rest * 171) >> 12
-    within = rest - 24 * plane
-    high = (within >= 12).astype(jnp.int32)
-    source = (48 * plane + 12 * (2 * high + core) + (within - 12 * high))[:1]
-    order = jnp.where(row_ids_of(768, 768) == source, 1.0, 0.0).astype(jnp.bfloat16)
-    order_ref[...] = order
-    flush(order_ref)
+def prepare_kernel(wait, flush, low_ref, send_ref, keep_ref):
+    lane = lane_ids(8, 1024)
+    core = lane >> 9
+    chip = (lane >> 4) & 31
+    rest = lane & 15
+    row = 48 * (chip >> 1) + 24 * (chip & 1) + 12 * core + rest
+    source = jnp.where(rest < 12, row, -1)[:1]
+    order = jnp.where(row_ids_of(768, 1024) == source, 1.0, 0.0).astype(jnp.bfloat16)
     ordered = jnp.dot(low_ref[...], order, preferred_element_type=jnp.float32).astype(jnp.bfloat16)
     first = lax.axis_index("core") == 0
-    keep_ref[...] = jnp.where(first, ordered[:, :384], ordered[:, 384:])
-    send_ref[...] = jnp.where(first, ordered[:, 384:], ordered[:, :384])
+    keep_ref[...] = jnp.where(first, ordered[:, :512], ordered[:, 512:])
+    send_ref[...] = jnp.where(first, ordered[:, 512:], ordered[:, :512])
 
 
 def attn_tile(got_ref, side, pair):
@@ -504,13 +507,25 @@
     return jnp.concatenate(parts, axis=0).astype(jnp.bfloat16)
 
 
+def branch_of(cot_ref, exit_ref):
+    active = column((exit_ref[...] > LAYER).astype(jnp.float32))
+    return jnp.where(active > 0.0, cot_ref[...].astype(jnp.float32), 0.0)
+
+
+def dhidden_kernel(wait, flush, cot_ref, exit_ref, down_ref, out_ref, vec_ref):
+    branch = branch_of(cot_ref, exit_ref)
+    vec_ref[...] = jnp.sum(branch, axis=0, keepdims=True)
+    out_ref[...] = lax.dot_general(
+        branch.astype(jnp.bfloat16), down_ref[...], trans_right, preferred_element_type=jnp.float32
+    )
+
+
 def middle_kernel(
     wait, flush, got_ref, tokens_ref, cot_ref, exit_ref, o_bias_ref, gain_ref, shift_ref,
-    up_bias_ref, o_own_ref, o_other_ref, up_ref, down_ref,
-    dn_ref, send_ref, keep_ref, mid_ref, ffn_ref, attn_ref, vec_ref,
-    acc_ref,
-):
-    first = lax.axis_index("core") == 0
+    up_bias_ref, o_own_ref, o_other_ref, up_ref, dhidden_ref,
+    dn_ref, core_ref, high_ref, cross_ref, here_ref, mid_ref, hidden_ref, attn_ref, vec_ref,
+    acc_ref, dpre_ref,
+):
     side = lax.axis_index("wa")
     for pair in range(3):
         rows = slice(pair * 128, (pair + 1) * 128)
@@ -527,51 +542,47 @@
     flush(mid_ref)
     normed, _, _ = norm_forward(middle, gain_ref[...], shift_ref[...])
     low = normed.astype(jnp.bfloat16)
-    active = column((exit_ref[...] > LAYER).astype(jnp.float32))
-    branch = jnp.where(active > 0.0, cot_ref[...].astype(jnp.float32), 0.0)
-    branch_low = branch.astype(jnp.bfloat16)
-    keep_ref[:, :768] = jnp.where(first, low, branch_low)
-    send_ref[:, :768] = jnp.where(first, branch_low, low)
-    vec_ref[:, 1536:] = jnp.sum(branch, axis=0, keepdims=True)
-    ffn = None
+    branch_low = branch_of(cot_ref, exit_ref).astype(jnp.bfloat16)
     dnormed = None
     wait(up_ref)
-    wait(down_ref)
+    wait(dhidden_ref)
     for begin in range(0, 1536, FF_TILE):
         columns = slice(begin, begin + FF_TILE)
-        outs = slice(768 + begin, 768 + begin + FF_TILE)
         pre_act = (
             jnp.dot(low, up_ref[:, columns], preferred_element_type=jnp.float32)
             + up_bias_ref[:, columns]
         )
         hidden_full, slope = gelu_pair(pre_act)
         hidden = hidden_full.astype(jnp.bfloat16)
-        dhidden = lax.dot_general(
-            branch_low, down_ref[columns], trans_right, preferred_element_type=jnp.float32
-        )
-        dpre = (dhidden * slope).astype(jnp.bfloat16)
+        hidden_ref[:, columns] = hidden
+        dpre = (dhidden_ref[:, columns] * slope).astype(jnp.bfloat16)
         vec_ref[:, columns] = jnp.sum(dpre.astype(jnp.float32), axis=0, keepdims=True)
-        keep_ref[:, outs] = jnp.where(first, dpre, hidden)
-        send_ref[:, outs] = jnp.where(first, hidden, dpre)
-        ffn_term = jnp.dot(hidden, down_ref[columns], preferred_element_type=jnp.float32)
+        dpre_ref[:, columns] = dpre
         dn_term = lax.dot_general(
             dpre, up_ref[:, columns], trans_right, preferred_element_type=jnp.float32
         )
-        ffn = ffn_term if ffn is None else ffn + ffn_term
         dnormed = dn_term if dnormed is None else dnormed + dn_term
-    ffn_ref[...] = ffn.astype(jnp.bfloat16)
     dn_ref[...] = dnormed.astype(jnp.bfloat16)
+    core, high = lax.axis_index("core"), lax.axis_index("zh")
+    for ref, offset in ((core_ref, 1), (high_ref, 2), (cross_ref, 3), (here_ref, 0)):
+        up_side = (core ^ (offset & 1)) == 0
+        first_half = (high ^ (offset >> 1)) == 0
+        ref[:, :768] = jnp.where(up_side, low, branch_low)
+        ref[:, 768:] = jnp.where(
+            up_side,
+            jnp.where(first_half, dpre_ref[:, :768], dpre_ref[:, 768:]),
+            jnp.where(first_half, hidden_ref[:, :768], hidden_ref[:, 768:]),
+        )
 
 
 def dheads_kernel(
-    wait, flush, dn_ref, other_ref, mid_ref, cot_ref, exit_ref, gain_ref, o_ref, attn_ref, order_ref,
-    pay_ref, send_ref, keep_ref, dmid_ref, vec_ref,
+    wait, flush, dn_ref, other_ref, mid_ref, cot_ref, exit_ref, gain_ref, attn_ref, o_ref,
+    pay_ref, both_ref, dmid_ref, vec_ref,
 ):
     middle = mid_ref[...]
     _, unit, inverse = norm_forward(middle, gain_ref[...], 0.0)
     dnormed = dn_ref[...].astype(jnp.float32) + other_ref[...].astype(jnp.float32)
-    active = column((exit_ref[...] > LAYER).astype(jnp.float32))
-    branch = jnp.where(active > 0.0, cot_ref[...].astype(jnp.float32), 0.0)
+    branch = branch_of(cot_ref, exit_ref)
     dmiddle = branch + norm_backward(dnormed, unit, inverse, gain_ref[...])
     dmid_ref[...] = dmiddle
     flush(dmid_ref)
@@ -598,42 +609,47 @@
             pay_ref[index + 1, 32:] = higher
     pay_ref[12:] = jnp.zeros((4, HALF, 128), jnp.bfloat16)
     flush(pay_ref)
-    wait(order_ref)
-    ordered = jnp.dot(low, order_ref[...], preferred_element_type=jnp.float32).astype(jnp.bfloat16)
-    first = lax.axis_index("core") == 0
-    keep_ref[:, :384] = jnp.where(first, ordered[:, :384], ordered[:, 384:])
-    send_ref[:, :384] = jnp.where(first, ordered[:, 384:], ordered[:, :384])
-    keep_ref[:, 384:] = attn_ref[...]
-    send_ref[:, 384:] = attn_ref[...]
-
-
-def o_products_kernel(wait, flush, keep_ref, sent_ref, far_ref, near_ref):
-    both = jnp.concatenate([keep_ref[...], sent_ref[...]], axis=0)
-    low = lax.axis_index("zh") == 0
-    product = lax.dot_general(
-        both[:, :384], both[:, 384:], trans_left, preferred_element_type=jnp.float32
-    )
-    spare = jnp.zeros((4, 384), jnp.float32)
-    for plane in range(16):
-        one = jnp.concatenate([product[24 * plane : 24 * plane + 12], spare], axis=0)
-        two = jnp.concatenate([product[24 * plane + 12 : 24 * plane + 24], spare], axis=0)
-        near_ref[plane] = jnp.where(low, one, two)
-        far_ref[plane] = jnp.where(low, two, one).astype(jnp.bfloat16)
-
-
-def ffn_products_kernel(wait, flush, keep_ref, sent_ref, out_ref):
-    for at in range(768, 2304, 384):
-        columns = slice(at, at + 384)
-        lefts = jnp.concatenate([keep_ref[:, :768], sent_ref[:, :768]], axis=0)
-        rights = jnp.concatenate([keep_ref[:, columns], sent_ref[:, columns]], axis=0)
-        out_ref[:, at - 768 : at - 384] = lax.dot_general(
+    both_ref[:, :768] = low
+    both_ref[:, 768:] = attn_ref[...]
+
+
+def ffn_products_kernel(
+    wait, flush, here_ref, core_ref, high_ref, cross_ref, both_ref, sent_ref,
+    up_ref, down_ref, two_ref, out_ref,
+):
+    pieces = (here_ref, core_ref, high_ref, cross_ref)
+    lefts = jnp.concatenate([ref[:, :768] for ref in pieces], axis=0)
+    for at in range(0, 768, 384):
+        rights = jnp.concatenate([ref[:, 768 + at : 1152 + at] for ref in pieces], axis=0)
+        out_ref[:, at : at + 384] = lax.dot_general(
             lefts, rights, trans_left, preferred_element_type=jnp.float32
         ).astype(jnp.bfloat16)
+    first = lax.axis_index("core") == 0
+    both = jnp.concatenate([both_ref[...], sent_ref[...]], axis=0)
+    out_ref[:, 768:1024] = lax.dot_general(
+        both[:, :768],
+        jnp.where(first, both[:, 768:1024], both[:, 896:]),
+        trans_left,
+        preferred_element_type=jnp.float32,
+    ).astype(jnp.bfloat16)
+    vec = jnp.concatenate([up_ref[...], down_ref[...], two_ref[...]], axis=1)
+    lines = [vec[:, 128 * row : 128 * (row + 1)] for row in range(36)]
+    lines = jnp.concatenate(lines + [jnp.zeros((12, 128), jnp.float32)], axis=0).astype(
+        jnp.bfloat16
+    )
+    for plane in range(16):
+        out_ref[48 * plane : 48 * plane + 48, 1024:] = lines
+
+
+def ffn_kernel(wait, flush, hidden_ref, down_ref, out_ref):
+    out_ref[...] = jnp.dot(
+        hidden_ref[...], down_ref[...], preferred_element_type=jnp.float32
+    ).astype(jnp.bfloat16)
 
 
 def dnormed_kernel(
-    wait, flush, got_ref, tokens_ref, ffn_ref, two_ref, q_ref, k_ref, v_ref,
-    grads_ref, vec_ref, dn_ref,
+    wait, flush, got_ref, tokens_ref, q_ref, k_ref, v_ref,
+    grads_ref, norm_ref, vec_ref, dn_ref,
 ):
     wide = lane_ids(HALF, 128) < HALF
     for pair in range(3):
@@ -642,8 +658,9 @@
         value_columns = slice(768 + pair * 128, 896 + pair * 128)
         for half in range(2):
             rows = slice(half * HALF, (half + 1) * HALF)
-            even = got_ref[4 * pair + half, :96].astype(jnp.float32)
-            odd = got_ref[4 * pair + 2 + half, :96].astype(jnp.float32)
+            at = 8 * pair + 2 * half
+            even = got_ref[at].astype(jnp.float32) + got_ref[at + 1].astype(jnp.float32)
+            odd = got_ref[at + 4].astype(jnp.float32) + got_ref[at + 5].astype(jnp.float32)
             grads_ref[rows, key_columns] = jnp.where(wide, even[:HALF], turn(odd[:HALF])).astype(
                 jnp.bfloat16
             )
@@ -671,8 +688,7 @@
     vec_ref[:, 768:1536] = jnp.sum(dnormed * unit, axis=0, keepdims=True)
     vec_ref[:, 1536:1920] = total[:, :384]
     vec_ref[:, 1920:2304] = total[:, 768:]
-    vec_ref[:, 2304:4608] = ffn_ref[...]
-    vec_ref[:, 4608:] = two_ref[...]
+    norm_ref[...] = vec_ref[:, :1536]
 
 
 def input_grad_kernel(
@@ -688,117 +704,118 @@
     )
 
 
-def far_kernel(wait, flush, kept_ref, taken_ref, far_ref):
-    far_ref[...] = (
-        kept_ref[BLOCKS:].astype(jnp.float32) + taken_ref[BLOCKS:].astype(jnp.float32)
+def output_kernel(
+    wait, flush, ffn_ref, other_ref, mid_ref, tokens_ref, exit_ref, bias_ref, out_ref
+):
+    active = column((exit_ref[...] > LAYER).astype(jnp.float32))
+    branch = ffn_ref[...].astype(jnp.float32) + other_ref[...].astype(jnp.float32) + bias_ref[...]
+    out_ref[...] = jnp.where(
+        active > 0.0, mid_ref[...] + branch, tokens_ref[...].astype(jnp.float32)
     ).astype(jnp.bfloat16)
 
 
-def merge_kernel(
-    wait, flush, kept_ref, taken_ref, far_ref, dq_ref, edge_ref, o_near_ref, o_far_ref, out_ref
-):
+def merge_kernel(wait, flush, kept_ref, taken_ref, dq_ref, edge_ref, out_ref):
+    high = lax.axis_index("zh")
     for block in range(BLOCKS):
-        pair = (
-            kept_ref[block].astype(jnp.float32)
-            + taken_ref[block].astype(jnp.float32)
-            + far_ref[block].astype(jnp.float32)
-        )
+        pair = kept_ref[block].astype(jnp.float32) + taken_ref[block].astype(jnp.float32)
         query = dq_ref[block]
         if block == BLOCKS - 1:
             pair = pair + edge_ref[:HALF].astype(jnp.float32)
             query = (query.astype(jnp.float32) + edge_ref[HALF:].astype(jnp.float32)).astype(
                 jnp.bfloat16
             )
-        out_ref[block, :HALF] = pair.astype(jnp.bfloat16)
-        out_ref[block, HALF:96] = query
-        product = o_near_ref[block] + o_far_ref[block].astype(jnp.float32)
-        for tile in range(3):
-            out_ref[block, 96 + 16 * tile : 112 + 16 * tile] = product[
-                :, 128 * tile : 128 * tile + 128
-            ].astype(jnp.bfloat16)
-
-
-def o_sums_kernel(wait, flush, got_ref, out_ref):
-    for tile in range(3):
-        rows = slice(96 + 16 * tile, 112 + 16 * tile)
-        total = got_ref[0, rows].astype(jnp.float32)
-        for source in range(1, 16):
-            total = total + got_ref[source, rows].astype(jnp.float32)
-        out_ref[:, 128 * tile : 128 * tile + 128] = total[:12]
+        out_ref[pl.ds(2 * block + high, 1), :HALF] = pair.astype(jnp.bfloat16)[None]
+        out_ref[pl.ds(2 * block + high, 1), HALF:] = query[None]
+        pair = kept_ref[BLOCKS + block].astype(jnp.float32) + taken_ref[BLOCKS + block].astype(
+            jnp.float32
+        )
+        out_ref[pl.ds(2 * block + 1 - high, 1), :HALF] = pair.astype(jnp.bfloat16)[None]
+        out_ref[pl.ds(2 * block + 1 - high, 1), HALF:] = jnp.zeros((1, 32, 128), jnp.bfloat16)
 
 
 def qkv_products_kernel(
-    wait, flush, keep_ref, sent_ref, grads_ref, grads_sent_ref, vec_ref, vec_sent_ref, out_ref
+    wait, flush, keep_ref, sent_ref, grads_ref, grads_sent_ref,
+    vec_ref, vec_sent_ref, wa_ref, cross_ref, out_ref,
 ):
     lefts = jnp.concatenate([keep_ref[...], sent_ref[...]], axis=0)
     vec = vec_ref[...] + vec_sent_ref[...]
+    norms = vec[:, :1536] + (wa_ref[...] + cross_ref[...])
+    vec = jnp.concatenate([norms, vec[:, 1536:]], axis=1)
     lines = jnp.concatenate(
-        [vec[:, 1152 * row : 1152 * (row + 1)] for row in range(6)]
-        + [jnp.zeros((2, 1152), jnp.float32)],
-        axis=0,
+        [vec[:, :1152], vec[:, 1152:], jnp.zeros((2, 1152), jnp.float32)], axis=0
     )
     for at in range(0, 1152, 384):
         columns = slice(at, at + 384)
         rights = jnp.concatenate([grads_ref[:, columns], grads_sent_ref[:, columns]], axis=0)
         product = lax.dot_general(lefts, rights, trans_left, preferred_element_type=jnp.float32)
-        for plane in range(16):
-            out_ref[plane, :, columns] = jnp.concatenate(
-                [product[24 * plane : 24 * plane + 24], lines[:, columns]], axis=0
+        for chip in range(32):
+            out_ref[chip, :, columns] = jnp.concatenate(
+                [product[16 * chip : 16 * chip + 12], lines[:, columns]], axis=0
             ).astype(jnp.bfloat16)
 
 
-def plane_sums_kernel(wait, flush, got_ref, far_ref, norm_ref, near_ref):
+def finish_kernel(
+    wait, flush, got_ref, q_ref, k_ref, v_ref, shift_out, gain_out, q_bias_out, v_bias_out
+):
+    both = got_ref[0].astype(jnp.float32)
+    for source in range(1, 32):
+        both = both + got_ref[source].astype(jnp.float32)
+    q_ref[...] = both[:12, :384]
+    k_ref[...] = both[:12, 384:768]
+    v_ref[...] = both[:12, 768:]
+    shift_out[...] = both[12:13, :768]
+    gain_out[:, :384] = both[12:13, 768:]
+    gain_out[:, 384:] = both[13:14, :384]
+    q_bias_out[...] = both[13:14, 384:768]
+    v_bias_out[...] = both[13:14, 768:]
+
+
+def ffn_sums_kernel(wait, flush, got_ref, core_ref, high_ref, cross_ref, here_ref):
     total = got_ref[0].astype(jnp.float32)
     for source in range(1, 16):
         total = total + got_ref[source].astype(jnp.float32)
+    me = 2 * lax.axis_index("zh") + lax.axis_index("core")
+    parts = [total[12 * index : 12 * index + 12, :1024] for index in range(4)]
+    vec = jnp.concatenate([total[row : row + 1, 1024:] for row in range(36)], axis=1)
+    vec = jnp.concatenate([vec, jnp.zeros((1, 512), jnp.float32)], axis=1)
+    lines = [vec[:, 1024 * row : 1024 * (row + 1)] for row in range(5)]
+    lines = jnp.concatenate(lines + [jnp.zeros((3, 1024), jnp.float32)], axis=0)
+
+    def part(offset):
+        value = parts[offset]
+        for index in range(1, 4):
+            value = jnp.where(me == index, parts[index ^ offset], value)
+        return value
+
+    for ref, offset in ((here_ref, 0), (core_ref, 1), (high_ref, 2), (cross_ref, 3)):
+        ref[:12] = part(offset)
+        ref[12:16] = jnp.zeros((4, 1024), jnp.float32)
+        ref[16:] = lines
+
+
+def ffn_finish_kernel(
+    wait, flush, here_ref, core_ref, high_ref, cross_ref,
+    up_ref, down_ref, o_ref, up_bias_out, down_bias_out, gain_out, shift_out, o_bias_out,
+):
+    first = lax.axis_index("core") == 0
     low = lax.axis_index("zh") == 0
-    spare = jnp.zeros((4, 1152), jnp.float32)
-    one, two, vec = total[:12], total[12:24], total[24:32]
-    near_ref[...] = jnp.concatenate([jnp.where(low, one, two), spare, vec], axis=0)
-    far_ref[...] = jnp.concatenate([jnp.where(low, two, one), spare, vec], axis=0)
-    norm_ref[...] = vec
-
-
-def finish_kernel(
-    wait, flush, near_ref, far_ref, wa_ref, cross_ref,
-    q_ref, k_ref, v_ref, shift_out, gain_out, q_bias_out, v_bias_out,
-    up_bias_out, down_bias_out, gain_two_out, shift_two_out, o_bias_out,
-):
-    both = near_ref[...] + far_ref[...]
-    q_ref[...] = both[:12, :384]
-    k_ref[...] = both[:12, 384:768]
-    v_ref[...] = both[:12, 768:]
-    vec = both[16:24]
-    norms = vec + (wa_ref[...] + cross_ref[...])
-    shift_out[...] = norms[0:1, :768]
-    gain_out[:, :384] = norms[0:1, 768:]
-    gain_out[:, 384:] = norms[1:2, :384]
-    q_bias_out[...] = vec[1:2, 384:768]
-    v_bias_out[...] = vec[1:2, 768:]
-    up_bias_out[:, :1152] = vec[2:3]
-    up_bias_out[:, 1152:] = vec[3:4, :384]
-    down_bias_out[...] = vec[3:4, 384:]
-    gain_two_out[...] = vec[4:5, :768]
-    shift_two_out[:, :384] = vec[4:5, 768:]
-    shift_two_out[:, 384:] = vec[5:6, :384]
-    o_bias_out[...] = vec[5:6, 384:]
-
-
-def sub_sums(summed):
-    mine = summed.shape[0] // 4
-    parts = summed.reshape(4, mine, summed.shape[1])
-    me = lax.axis_index(("zh", "core"))
-
-    def part(index):
-        return lax.dynamic_index_in_dim(parts, index, 0, keepdims=False)
-
-    here = part(me)
-    core_way = lax.ppermute(part(jnp.bitwise_xor(me, 1)), "core", SWAP)
-    z_way = lax.ppermute(part(jnp.bitwise_xor(me, 2)), "zh", SWAP)
-    cross_way = lax.ppermute(part(jnp.bitwise_xor(me, 3)), ("zh", "core"), CROSS)
-    mine_sum, other_sum = here + z_way, core_way + cross_way
-    first = lax.axis_index("core") == 0
-    return jnp.where(first, mine_sum, other_sum), jnp.where(first, other_sum, mine_sum)
+    here, core, high, cross = [
+        ref[:12, :768] for ref in (here_ref, core_ref, high_ref, cross_ref)
+    ]
+    up_ref[:, :768] = jnp.where(first, jnp.where(low, here, high), jnp.where(low, core, cross))
+    up_ref[:, 768:] = jnp.where(first, jnp.where(low, high, here), jnp.where(low, cross, core))
+    down_ref[:, :768] = jnp.where(first, jnp.where(low, core, cross), jnp.where(low, here, high))
+    down_ref[:, 768:] = jnp.where(first, jnp.where(low, cross, core), jnp.where(low, high, here))
+    mine = here_ref[:12, 768:] + high_ref[:12, 768:]
+    other = core_ref[:12, 768:] + cross_ref[:12, 768:]
+    o_ref[:, :256] = jnp.where(first, mine, other)
+    o_ref[:, 256:] = jnp.where(first, other[:, 128:], mine[:, 128:])
+    vec = (here_ref[16:] + core_ref[16:]) + (high_ref[16:] + cross_ref[16:])
+    vec = jnp.concatenate([vec[row : row + 1] for row in range(5)], axis=1)
+    begin = 0
+    for ref in (up_bias_out, down_bias_out, gain_out, shift_out, o_bias_out):
+        ref[...] = vec[:, begin : begin + ref.shape[1]]
+        begin += ref.shape[1]
 
 
 def on_device(
@@ -838,10 +855,10 @@
     own = lax.all_to_all(payload, PLANE, 0, 0, tiled=True)
     low_one, o_given = lax.optimization_barrier((low_one, o_weight))
     o_other = lax.ppermute(o_given, "wa", SWAP)
-    x_send, order, x_keep = call(
+    x_send, x_keep = call(
         prepare_kernel, "prepare",
         copied(low_one),
-        [("v", whole(128, 384)), ("d", whole(768, 768)), ("d", whole(128, 384))],
+        [("v", whole(128, 512)), ("d", whole(128, 512))],
     )
     own, x_send, o_other = lax.optimization_barrier((own, x_send, o_other))
     pairs = own[:, :HALF]
@@ -852,124 +869,149 @@
     three = lax.ppermute(two, "core", SWAP)
     x_sent = lax.ppermute(x_send, "core", SWAP)
     back, kv, q_rows, start_rows, full_rows = attend(own, one, two, three, edge)
+    dhidden, vec_down = call(
+        dhidden_kernel, "dhidden",
+        copied(cotangent, exit_layer, down_weight),
+        [("d", whole(128, 1536, dtype=f32)), ("d", whole(1, 768, dtype=f32))],
+    )
     got = lax.all_to_all(back, ("x", "y", "wa"), 0, 0, tiled=True)
-    dn_two, send, keep, middle, ffn, attn_low, vec_ffn = call(
+    dn_two, ffn_core, ffn_high, ffn_cross, ffn_here, middle, hidden, attn_low, vec_up = call(
         middle_kernel, "middle",
         [("v", got)]
         + copied(
             tokens, cotangent, exit_layer, o_bias, ln2_gain, ln2_shift, up_bias, o_weight, o_other,
-            up_weight, down_weight,
+            up_weight, dhidden,
         ),
         [
             ("v", whole(128, 768)),
-            ("v", whole(128, 2304)),
-            ("v", whole(128, 2304)),
+            ("v", whole(128, 1536)),
+            ("v", whole(128, 1536)),
+            ("v", whole(128, 1536)),
+            ("v", whole(128, 1536)),
             ("d", whole(128, 768, dtype=f32)),
-            ("d", whole(128, 768)),
+            ("d", whole(128, 1536)),
             ("d", whole(128, 384)),
-            ("d", whole(1, 2304, dtype=f32)),
+            ("d", whole(1, 1536, dtype=f32)),
         ],
-        [pltpu.VMEM((128, 384), jnp.bfloat16)],
+        [pltpu.VMEM((128, 384), jnp.bfloat16), pltpu.VMEM((128, 1536), jnp.bfloat16)],
         lazy=(8, 9, 10, 11),
     )
     dn_two_other = lax.ppermute(dn_two, "wa", SWAP)
-    sent = lax.ppermute(send, "core", SWAP)
-    ffn_products = call(
-        ffn_products_kernel, "ffn_products",
-        [("v", keep), ("v", sent)],
-        [("d", whole(768, 1536))],
-    )
-    dh_payload, o_send, o_keep, dmiddle, vec_two = call(
+    ffn_high = lax.ppermute(ffn_high, "zh", SWAP)
+    ffn_cross = lax.ppermute(ffn_cross, ("zh", "core"), CROSS)
+    ffn_core = lax.ppermute(ffn_core, "core", SWAP)
+    ffn = call(ffn_kernel, "ffn", copied(hidden, down_weight), [("v", whole(128, 768))], cost=0)
+    dn_two_other, ffn = lax.optimization_barrier((dn_two_other, ffn))
+    dh_payload, dattn_attn, dmiddle, vec_two = call(
         dheads_kernel, "dheads",
         [("v", dn_two), ("v", dn_two_other)]
-        + copied(middle, cotangent, exit_layer, ln2_gain, o_weight, attn_low, order),
+        + copied(middle, cotangent, exit_layer, ln2_gain, attn_low, o_weight),
         [
             ("d", whole(16, HALF, 128)),
-            ("v", whole(128, 768)),
-            ("v", whole(128, 768)),
+            ("v", whole(128, 1152)),
             ("d", whole(128, 768, dtype=f32)),
             ("d", whole(1, 2304, dtype=f32)),
         ],
-        lazy=(6, 8),
+        lazy=(7,),
+        cost=0,
     )
     dh = lax.all_to_all(dh_payload, PLANE, 0, 0, tiled=True)
-    o_sent = lax.ppermute(o_send, "core", SWAP)
-    o_far, o_near = call(
-        o_products_kernel, "o_products",
-        [("v", o_keep), ("v", o_sent)],
-        [("v", whole(16, 16, 384)), ("d", whole(16, 16, 384, dtype=f32))],
-    )
-    o_got = lax.ppermute(o_far, "zh", SWAP)
-    dh, ffn_products, o_got = lax.optimization_barrier((dh, ffn_products, o_got))
-    ffn_blocks = lax.all_to_all(
-        ffn_products.reshape(16, 48, 1536), PLANE, 0, 0, tiled=True
-    )
+    dattn_sent = lax.ppermute(dattn_attn, "core", SWAP)
+    ffn_products = call(
+        ffn_products_kernel, "ffn_products",
+        [("v", ffn_here), ("v", ffn_core), ("v", ffn_high), ("v", ffn_cross)]
+        + [("v", dattn_attn), ("v", dattn_sent)]
+        + copied(vec_up, vec_down, vec_two),
+        [("d", whole(768, 1152))],
+    )
+    ffn_blocks = lax.all_to_all(ffn_products.reshape(16, 48, 1152), PLANE, 0, 0, tiled=True)
+    ffn_other = lax.ppermute(ffn, "wa", SWAP)
     given, kept, dq, edge_grad = attend_grad(kv, q_rows, start_rows, full_rows, dh)
+    given, ffn_other = lax.optimization_barrier((given, ffn_other))
     edge_got = lax.ppermute(edge_grad, "y", ((0, 1), (2, 3)))
     taken = lax.ppermute(given, "core", SWAP)
-    far = call(far_kernel, "far", [("v", kept), ("v", taken)], [("v", whole(BLOCKS, HALF, 128))])
-    far = lax.ppermute(far, "zh", SWAP)
     merged = call(
         merge_kernel, "merge",
-        [("v", kept), ("v", taken), ("v", far), ("v", dq), ("v", edge_got)] + copied(o_near, o_got),
-        [("d", whole(BLOCKS, 144, 128))],
-    )
-    merged, ffn_blocks, ffn = lax.optimization_barrier((merged, ffn_blocks, ffn))
-    grads = lax.all_to_all(merged, PLANE, 0, 0, tiled=True)
-    grads_rows, vec, dn_one = call(
+        [("v", kept), ("v", taken), ("v", dq), ("v", edge_got)],
+        [("d", whole(2 * BLOCKS, 96, 128))],
+    )
+    merged, ffn_blocks = lax.optimization_barrier((merged, ffn_blocks))
+    grads = lax.all_to_all(merged, CHIPS, 0, 0, tiled=True)
+    ffn_core, ffn_high, ffn_cross, ffn_here = call(
+        ffn_sums_kernel, "ffn_sums", copied(ffn_blocks),
+        [("v", whole(24, 1024, dtype=f32)) for _ in range(4)],
+        cost=0,
+    )
+    ffn_core = lax.ppermute(ffn_core, "core", SWAP)
+    ffn_high = lax.ppermute(ffn_high, "zh", SWAP)
+    ffn_cross = lax.ppermute(ffn_cross, ("zh", "core"), CROSS)
+    grads, ffn_core, ffn_high, ffn_cross, x_sent = lax.optimization_barrier(
+        (grads, ffn_core, ffn_high, ffn_cross, x_sent)
+    )
+    grads_rows, norms, vec, dn_one = call(
         dnormed_kernel, "dnormed",
-        [("v", grads)] + copied(tokens, vec_ffn, vec_two, q_weight, k_weight, v_weight),
-        [("v", whole(128, 1152)), ("v", whole(1, 6912, dtype=f32)), ("v", whole(128, 768))],
-        lazy=(4, 5, 6),
-    )
-    o_weight_grad_t = call(
-        o_sums_kernel, "o_sums", [("v", grads)], [("d", whole(12, 384, dtype=f32))]
-    )
+        [("v", grads)] + copied(tokens, q_weight, k_weight, v_weight),
+        [
+            ("v", whole(128, 1152)),
+            ("v", whole(1, 1536, dtype=f32)),
+            ("v", whole(1, 2304, dtype=f32)),
+            ("v", whole(128, 768)),
+        ],
+        lazy=(2, 3, 4),
+        cost=0,
+    )
+    dn_one_other = lax.ppermute(dn_one, "wa", SWAP)
     grads_sent = lax.ppermute(grads_rows, "core", SWAP)
     vec_sent = lax.ppermute(vec, "core", SWAP)
+    norms_wa = lax.ppermute(norms, "wa", SWAP)
+    norms_cross = lax.ppermute(norms, ("core", "wa"), CROSS)
     products = call(
         qkv_products_kernel, "qkv_products",
         copied(x_keep, x_sent)
-        + [("v", grads_rows), ("v", grads_sent), ("v", vec), ("v", vec_sent)],
-        [("d", whole(16, 32, 1152))],
-    )
-    products = lax.all_to_all(products, PLANE, 0, 0, tiled=True)
-    far_sums, norm_sums, near_sums = call(
-        plane_sums_kernel, "plane_sums",
-        [("v", products)],
-        [
-            ("v", whole(24, 1152, dtype=f32)),
-            ("v", whole(8, 1152, dtype=f32)),
-            ("v", whole(24, 1152, dtype=f32)),
-        ],
-    )
-    far_sums = lax.ppermute(far_sums, "zh", SWAP)
-    wa_sums = lax.ppermute(norm_sums, "wa", SWAP)
-    cross_sums = lax.ppermute(norm_sums, ("zh", "wa"), CROSS)
-    dn_one_other = lax.ppermute(dn_one, "wa", SWAP)
-    up_weight_grad, down_weight_grad_t = sub_sums(jnp.sum(ffn_blocks.astype(f32), axis=0))
-    ffn_out = ffn.astype(f32) + lax.ppermute(ffn, "wa", SWAP).astype(f32) + down_bias
-    output = jnp.where(
-        (exit_layer > LAYER)[:, None], middle + ffn_out, tokens.astype(f32)
-    ).astype(jnp.bfloat16)
+        + [("v", grads_rows), ("v", grads_sent), ("v", vec), ("v", vec_sent)]
+        + [("v", norms_wa), ("v", norms_cross)],
+        [("d", whole(32, 16, 1152))],
+        cost=0,
+    )
+    products, dn_one_other = lax.optimization_barrier((products, dn_one_other))
+    products = lax.all_to_all(products, CHIPS, 0, 0, tiled=True)
+    output = call(
+        output_kernel, "output",
+        [("v", ffn), ("v", ffn_other)] + copied(middle, tokens, exit_layer, down_bias),
+        [("d", whole(128, 768))],
+        cost=0,
+    )
+    (
+        up_weight_grad, down_weight_grad_t, o_weight_grad_t,
+        up_bias_grad, down_bias_grad, ln2_gain_grad, ln2_shift_grad, o_bias_grad,
+    ) = call(
+        ffn_finish_kernel, "ffn_finish",
+        [("v", ffn_here), ("v", ffn_core), ("v", ffn_high), ("v", ffn_cross)],
+        [("d", whole(12, 1536, dtype=f32)) for _ in range(2)]
+        + [("d", whole(12, 384, dtype=f32))]
+        + [("d", whole(count, dtype=f32)) for count in (1536, 768, 768, 768, 768)],
+        cost=0,
+    )
     input_grad = call(
         input_grad_kernel, "input_grad",
         [("v", dn_one), ("v", dn_one_other)]
         + copied(tokens, cotangent, exit_layer, ln1_gain, dmiddle),
         [("d", whole(128, 768, dtype=f32))],
+        cost=0,
+    )
+    (
+        products, output, input_grad, up_weight_grad, down_weight_grad_t
+    ) = lax.optimization_barrier(
+        (products, output, input_grad, up_weight_grad, down_weight_grad_t)
     )
     (
         q_weight_grad, k_weight_grad, v_weight_grad,
         ln1_shift_grad, ln1_gain_grad, q_bias_grad, v_bias_grad,
-        up_bias_grad, down_bias_grad, ln2_gain_grad, ln2_shift_grad, o_bias_grad,
     ) = call(
         finish_kernel, "finish",
-        [("v", near_sums), ("v", far_sums), ("v", wa_sums), ("v", cross_sums)],
+        [("v", products)],
         [("d", whole(12, 384, dtype=f32)) for _ in range(3)]
-        + [
-            ("d", whole(count, dtype=f32))
-            for count in (768, 768, 384, 384, 1536, 768, 768, 768, 768)
-        ],
+        + [("d", whole(count, dtype=f32)) for count in (768, 768, 384, 384)],
     )
     return (
         output,

time: 207 us -> 198 us (0.957)
  blocking collectives: 36.7 us -> 0 us
  waiting for transfers between devices: 30.9 us -> 55.7 us
  other arithmetic: 5.22 us -> 0 us
  starting transfers between devices: 60.9 us -> 65.9 us
  Pallas kernels: 67.4 us -> 70.9 us
    all_to_all x2 -> x0, blocking collectives: 36.7 us -> none  [the longest x1 20.8 us: on_device(): grads = lax.all_to_all(merged, PLANE, 0, 0, tiled=True)]
    all_to_all x2 -> x4, waiting for transfers between devices: 6.52 us -> 22 us  [the longest x1 11 us: on_device(): products = lax.all_to_all(products, CHIPS, 0, 0, tiled=True)]
    ppermute x11 -> x10, waiting for transfers between devices: 9.8 us -> 23.5 us  [the longest x2 9.19 us: on_device(): ffn_high = lax.ppermute(ffn_high, 'zh', SWAP)]
    all_to_all x2 -> x4, starting transfers between devices: 10.6 us -> 22 us  [the longest x1 7.68 us: on_device(): grads = lax.all_to_all(merged, CHIPS, 0, 0, tiled=True)]
    pallas_call x16 -> x17, Pallas kernels: 67.4 us -> 70.9 us  [call(): pl.pallas_call(body, out_shape=tuple((out for _, out in outs)), in_specs=...]
    ppermute x11 -> x10, starting transfers between devices: 15.6 us -> 12.2 us  [the longest x2 4.78 us: on_device(): ffn_high = lax.ppermute(ffn_high, 'zh', SWAP)]
    ppermute x1, waiting for transfers between devices: 2.55 us -> 0.01 us  [on_device(): dn_two_other = lax.ppermute(dn_two, 'wa', SWAP)]
  transfers between devices with their start and end apart: 27 -> 28, of which waited for: 13 -> 11; matrix products, arithmetic and copies ran while one was open for 3% -> 0% of each run, Pallas kernels for 20% -> 25%
where the time goes in v1:
time: 198 us; the launch traced here: 196 us
  Pallas kernels  70.9 us (36%)
  starting transfers between devices  65.9 us (33%)
  waiting for transfers between devices  55.7 us (28%)
  local copies, waits for them, and re-layouts  2.43 us (1%)
    pallas_call x17, Pallas kernels, call(): pl.pallas_call(body, out_shape=tuple((out for _, out in outs)), in_specs=...  70.9 us
    all_to_all x1, waiting for transfers between devices, on_device(): products = lax.all_to_all(products, CHIPS, 0, 0, tiled=True)  11 us
    ppermute x2, waiting for transfers between devices, on_device(): ffn_high = lax.ppermute(ffn_high, 'zh', SWAP)  9.19 us
    ppermute x2, waiting for transfers between devices, on_device(): ffn_cross = lax.ppermute(ffn_cross, ('zh', 'core'), CROSS)  8.85 us
    all_to_all x1, starting transfers between devices, on_device(): grads = lax.all_to_all(merged, CHIPS, 0, 0, tiled=True)  7.68 us
    all_to_all x1, waiting for transfers between devices, on_device(): got = lax.all_to_all(back, ('x', 'y', 'wa'), 0, 0, tiled=True)  7.64 us
    all_to_all x1, starting transfers between devices, on_device(): own = lax.all_to_all(payload, PLANE, 0, 0, tiled=True)  6.8 us
    all_to_all x1, waiting for transfers between devices, on_device(): own = lax.all_to_all(payload, PLANE, 0, 0, tiled=True)  6 us
  transfers between devices with their start and end apart: 28, of which 11 were waited for; matrix products, arithmetic and copies ran while one was open for 0% of the time, Pallas kernels for 25%

profile of v1, /device:TPU:1, one launch (start us, length us, event | category | flops | bytes accessed | tf_op | source)
XLA Modules:
  0.0 196.1 jit_solution(7832625670110307196)
XLA Ops:
  0.7 3.2 %project.1 = (bf16[16,112,128]{2,1,0:T(8,128)(2,1)}, bf16[128,768]{1,0:T(8,128)(2,1)}) custom-call(bf16[128,768]{1,0:T(8,128)(2,1)} %refs_2_.9, s32[128]{0:T(128)} %refs_1_.5, f32[768]{0:T(1024)} %refs_5_.9, f32[768]{0:T(1024)} %refs_3_.6, f32[384]{0:T(512)} %refs_4_.6, f32[384]{0:T(512)} %refs_5_.5, bf16[768,384]{1,0:T(8,128)(2,1)} %refs_2_.8, ...), custom_call_target="tpu_custom_call" | custom-call | flops 2000000000 | tf_op jit(solution)/shard_map/project/pallas_call | solution.py:138
  3.8 2.5 %collective-permute-start = (bf16[384,768]{1,0:T(8,128)(2,1)}, bf16[384,768]{1,0:T(8,128)(2,1)}, u32[]{:S(2)}, u32[]{:S(2)}) collective-permute-start(bf16[384,768]{1,0:T(8,128)(2,1)} %refs_7_.5), channel_id=1, source_target_pairs={{0,1},{1,0},{2,3},{3,2},{4,5},{5,4},{6,7},{7,6},{8,9},{9,8},{10,11... | collective-permute-start | bytes 1769480 | tf_op jit(solution)/shard_map/ppermute | solution.py:857
  6.4 6.8 %all-to-all-start = ((bf16[16,112,128]{2,1,0:T(8,128)(2,1)}), bf16[16,112,128]{2,1,0:T(8,128)(2,1)}, u32[]{:S(2)}, u32[]{:S(2)}) async-start(bf16[16,112,128]{2,1,0:T(8,128)(2,1)} %get-tuple-element.96), calls=%async_computation | async-start | bytes 917504 | tf_op jit(solution)/shard_map/all_to_all | solution.py:855
  13.2 2.6 %prepare.1 = (bf16[128,512]{1,0:T(8,128)(2,1)}, bf16[128,512]{1,0:T(8,128)(2,1)}) custom-call(bf16[128,768]{1,0:T(8,128)(2,1)} %get-tuple-element.94.refs_0_), custom_call_target="tpu_custom_call" | custom-call | flops 2000000000 | tf_op jit(solution)/shard_map/prepare/pallas_call | solution.py:138
  15.8 6.0 %all-to-all-done.refs_0_ = bf16[16,112,128]{2,1,0:T(8,128)(2,1)} async-done(((bf16[16,112,128]{2,1,0:T(8,128)(2,1)}), bf16[16,112,128]{2,1,0:T(8,128)(2,1)}, u32[]{:S(2)}, u32[]{:S(2)}) %all-to-all-start) | async-done | bytes 458784 | tf_op jit(solution)/shard_map/all_to_all | solution.py:855
  21.8 1.0 slice.6
  22.8 3.4 %collective-permute-start.2 = (bf16[16,64,128]{2,1,0:T(8,128)(2,1)S(1)}, bf16[16,64,128]{2,1,0:T(8,128)(2,1)S(1)}, u32[]{:S(2)}, u32[]{:S(2)}) collective-permute-start(bf16[16,64,128]{2,1,0:T(8,128)(2,1)S(1)} %slice.6), channel_id=1, source_target_pairs={{0,4},{4,0},{1,5},{5,1},{2,6},{6,2},{3,7},{7,3},{8,12},{12,8},{9,1... | collective-permute-start | bytes 786440 | tf_op jit(solution)/shard_map/ppermute | solution.py:867
  26.2 0.8 slice_bitcast_fusion
  27.0 1.3 collective-permute-start.3
  28.2 3.5 %collective-permute-start.1 = (bf16[16,64,128]{2,1,0:T(8,128)(2,1)S(1)}, bf16[16,64,128]{2,1,0:T(8,128)(2,1)S(1)}, u32[]{:S(2)}, u32[]{:S(2)}) collective-permute-start(bf16[16,64,128]{2,1,0:T(8,128)(2,1)S(1)} %slice.6), channel_id=1, source_target_pairs={{0,2},{2,0},{1,3},{3,1},{4,6},{6,4},{5,7},{7,5},{8,10},{10,8},{9,1... | collective-permute-start | bytes 786440 | tf_op jit(solution)/shard_map/ppermute | solution.py:865
  31.9 4.4 %collective-permute-start.4 = (bf16[16,64,128]{2,1,0:T(8,128)(2,1)S(1)}, bf16[16,64,128]{2,1,0:T(8,128)(2,1)}, u32[]{:S(2)}, u32[]{:S(2)}) collective-permute-start(bf16[16,64,128]{2,1,0:T(8,128)(2,1)S(1)} %collective-permute-done.2.refs_2_), channel_id=1, source_target_pairs={{0,2},{2,0},{1,3},{3,1},{4,6},{6,4},{5,7},{7,5},{8,10},{10,8},{9,1... | collective-permute-start | bytes 786440 | tf_op jit(solution)/shard_map/ppermute | solution.py:869
  36.2 0.7 copy-done.1
  37.5 6.3 %attend.1 = (bf16[32,64,128]{2,1,0:T(8,128)(2,1)}, bf16[17,256,128]{2,1,0:T(8,128)(2,1)}, bf16[1088,128]{1,0:T(8,128)(2,1)}, f32[1088,128]{1,0:T(8,128)}, f32[1088,128]{1,0:T(8,128)}) custom-call(bf16[16,112,128]{2,1,0:T(8,128)(2,1)} %all-to-all-done.refs_0_, bf16[16,64,128]{2,1,0:T(8,128)(2,1)} %copy-done.1, bf16[16,64,128]{2,1,0:T(8,128)(2,1)} %copy-done, ...), custom_call_target="tpu_custom_call" | custom-call | flops 3000000000 | tf_op jit(solution)/shard_map/attend/pallas_call | solution.py:138
  43.8 4.6 %all-to-all-start.1 = ((bf16[32,64,128]{2,1,0:T(8,128)(2,1)}), bf16[32,64,128]{2,1,0:T(8,128)(2,1)}, u32[]{:S(2)}, u32[]{:S(2)}) async-start(bf16[32,64,128]{2,1,0:T(8,128)(2,1)} %get-tuple-element.106), calls=%async_computation.1 | async-start | bytes 1048576 | tf_op jit(solution)/shard_map/all_to_all | solution.py:877
  48.5 3.7 %dhidden.1 = (f32[128,1536]{1,0:T(8,128)}, f32[1,768]{1,0:T(1,128)}) custom-call(bf16[128,768]{1,0:T(8,128)(2,1)} %refs_3_.11, s32[128]{0:T(128)} %refs_4_.11, bf16[1536,768]{1,0:T(8,128)(2,1)} %refs_1_.8), custom_call_target="tpu_custom_call" | custom-call | flops 2000000000 | tf_op jit(solution)/shard_map/dhidden/pallas_call | solution.py:138
  52.2 7.6 %all-to-all-done.1.refs_0_ = bf16[32,64,128]{2,1,0:T(8,128)(2,1)} async-done(((bf16[32,64,128]{2,1,0:T(8,128)(2,1)}), bf16[32,64,128]{2,1,0:T(8,128)(2,1)}, u32[]{:S(2)}, u32[]{:S(2)}) %all-to-all-start.1) | async-done | bytes 524320 | tf_op jit(solution)/shard_map/all_to_all | solution.py:877
  59.8 6.9 %middle.1 = (bf16[128,768]{1,0:T(8,128)(2,1)}, bf16[128,1536]{1,0:T(8,128)(2,1)}, bf16[128,1536]{1,0:T(8,128)(2,1)}, bf16[128,1536]{1,0:T(8,128)(2,1)}, bf16[128...) custom-call(bf16[32,64,128]{2,1,0:T(8,128)(2,1)} %all-to-all-done.1., ...), custom_call_target="tpu_custom_call" | custom-call | flops 2000000000 | tf_op jit(solution)/shard_map/middle/pallas_call | solution.py:138
  67.1 1.9 collective-permute-start.9
  69.0 1.5 collective-permute-start.10
  70.6 1.6 collective-permute-start.11
  72.2 3.0 %ffn.1.refs_0_ = bf16[128,768]{1,0:T(8,128)(2,1)} custom-call(bf16[128,1536]{1,0:T(8,128)(2,1)} %get-tuple-element.110.refs_0_, bf16[1536,768]{1,0:T(8,128)(2,1)} %refs_1_.8), custom_call_target="tpu_custom_call" | custom-call | tf_op jit(solution)/shard_map/ffn/pallas_call | solution.py:138
  75.2 4.5 %dheads.1 = (bf16[16,64,128]{2,1,0:T(8,128)(2,1)}, bf16[128,1152]{1,0:T(8,128)(2,1)}, f32[128,768]{1,0:T(8,128)}, f32[1,2304]{1,0:T(1,128)}) custom-call(bf16[128,768]{1,0:T(8,128)(2,1)} %get-tuple-element.109.refs_0_, bf16[128,768]{1,0:T(8,128)(2,1)} %collective-permute-done.5.refs_1_, f32[128,768]{1,0:T(8,128)} %get-tuple-element.112.refs_2_, ...), custom_call_target="tpu_custom_call" | custom-call | tf_op jit(solution)/shard_map/dheads/pallas_call | solution.py:138
  80.4 4.2 %all-to-all-start.2 = ((bf16[16,64,128]{2,1,0:T(8,128)(2,1)}), bf16[16,64,128]{2,1,0:T(8,128)(2,1)}, u32[]{:S(2)}, u32[]{:S(2)}) async-start(bf16[16,64,128]{2,1,0:T(8,128)(2,1)} %get-tuple-element.114), calls=%async_computation.2 | async-start | bytes 524288 | tf_op jit(solution)/shard_map/all_to_all | solution.py:918
  84.6 1.0 collective-permute-start.6
  85.6 6.5 %collective-permute-done.11.refs_3_ = bf16[128,1536]{1,0:T(8,128)(2,1)} collective-permute-done((bf16[128,1536]{1,0:T(8,128)(2,1)}, bf16[128,1536]{1,0:T(8,128)(2,1)}, u32[]{:S(2)}, u32[]{:S(2)}) %collective-permute-start.11) | collective-permute-done | bytes 393248 | tf_op jit(solution)/shard_map/ppermute | solution.py:901
  92.1 4.6 %ffn_products.1 = bf16[768,1152]{1,0:T(8,128)(2,1)} custom-call(bf16[128,1536]{1,0:T(8,128)(2,1)} %get-tuple-element.121.refs_0_, bf16[128,1536]{1,0:T(8,128)(2,1)} %collective-permute-done.9.refs_1_, bf16[128,1536]{1,0:T(8,128)(2,1)} %collective-permute-done.10.refs_2_, bf16[128,1536]{1,0:T(8,128)(2,1)} %collective-permute-done.11.refs_3_, ...), custom_call_target="tpu_custom_call" | custom-call | flops 2000000000 | tf_op jit(solution)/shard_map/ffn_products/pallas_call | solution.py:138
  96.7 4.4 %all-to-all-start.3 = ((bf16[16,48,1152]{2,1,0:T(8,128)(2,1)}), bf16[16,48,1152]{2,1,0:T(8,128)(2,1)}, u32[]{:S(2)}, u32[]{:S(2)}) async-start(bf16[16,48,1152]{2,1,0:T(8,128)(2,1)} %bitcast.3), calls=%async_computation.3 | async-start | bytes 3538944 | tf_op jit(solution)/shard_map/all_to_all | solution.py:927
  101.2 13.4 %attend_grad.1 = (bf16[32,64,128]{2,1,0:T(8,128)(2,1)}, bf16[32,64,128]{2,1,0:T(8,128)(2,1)}, bf16[16,32,128]{2,1,0:T(8,128)(2,1)}, bf16[96,128]{1,0:T(8,128)(2,1)}) custom-call(bf16[17,256,128]{2,1,0:T(8,128)(2,1)} %get-tuple-element.102.refs_0_, bf16[1088,128]{1,0:T(8,128)(2,1)} %get-tuple-element.103.refs_1_, f32[1088,128]{1,0:T(8,128)} %get-tuple-element.104.refs_2_, ...), custom_call_target="tpu_custom_call" | custom-call | flops 40000000000 | tf_op jit(solution)/shard_map/attend_grad/pallas_call | solution.py:138
  114.6 3.7 %collective-permute-start.8 = (bf16[96,128]{1,0:T(8,128)(2,1)}, bf16[96,128]{1,0:T(8,128)(2,1)}, u32[]{:S(2)}, u32[]{:S(2)}) collective-permute-start(bf16[96,128]{1,0:T(8,128)(2,1)} %get-tuple-element.120), channel_id=1, source_target_pairs={{0,8},{16,24},{1,9},{17,25},{2,10},{18,26},{3,11},{19,27},{4,12},{... | collective-permute-start | bytes 73736 | tf_op jit(solution)/shard_map/ppermute | solution.py:931
  118.3 3.5 %collective-permute-done.8.refs_3_ = bf16[96,128]{1,0:T(8,128)(2,1)} collective-permute-done((bf16[96,128]{1,0:T(8,128)(2,1)}, bf16[96,128]{1,0:T(8,128)(2,1)}, u32[]{:S(2)}, u32[]{:S(2)}) %collective-permute-start.8) | collective-permute-done | bytes 24608 | tf_op jit(solution)/shard_map/ppermute | solution.py:931
  121.8 2.3 %merge.1 = bf16[32,96,128]{2,1,0:T(8,128)(2,1)} custom-call(bf16[32,64,128]{2,1,0:T(8,128)(2,1)} %get-tuple-element.115.refs_0_, bf16[32,64,128]{2,1,0:T(8,128)(2,1)} %collective-permute-done.7.refs_1_, bf16[16,32,128]{2,1,0:T(8,128)(2,1)} %get-tuple-element.119.refs_2_, bf16[96,128]{1,0:T(8,128)(2,1)} %collective-permute-done.8.refs_3_), custom_call_target="tpu_custom_call" | custom-call | flops 2000000000 | tf_op jit(solution)/shard_map/merge/pallas_call | solution.py:138
  124.1 3.3 %all-to-all-done.3.refs_0_ = bf16[16,48,1152]{2,1,0:T(8,128)(2,1)} async-done(((bf16[16,48,1152]{2,1,0:T(8,128)(2,1)}), bf16[16,48,1152]{2,1,0:T(8,128)(2,1)}, u32[]{:S(2)}, u32[]{:S(2)}) %all-to-all-start.3) | async-done | bytes 1769504 | tf_op jit(solution)/shard_map/all_to_all | solution.py:927
  127.4 7.7 %all-to-all-start.4 = ((bf16[32,96,128]{2,1,0:T(8,128)(2,1)}), bf16[32,96,128]{2,1,0:T(8,128)(2,1)}, u32[]{:S(2)}, u32[]{:S(2)}) async-start(bf16[32,96,128]{2,1,0:T(8,128)(2,1)} %merge.1), calls=%async_computation.4 | async-start | bytes 1572864 | tf_op jit(solution)/shard_map/all_to_all | solution.py:939
  135.1 0.8 collective-permute-start.16
  135.9 2.5 %ffn_sums.1 = (f32[24,1024]{1,0:T(8,128)}, f32[24,1024]{1,0:T(8,128)}, f32[24,1024]{1,0:T(8,128)}, f32[24,1024]{1,0:T(8,128)}) custom-call(bf16[16,48,1152]{2,1,0:T(8,128)(2,1)} %all-to-all-done.3.refs_0_), custom_call_target="tpu_custom_call" | custom-call | tf_op jit(solution)/shard_map/ffn_sums/pallas_call | solution.py:138
  138.5 3.2 %collective-permute-start.14 = (f32[24,1024]{1,0:T(8,128)}, f32[24,1024]{1,0:T(8,128)}, u32[]{:S(2)}, u32[]{:S(2)}) collective-permute-start(f32[24,1024]{1,0:T(8,128)} %get-tuple-element.132), channel_id=1, source_target_pairs={{0,4},{4,0},{1,5},{5,1},{2,6},{6,2},{3,7},{7,3},{8,12},{12,8},{9,1... | collective-permute-start | bytes 294920 | tf_op jit(solution)/shard_map/ppermute | solution.py:946
  142.1 9.2 %collective-permute-done.14.refs_2_ = f32[24,1024]{1,0:T(8,128)} collective-permute-done((f32[24,1024]{1,0:T(8,128)}, f32[24,1024]{1,0:T(8,128)}, u32[]{:S(2)}, u32[]{:S(2)}) %collective-permute-start.14) | collective-permute-done | bytes 98336 | tf_op jit(solution)/shard_map/ppermute | solution.py:946
  151.3 2.4 %collective-permute-done.15.refs_3_ = f32[24,1024]{1,0:T(8,128)} collective-permute-done((f32[24,1024]{1,0:T(8,128)}, f32[24,1024]{1,0:T(8,128)}, u32[]{:S(2)}, u32[]{:S(2)}) %collective-permute-start.15) | collective-permute-done | bytes 98336 | tf_op jit(solution)/shard_map/ppermute | solution.py:947
  153.7 4.1 %dnormed.1 = (bf16[128,1152]{1,0:T(8,128)(2,1)}, f32[1,1536]{1,0:T(1,128)}, f32[1,2304]{1,0:T(1,128)}, bf16[128,768]{1,0:T(8,128)(2,1)}) custom-call(bf16[32,96,128]{2,1,0:T(8,128)(2,1)} %all-to-all-done.4.refs_0_, bf16[128,768]{1,0:T(8,128)(2,1)} %refs_2_.9, bf16[768,384]{1,0:T(8,128)(2,1)} %refs_2_.8, bf16[768,384]{1,0:T(8,128)(2,1)} %refs_3_.9, ...), custom_call_target="tpu_custom_call" | custom-call | tf_op jit(solution)/shard_map/dnormed/pallas_call | solution.py:138
  158.4 1.7 collective-permute-start.20
  160.2 5.4 %collective-permute-done.20.refs_7_ = f32[1,1536]{1,0:T(1,128)} collective-permute-done((f32[1,1536]{1,0:T(1,128)}, f32[1,1536]{1,0:T(1,128)}, u32[]{:S(2)}, u32[]{:S(2)}) %collective-permute-start.20) | collective-permute-done | bytes 6176 | tf_op jit(solution)/shard_map/ppermute | solution.py:967
  165.6 3.7 %qkv_products.1 = bf16[32,16,1152]{2,1,0:T(8,128)(2,1)} custom-call(bf16[128,512]{1,0:T(8,128)(2,1)} %get-tuple-element.95.refs_0_, bf16[128,512]{1,0:T(8,128)(2,1)} %collective-permute-done.16.refs_1_, bf16[128,1152]{1,0:T(8,128)(2,1)} %get-tuple-element.137.refs_2_, bf16[128,1152]{1,0:T(8,128)(2,1)} %collective-permute-done.17.refs_3_, ...), custom_call_target="tpu_custom_call" | custom-call | tf_op jit(solution)/shard_map/qkv_products/pallas_call | solution.py:138
  169.3 5.2 %all-to-all-start.5 = ((bf16[32,16,1152]{2,1,0:T(8,128)(2,1)}), bf16[32,16,1152]{2,1,0:T(8,128)(2,1)}, u32[]{:S(2)}, u32[]{:S(2)}) async-start(bf16[32,16,1152]{2,1,0:T(8,128)(2,1)} %qkv_products.1), calls=%async_computation.5 | async-start | bytes 2359296 | tf_op jit(solution)/shard_map/all_to_all | solution.py:977
  174.6 2.9 %output.1 = bf16[128,768]{1,0:T(8,128)(2,1)} custom-call(bf16[128,768]{1,0:T(8,128)(2,1)} %ffn.1.refs_0_, bf16[128,768]{1,0:T(8,128)(2,1)} %collective-permute-done.6.refs_1_, f32[128,768]{1,0:T(8,128)} %get-tuple-element.112.refs_2_, bf16[128,768]{1,0:T(8,128)(2,1)} %refs_2_.9, s32[128]{0:T(128)} %refs_4_.11, f32[768]{0:T(1024)} %refs_5_.8), custom_call_target="tpu_custom_call" | custom-call | tf_op jit(solution)/shard_map/output/pallas_call | solution.py:138
  177.5 1.8 ffn_finish.1
  179.3 3.4 %input_grad.1 = f32[128,768]{1,0:T(8,128)} custom-call(bf16[128,768]{1,0:T(8,128)(2,1)} %get-tuple-element.140.refs_0_, bf16[128,768]{1,0:T(8,128)(2,1)} %collective-permute-done.21.refs_1_, bf16[128,768]{1,0:T(8,128)(2,1)} %refs_2_.9, bf16[128,768]{1,0:T(8,128)(2,1)} %refs_3_.11, s32[128]{0:T(128)} %refs_4_.11, f32[768]{0:T(1024)} %refs_5_.9, ...), custom_call_target="tpu_custom_call" | custom-call | tf_op jit(solution)/shard_map/input_grad/pallas_call | solution.py:138
  182.7 11.0 %all-to-all-done.5.refs_0_ = bf16[32,16,1152]{2,1,0:T(8,128)(2,1)} async-done(((bf16[32,16,1152]{2,1,0:T(8,128)(2,1)}), bf16[32,16,1152]{2,1,0:T(8,128)(2,1)}, u32[]{:S(2)}, u32[]{:S(2)}) %all-to-all-start.5) | async-done | bytes 1179680 | tf_op jit(solution)/shard_map/all_to_all | solution.py:977
  193.8 2.1 %finish.1 = (f32[12,384]{1,0:T(8,128)}, f32[12,384]{1,0:T(8,128)}, f32[12,384]{1,0:T(8,128)}, f32[768]{0:T(1024)}, f32[768]{0:T(1024)}, /*index=5*/f32[384]{0:T(512)}, f32[384]{0:T(512)}) custom-call(bf16[32,16,1152]{2,1,0:T(8,128)(2,1)} %all-to-all-done.5.refs_0_), custom_call_target="tpu_custom_call" | custom-call | flops 2000000000 | tf_op jit(solution)/shard_map/finish/pallas_call | solution.py:138
  (33 shorter events, 3.1 us)
Async XLA Ops:
  3.8 18.0 %collective-permute-start = (bf16[384,768]{1,0:T(8,128)(2,1)}, bf16[384,768]{1,0:T(8,128)(2,1)}, u32[]{:S(2)}, u32[]{:S(2)}) collective-permute-start(bf16[384,768]{1,0:T(8,128)(2,1)} %refs_7_.5), channel_id=1, source_target_pairs={{0,1},{1,0},{2,3},{3,2},{4,5},{5,4},{6,7},{7,6},{8,9},{9,8},{10,11... | collective-permute-start | bytes 1769480 | tf_op jit(solution)/shard_map/ppermute | solution.py:857
  6.4 15.5 %all-to-all-start = ((bf16[16,112,128]{2,1,0:T(8,128)(2,1)}), bf16[16,112,128]{2,1,0:T(8,128)(2,1)}, u32[]{:S(2)}, u32[]{:S(2)}) async-start(bf16[16,112,128]{2,1,0:T(8,128)(2,1)} %get-tuple-element.96), calls=%async_computation | async-start | bytes 917504 | tf_op jit(solution)/shard_map/all_to_all | solution.py:855
  22.8 9.0 %collective-permute-start.2 = (bf16[16,64,128]{2,1,0:T(8,128)(2,1)S(1)}, bf16[16,64,128]{2,1,0:T(8,128)(2,1)S(1)}, u32[]{:S(2)}, u32[]{:S(2)}) collective-permute-start(bf16[16,64,128]{2,1,0:T(8,128)(2,1)S(1)} %slice.6), channel_id=1, source_target_pairs={{0,4},{4,0},{1,5},{5,1},{2,6},{6,2},{3,7},{7,3},{8,12},{12,8},{9,1... | collective-permute-start | bytes 786440 | tf_op jit(solution)/shard_map/ppermute | solution.py:867
  27.0 4.9 %collective-permute-start.3 = (bf16[112,128]{1,0:T(8,128)(2,1)S(1)}, bf16[112,128]{1,0:T(8,128)(2,1)S(1)}, u32[]{:S(2)}, u32[]{:S(2)}) collective-permute-start(bf16[112,128]{1,0:T(8,128)(2,1)S(1)} %slice_bitcast_fusion), channel_id=1, source_target_pairs={{8,0},{24,16},{9,1},{25,17},{10,2},{26,18},{11,3},{27,19},{12,4},{... | collective-permute-start | bytes 86024 | tf_op jit(solution)/shard_map/ppermute | solution.py:866
  28.2 8.0 %collective-permute-start.1 = (bf16[16,64,128]{2,1,0:T(8,128)(2,1)S(1)}, bf16[16,64,128]{2,1,0:T(8,128)(2,1)S(1)}, u32[]{:S(2)}, u32[]{:S(2)}) collective-permute-start(bf16[16,64,128]{2,1,0:T(8,128)(2,1)S(1)} %slice.6), channel_id=1, source_target_pairs={{0,2},{2,0},{1,3},{3,1},{4,6},{6,4},{5,7},{7,5},{8,10},{10,8},{9,1... | collective-permute-start | bytes 786440 | tf_op jit(solution)/shard_map/ppermute | solution.py:865
  31.9 4.4 %copy-start.2 = (bf16[112,128]{1,0:T(8,128)(2,1)}, bf16[112,128]{1,0:T(8,128)(2,1)S(1)}, u32[]{:S(2)}) copy-start(bf16[112,128]{1,0:T(8,128)(2,1)S(1)} %collective-permute-done.3.refs_4_) | copy-start | bytes 86020
  31.9 4.4 %copy-start = (bf16[16,64,128]{2,1,0:T(8,128)(2,1)}, bf16[16,64,128]{2,1,0:T(8,128)(2,1)S(1)}, u32[]{:S(2)}) copy-start(bf16[16,64,128]{2,1,0:T(8,128)(2,1)S(1)} %collective-permute-done.2.refs_2_) | copy-start | bytes 786436
  31.9 5.6 %collective-permute-start.4 = (bf16[16,64,128]{2,1,0:T(8,128)(2,1)S(1)}, bf16[16,64,128]{2,1,0:T(8,128)(2,1)}, u32[]{:S(2)}, u32[]{:S(2)}) collective-permute-start(bf16[16,64,128]{2,1,0:T(8,128)(2,1)S(1)} %collective-permute-done.2.refs_2_), channel_id=1, source_target_pairs={{0,2},{2,0},{1,3},{3,1},{4,6},{6,4},{5,7},{7,5},{8,10},{10,8},{9,1... | collective-permute-start | bytes 786440 | tf_op jit(solution)/shard_map/ppermute | solution.py:869
  36.2 0.7 copy-start.1
  43.8 15.9 %all-to-all-start.1 = ((bf16[32,64,128]{2,1,0:T(8,128)(2,1)}), bf16[32,64,128]{2,1,0:T(8,128)(2,1)}, u32[]{:S(2)}, u32[]{:S(2)}) async-start(bf16[32,64,128]{2,1,0:T(8,128)(2,1)} %get-tuple-element.106), calls=%async_computation.1 | async-start | bytes 1048576 | tf_op jit(solution)/shard_map/all_to_all | solution.py:877
  66.7 8.5 %collective-permute-start.5 = (bf16[128,768]{1,0:T(8,128)(2,1)}, bf16[128,768]{1,0:T(8,128)(2,1)}, u32[]{:S(2)}, u32[]{:S(2)}) collective-permute-start(bf16[128,768]{1,0:T(8,128)(2,1)} %get-tuple-element.109.refs_0_), channel_id=1, source_target_pairs={{0,1},{1,0},{2,3},{3,2},{4,5},{5,4},{6,7},{7,6},{8,9},{9,8},{10,11... | collective-permute-start | bytes 589832 | tf_op jit(solution)/shard_map/ppermute | solution.py:899
  67.1 18.5 %collective-permute-start.9 = (bf16[128,1536]{1,0:T(8,128)(2,1)}, bf16[128,1536]{1,0:T(8,128)(2,1)}, u32[]{:S(2)}, u32[]{:S(2)}) collective-permute-start(bf16[128,1536]{1,0:T(8,128)(2,1)} %get-tuple-element.122), channel_id=1, source_target_pairs={{0,2},{2,0},{1,3},{3,1},{4,6},{6,4},{5,7},{7,5},{8,10},{10,8},{9,1... | collective-permute-start | bytes 1179656 | tf_op jit(solution)/shard_map/ppermute | solution.py:902
  69.0 16.6 %collective-permute-start.10 = (bf16[128,1536]{1,0:T(8,128)(2,1)}, bf16[128,1536]{1,0:T(8,128)(2,1)}, u32[]{:S(2)}, u32[]{:S(2)}) collective-permute-start(bf16[128,1536]{1,0:T(8,128)(2,1)} %get-tuple-element.123), channel_id=1, source_target_pairs={{0,4},{4,0},{1,5},{5,1},{2,6},{6,2},{3,7},{7,3},{8,12},{12,8},{9,1... | collective-permute-start | bytes 1179656 | tf_op jit(solution)/shard_map/ppermute | solution.py:900
  70.6 21.5 %collective-permute-start.11 = (bf16[128,1536]{1,0:T(8,128)(2,1)}, bf16[128,1536]{1,0:T(8,128)(2,1)}, u32[]{:S(2)}, u32[]{:S(2)}) collective-permute-start(bf16[128,1536]{1,0:T(8,128)(2,1)} %get-tuple-element.124), channel_id=1, source_target_pairs={{0,6},{2,4},{4,2},{6,0},{1,7},{3,5},{5,3},{7,1},{8,14},{10,12},{12... | collective-permute-start | bytes 1179656 | tf_op jit(solution)/shard_map/ppermute | solution.py:901
  79.7 12.4 %collective-permute-start.12 = (bf16[128,1152]{1,0:T(8,128)(2,1)}, bf16[128,1152]{1,0:T(8,128)(2,1)}, u32[]{:S(2)}, u32[]{:S(2)}) collective-permute-start(bf16[128,1152]{1,0:T(8,128)(2,1)} %get-tuple-element.125.refs_4_), channel_id=1, source_target_pairs={{0,2},{2,0},{1,3},{3,1},{4,6},{6,4},{5,7},{7,5},{8,10},{10,8},{9,1... | collective-permute-start | bytes 884744 | tf_op jit(solution)/shard_map/ppermute | solution.py:919
  80.4 16.4 %all-to-all-start.2 = ((bf16[16,64,128]{2,1,0:T(8,128)(2,1)}), bf16[16,64,128]{2,1,0:T(8,128)(2,1)}, u32[]{:S(2)}, u32[]{:S(2)}) async-start(bf16[16,64,128]{2,1,0:T(8,128)(2,1)} %get-tuple-element.114), calls=%async_computation.2 | async-start | bytes 524288 | tf_op jit(solution)/shard_map/all_to_all | solution.py:918
  84.6 30.0 %collective-permute-start.6 = (bf16[128,768]{1,0:T(8,128)(2,1)}, bf16[128,768]{1,0:T(8,128)(2,1)}, u32[]{:S(2)}, u32[]{:S(2)}) collective-permute-start(bf16[128,768]{1,0:T(8,128)(2,1)} %ffn.1.refs_0_), channel_id=1, source_target_pairs={{0,1},{1,0},{2,3},{3,2},{4,5},{5,4},{6,7},{7,6},{8,9},{9,8},{10,11... | collective-permute-start | bytes 589832 | tf_op jit(solution)/shard_map/ppermute | solution.py:928
  96.7 30.6 %all-to-all-start.3 = ((bf16[16,48,1152]{2,1,0:T(8,128)(2,1)}), bf16[16,48,1152]{2,1,0:T(8,128)(2,1)}, u32[]{:S(2)}, u32[]{:S(2)}) async-start(bf16[16,48,1152]{2,1,0:T(8,128)(2,1)} %bitcast.3), calls=%async_computation.3 | async-start | bytes 3538944 | tf_op jit(solution)/shard_map/all_to_all | solution.py:927
  114.5 7.3 %collective-permute-start.7 = (bf16[32,64,128]{2,1,0:T(8,128)(2,1)}, bf16[32,64,128]{2,1,0:T(8,128)(2,1)}, u32[]{:S(2)}, u32[]{:S(2)}) collective-permute-start(bf16[32,64,128]{2,1,0:T(8,128)(2,1)} %get-tuple-element.118), channel_id=1, source_target_pairs={{0,2},{2,0},{1,3},{3,1},{4,6},{6,4},{5,7},{7,5},{8,10},{10,8},{9,1... | collective-permute-start | bytes 1572872 | tf_op jit(solution)/shard_map/ppermute | solution.py:932
  114.6 7.2 %collective-permute-start.8 = (bf16[96,128]{1,0:T(8,128)(2,1)}, bf16[96,128]{1,0:T(8,128)(2,1)}, u32[]{:S(2)}, u32[]{:S(2)}) collective-permute-start(bf16[96,128]{1,0:T(8,128)(2,1)} %get-tuple-element.120), channel_id=1, source_target_pairs={{0,8},{16,24},{1,9},{17,25},{2,10},{18,26},{3,11},{19,27},{4,12},{... | collective-permute-start | bytes 73736 | tf_op jit(solution)/shard_map/ppermute | solution.py:931
  127.4 26.3 %all-to-all-start.4 = ((bf16[32,96,128]{2,1,0:T(8,128)(2,1)}), bf16[32,96,128]{2,1,0:T(8,128)(2,1)}, u32[]{:S(2)}, u32[]{:S(2)}) async-start(bf16[32,96,128]{2,1,0:T(8,128)(2,1)} %merge.1), calls=%async_computation.4 | async-start | bytes 1572864 | tf_op jit(solution)/shard_map/all_to_all | solution.py:939
  135.1 7.1 %collective-permute-start.16 = (bf16[128,512]{1,0:T(8,128)(2,1)}, bf16[128,512]{1,0:T(8,128)(2,1)}, u32[]{:S(2)}, u32[]{:S(2)}) collective-permute-start(bf16[128,512]{1,0:T(8,128)(2,1)} %get-tuple-element.134), channel_id=1, source_target_pairs={{0,2},{2,0},{1,3},{3,1},{4,6},{6,4},{5,7},{7,5},{8,10},{10,8},{9,1... | collective-permute-start | bytes 393224 | tf_op jit(solution)/shard_map/ppermute | solution.py:870
  138.4 3.7 %collective-permute-start.13 = (f32[24,1024]{1,0:T(8,128)}, f32[24,1024]{1,0:T(8,128)}, u32[]{:S(2)}, u32[]{:S(2)}) collective-permute-start(f32[24,1024]{1,0:T(8,128)} %get-tuple-element.131), channel_id=1, source_target_pairs={{0,2},{2,0},{1,3},{3,1},{4,6},{6,4},{5,7},{7,5},{8,10},{10,8},{9,1... | collective-permute-start | bytes 294920 | tf_op jit(solution)/shard_map/ppermute | solution.py:945
  138.5 12.8 %collective-permute-start.14 = (f32[24,1024]{1,0:T(8,128)}, f32[24,1024]{1,0:T(8,128)}, u32[]{:S(2)}, u32[]{:S(2)}) collective-permute-start(f32[24,1024]{1,0:T(8,128)} %get-tuple-element.132), channel_id=1, source_target_pairs={{0,4},{4,0},{1,5},{5,1},{2,6},{6,2},{3,7},{7,3},{8,12},{12,8},{9,1... | collective-permute-start | bytes 294920 | tf_op jit(solution)/shard_map/ppermute | solution.py:946
  141.7 12.0 %collective-permute-start.15 = (f32[24,1024]{1,0:T(8,128)}, f32[24,1024]{1,0:T(8,128)}, u32[]{:S(2)}, u32[]{:S(2)}) collective-permute-start(f32[24,1024]{1,0:T(8,128)} %get-tuple-element.133), channel_id=1, source_target_pairs={{0,6},{2,4},{4,2},{6,0},{1,7},{3,5},{5,3},{7,1},{8,14},{10,12},{12... | collective-permute-start | bytes 294920 | tf_op jit(solution)/shard_map/ppermute | solution.py:947
  157.8 7.9 %collective-permute-start.17 = (bf16[128,1152]{1,0:T(8,128)(2,1)}, bf16[128,1152]{1,0:T(8,128)(2,1)}, u32[]{:S(2)}, u32[]{:S(2)}) collective-permute-start(bf16[128,1152]{1,0:T(8,128)(2,1)} %get-tuple-element.137.refs_2_), channel_id=1, source_target_pairs={{0,2},{2,0},{1,3},{3,1},{4,6},{6,4},{5,7},{7,5},{8,10},{10,8},{9,1... | collective-permute-start | bytes 884744 | tf_op jit(solution)/shard_map/ppermute | solution.py:964
  158.2 11.1 %collective-permute-start.21 = (bf16[128,768]{1,0:T(8,128)(2,1)}, bf16[128,768]{1,0:T(8,128)(2,1)}, u32[]{:S(2)}, u32[]{:S(2)}) collective-permute-start(bf16[128,768]{1,0:T(8,128)(2,1)} %get-tuple-element.140.refs_0_), channel_id=1, source_target_pairs={{0,1},{1,0},{2,3},{3,2},{4,5},{5,4},{6,7},{7,6},{8,9},{9,8},{10,11... | collective-permute-start | bytes 589832 | tf_op jit(solution)/shard_map/ppermute | solution.py:963
  158.2 7.4 %collective-permute-start.18 = (f32[1,2304]{1,0:T(1,128)}, f32[1,2304]{1,0:T(1,128)}, u32[]{:S(2)}, u32[]{:S(2)}) collective-permute-start(f32[1,2304]{1,0:T(1,128)} %get-tuple-element.138.refs_4_), channel_id=1, source_target_pairs={{0,2},{2,0},{1,3},{3,1},{4,6},{6,4},{5,7},{7,5},{8,10},{10,8},{9,1... | collective-permute-start | bytes 27656 | tf_op jit(solution)/shard_map/ppermute | solution.py:965
  158.4 7.2 %collective-permute-start.20 = (f32[1,1536]{1,0:T(1,128)}, f32[1,1536]{1,0:T(1,128)}, u32[]{:S(2)}, u32[]{:S(2)}) collective-permute-start(f32[1,1536]{1,0:T(1,128)} %get-tuple-element.139), channel_id=1, source_target_pairs={{0,3},{1,2},{2,1},{3,0},{4,7},{5,6},{6,5},{7,4},{8,11},{9,10},{10,... | collective-permute-start | bytes 18440 | tf_op jit(solution)/shard_map/ppermute | solution.py:967
  160.1 5.5 %collective-permute-start.19 = (f32[1,1536]{1,0:T(1,128)}, f32[1,1536]{1,0:T(1,128)}, u32[]{:S(2)}, u32[]{:S(2)}) collective-permute-start(f32[1,1536]{1,0:T(1,128)} %get-tuple-element.139), channel_id=1, source_target_pairs={{0,1},{1,0},{2,3},{3,2},{4,5},{5,4},{6,7},{7,6},{8,9},{9,8},{10,11... | collective-permute-start | bytes 18440 | tf_op jit(solution)/shard_map/ppermute | solution.py:966
  169.3 24.4 %all-to-all-start.5 = ((bf16[32,16,1152]{2,1,0:T(8,128)(2,1)}), bf16[32,16,1152]{2,1,0:T(8,128)(2,1)}, u32[]{:S(2)}, u32[]{:S(2)}) async-start(bf16[32,16,1152]{2,1,0:T(8,128)(2,1)} %qkv_products.1), calls=%async_computation.5 | async-start | bytes 2359296 | tf_op jit(solution)/shard_map/all_to_all | solution.py:977

commit v2 on v1

--- a/solution.py
+++ b/solution.py
@@ -576,7 +576,7 @@
 
 
 def dheads_kernel(
-    wait, flush, dn_ref, other_ref, mid_ref, cot_ref, exit_ref, gain_ref, attn_ref, o_ref,
+    wait, flush, dn_ref, other_ref, mid_ref, cot_ref, exit_ref, gain_ref, attn_ref, up_ref, down_ref, o_ref,
     pay_ref, both_ref, dmid_ref, vec_ref,
 ):
     middle = mid_ref[...]
@@ -587,9 +587,11 @@
     dmid_ref[...] = dmiddle
     flush(dmid_ref)
     low = dmiddle.astype(jnp.bfloat16)
-    vec_ref[:, :768] = jnp.sum(dnormed * unit, axis=0, keepdims=True)
-    vec_ref[:, 768:1536] = jnp.sum(dnormed, axis=0, keepdims=True)
-    vec_ref[:, 1536:] = jnp.sum(low.astype(jnp.float32), axis=0, keepdims=True)
+    vec_ref[:, :1536] = up_ref[...]
+    vec_ref[:, 1536:2304] = down_ref[...]
+    vec_ref[:, 2304:3072] = jnp.sum(dnormed * unit, axis=0, keepdims=True)
+    vec_ref[:, 3072:3840] = jnp.sum(dnormed, axis=0, keepdims=True)
+    vec_ref[:, 3840:] = jnp.sum(low.astype(jnp.float32), axis=0, keepdims=True)
     wait(o_ref)
     for pair in range(3):
         dheads = lax.dot_general(
@@ -615,7 +617,7 @@
 
 def ffn_products_kernel(
     wait, flush, here_ref, core_ref, high_ref, cross_ref, both_ref, sent_ref,
-    up_ref, down_ref, two_ref, out_ref,
+    vec_ref, vec_sent_ref, out_ref,
 ):
     pieces = (here_ref, core_ref, high_ref, cross_ref)
     lefts = jnp.concatenate([ref[:, :768] for ref in pieces], axis=0)
@@ -626,19 +628,19 @@
         ).astype(jnp.bfloat16)
     first = lax.axis_index("core") == 0
     both = jnp.concatenate([both_ref[...], sent_ref[...]], axis=0)
-    out_ref[:, 768:1024] = lax.dot_general(
+    product = lax.dot_general(
         both[:, :768],
         jnp.where(first, both[:, 768:1024], both[:, 896:]),
         trans_left,
         preferred_element_type=jnp.float32,
-    ).astype(jnp.bfloat16)
-    vec = jnp.concatenate([up_ref[...], down_ref[...], two_ref[...]], axis=1)
+    )
+    out_ref[:, 896:] = product[:, 128:].astype(jnp.bfloat16)
+    vec = vec_ref[...] + vec_sent_ref[...]
     lines = [vec[:, 128 * row : 128 * (row + 1)] for row in range(36)]
-    lines = jnp.concatenate(lines + [jnp.zeros((12, 128), jnp.float32)], axis=0).astype(
-        jnp.bfloat16
-    )
+    lines = jnp.concatenate(lines + [jnp.zeros((12, 128), jnp.float32)], axis=0)
     for plane in range(16):
-        out_ref[48 * plane : 48 * plane + 48, 1024:] = lines
+        rows = slice(48 * plane, 48 * plane + 48)
+        out_ref[rows, 768:896] = jnp.where(first, product[rows, :128], lines).astype(jnp.bfloat16)
 
 
 def ffn_kernel(wait, flush, hidden_ref, down_ref, out_ref):
@@ -776,7 +778,7 @@
         total = total + got_ref[source].astype(jnp.float32)
     me = 2 * lax.axis_index("zh") + lax.axis_index("core")
     parts = [total[12 * index : 12 * index + 12, :1024] for index in range(4)]
-    vec = jnp.concatenate([total[row : row + 1, 1024:] for row in range(36)], axis=1)
+    vec = jnp.concatenate([total[row : row + 1, 768:896] for row in range(36)], axis=1)
     vec = jnp.concatenate([vec, jnp.zeros((1, 512), jnp.float32)], axis=1)
     lines = [vec[:, 1024 * row : 1024 * (row + 1)] for row in range(5)]
     lines = jnp.concatenate(lines + [jnp.zeros((3, 1024), jnp.float32)], axis=0)
@@ -788,9 +790,10 @@
         return value
 
     for ref, offset in ((here_ref, 0), (core_ref, 1), (high_ref, 2), (cross_ref, 3)):
-        ref[:12] = part(offset)
-        ref[12:16] = jnp.zeros((4, 1024), jnp.float32)
-        ref[16:] = lines
+        ref[...] = jnp.concatenate(
+            [part(offset), jnp.zeros((4, 1024), jnp.float32), lines, jnp.zeros((8, 1024), jnp.float32)],
+            axis=0,
+        ).astype(ref.dtype)
 
 
 def ffn_finish_kernel(
@@ -799,18 +802,17 @@
 ):
     first = lax.axis_index("core") == 0
     low = lax.axis_index("zh") == 0
-    here, core, high, cross = [
-        ref[:12, :768] for ref in (here_ref, core_ref, high_ref, cross_ref)
-    ]
+    alls = [ref[...].astype(jnp.float32) for ref in (here_ref, core_ref, high_ref, cross_ref)]
+    here, core, high, cross = [value[:12, :768] for value in alls]
     up_ref[:, :768] = jnp.where(first, jnp.where(low, here, high), jnp.where(low, core, cross))
     up_ref[:, 768:] = jnp.where(first, jnp.where(low, high, here), jnp.where(low, cross, core))
     down_ref[:, :768] = jnp.where(first, jnp.where(low, core, cross), jnp.where(low, here, high))
     down_ref[:, 768:] = jnp.where(first, jnp.where(low, cross, core), jnp.where(low, high, here))
-    mine = here_ref[:12, 768:] + high_ref[:12, 768:]
-    other = core_ref[:12, 768:] + cross_ref[:12, 768:]
-    o_ref[:, :256] = jnp.where(first, mine, other)
-    o_ref[:, 256:] = jnp.where(first, other[:, 128:], mine[:, 128:])
-    vec = (here_ref[16:] + core_ref[16:]) + (high_ref[16:] + cross_ref[16:])
+    mine = alls[0][:, 768:] + alls[2][:, 768:]
+    other = alls[1][:, 768:] + alls[3][:, 768:]
+    o_ref[:, :256] = jnp.where(first, mine, other)[:12]
+    o_ref[:, 256:] = jnp.where(first, other[:, 128:], mine[:, 128:])[:12]
+    vec = jnp.where(first, alls[1][16:24] + alls[3][16:24], alls[0][16:24] + alls[2][16:24])
     vec = jnp.concatenate([vec[row : row + 1] for row in range(5)], axis=1)
     begin = 0
     for ref in (up_bias_out, down_bias_out, gain_out, shift_out, o_bias_out):
@@ -905,26 +907,26 @@
     dh_payload, dattn_attn, dmiddle, vec_two = call(
         dheads_kernel, "dheads",
         [("v", dn_two), ("v", dn_two_other)]
-        + copied(middle, cotangent, exit_layer, ln2_gain, attn_low, o_weight),
+        + copied(middle, cotangent, exit_layer, ln2_gain, attn_low, vec_up, vec_down, o_weight),
         [
             ("d", whole(16, HALF, 128)),
             ("v", whole(128, 1152)),
             ("d", whole(128, 768, dtype=f32)),
-            ("d", whole(1, 2304, dtype=f32)),
+            ("v", whole(1, 4608, dtype=f32)),
         ],
-        lazy=(7,),
+        lazy=(9,),
         cost=0,
     )
     dh = lax.all_to_all(dh_payload, PLANE, 0, 0, tiled=True)
     dattn_sent = lax.ppermute(dattn_attn, "core", SWAP)
+    vec_two_sent = lax.ppermute(vec_two, "core", SWAP)
     ffn_products = call(
         ffn_products_kernel, "ffn_products",
         [("v", ffn_here), ("v", ffn_core), ("v", ffn_high), ("v", ffn_cross)]
-        + [("v", dattn_attn), ("v", dattn_sent)]
-        + copied(vec_up, vec_down, vec_two),
-        [("d", whole(768, 1152))],
-    )
-    ffn_blocks = lax.all_to_all(ffn_products.reshape(16, 48, 1152), PLANE, 0, 0, tiled=True)
+        + [("v", dattn_attn), ("v", dattn_sent), ("v", vec_two), ("v", vec_two_sent)],
+        [("d", whole(768, 1024))],
+    )
+    ffn_blocks = lax.all_to_all(ffn_products.reshape(16, 48, 1024), PLANE, 0, 0, tiled=True)
     ffn_other = lax.ppermute(ffn, "wa", SWAP)
     given, kept, dq, edge_grad = attend_grad(kv, q_rows, start_rows, full_rows, dh)
     given, ffn_other = lax.optimization_barrier((given, ffn_other))
@@ -939,7 +941,7 @@
     grads = lax.all_to_all(merged, CHIPS, 0, 0, tiled=True)
     ffn_core, ffn_high, ffn_cross, ffn_here = call(
         ffn_sums_kernel, "ffn_sums", copied(ffn_blocks),
-        [("v", whole(24, 1024, dtype=f32)) for _ in range(4)],
+        [("v", whole(32, 1024)) for _ in range(3)] + [("v", whole(32, 1024, dtype=f32))],
         cost=0,
     )
     ffn_core = lax.ppermute(ffn_core, "core", SWAP)
@@ -960,11 +962,12 @@
         lazy=(2, 3, 4),
         cost=0,
     )
-    dn_one_other = lax.ppermute(dn_one, "wa", SWAP)
     grads_sent = lax.ppermute(grads_rows, "core", SWAP)
     vec_sent = lax.ppermute(vec, "core", SWAP)
     norms_wa = lax.ppermute(norms, "wa", SWAP)
     norms_cross = lax.ppermute(norms, ("core", "wa"), CROSS)
+    norms_wa, norms_cross, dn_one = lax.optimization_barrier((norms_wa, norms_cross, dn_one))
+    dn_one_other = lax.ppermute(dn_one, "wa", SWAP)
     products = call(
         qkv_products_kernel, "qkv_products",
         copied(x_keep, x_sent)
@@ -973,7 +976,6 @@
         [("d", whole(32, 16, 1152))],
         cost=0,
     )
-    products, dn_one_other = lax.optimization_barrier((products, dn_one_other))
     products = lax.all_to_all(products, CHIPS, 0, 0, tiled=True)
     output = call(
         output_kernel, "output",

time: 198 us -> 192 us (0.970)
  waiting for transfers between devices: 55.7 us -> 49.1 us
    ppermute x1, waiting for transfers between devices: 0.01 us -> 12 us  [on_device(): dn_one_other = lax.ppermute(dn_one, 'wa', SWAP)]
    all_to_all x1, waiting for transfers between devices: 11 us -> 0.01 us  [on_device(): products = lax.all_to_all(products, CHIPS, 0, 0, tiled=True)]
    ppermute x1, waiting for transfers between devices: 5.44 us -> 1.62 us  [on_device(): norms_cross = lax.ppermute(norms, ('core', 'wa'), CROSS)]
    ppermute x1, waiting for transfers between devices: 3.48 us -> 0.85 us  [on_device(): edge_got = lax.ppermute(edge_grad, 'y', ((0, 1), (2, 3)))]
    ppermute x2, waiting for transfers between devices: 8.85 us -> 6.57 us  [on_device(): ffn_cross = lax.ppermute(ffn_cross, ('zh', 'core'), CROSS)]
  transfers between devices with their start and end apart: 28 -> 29, of which waited for: 11 -> 12; matrix products, arithmetic and copies ran while one was open for 0% -> 0% of each run, Pallas kernels for 25% -> 23%
where the time goes in v2:
time: 192 us; the launch traced here: 189 us
  Pallas kernels  70.1 us (37%)
  starting transfers between devices  66.2 us (34%)
  waiting for transfers between devices  49.1 us (26%)
  local copies, waits for them, and re-layouts  2.43 us (1%)
    pallas_call x17, Pallas kernels, call(): pl.pallas_call(body, out_shape=tuple((out for _, out in outs)), in_specs=...  70.1 us
    ppermute x1, waiting for transfers between devices, on_device(): dn_one_other = lax.ppermute(dn_one, 'wa', SWAP)  12 us
    ppermute x2, waiting for transfers between devices, on_device(): ffn_high = lax.ppermute(ffn_high, 'zh', SWAP)  8.26 us
    all_to_all x1, waiting for transfers between devices, on_device(): got = lax.all_to_all(back, ('x', 'y', 'wa'), 0, 0, tiled=True)  7.65 us
    all_to_all x1, starting transfers between devices, on_device(): grads = lax.all_to_all(merged, CHIPS, 0, 0, tiled=True)  6.86 us
    all_to_all x1, starting transfers between devices, on_device(): own = lax.all_to_all(payload, PLANE, 0, 0, tiled=True)  6.8 us
    ppermute x2, waiting for transfers between devices, on_device(): ffn_cross = lax.ppermute(ffn_cross, ('zh', 'core'), CROSS)  6.57 us
    all_to_all x1, waiting for transfers between devices, on_device(): own = lax.all_to_all(payload, PLANE, 0, 0, tiled=True)  5.99 us
  transfers between devices with their start and end apart: 29, of which 12 were waited for; matrix products, arithmetic and copies ran while one was open for 0% of the time, Pallas kernels for 23%

profile of v2, /device:TPU:1, one launch (start us, length us, event | category | flops | bytes accessed | tf_op | source)
XLA Modules:
  0.0 188.9 jit_solution(1351505695953909857)
XLA Ops:
  0.7 3.2 %project.1 = (bf16[16,112,128]{2,1,0:T(8,128)(2,1)}, bf16[128,768]{1,0:T(8,128)(2,1)}) custom-call(bf16[128,768]{1,0:T(8,128)(2,1)} %refs_2_.9, s32[128]{0:T(128)} %refs_1_.5, f32[768]{0:T(1024)} %refs_5_.9, f32[768]{0:T(1024)} %refs_3_.6, f32[384]{0:T(512)} %refs_4_.6, f32[384]{0:T(512)} %refs_5_.5, bf16[768,384]{1,0:T(8,128)(2,1)} %refs_2_.8, ...), custom_call_target="tpu_custom_call" | custom-call | flops 2000000000 | tf_op jit(solution)/shard_map/project/pallas_call | solution.py:138
  3.9 2.5 %collective-permute-start = (bf16[384,768]{1,0:T(8,128)(2,1)}, bf16[384,768]{1,0:T(8,128)(2,1)}, u32[]{:S(2)}, u32[]{:S(2)}) collective-permute-start(bf16[384,768]{1,0:T(8,128)(2,1)} %refs_9_.1), channel_id=1, source_target_pairs={{0,1},{1,0},{2,3},{3,2},{4,5},{5,4},{6,7},{7,6},{8,9},{9,8},{10,11... | collective-permute-start | bytes 1769480 | tf_op jit(solution)/shard_map/ppermute | solution.py:859
  6.4 6.8 %all-to-all-start = ((bf16[16,112,128]{2,1,0:T(8,128)(2,1)}), bf16[16,112,128]{2,1,0:T(8,128)(2,1)}, u32[]{:S(2)}, u32[]{:S(2)}) async-start(bf16[16,112,128]{2,1,0:T(8,128)(2,1)} %get-tuple-element.97), calls=%async_computation | async-start | bytes 917504 | tf_op jit(solution)/shard_map/all_to_all | solution.py:857
  13.2 2.7 %prepare.1 = (bf16[128,512]{1,0:T(8,128)(2,1)}, bf16[128,512]{1,0:T(8,128)(2,1)}) custom-call(bf16[128,768]{1,0:T(8,128)(2,1)} %get-tuple-element.95.refs_0_), custom_call_target="tpu_custom_call" | custom-call | flops 2000000000 | tf_op jit(solution)/shard_map/prepare/pallas_call | solution.py:138
  15.9 6.0 %all-to-all-done.refs_0_ = bf16[16,112,128]{2,1,0:T(8,128)(2,1)} async-done(((bf16[16,112,128]{2,1,0:T(8,128)(2,1)}), bf16[16,112,128]{2,1,0:T(8,128)(2,1)}, u32[]{:S(2)}, u32[]{:S(2)}) %all-to-all-start) | async-done | bytes 458784 | tf_op jit(solution)/shard_map/all_to_all | solution.py:857
  21.9 1.0 slice.6
  22.8 3.4 %collective-permute-start.2 = (bf16[16,64,128]{2,1,0:T(8,128)(2,1)S(1)}, bf16[16,64,128]{2,1,0:T(8,128)(2,1)S(1)}, u32[]{:S(2)}, u32[]{:S(2)}) collective-permute-start(bf16[16,64,128]{2,1,0:T(8,128)(2,1)S(1)} %slice.6), channel_id=1, source_target_pairs={{0,4},{4,0},{1,5},{5,1},{2,6},{6,2},{3,7},{7,3},{8,12},{12,8},{9,1... | collective-permute-start | bytes 786440 | tf_op jit(solution)/shard_map/ppermute | solution.py:869
  26.2 0.8 slice_bitcast_fusion
  27.0 1.3 collective-permute-start.3
  28.3 3.5 %collective-permute-start.1 = (bf16[16,64,128]{2,1,0:T(8,128)(2,1)S(1)}, bf16[16,64,128]{2,1,0:T(8,128)(2,1)S(1)}, u32[]{:S(2)}, u32[]{:S(2)}) collective-permute-start(bf16[16,64,128]{2,1,0:T(8,128)(2,1)S(1)} %slice.6), channel_id=1, source_target_pairs={{0,2},{2,0},{1,3},{3,1},{4,6},{6,4},{5,7},{7,5},{8,10},{10,8},{9,1... | collective-permute-start | bytes 786440 | tf_op jit(solution)/shard_map/ppermute | solution.py:867
  31.9 4.4 %collective-permute-start.4 = (bf16[16,64,128]{2,1,0:T(8,128)(2,1)S(1)}, bf16[16,64,128]{2,1,0:T(8,128)(2,1)}, u32[]{:S(2)}, u32[]{:S(2)}) collective-permute-start(bf16[16,64,128]{2,1,0:T(8,128)(2,1)S(1)} %collective-permute-done.2.refs_2_), channel_id=1, source_target_pairs={{0,2},{2,0},{1,3},{3,1},{4,6},{6,4},{5,7},{7,5},{8,10},{10,8},{9,1... | collective-permute-start | bytes 786440 | tf_op jit(solution)/shard_map/ppermute | solution.py:871
  37.5 6.3 %attend.1 = (bf16[32,64,128]{2,1,0:T(8,128)(2,1)}, bf16[17,256,128]{2,1,0:T(8,128)(2,1)}, bf16[1088,128]{1,0:T(8,128)(2,1)}, f32[1088,128]{1,0:T(8,128)}, f32[1088,128]{1,0:T(8,128)}) custom-call(bf16[16,112,128]{2,1,0:T(8,128)(2,1)} %all-to-all-done.refs_0_, bf16[16,64,128]{2,1,0:T(8,128)(2,1)} %copy-done.1, bf16[16,64,128]{2,1,0:T(8,128)(2,1)} %copy-done, ...), custom_call_target="tpu_custom_call" | custom-call | flops 3000000000 | tf_op jit(solution)/shard_map/attend/pallas_call | solution.py:138
  43.9 4.6 %all-to-all-start.1 = ((bf16[32,64,128]{2,1,0:T(8,128)(2,1)}), bf16[32,64,128]{2,1,0:T(8,128)(2,1)}, u32[]{:S(2)}, u32[]{:S(2)}) async-start(bf16[32,64,128]{2,1,0:T(8,128)(2,1)} %get-tuple-element.107), calls=%async_computation.1 | async-start | bytes 1048576 | tf_op jit(solution)/shard_map/all_to_all | solution.py:879
  48.5 3.7 %dhidden.1 = (f32[128,1536]{1,0:T(8,128)}, f32[1,768]{1,0:T(1,128)}) custom-call(bf16[128,768]{1,0:T(8,128)(2,1)} %refs_3_.11, s32[128]{0:T(128)} %refs_4_.11, bf16[1536,768]{1,0:T(8,128)(2,1)} %refs_1_.8), custom_call_target="tpu_custom_call" | custom-call | flops 2000000000 | tf_op jit(solution)/shard_map/dhidden/pallas_call | solution.py:138
  52.2 7.6 %all-to-all-done.1.refs_0_ = bf16[32,64,128]{2,1,0:T(8,128)(2,1)} async-done(((bf16[32,64,128]{2,1,0:T(8,128)(2,1)}), bf16[32,64,128]{2,1,0:T(8,128)(2,1)}, u32[]{:S(2)}, u32[]{:S(2)}) %all-to-all-start.1) | async-done | bytes 524320 | tf_op jit(solution)/shard_map/all_to_all | solution.py:879
  59.8 6.9 %middle.1 = (bf16[128,768]{1,0:T(8,128)(2,1)}, bf16[128,1536]{1,0:T(8,128)(2,1)}, bf16[128,1536]{1,0:T(8,128)(2,1)}, bf16[128,1536]{1,0:T(8,128)(2,1)}, bf16[128...) custom-call(bf16[32,64,128]{2,1,0:T(8,128)(2,1)} %all-to-all-done.1., ...), custom_call_target="tpu_custom_call" | custom-call | flops 2000000000 | tf_op jit(solution)/shard_map/middle/pallas_call | solution.py:138
  67.1 1.9 %collective-permute-start.9 = (bf16[128,1536]{1,0:T(8,128)(2,1)}, bf16[128,1536]{1,0:T(8,128)(2,1)}, u32[]{:S(2)}, u32[]{:S(2)}) collective-permute-start(bf16[128,1536]{1,0:T(8,128)(2,1)} %get-tuple-element.125), channel_id=1, source_target_pairs={{0,2},{2,0},{1,3},{3,1},{4,6},{6,4},{5,7},{7,5},{8,10},{10,8},{9,1... | collective-permute-start | bytes 1179656 | tf_op jit(solution)/shard_map/ppermute | solution.py:904
  69.1 1.5 collective-permute-start.10
  70.6 1.6 collective-permute-start.11
  72.2 3.0 %ffn.1.refs_0_ = bf16[128,768]{1,0:T(8,128)(2,1)} custom-call(bf16[128,1536]{1,0:T(8,128)(2,1)} %get-tuple-element.111.refs_0_, bf16[1536,768]{1,0:T(8,128)(2,1)} %refs_1_.8), custom_call_target="tpu_custom_call" | custom-call | tf_op jit(solution)/shard_map/ffn/pallas_call | solution.py:138
  75.2 4.6 %dheads.1 = (bf16[16,64,128]{2,1,0:T(8,128)(2,1)}, bf16[128,1152]{1,0:T(8,128)(2,1)}, f32[128,768]{1,0:T(8,128)}, f32[1,4608]{1,0:T(1,128)}) custom-call(bf16[128,768]{1,0:T(8,128)(2,1)} %get-tuple-element.110.refs_0_, bf16[128,768]{1,0:T(8,128)(2,1)} %collective-permute-done.5.refs_1_, f32[128,768]{1,0:T(8,128)} %get-tuple-element.113.refs_2_, ...), custom_call_target="tpu_custom_call" | custom-call | tf_op jit(solution)/shard_map/dheads/pallas_call | solution.py:138
  80.5 4.2 %all-to-all-start.2 = ((bf16[16,64,128]{2,1,0:T(8,128)(2,1)}), bf16[16,64,128]{2,1,0:T(8,128)(2,1)}, u32[]{:S(2)}, u32[]{:S(2)}) async-start(bf16[16,64,128]{2,1,0:T(8,128)(2,1)} %get-tuple-element.117), calls=%async_computation.2 | async-start | bytes 524288 | tf_op jit(solution)/shard_map/all_to_all | solution.py:920
  85.0 1.5 collective-permute-done.13.refs_7_
  86.5 0.7 collective-permute-start.6
  87.2 4.9 %collective-permute-done.11.refs_3_ = bf16[128,1536]{1,0:T(8,128)(2,1)} collective-permute-done((bf16[128,1536]{1,0:T(8,128)(2,1)}, bf16[128,1536]{1,0:T(8,128)(2,1)}, u32[]{:S(2)}, u32[]{:S(2)}) %collective-permute-start.11) | collective-permute-done | bytes 393248 | tf_op jit(solution)/shard_map/ppermute | solution.py:903
  92.1 3.8 %ffn_products.1 = bf16[768,1024]{1,0:T(8,128)(2,1)} custom-call(bf16[128,1536]{1,0:T(8,128)(2,1)} %get-tuple-element.124.refs_0_, bf16[128,1536]{1,0:T(8,128)(2,1)} %collective-permute-done.9.refs_1_, bf16[128,1536]{1,0:T(8,128)(2,1)} %collective-permute-done.10.refs_2_, bf16[128,1536]{1,0:T(8,128)(2,1)} %collective-permute-done.11.refs_3_, ...), custom_call_target="tpu_custom_call" | custom-call | flops 2000000000 | tf_op jit(solution)/shard_map/ffn_products/pallas_call | solution.py:138
  96.0 4.4 %all-to-all-start.3 = ((bf16[16,48,1024]{2,1,0:T(8,128)(2,1)}), bf16[16,48,1024]{2,1,0:T(8,128)(2,1)}, u32[]{:S(2)}, u32[]{:S(2)}) async-start(bf16[16,48,1024]{2,1,0:T(8,128)(2,1)} %bitcast.3), calls=%async_computation.3 | async-start | bytes 3145728 | tf_op jit(solution)/shard_map/all_to_all | solution.py:929
  100.4 13.4 %attend_grad.1 = (bf16[32,64,128]{2,1,0:T(8,128)(2,1)}, bf16[32,64,128]{2,1,0:T(8,128)(2,1)}, bf16[16,32,128]{2,1,0:T(8,128)(2,1)}, bf16[96,128]{1,0:T(8,128)(2,1)}) custom-call(bf16[17,256,128]{2,1,0:T(8,128)(2,1)} %get-tuple-element.103.refs_0_, bf16[1088,128]{1,0:T(8,128)(2,1)} %get-tuple-element.104.refs_1_, f32[1088,128]{1,0:T(8,128)} %get-tuple-element.105.refs_2_, ...), custom_call_target="tpu_custom_call" | custom-call | flops 40000000000 | tf_op jit(solution)/shard_map/attend_grad/pallas_call | solution.py:138
  113.9 3.7 %collective-permute-start.8 = (bf16[96,128]{1,0:T(8,128)(2,1)}, bf16[96,128]{1,0:T(8,128)(2,1)}, u32[]{:S(2)}, u32[]{:S(2)}) collective-permute-start(bf16[96,128]{1,0:T(8,128)(2,1)} %get-tuple-element.123), channel_id=1, source_target_pairs={{0,8},{16,24},{1,9},{17,25},{2,10},{18,26},{3,11},{19,27},{4,12},{... | collective-permute-start | bytes 73736 | tf_op jit(solution)/shard_map/ppermute | solution.py:933
  117.6 0.8 collective-permute-done.8.refs_3_
  118.4 2.3 %merge.1 = bf16[32,96,128]{2,1,0:T(8,128)(2,1)} custom-call(bf16[32,64,128]{2,1,0:T(8,128)(2,1)} %get-tuple-element.118.refs_0_, bf16[32,64,128]{2,1,0:T(8,128)(2,1)} %collective-permute-done.7.refs_1_, bf16[16,32,128]{2,1,0:T(8,128)(2,1)} %get-tuple-element.122.refs_2_, bf16[96,128]{1,0:T(8,128)(2,1)} %collective-permute-done.8.refs_3_), custom_call_target="tpu_custom_call" | custom-call | flops 2000000000 | tf_op jit(solution)/shard_map/merge/pallas_call | solution.py:138
  120.7 3.9 %all-to-all-done.3.refs_0_ = bf16[16,48,1024]{2,1,0:T(8,128)(2,1)} async-done(((bf16[16,48,1024]{2,1,0:T(8,128)(2,1)}), bf16[16,48,1024]{2,1,0:T(8,128)(2,1)}, u32[]{:S(2)}, u32[]{:S(2)}) %all-to-all-start.3) | async-done | bytes 1572896 | tf_op jit(solution)/shard_map/all_to_all | solution.py:929
  124.6 6.9 %all-to-all-start.4 = ((bf16[32,96,128]{2,1,0:T(8,128)(2,1)}), bf16[32,96,128]{2,1,0:T(8,128)(2,1)}, u32[]{:S(2)}, u32[]{:S(2)}) async-start(bf16[32,96,128]{2,1,0:T(8,128)(2,1)} %merge.1), calls=%async_computation.4 | async-start | bytes 1572864 | tf_op jit(solution)/shard_map/all_to_all | solution.py:941
  131.5 0.8 collective-permute-start.17
  132.4 2.4 %ffn_sums.1 = (bf16[32,1024]{1,0:T(8,128)(2,1)}, bf16[32,1024]{1,0:T(8,128)(2,1)}, bf16[32,1024]{1,0:T(8,128)(2,1)}, f32[32,1024]{1,0:T(8,128)}) custom-call(bf16[16,48,1024]{2,1,0:T(8,128)(2,1)} %all-to-all-done.3.refs_0_), custom_call_target="tpu_custom_call" | custom-call | tf_op jit(solution)/shard_map/ffn_sums/pallas_call | solution.py:138
  135.1 3.0 %collective-permute-start.15 = (bf16[32,1024]{1,0:T(8,128)(2,1)}, bf16[32,1024]{1,0:T(8,128)(2,1)}, u32[]{:S(2)}, u32[]{:S(2)}) collective-permute-start(bf16[32,1024]{1,0:T(8,128)(2,1)} %get-tuple-element.133), channel_id=1, source_target_pairs={{0,4},{4,0},{1,5},{5,1},{2,6},{6,2},{3,7},{7,3},{8,12},{12,8},{9,1... | collective-permute-start | bytes 196616 | tf_op jit(solution)/shard_map/ppermute | solution.py:948
  138.7 8.3 %collective-permute-done.15.refs_2_ = bf16[32,1024]{1,0:T(8,128)(2,1)} collective-permute-done((bf16[32,1024]{1,0:T(8,128)(2,1)}, bf16[32,1024]{1,0:T(8,128)(2,1)}, u32[]{:S(2)}, u32[]{:S(2)}) %collective-permute-start.15) | collective-permute-done | bytes 65568 | tf_op jit(solution)/shard_map/ppermute | solution.py:948
  147.0 1.7 collective-permute-done.16.refs_3_
  148.7 4.0 %dnormed.1 = (bf16[128,1152]{1,0:T(8,128)(2,1)}, f32[1,1536]{1,0:T(1,128)}, f32[1,2304]{1,0:T(1,128)}, bf16[128,768]{1,0:T(8,128)(2,1)}) custom-call(bf16[32,96,128]{2,1,0:T(8,128)(2,1)} %all-to-all-done.4.refs_0_, bf16[128,768]{1,0:T(8,128)(2,1)} %refs_2_.9, bf16[768,384]{1,0:T(8,128)(2,1)} %refs_2_.8, bf16[768,384]{1,0:T(8,128)(2,1)} %refs_3_.9, ...), custom_call_target="tpu_custom_call" | custom-call | tf_op jit(solution)/shard_map/dnormed/pallas_call | solution.py:138
  153.7 1.4 collective-permute-start.20
  155.0 1.6 collective-permute-done.21.refs_7_
  156.7 3.7 %qkv_products.1 = bf16[32,16,1152]{2,1,0:T(8,128)(2,1)} custom-call(bf16[128,512]{1,0:T(8,128)(2,1)} %get-tuple-element.96.refs_0_, bf16[128,512]{1,0:T(8,128)(2,1)} %collective-permute-done.17.refs_1_, bf16[128,1152]{1,0:T(8,128)(2,1)} %get-tuple-element.138.refs_2_, bf16[128,1152]{1,0:T(8,128)(2,1)} %collective-permute-done.18.refs_3_, ...), custom_call_target="tpu_custom_call" | custom-call | tf_op jit(solution)/shard_map/qkv_products/pallas_call | solution.py:138
  160.4 5.5 %all-to-all-start.5 = ((bf16[32,16,1152]{2,1,0:T(8,128)(2,1)}), bf16[32,16,1152]{2,1,0:T(8,128)(2,1)}, u32[]{:S(2)}, u32[]{:S(2)}) async-start(bf16[32,16,1152]{2,1,0:T(8,128)(2,1)} %qkv_products.1), calls=%async_computation.5 | async-start | bytes 2359296 | tf_op jit(solution)/shard_map/all_to_all | solution.py:979
  166.5 2.9 %output.1 = bf16[128,768]{1,0:T(8,128)(2,1)} custom-call(bf16[128,768]{1,0:T(8,128)(2,1)} %ffn.1.refs_0_, bf16[128,768]{1,0:T(8,128)(2,1)} %collective-permute-done.6.refs_1_, f32[128,768]{1,0:T(8,128)} %get-tuple-element.113.refs_2_, bf16[128,768]{1,0:T(8,128)(2,1)} %refs_2_.9, s32[128]{0:T(128)} %refs_4_.11, f32[768]{0:T(1024)} %refs_5_.8), custom_call_target="tpu_custom_call" | custom-call | tf_op jit(solution)/shard_map/output/pallas_call | solution.py:138
  169.4 1.8 ffn_finish.1
  171.1 12.0 %collective-permute-done.22.refs_1_ = bf16[128,768]{1,0:T(8,128)(2,1)} collective-permute-done((bf16[128,768]{1,0:T(8,128)(2,1)}, bf16[128,768]{1,0:T(8,128)(2,1)}, u32[]{:S(2)}, u32[]{:S(2)}) %collective-permute-start.22) | collective-permute-done | bytes 196640 | tf_op jit(solution)/shard_map/ppermute | solution.py:970
  183.1 3.4 %input_grad.1 = f32[128,768]{1,0:T(8,128)} custom-call(bf16[128,768]{1,0:T(8,128)(2,1)} %get-tuple-element.145.refs_0_, bf16[128,768]{1,0:T(8,128)(2,1)} %collective-permute-done.22.refs_1_, bf16[128,768]{1,0:T(8,128)(2,1)} %refs_2_.9, bf16[128,768]{1,0:T(8,128)(2,1)} %refs_3_.11, s32[128]{0:T(128)} %refs_4_.11, f32[768]{0:T(1024)} %refs_5_.9, ...), custom_call_target="tpu_custom_call" | custom-call | tf_op jit(solution)/shard_map/input_grad/pallas_call | solution.py:138
  186.6 2.1 %finish.1 = (f32[12,384]{1,0:T(8,128)}, f32[12,384]{1,0:T(8,128)}, f32[12,384]{1,0:T(8,128)}, f32[768]{0:T(1024)}, f32[768]{0:T(1024)}, /*index=5*/f32[384]{0:T(512)}, f32[384]{0:T(512)}) custom-call(bf16[32,16,1152]{2,1,0:T(8,128)(2,1)} %all-to-all-done.5.refs_0_), custom_call_target="tpu_custom_call" | custom-call | flops 2000000000 | tf_op jit(solution)/shard_map/finish/pallas_call | solution.py:138
  (35 shorter events, 5.4 us)
Async XLA Ops:
  3.9 18.0 %collective-permute-start = (bf16[384,768]{1,0:T(8,128)(2,1)}, bf16[384,768]{1,0:T(8,128)(2,1)}, u32[]{:S(2)}, u32[]{:S(2)}) collective-permute-start(bf16[384,768]{1,0:T(8,128)(2,1)} %refs_9_.1), channel_id=1, source_target_pairs={{0,1},{1,0},{2,3},{3,2},{4,5},{5,4},{6,7},{7,6},{8,9},{9,8},{10,11... | collective-permute-start | bytes 1769480 | tf_op jit(solution)/shard_map/ppermute | solution.py:859
  6.4 15.5 %all-to-all-start = ((bf16[16,112,128]{2,1,0:T(8,128)(2,1)}), bf16[16,112,128]{2,1,0:T(8,128)(2,1)}, u32[]{:S(2)}, u32[]{:S(2)}) async-start(bf16[16,112,128]{2,1,0:T(8,128)(2,1)} %get-tuple-element.97), calls=%async_computation | async-start | bytes 917504 | tf_op jit(solution)/shard_map/all_to_all | solution.py:857
  22.8 9.0 %collective-permute-start.2 = (bf16[16,64,128]{2,1,0:T(8,128)(2,1)S(1)}, bf16[16,64,128]{2,1,0:T(8,128)(2,1)S(1)}, u32[]{:S(2)}, u32[]{:S(2)}) collective-permute-start(bf16[16,64,128]{2,1,0:T(8,128)(2,1)S(1)} %slice.6), channel_id=1, source_target_pairs={{0,4},{4,0},{1,5},{5,1},{2,6},{6,2},{3,7},{7,3},{8,12},{12,8},{9,1... | collective-permute-start | bytes 786440 | tf_op jit(solution)/shard_map/ppermute | solution.py:869
  27.0 4.9 %collective-permute-start.3 = (bf16[112,128]{1,0:T(8,128)(2,1)S(1)}, bf16[112,128]{1,0:T(8,128)(2,1)S(1)}, u32[]{:S(2)}, u32[]{:S(2)}) collective-permute-start(bf16[112,128]{1,0:T(8,128)(2,1)S(1)} %slice_bitcast_fusion), channel_id=1, source_target_pairs={{8,0},{24,16},{9,1},{25,17},{10,2},{26,18},{11,3},{27,19},{12,4},{... | collective-permute-start | bytes 86024 | tf_op jit(solution)/shard_map/ppermute | solution.py:868
  28.3 8.0 %collective-permute-start.1 = (bf16[16,64,128]{2,1,0:T(8,128)(2,1)S(1)}, bf16[16,64,128]{2,1,0:T(8,128)(2,1)S(1)}, u32[]{:S(2)}, u32[]{:S(2)}) collective-permute-start(bf16[16,64,128]{2,1,0:T(8,128)(2,1)S(1)} %slice.6), channel_id=1, source_target_pairs={{0,2},{2,0},{1,3},{3,1},{4,6},{6,4},{5,7},{7,5},{8,10},{10,8},{9,1... | collective-permute-start | bytes 786440 | tf_op jit(solution)/shard_map/ppermute | solution.py:867
  31.9 4.4 %copy-start.2 = (bf16[112,128]{1,0:T(8,128)(2,1)}, bf16[112,128]{1,0:T(8,128)(2,1)S(1)}, u32[]{:S(2)}) copy-start(bf16[112,128]{1,0:T(8,128)(2,1)S(1)} %collective-permute-done.3.refs_4_) | copy-start | bytes 86020
  31.9 4.4 %copy-start = (bf16[16,64,128]{2,1,0:T(8,128)(2,1)}, bf16[16,64,128]{2,1,0:T(8,128)(2,1)S(1)}, u32[]{:S(2)}) copy-start(bf16[16,64,128]{2,1,0:T(8,128)(2,1)S(1)} %collective-permute-done.2.refs_2_) | copy-start | bytes 786436
  31.9 5.6 %collective-permute-start.4 = (bf16[16,64,128]{2,1,0:T(8,128)(2,1)S(1)}, bf16[16,64,128]{2,1,0:T(8,128)(2,1)}, u32[]{:S(2)}, u32[]{:S(2)}) collective-permute-start(bf16[16,64,128]{2,1,0:T(8,128)(2,1)S(1)} %collective-permute-done.2.refs_2_), channel_id=1, source_target_pairs={{0,2},{2,0},{1,3},{3,1},{4,6},{6,4},{5,7},{7,5},{8,10},{10,8},{9,1... | collective-permute-start | bytes 786440 | tf_op jit(solution)/shard_map/ppermute | solution.py:871
  36.2 0.7 copy-start.1
  43.9 15.9 %all-to-all-start.1 = ((bf16[32,64,128]{2,1,0:T(8,128)(2,1)}), bf16[32,64,128]{2,1,0:T(8,128)(2,1)}, u32[]{:S(2)}, u32[]{:S(2)}) async-start(bf16[32,64,128]{2,1,0:T(8,128)(2,1)} %get-tuple-element.107), calls=%async_computation.1 | async-start | bytes 1048576 | tf_op jit(solution)/shard_map/all_to_all | solution.py:879
  66.7 8.5 %collective-permute-start.5 = (bf16[128,768]{1,0:T(8,128)(2,1)}, bf16[128,768]{1,0:T(8,128)(2,1)}, u32[]{:S(2)}, u32[]{:S(2)}) collective-permute-start(bf16[128,768]{1,0:T(8,128)(2,1)} %get-tuple-element.110.refs_0_), channel_id=1, source_target_pairs={{0,1},{1,0},{2,3},{3,2},{4,5},{5,4},{6,7},{7,6},{8,9},{9,8},{10,11... | collective-permute-start | bytes 589832 | tf_op jit(solution)/shard_map/ppermute | solution.py:901
  67.1 20.1 %collective-permute-start.9 = (bf16[128,1536]{1,0:T(8,128)(2,1)}, bf16[128,1536]{1,0:T(8,128)(2,1)}, u32[]{:S(2)}, u32[]{:S(2)}) collective-permute-start(bf16[128,1536]{1,0:T(8,128)(2,1)} %get-tuple-element.125), channel_id=1, source_target_pairs={{0,2},{2,0},{1,3},{3,1},{4,6},{6,4},{5,7},{7,5},{8,10},{10,8},{9,1... | collective-permute-start | bytes 1179656 | tf_op jit(solution)/shard_map/ppermute | solution.py:904
  69.1 18.2 %collective-permute-start.10 = (bf16[128,1536]{1,0:T(8,128)(2,1)}, bf16[128,1536]{1,0:T(8,128)(2,1)}, u32[]{:S(2)}, u32[]{:S(2)}) collective-permute-start(bf16[128,1536]{1,0:T(8,128)(2,1)} %get-tuple-element.126), channel_id=1, source_target_pairs={{0,4},{4,0},{1,5},{5,1},{2,6},{6,2},{3,7},{7,3},{8,12},{12,8},{9,1... | collective-permute-start | bytes 1179656 | tf_op jit(solution)/shard_map/ppermute | solution.py:902
  70.6 21.5 %collective-permute-start.11 = (bf16[128,1536]{1,0:T(8,128)(2,1)}, bf16[128,1536]{1,0:T(8,128)(2,1)}, u32[]{:S(2)}, u32[]{:S(2)}) collective-permute-start(bf16[128,1536]{1,0:T(8,128)(2,1)} %get-tuple-element.127), channel_id=1, source_target_pairs={{0,6},{2,4},{4,2},{6,0},{1,7},{3,5},{5,3},{7,1},{8,14},{10,12},{12... | collective-permute-start | bytes 1179656 | tf_op jit(solution)/shard_map/ppermute | solution.py:903
  79.8 12.3 %collective-permute-start.12 = (bf16[128,1152]{1,0:T(8,128)(2,1)}, bf16[128,1152]{1,0:T(8,128)(2,1)}, u32[]{:S(2)}, u32[]{:S(2)}) collective-permute-start(bf16[128,1152]{1,0:T(8,128)(2,1)} %get-tuple-element.128.refs_4_), channel_id=1, source_target_pairs={{0,2},{2,0},{1,3},{3,1},{4,6},{6,4},{5,7},{7,5},{8,10},{10,8},{9,1... | collective-permute-start | bytes 884744 | tf_op jit(solution)/shard_map/ppermute | solution.py:921
  80.5 15.5 %all-to-all-start.2 = ((bf16[16,64,128]{2,1,0:T(8,128)(2,1)}), bf16[16,64,128]{2,1,0:T(8,128)(2,1)}, u32[]{:S(2)}, u32[]{:S(2)}) async-start(bf16[16,64,128]{2,1,0:T(8,128)(2,1)} %get-tuple-element.117), calls=%async_computation.2 | async-start | bytes 524288 | tf_op jit(solution)/shard_map/all_to_all | solution.py:920
  84.7 1.8 collective-permute-start.13
  86.5 27.3 %collective-permute-start.6 = (bf16[128,768]{1,0:T(8,128)(2,1)}, bf16[128,768]{1,0:T(8,128)(2,1)}, u32[]{:S(2)}, u32[]{:S(2)}) collective-permute-start(bf16[128,768]{1,0:T(8,128)(2,1)} %ffn.1.refs_0_), channel_id=1, source_target_pairs={{0,1},{1,0},{2,3},{3,2},{4,5},{5,4},{6,7},{7,6},{8,9},{9,8},{10,11... | collective-permute-start | bytes 589832 | tf_op jit(solution)/shard_map/ppermute | solution.py:930
  96.0 28.7 %all-to-all-start.3 = ((bf16[16,48,1024]{2,1,0:T(8,128)(2,1)}), bf16[16,48,1024]{2,1,0:T(8,128)(2,1)}, u32[]{:S(2)}, u32[]{:S(2)}) async-start(bf16[16,48,1024]{2,1,0:T(8,128)(2,1)} %bitcast.3), calls=%async_computation.3 | async-start | bytes 3145728 | tf_op jit(solution)/shard_map/all_to_all | solution.py:929
  113.8 4.6 %collective-permute-start.7 = (bf16[32,64,128]{2,1,0:T(8,128)(2,1)}, bf16[32,64,128]{2,1,0:T(8,128)(2,1)}, u32[]{:S(2)}, u32[]{:S(2)}) collective-permute-start(bf16[32,64,128]{2,1,0:T(8,128)(2,1)} %get-tuple-element.121), channel_id=1, source_target_pairs={{0,2},{2,0},{1,3},{3,1},{4,6},{6,4},{5,7},{7,5},{8,10},{10,8},{9,1... | collective-permute-start | bytes 1572872 | tf_op jit(solution)/shard_map/ppermute | solution.py:934
  113.9 4.5 %collective-permute-start.8 = (bf16[96,128]{1,0:T(8,128)(2,1)}, bf16[96,128]{1,0:T(8,128)(2,1)}, u32[]{:S(2)}, u32[]{:S(2)}) collective-permute-start(bf16[96,128]{1,0:T(8,128)(2,1)} %get-tuple-element.123), channel_id=1, source_target_pairs={{0,8},{16,24},{1,9},{17,25},{2,10},{18,26},{3,11},{19,27},{4,12},{... | collective-permute-start | bytes 73736 | tf_op jit(solution)/shard_map/ppermute | solution.py:933
  124.6 24.0 %all-to-all-start.4 = ((bf16[32,96,128]{2,1,0:T(8,128)(2,1)}), bf16[32,96,128]{2,1,0:T(8,128)(2,1)}, u32[]{:S(2)}, u32[]{:S(2)}) async-start(bf16[32,96,128]{2,1,0:T(8,128)(2,1)} %merge.1), calls=%async_computation.4 | async-start | bytes 1572864 | tf_op jit(solution)/shard_map/all_to_all | solution.py:941
  131.5 7.2 %collective-permute-start.17 = (bf16[128,512]{1,0:T(8,128)(2,1)}, bf16[128,512]{1,0:T(8,128)(2,1)}, u32[]{:S(2)}, u32[]{:S(2)}) collective-permute-start(bf16[128,512]{1,0:T(8,128)(2,1)} %get-tuple-element.135), channel_id=1, source_target_pairs={{0,2},{2,0},{1,3},{3,1},{4,6},{6,4},{5,7},{7,5},{8,10},{10,8},{9,1... | collective-permute-start | bytes 393224 | tf_op jit(solution)/shard_map/ppermute | solution.py:872
  134.7 4.0 %collective-permute-start.14 = (bf16[32,1024]{1,0:T(8,128)(2,1)}, bf16[32,1024]{1,0:T(8,128)(2,1)}, u32[]{:S(2)}, u32[]{:S(2)}) collective-permute-start(bf16[32,1024]{1,0:T(8,128)(2,1)} %get-tuple-element.132), channel_id=1, source_target_pairs={{0,2},{2,0},{1,3},{3,1},{4,6},{6,4},{5,7},{7,5},{8,10},{10,8},{9,1... | collective-permute-start | bytes 196616 | tf_op jit(solution)/shard_map/ppermute | solution.py:947
  135.1 11.9 %collective-permute-start.15 = (bf16[32,1024]{1,0:T(8,128)(2,1)}, bf16[32,1024]{1,0:T(8,128)(2,1)}, u32[]{:S(2)}, u32[]{:S(2)}) collective-permute-start(bf16[32,1024]{1,0:T(8,128)(2,1)} %get-tuple-element.133), channel_id=1, source_target_pairs={{0,4},{4,0},{1,5},{5,1},{2,6},{6,2},{3,7},{7,3},{8,12},{12,8},{9,1... | collective-permute-start | bytes 196616 | tf_op jit(solution)/shard_map/ppermute | solution.py:948
  138.1 10.6 %collective-permute-start.16 = (bf16[32,1024]{1,0:T(8,128)(2,1)}, bf16[32,1024]{1,0:T(8,128)(2,1)}, u32[]{:S(2)}, u32[]{:S(2)}) collective-permute-start(bf16[32,1024]{1,0:T(8,128)(2,1)} %get-tuple-element.134), channel_id=1, source_target_pairs={{0,6},{2,4},{4,2},{6,0},{1,7},{3,5},{5,3},{7,1},{8,14},{10,12},{12... | collective-permute-start | bytes 196616 | tf_op jit(solution)/shard_map/ppermute | solution.py:949
  152.7 4.0 %collective-permute-start.18 = (bf16[128,1152]{1,0:T(8,128)(2,1)}, bf16[128,1152]{1,0:T(8,128)(2,1)}, u32[]{:S(2)}, u32[]{:S(2)}) collective-permute-start(bf16[128,1152]{1,0:T(8,128)(2,1)} %get-tuple-element.138.refs_2_), channel_id=1, source_target_pairs={{0,2},{2,0},{1,3},{3,1},{4,6},{6,4},{5,7},{7,5},{8,10},{10,8},{9,1... | collective-permute-start | bytes 884744 | tf_op jit(solution)/shard_map/ppermute | solution.py:965
  153.2 3.5 %collective-permute-start.19 = (f32[1,2304]{1,0:T(1,128)}, f32[1,2304]{1,0:T(1,128)}, u32[]{:S(2)}, u32[]{:S(2)}) collective-permute-start(f32[1,2304]{1,0:T(1,128)} %get-tuple-element.139.refs_4_), channel_id=1, source_target_pairs={{0,2},{2,0},{1,3},{3,1},{4,6},{6,4},{5,7},{7,5},{8,10},{10,8},{9,1... | collective-permute-start | bytes 27656 | tf_op jit(solution)/shard_map/ppermute | solution.py:966
  153.3 3.4 %collective-permute-start.21 = (f32[1,1536]{1,0:T(1,128)}, f32[1,1536]{1,0:T(1,128)}, u32[]{:S(2)}, u32[]{:S(2)}) collective-permute-start(f32[1,1536]{1,0:T(1,128)} %get-tuple-element.140), channel_id=1, source_target_pairs={{0,3},{1,2},{2,1},{3,0},{4,7},{5,6},{6,5},{7,4},{8,11},{9,10},{10,... | collective-permute-start | bytes 18440 | tf_op jit(solution)/shard_map/ppermute | solution.py:968
  153.7 3.0 %collective-permute-start.20 = (f32[1,1536]{1,0:T(1,128)}, f32[1,1536]{1,0:T(1,128)}, u32[]{:S(2)}, u32[]{:S(2)}) collective-permute-start(f32[1,1536]{1,0:T(1,128)} %get-tuple-element.140), channel_id=1, source_target_pairs={{0,1},{1,0},{2,3},{3,2},{4,5},{5,4},{6,7},{7,6},{8,9},{9,8},{10,11... | collective-permute-start | bytes 18440 | tf_op jit(solution)/shard_map/ppermute | solution.py:967
  160.4 26.2 %all-to-all-start.5 = ((bf16[32,16,1152]{2,1,0:T(8,128)(2,1)}), bf16[32,16,1152]{2,1,0:T(8,128)(2,1)}, u32[]{:S(2)}, u32[]{:S(2)}) async-start(bf16[32,16,1152]{2,1,0:T(8,128)(2,1)} %qkv_products.1), calls=%async_computation.5 | async-start | bytes 2359296 | tf_op jit(solution)/shard_map/all_to_all | solution.py:979
  165.9 17.3 %collective-permute-start.22 = (bf16[128,768]{1,0:T(8,128)(2,1)}, bf16[128,768]{1,0:T(8,128)(2,1)}, u32[]{:S(2)}, u32[]{:S(2)}) collective-permute-start(bf16[128,768]{1,0:T(8,128)(2,1)} %get-tuple-element.145.refs_0_), channel_id=1, source_target_pairs={{0,1},{1,0},{2,3},{3,2},{4,5},{5,4},{6,7},{7,6},{8,9},{9,8},{10,11... | collective-permute-start | bytes 589832 | tf_op jit(solution)/shard_map/ppermute | solution.py:970

commit v3 on v2

--- a/solution.py
+++ b/solution.py
@@ -477,17 +477,16 @@
 
 
 def prepare_kernel(wait, flush, low_ref, send_ref, keep_ref):
-    lane = lane_ids(8, 1024)
-    core = lane >> 9
-    chip = (lane >> 4) & 31
-    rest = lane & 15
-    row = 48 * (chip >> 1) + 24 * (chip & 1) + 12 * core + rest
-    source = jnp.where(rest < 12, row, -1)[:1]
-    order = jnp.where(row_ids_of(768, 1024) == source, 1.0, 0.0).astype(jnp.bfloat16)
+    lane = lane_ids(8, 768)
+    core = (lane >= 384).astype(jnp.int32)
+    within = lane - 384 * core
+    chip = (within * 171) >> 11
+    source = (24 * chip + 12 * core + (within - 12 * chip))[:1]
+    order = jnp.where(row_ids_of(768, 768) == source, 1.0, 0.0).astype(jnp.bfloat16)
     ordered = jnp.dot(low_ref[...], order, preferred_element_type=jnp.float32).astype(jnp.bfloat16)
     first = lax.axis_index("core") == 0
-    keep_ref[...] = jnp.where(first, ordered[:, :512], ordered[:, 512:])
-    send_ref[...] = jnp.where(first, ordered[:, 512:], ordered[:, :512])
+    keep_ref[...] = jnp.where(first, ordered[:, :384], ordered[:, 384:])
+    send_ref[...] = jnp.where(first, ordered[:, 384:], ordered[:, :384])
 
 
 def attn_tile(got_ref, side, pair):
@@ -738,38 +737,43 @@
 def qkv_products_kernel(
     wait, flush, keep_ref, sent_ref, grads_ref, grads_sent_ref,
     vec_ref, vec_sent_ref, wa_ref, cross_ref, out_ref,
+    product_ref,
 ):
     lefts = jnp.concatenate([keep_ref[...], sent_ref[...]], axis=0)
+    for at in range(0, 1152, 384):
+        columns = slice(at, at + 384)
+        rights = jnp.concatenate([grads_ref[:, columns], grads_sent_ref[:, columns]], axis=0)
+        product_ref[:, columns] = lax.dot_general(
+            lefts, rights, trans_left, preferred_element_type=jnp.float32
+        )
     vec = vec_ref[...] + vec_sent_ref[...]
     norms = vec[:, :1536] + (wa_ref[...] + cross_ref[...])
     vec = jnp.concatenate([norms, vec[:, 1536:]], axis=1)
-    lines = jnp.concatenate(
-        [vec[:, :1152], vec[:, 1152:], jnp.zeros((2, 1152), jnp.float32)], axis=0
-    )
-    for at in range(0, 1152, 384):
-        columns = slice(at, at + 384)
-        rights = jnp.concatenate([grads_ref[:, columns], grads_sent_ref[:, columns]], axis=0)
-        product = lax.dot_general(lefts, rights, trans_left, preferred_element_type=jnp.float32)
-        for chip in range(32):
-            out_ref[chip, :, columns] = jnp.concatenate(
-                [product[16 * chip : 16 * chip + 12], lines[:, columns]], axis=0
-            ).astype(jnp.bfloat16)
+    lines = [vec[:, 128 * row : 128 * (row + 1)] for row in range(18)]
+    lines = jnp.concatenate(lines + [jnp.zeros((2, 128), jnp.float32)], axis=0)
+    for pair in range(16):
+        block = product_ref[24 * pair : 24 * pair + 24]
+        for half in range(2):
+            rows = slice(12 * half, 12 * half + 12)
+            tiles = [block[rows, 128 * tile : 128 * tile + 128] for tile in range(9)]
+            out_ref[2 * pair + half] = jnp.concatenate(tiles + [lines], axis=0).astype(jnp.bfloat16)
 
 
 def finish_kernel(
     wait, flush, got_ref, q_ref, k_ref, v_ref, shift_out, gain_out, q_bias_out, v_bias_out
 ):
-    both = got_ref[0].astype(jnp.float32)
+    total = got_ref[0].astype(jnp.float32)
     for source in range(1, 32):
-        both = both + got_ref[source].astype(jnp.float32)
-    q_ref[...] = both[:12, :384]
-    k_ref[...] = both[:12, 384:768]
-    v_ref[...] = both[:12, 768:]
-    shift_out[...] = both[12:13, :768]
-    gain_out[:, :384] = both[12:13, 768:]
-    gain_out[:, 384:] = both[13:14, :384]
-    q_bias_out[...] = both[13:14, 384:768]
-    v_bias_out[...] = both[13:14, 768:]
+        total = total + got_ref[source].astype(jnp.float32)
+    for at, ref in enumerate((q_ref, k_ref, v_ref)):
+        for tile in range(3):
+            row = 36 * at + 12 * tile
+            ref[:, 128 * tile : 128 * tile + 128] = total[row : row + 12]
+    row = 108
+    for ref in (shift_out, gain_out, q_bias_out, v_bias_out):
+        for tile in range(ref.shape[1] // 128):
+            ref[:, 128 * tile : 128 * tile + 128] = total[row : row + 1]
+            row += 1
 
 
 def ffn_sums_kernel(wait, flush, got_ref, core_ref, high_ref, cross_ref, here_ref):
@@ -860,7 +864,7 @@
     x_send, x_keep = call(
         prepare_kernel, "prepare",
         copied(low_one),
-        [("v", whole(128, 512)), ("d", whole(128, 512))],
+        [("v", whole(128, 384)), ("d", whole(128, 384))],
     )
     own, x_send, o_other = lax.optimization_barrier((own, x_send, o_other))
     pairs = own[:, :HALF]
@@ -973,7 +977,8 @@
         copied(x_keep, x_sent)
         + [("v", grads_rows), ("v", grads_sent), ("v", vec), ("v", vec_sent)]
         + [("v", norms_wa), ("v", norms_cross)],
-        [("d", whole(32, 16, 1152))],
+        [("d", whole(32, 128, 128))],
+        [pltpu.VMEM((384, 1152), f32)],
         cost=0,
     )
     products = lax.all_to_all(products, CHIPS, 0, 0, tiled=True)

time: 192 us -> 190 us (0.990)
  no operation moved by 1% of the time
where the time goes in v3:
time: 190 us; the launch traced here: 188 us
  Pallas kernels  69.7 us (37%)
  starting transfers between devices  66.2 us (35%)
  waiting for transfers between devices  48.7 us (26%)
  local copies, waits for them, and re-layouts  2.43 us (1%)
    pallas_call x17, Pallas kernels, call(): pl.pallas_call(body, out_shape=tuple((out for _, out in outs)), in_specs=...  69.7 us
    ppermute x1, waiting for transfers between devices, on_device(): dn_one_other = lax.ppermute(dn_one, 'wa', SWAP)  11.5 us
    ppermute x2, waiting for transfers between devices, on_device(): ffn_high = lax.ppermute(ffn_high, 'zh', SWAP)  8.28 us
    all_to_all x1, waiting for transfers between devices, on_device(): got = lax.all_to_all(back, ('x', 'y', 'wa'), 0, 0, tiled=True)  7.64 us
    all_to_all x1, starting transfers between devices, on_device(): grads = lax.all_to_all(merged, CHIPS, 0, 0, tiled=True)  6.91 us
    all_to_all x1, starting transfers between devices, on_device(): own = lax.all_to_all(payload, PLANE, 0, 0, tiled=True)  6.8 us
    ppermute x2, waiting for transfers between devices, on_device(): ffn_cross = lax.ppermute(ffn_cross, ('zh', 'core'), CROSS)  6.59 us
    all_to_all x1, waiting for transfers between devices, on_device(): own = lax.all_to_all(payload, PLANE, 0, 0, tiled=True)  6.08 us
  transfers between devices with their start and end apart: 29, of which 12 were waited for; matrix products, arithmetic and copies ran while one was open for 0% of the time, Pallas kernels for 23%

profile of v3, /device:TPU:1, one launch (start us, length us, event | category | flops | bytes accessed | tf_op | source)
XLA Modules:
  0.0 188.1 jit_solution(13192147626220872387)
XLA Ops:
  0.7 3.2 %project.1 = (bf16[16,112,128]{2,1,0:T(8,128)(2,1)}, bf16[128,768]{1,0:T(8,128)(2,1)}) custom-call(bf16[128,768]{1,0:T(8,128)(2,1)} %refs_2_.9, s32[128]{0:T(128)} %refs_1_.5, f32[768]{0:T(1024)} %refs_5_.9, f32[768]{0:T(1024)} %refs_3_.6, f32[384]{0:T(512)} %refs_4_.6, f32[384]{0:T(512)} %refs_5_.5, bf16[768,384]{1,0:T(8,128)(2,1)} %refs_2_.8, ...), custom_call_target="tpu_custom_call" | custom-call | flops 2000000000 | tf_op jit(solution)/shard_map/project/pallas_call | solution.py:138
  3.8 2.5 %collective-permute-start = (bf16[384,768]{1,0:T(8,128)(2,1)}, bf16[384,768]{1,0:T(8,128)(2,1)}, u32[]{:S(2)}, u32[]{:S(2)}) collective-permute-start(bf16[384,768]{1,0:T(8,128)(2,1)} %refs_9_.1), channel_id=1, source_target_pairs={{0,1},{1,0},{2,3},{3,2},{4,5},{5,4},{6,7},{7,6},{8,9},{9,8},{10,11... | collective-permute-start | bytes 1769480 | tf_op jit(solution)/shard_map/ppermute | solution.py:863
  6.4 6.8 %all-to-all-start = ((bf16[16,112,128]{2,1,0:T(8,128)(2,1)}), bf16[16,112,128]{2,1,0:T(8,128)(2,1)}, u32[]{:S(2)}, u32[]{:S(2)}) async-start(bf16[16,112,128]{2,1,0:T(8,128)(2,1)} %get-tuple-element.97), calls=%async_computation | async-start | bytes 917504 | tf_op jit(solution)/shard_map/all_to_all | solution.py:861
  13.2 2.6 %prepare.1 = (bf16[128,384]{1,0:T(8,128)(2,1)}, bf16[128,384]{1,0:T(8,128)(2,1)}) custom-call(bf16[128,768]{1,0:T(8,128)(2,1)} %get-tuple-element.95.refs_0_), custom_call_target="tpu_custom_call" | custom-call | flops 2000000000 | tf_op jit(solution)/shard_map/prepare/pallas_call | solution.py:138
  15.8 6.1 %all-to-all-done.refs_0_ = bf16[16,112,128]{2,1,0:T(8,128)(2,1)} async-done(((bf16[16,112,128]{2,1,0:T(8,128)(2,1)}), bf16[16,112,128]{2,1,0:T(8,128)(2,1)}, u32[]{:S(2)}, u32[]{:S(2)}) %all-to-all-start) | async-done | bytes 458784 | tf_op jit(solution)/shard_map/all_to_all | solution.py:861
  21.9 1.0 slice.6
  22.8 3.4 %collective-permute-start.2 = (bf16[16,64,128]{2,1,0:T(8,128)(2,1)S(1)}, bf16[16,64,128]{2,1,0:T(8,128)(2,1)S(1)}, u32[]{:S(2)}, u32[]{:S(2)}) collective-permute-start(bf16[16,64,128]{2,1,0:T(8,128)(2,1)S(1)} %slice.6), channel_id=1, source_target_pairs={{0,4},{4,0},{1,5},{5,1},{2,6},{6,2},{3,7},{7,3},{8,12},{12,8},{9,1... | collective-permute-start | bytes 786440 | tf_op jit(solution)/shard_map/ppermute | solution.py:873
  26.2 0.8 slice_bitcast_fusion
  27.0 1.3 collective-permute-start.3
  28.3 3.5 %collective-permute-start.1 = (bf16[16,64,128]{2,1,0:T(8,128)(2,1)S(1)}, bf16[16,64,128]{2,1,0:T(8,128)(2,1)S(1)}, u32[]{:S(2)}, u32[]{:S(2)}) collective-permute-start(bf16[16,64,128]{2,1,0:T(8,128)(2,1)S(1)} %slice.6), channel_id=1, source_target_pairs={{0,2},{2,0},{1,3},{3,1},{4,6},{6,4},{5,7},{7,5},{8,10},{10,8},{9,1... | collective-permute-start | bytes 786440 | tf_op jit(solution)/shard_map/ppermute | solution.py:871
  31.9 4.4 %collective-permute-start.4 = (bf16[16,64,128]{2,1,0:T(8,128)(2,1)S(1)}, bf16[16,64,128]{2,1,0:T(8,128)(2,1)}, u32[]{:S(2)}, u32[]{:S(2)}) collective-permute-start(bf16[16,64,128]{2,1,0:T(8,128)(2,1)S(1)} %collective-permute-done.2.refs_2_), channel_id=1, source_target_pairs={{0,2},{2,0},{1,3},{3,1},{4,6},{6,4},{5,7},{7,5},{8,10},{10,8},{9,1... | collective-permute-start | bytes 786440 | tf_op jit(solution)/shard_map/ppermute | solution.py:875
  37.5 6.3 %attend.1 = (bf16[32,64,128]{2,1,0:T(8,128)(2,1)}, bf16[17,256,128]{2,1,0:T(8,128)(2,1)}, bf16[1088,128]{1,0:T(8,128)(2,1)}, f32[1088,128]{1,0:T(8,128)}, f32[1088,128]{1,0:T(8,128)}) custom-call(bf16[16,112,128]{2,1,0:T(8,128)(2,1)} %all-to-all-done.refs_0_, bf16[16,64,128]{2,1,0:T(8,128)(2,1)} %copy-done.1, bf16[16,64,128]{2,1,0:T(8,128)(2,1)} %copy-done, ...), custom_call_target="tpu_custom_call" | custom-call | flops 3000000000 | tf_op jit(solution)/shard_map/attend/pallas_call | solution.py:138
  43.9 4.6 %all-to-all-start.1 = ((bf16[32,64,128]{2,1,0:T(8,128)(2,1)}), bf16[32,64,128]{2,1,0:T(8,128)(2,1)}, u32[]{:S(2)}, u32[]{:S(2)}) async-start(bf16[32,64,128]{2,1,0:T(8,128)(2,1)} %get-tuple-element.107), calls=%async_computation.1 | async-start | bytes 1048576 | tf_op jit(solution)/shard_map/all_to_all | solution.py:883
  48.5 3.7 %dhidden.1 = (f32[128,1536]{1,0:T(8,128)}, f32[1,768]{1,0:T(1,128)}) custom-call(bf16[128,768]{1,0:T(8,128)(2,1)} %refs_3_.11, s32[128]{0:T(128)} %refs_4_.11, bf16[1536,768]{1,0:T(8,128)(2,1)} %refs_1_.8), custom_call_target="tpu_custom_call" | custom-call | flops 2000000000 | tf_op jit(solution)/shard_map/dhidden/pallas_call | solution.py:138
  52.2 7.6 %all-to-all-done.1.refs_0_ = bf16[32,64,128]{2,1,0:T(8,128)(2,1)} async-done(((bf16[32,64,128]{2,1,0:T(8,128)(2,1)}), bf16[32,64,128]{2,1,0:T(8,128)(2,1)}, u32[]{:S(2)}, u32[]{:S(2)}) %all-to-all-start.1) | async-done | bytes 524320 | tf_op jit(solution)/shard_map/all_to_all | solution.py:883
  59.8 6.8 %middle.1 = (bf16[128,768]{1,0:T(8,128)(2,1)}, bf16[128,1536]{1,0:T(8,128)(2,1)}, bf16[128,1536]{1,0:T(8,128)(2,1)}, bf16[128,1536]{1,0:T(8,128)(2,1)}, bf16[128...) custom-call(bf16[32,64,128]{2,1,0:T(8,128)(2,1)} %all-to-all-done.1., ...), custom_call_target="tpu_custom_call" | custom-call | flops 2000000000 | tf_op jit(solution)/shard_map/middle/pallas_call | solution.py:138
  67.1 1.9 %collective-permute-start.9 = (bf16[128,1536]{1,0:T(8,128)(2,1)}, bf16[128,1536]{1,0:T(8,128)(2,1)}, u32[]{:S(2)}, u32[]{:S(2)}) collective-permute-start(bf16[128,1536]{1,0:T(8,128)(2,1)} %get-tuple-element.125), channel_id=1, source_target_pairs={{0,2},{2,0},{1,3},{3,1},{4,6},{6,4},{5,7},{7,5},{8,10},{10,8},{9,1... | collective-permute-start | bytes 1179656 | tf_op jit(solution)/shard_map/ppermute | solution.py:908
  69.0 1.5 collective-permute-start.10
  70.6 1.6 collective-permute-start.11
  72.2 3.0 %ffn.1.refs_0_ = bf16[128,768]{1,0:T(8,128)(2,1)} custom-call(bf16[128,1536]{1,0:T(8,128)(2,1)} %get-tuple-element.111.refs_0_, bf16[1536,768]{1,0:T(8,128)(2,1)} %refs_1_.8), custom_call_target="tpu_custom_call" | custom-call | tf_op jit(solution)/shard_map/ffn/pallas_call | solution.py:138
  75.2 4.6 %dheads.1 = (bf16[16,64,128]{2,1,0:T(8,128)(2,1)}, bf16[128,1152]{1,0:T(8,128)(2,1)}, f32[128,768]{1,0:T(8,128)}, f32[1,4608]{1,0:T(1,128)}) custom-call(bf16[128,768]{1,0:T(8,128)(2,1)} %get-tuple-element.110.refs_0_, bf16[128,768]{1,0:T(8,128)(2,1)} %collective-permute-done.5.refs_1_, f32[128,768]{1,0:T(8,128)} %get-tuple-element.113.refs_2_, ...), custom_call_target="tpu_custom_call" | custom-call | tf_op jit(solution)/shard_map/dheads/pallas_call | solution.py:138
  80.4 4.2 %all-to-all-start.2 = ((bf16[16,64,128]{2,1,0:T(8,128)(2,1)}), bf16[16,64,128]{2,1,0:T(8,128)(2,1)}, u32[]{:S(2)}, u32[]{:S(2)}) async-start(bf16[16,64,128]{2,1,0:T(8,128)(2,1)} %get-tuple-element.117), calls=%async_computation.2 | async-start | bytes 524288 | tf_op jit(solution)/shard_map/all_to_all | solution.py:924
  84.9 1.5 collective-permute-done.13.refs_7_
  86.4 0.7 collective-permute-start.6
  87.2 4.9 %collective-permute-done.11.refs_3_ = bf16[128,1536]{1,0:T(8,128)(2,1)} collective-permute-done((bf16[128,1536]{1,0:T(8,128)(2,1)}, bf16[128,1536]{1,0:T(8,128)(2,1)}, u32[]{:S(2)}, u32[]{:S(2)}) %collective-permute-start.11) | collective-permute-done | bytes 393248 | tf_op jit(solution)/shard_map/ppermute | solution.py:907
  92.1 3.9 %ffn_products.1 = bf16[768,1024]{1,0:T(8,128)(2,1)} custom-call(bf16[128,1536]{1,0:T(8,128)(2,1)} %get-tuple-element.124.refs_0_, bf16[128,1536]{1,0:T(8,128)(2,1)} %collective-permute-done.9.refs_1_, bf16[128,1536]{1,0:T(8,128)(2,1)} %collective-permute-done.10.refs_2_, bf16[128,1536]{1,0:T(8,128)(2,1)} %collective-permute-done.11.refs_3_, ...), custom_call_target="tpu_custom_call" | custom-call | flops 2000000000 | tf_op jit(solution)/shard_map/ffn_products/pallas_call | solution.py:138
  95.9 4.4 %all-to-all-start.3 = ((bf16[16,48,1024]{2,1,0:T(8,128)(2,1)}), bf16[16,48,1024]{2,1,0:T(8,128)(2,1)}, u32[]{:S(2)}, u32[]{:S(2)}) async-start(bf16[16,48,1024]{2,1,0:T(8,128)(2,1)} %bitcast.3), calls=%async_computation.3 | async-start | bytes 3145728 | tf_op jit(solution)/shard_map/all_to_all | solution.py:933
  100.4 13.4 %attend_grad.1 = (bf16[32,64,128]{2,1,0:T(8,128)(2,1)}, bf16[32,64,128]{2,1,0:T(8,128)(2,1)}, bf16[16,32,128]{2,1,0:T(8,128)(2,1)}, bf16[96,128]{1,0:T(8,128)(2,1)}) custom-call(bf16[17,256,128]{2,1,0:T(8,128)(2,1)} %get-tuple-element.103.refs_0_, bf16[1088,128]{1,0:T(8,128)(2,1)} %get-tuple-element.104.refs_1_, f32[1088,128]{1,0:T(8,128)} %get-tuple-element.105.refs_2_, ...), custom_call_target="tpu_custom_call" | custom-call | flops 40000000000 | tf_op jit(solution)/shard_map/attend_grad/pallas_call | solution.py:138
  113.9 3.7 %collective-permute-start.8 = (bf16[96,128]{1,0:T(8,128)(2,1)}, bf16[96,128]{1,0:T(8,128)(2,1)}, u32[]{:S(2)}, u32[]{:S(2)}) collective-permute-start(bf16[96,128]{1,0:T(8,128)(2,1)} %get-tuple-element.123), channel_id=1, source_target_pairs={{0,8},{16,24},{1,9},{17,25},{2,10},{18,26},{3,11},{19,27},{4,12},{... | collective-permute-start | bytes 73736 | tf_op jit(solution)/shard_map/ppermute | solution.py:937
  117.6 0.7 collective-permute-done.8.refs_3_
  118.3 2.2 %merge.1 = bf16[32,96,128]{2,1,0:T(8,128)(2,1)} custom-call(bf16[32,64,128]{2,1,0:T(8,128)(2,1)} %get-tuple-element.118.refs_0_, bf16[32,64,128]{2,1,0:T(8,128)(2,1)} %collective-permute-done.7.refs_1_, bf16[16,32,128]{2,1,0:T(8,128)(2,1)} %get-tuple-element.122.refs_2_, bf16[96,128]{1,0:T(8,128)(2,1)} %collective-permute-done.8.refs_3_), custom_call_target="tpu_custom_call" | custom-call | flops 2000000000 | tf_op jit(solution)/shard_map/merge/pallas_call | solution.py:138
  120.6 4.0 %all-to-all-done.3.refs_0_ = bf16[16,48,1024]{2,1,0:T(8,128)(2,1)} async-done(((bf16[16,48,1024]{2,1,0:T(8,128)(2,1)}), bf16[16,48,1024]{2,1,0:T(8,128)(2,1)}, u32[]{:S(2)}, u32[]{:S(2)}) %all-to-all-start.3) | async-done | bytes 1572896 | tf_op jit(solution)/shard_map/all_to_all | solution.py:933
  124.6 6.9 %all-to-all-start.4 = ((bf16[32,96,128]{2,1,0:T(8,128)(2,1)}), bf16[32,96,128]{2,1,0:T(8,128)(2,1)}, u32[]{:S(2)}, u32[]{:S(2)}) async-start(bf16[32,96,128]{2,1,0:T(8,128)(2,1)} %merge.1), calls=%async_computation.4 | async-start | bytes 1572864 | tf_op jit(solution)/shard_map/all_to_all | solution.py:945
  131.5 0.8 collective-permute-start.17
  132.4 2.4 %ffn_sums.1 = (bf16[32,1024]{1,0:T(8,128)(2,1)}, bf16[32,1024]{1,0:T(8,128)(2,1)}, bf16[32,1024]{1,0:T(8,128)(2,1)}, f32[32,1024]{1,0:T(8,128)}) custom-call(bf16[16,48,1024]{2,1,0:T(8,128)(2,1)} %all-to-all-done.3.refs_0_), custom_call_target="tpu_custom_call" | custom-call | tf_op jit(solution)/shard_map/ffn_sums/pallas_call | solution.py:138
  135.1 3.0 %collective-permute-start.15 = (bf16[32,1024]{1,0:T(8,128)(2,1)}, bf16[32,1024]{1,0:T(8,128)(2,1)}, u32[]{:S(2)}, u32[]{:S(2)}) collective-permute-start(bf16[32,1024]{1,0:T(8,128)(2,1)} %get-tuple-element.133), channel_id=1, source_target_pairs={{0,4},{4,0},{1,5},{5,1},{2,6},{6,2},{3,7},{7,3},{8,12},{12,8},{9,1... | collective-permute-start | bytes 196616 | tf_op jit(solution)/shard_map/ppermute | solution.py:952
  138.7 8.3 %collective-permute-done.15.refs_2_ = bf16[32,1024]{1,0:T(8,128)(2,1)} collective-permute-done((bf16[32,1024]{1,0:T(8,128)(2,1)}, bf16[32,1024]{1,0:T(8,128)(2,1)}, u32[]{:S(2)}, u32[]{:S(2)}) %collective-permute-start.15) | collective-permute-done | bytes 65568 | tf_op jit(solution)/shard_map/ppermute | solution.py:952
  147.0 1.7 collective-permute-done.16.refs_3_
  148.7 4.0 %dnormed.1 = (bf16[128,1152]{1,0:T(8,128)(2,1)}, f32[1,1536]{1,0:T(1,128)}, f32[1,2304]{1,0:T(1,128)}, bf16[128,768]{1,0:T(8,128)(2,1)}) custom-call(bf16[32,96,128]{2,1,0:T(8,128)(2,1)} %all-to-all-done.4.refs_0_, bf16[128,768]{1,0:T(8,128)(2,1)} %refs_2_.9, bf16[768,384]{1,0:T(8,128)(2,1)} %refs_2_.8, bf16[768,384]{1,0:T(8,128)(2,1)} %refs_3_.9, ...), custom_call_target="tpu_custom_call" | custom-call | tf_op jit(solution)/shard_map/dnormed/pallas_call | solution.py:138
  153.7 1.4 collective-permute-start.20
  155.1 1.6 collective-permute-done.21.refs_7_
  156.7 3.5 %qkv_products.1 = bf16[32,128,128]{2,1,0:T(8,128)(2,1)} custom-call(bf16[128,384]{1,0:T(8,128)(2,1)} %get-tuple-element.96.refs_0_, bf16[128,384]{1,0:T(8,128)(2,1)} %collective-permute-done.17.refs_1_, bf16[128,1152]{1,0:T(8,128)(2,1)} %get-tuple-element.138.refs_2_, bf16[128,1152]{1,0:T(8,128)(2,1)} %collective-permute-done.18.refs_3_, ...), custom_call_target="tpu_custom_call" | custom-call | tf_op jit(solution)/shard_map/qkv_products/pallas_call | solution.py:138
  160.2 5.4 %all-to-all-start.5 = ((bf16[32,128,128]{2,1,0:T(8,128)(2,1)}), bf16[32,128,128]{2,1,0:T(8,128)(2,1)}, u32[]{:S(2)}, u32[]{:S(2)}) async-start(bf16[32,128,128]{2,1,0:T(8,128)(2,1)} %qkv_products.1), calls=%async_computation.5 | async-start | bytes 2097152 | tf_op jit(solution)/shard_map/all_to_all | solution.py:984
  166.3 2.9 %output.1 = bf16[128,768]{1,0:T(8,128)(2,1)} custom-call(bf16[128,768]{1,0:T(8,128)(2,1)} %ffn.1.refs_0_, bf16[128,768]{1,0:T(8,128)(2,1)} %collective-permute-done.6.refs_1_, f32[128,768]{1,0:T(8,128)} %get-tuple-element.113.refs_2_, bf16[128,768]{1,0:T(8,128)(2,1)} %refs_2_.9, s32[128]{0:T(128)} %refs_4_.11, f32[768]{0:T(1024)} %refs_5_.8), custom_call_target="tpu_custom_call" | custom-call | tf_op jit(solution)/shard_map/output/pallas_call | solution.py:138
  169.2 1.8 ffn_finish.1
  170.9 11.5 %collective-permute-done.22.refs_1_ = bf16[128,768]{1,0:T(8,128)(2,1)} collective-permute-done((bf16[128,768]{1,0:T(8,128)(2,1)}, bf16[128,768]{1,0:T(8,128)(2,1)}, u32[]{:S(2)}, u32[]{:S(2)}) %collective-permute-start.22) | collective-permute-done | bytes 196640 | tf_op jit(solution)/shard_map/ppermute | solution.py:974
  182.5 3.4 %input_grad.1 = f32[128,768]{1,0:T(8,128)} custom-call(bf16[128,768]{1,0:T(8,128)(2,1)} %get-tuple-element.145.refs_0_, bf16[128,768]{1,0:T(8,128)(2,1)} %collective-permute-done.22.refs_1_, bf16[128,768]{1,0:T(8,128)(2,1)} %refs_2_.9, bf16[128,768]{1,0:T(8,128)(2,1)} %refs_3_.11, s32[128]{0:T(128)} %refs_4_.11, f32[768]{0:T(1024)} %refs_5_.9, ...), custom_call_target="tpu_custom_call" | custom-call | tf_op jit(solution)/shard_map/input_grad/pallas_call | solution.py:138
  185.9 2.0 %finish.1 = (f32[12,384]{1,0:T(8,128)}, f32[12,384]{1,0:T(8,128)}, f32[12,384]{1,0:T(8,128)}, f32[768]{0:T(1024)}, f32[768]{0:T(1024)}, /*index=5*/f32[384]{0:T(512)}, f32[384]{0:T(512)}) custom-call(bf16[32,128,128]{2,1,0:T(8,128)(2,1)} %all-to-all-done.5.refs_0_), custom_call_target="tpu_custom_call" | custom-call | flops 2000000000 | tf_op jit(solution)/shard_map/finish/pallas_call | solution.py:138
  (35 shorter events, 5.5 us)
Async XLA Ops:
  3.8 18.0 %collective-permute-start = (bf16[384,768]{1,0:T(8,128)(2,1)}, bf16[384,768]{1,0:T(8,128)(2,1)}, u32[]{:S(2)}, u32[]{:S(2)}) collective-permute-start(bf16[384,768]{1,0:T(8,128)(2,1)} %refs_9_.1), channel_id=1, source_target_pairs={{0,1},{1,0},{2,3},{3,2},{4,5},{5,4},{6,7},{7,6},{8,9},{9,8},{10,11... | collective-permute-start | bytes 1769480 | tf_op jit(solution)/shard_map/ppermute | solution.py:863
  6.4 15.5 %all-to-all-start = ((bf16[16,112,128]{2,1,0:T(8,128)(2,1)}), bf16[16,112,128]{2,1,0:T(8,128)(2,1)}, u32[]{:S(2)}, u32[]{:S(2)}) async-start(bf16[16,112,128]{2,1,0:T(8,128)(2,1)} %get-tuple-element.97), calls=%async_computation | async-start | bytes 917504 | tf_op jit(solution)/shard_map/all_to_all | solution.py:861
  22.8 9.0 %collective-permute-start.2 = (bf16[16,64,128]{2,1,0:T(8,128)(2,1)S(1)}, bf16[16,64,128]{2,1,0:T(8,128)(2,1)S(1)}, u32[]{:S(2)}, u32[]{:S(2)}) collective-permute-start(bf16[16,64,128]{2,1,0:T(8,128)(2,1)S(1)} %slice.6), channel_id=1, source_target_pairs={{0,4},{4,0},{1,5},{5,1},{2,6},{6,2},{3,7},{7,3},{8,12},{12,8},{9,1... | collective-permute-start | bytes 786440 | tf_op jit(solution)/shard_map/ppermute | solution.py:873
  27.0 4.9 %collective-permute-start.3 = (bf16[112,128]{1,0:T(8,128)(2,1)S(1)}, bf16[112,128]{1,0:T(8,128)(2,1)S(1)}, u32[]{:S(2)}, u32[]{:S(2)}) collective-permute-start(bf16[112,128]{1,0:T(8,128)(2,1)S(1)} %slice_bitcast_fusion), channel_id=1, source_target_pairs={{8,0},{24,16},{9,1},{25,17},{10,2},{26,18},{11,3},{27,19},{12,4},{... | collective-permute-start | bytes 86024 | tf_op jit(solution)/shard_map/ppermute | solution.py:872
  28.3 8.0 %collective-permute-start.1 = (bf16[16,64,128]{2,1,0:T(8,128)(2,1)S(1)}, bf16[16,64,128]{2,1,0:T(8,128)(2,1)S(1)}, u32[]{:S(2)}, u32[]{:S(2)}) collective-permute-start(bf16[16,64,128]{2,1,0:T(8,128)(2,1)S(1)} %slice.6), channel_id=1, source_target_pairs={{0,2},{2,0},{1,3},{3,1},{4,6},{6,4},{5,7},{7,5},{8,10},{10,8},{9,1... | collective-permute-start | bytes 786440 | tf_op jit(solution)/shard_map/ppermute | solution.py:871
  31.9 4.4 %copy-start.2 = (bf16[112,128]{1,0:T(8,128)(2,1)}, bf16[112,128]{1,0:T(8,128)(2,1)S(1)}, u32[]{:S(2)}) copy-start(bf16[112,128]{1,0:T(8,128)(2,1)S(1)} %collective-permute-done.3.refs_4_) | copy-start | bytes 86020
  31.9 4.4 %copy-start = (bf16[16,64,128]{2,1,0:T(8,128)(2,1)}, bf16[16,64,128]{2,1,0:T(8,128)(2,1)S(1)}, u32[]{:S(2)}) copy-start(bf16[16,64,128]{2,1,0:T(8,128)(2,1)S(1)} %collective-permute-done.2.refs_2_) | copy-start | bytes 786436
  31.9 5.6 %collective-permute-start.4 = (bf16[16,64,128]{2,1,0:T(8,128)(2,1)S(1)}, bf16[16,64,128]{2,1,0:T(8,128)(2,1)}, u32[]{:S(2)}, u32[]{:S(2)}) collective-permute-start(bf16[16,64,128]{2,1,0:T(8,128)(2,1)S(1)} %collective-permute-done.2.refs_2_), channel_id=1, source_target_pairs={{0,2},{2,0},{1,3},{3,1},{4,6},{6,4},{5,7},{7,5},{8,10},{10,8},{9,1... | collective-permute-start | bytes 786440 | tf_op jit(solution)/shard_map/ppermute | solution.py:875
  36.2 0.7 copy-start.1
  43.9 15.9 %all-to-all-start.1 = ((bf16[32,64,128]{2,1,0:T(8,128)(2,1)}), bf16[32,64,128]{2,1,0:T(8,128)(2,1)}, u32[]{:S(2)}, u32[]{:S(2)}) async-start(bf16[32,64,128]{2,1,0:T(8,128)(2,1)} %get-tuple-element.107), calls=%async_computation.1 | async-start | bytes 1048576 | tf_op jit(solution)/shard_map/all_to_all | solution.py:883
  66.7 8.5 %collective-permute-start.5 = (bf16[128,768]{1,0:T(8,128)(2,1)}, bf16[128,768]{1,0:T(8,128)(2,1)}, u32[]{:S(2)}, u32[]{:S(2)}) collective-permute-start(bf16[128,768]{1,0:T(8,128)(2,1)} %get-tuple-element.110.refs_0_), channel_id=1, source_target_pairs={{0,1},{1,0},{2,3},{3,2},{4,5},{5,4},{6,7},{7,6},{8,9},{9,8},{10,11... | collective-permute-start | bytes 589832 | tf_op jit(solution)/shard_map/ppermute | solution.py:905
  67.1 20.1 %collective-permute-start.9 = (bf16[128,1536]{1,0:T(8,128)(2,1)}, bf16[128,1536]{1,0:T(8,128)(2,1)}, u32[]{:S(2)}, u32[]{:S(2)}) collective-permute-start(bf16[128,1536]{1,0:T(8,128)(2,1)} %get-tuple-element.125), channel_id=1, source_target_pairs={{0,2},{2,0},{1,3},{3,1},{4,6},{6,4},{5,7},{7,5},{8,10},{10,8},{9,1... | collective-permute-start | bytes 1179656 | tf_op jit(solution)/shard_map/ppermute | solution.py:908
  69.0 18.1 %collective-permute-start.10 = (bf16[128,1536]{1,0:T(8,128)(2,1)}, bf16[128,1536]{1,0:T(8,128)(2,1)}, u32[]{:S(2)}, u32[]{:S(2)}) collective-permute-start(bf16[128,1536]{1,0:T(8,128)(2,1)} %get-tuple-element.126), channel_id=1, source_target_pairs={{0,4},{4,0},{1,5},{5,1},{2,6},{6,2},{3,7},{7,3},{8,12},{12,8},{9,1... | collective-permute-start | bytes 1179656 | tf_op jit(solution)/shard_map/ppermute | solution.py:906
  70.6 21.5 %collective-permute-start.11 = (bf16[128,1536]{1,0:T(8,128)(2,1)}, bf16[128,1536]{1,0:T(8,128)(2,1)}, u32[]{:S(2)}, u32[]{:S(2)}) collective-permute-start(bf16[128,1536]{1,0:T(8,128)(2,1)} %get-tuple-element.127), channel_id=1, source_target_pairs={{0,6},{2,4},{4,2},{6,0},{1,7},{3,5},{5,3},{7,1},{8,14},{10,12},{12... | collective-permute-start | bytes 1179656 | tf_op jit(solution)/shard_map/ppermute | solution.py:907
  79.8 12.3 %collective-permute-start.12 = (bf16[128,1152]{1,0:T(8,128)(2,1)}, bf16[128,1152]{1,0:T(8,128)(2,1)}, u32[]{:S(2)}, u32[]{:S(2)}) collective-permute-start(bf16[128,1152]{1,0:T(8,128)(2,1)} %get-tuple-element.128.refs_4_), channel_id=1, source_target_pairs={{0,2},{2,0},{1,3},{3,1},{4,6},{6,4},{5,7},{7,5},{8,10},{10,8},{9,1... | collective-permute-start | bytes 884744 | tf_op jit(solution)/shard_map/ppermute | solution.py:925
  80.4 15.5 %all-to-all-start.2 = ((bf16[16,64,128]{2,1,0:T(8,128)(2,1)}), bf16[16,64,128]{2,1,0:T(8,128)(2,1)}, u32[]{:S(2)}, u32[]{:S(2)}) async-start(bf16[16,64,128]{2,1,0:T(8,128)(2,1)} %get-tuple-element.117), calls=%async_computation.2 | async-start | bytes 524288 | tf_op jit(solution)/shard_map/all_to_all | solution.py:924
  84.6 1.8 collective-permute-start.13
  86.4 27.4 %collective-permute-start.6 = (bf16[128,768]{1,0:T(8,128)(2,1)}, bf16[128,768]{1,0:T(8,128)(2,1)}, u32[]{:S(2)}, u32[]{:S(2)}) collective-permute-start(bf16[128,768]{1,0:T(8,128)(2,1)} %ffn.1.refs_0_), channel_id=1, source_target_pairs={{0,1},{1,0},{2,3},{3,2},{4,5},{5,4},{6,7},{7,6},{8,9},{9,8},{10,11... | collective-permute-start | bytes 589832 | tf_op jit(solution)/shard_map/ppermute | solution.py:934
  95.9 28.6 %all-to-all-start.3 = ((bf16[16,48,1024]{2,1,0:T(8,128)(2,1)}), bf16[16,48,1024]{2,1,0:T(8,128)(2,1)}, u32[]{:S(2)}, u32[]{:S(2)}) async-start(bf16[16,48,1024]{2,1,0:T(8,128)(2,1)} %bitcast.3), calls=%async_computation.3 | async-start | bytes 3145728 | tf_op jit(solution)/shard_map/all_to_all | solution.py:933
  113.8 4.5 %collective-permute-start.7 = (bf16[32,64,128]{2,1,0:T(8,128)(2,1)}, bf16[32,64,128]{2,1,0:T(8,128)(2,1)}, u32[]{:S(2)}, u32[]{:S(2)}) collective-permute-start(bf16[32,64,128]{2,1,0:T(8,128)(2,1)} %get-tuple-element.121), channel_id=1, source_target_pairs={{0,2},{2,0},{1,3},{3,1},{4,6},{6,4},{5,7},{7,5},{8,10},{10,8},{9,1... | collective-permute-start | bytes 1572872 | tf_op jit(solution)/shard_map/ppermute | solution.py:938
  113.9 4.4 %collective-permute-start.8 = (bf16[96,128]{1,0:T(8,128)(2,1)}, bf16[96,128]{1,0:T(8,128)(2,1)}, u32[]{:S(2)}, u32[]{:S(2)}) collective-permute-start(bf16[96,128]{1,0:T(8,128)(2,1)} %get-tuple-element.123), channel_id=1, source_target_pairs={{0,8},{16,24},{1,9},{17,25},{2,10},{18,26},{3,11},{19,27},{4,12},{... | collective-permute-start | bytes 73736 | tf_op jit(solution)/shard_map/ppermute | solution.py:937
  124.6 24.1 %all-to-all-start.4 = ((bf16[32,96,128]{2,1,0:T(8,128)(2,1)}), bf16[32,96,128]{2,1,0:T(8,128)(2,1)}, u32[]{:S(2)}, u32[]{:S(2)}) async-start(bf16[32,96,128]{2,1,0:T(8,128)(2,1)} %merge.1), calls=%async_computation.4 | async-start | bytes 1572864 | tf_op jit(solution)/shard_map/all_to_all | solution.py:945
  131.5 7.2 %collective-permute-start.17 = (bf16[128,384]{1,0:T(8,128)(2,1)}, bf16[128,384]{1,0:T(8,128)(2,1)}, u32[]{:S(2)}, u32[]{:S(2)}) collective-permute-start(bf16[128,384]{1,0:T(8,128)(2,1)} %get-tuple-element.135), channel_id=1, source_target_pairs={{0,2},{2,0},{1,3},{3,1},{4,6},{6,4},{5,7},{7,5},{8,10},{10,8},{9,1... | collective-permute-start | bytes 294920 | tf_op jit(solution)/shard_map/ppermute | solution.py:876
  134.7 4.0 %collective-permute-start.14 = (bf16[32,1024]{1,0:T(8,128)(2,1)}, bf16[32,1024]{1,0:T(8,128)(2,1)}, u32[]{:S(2)}, u32[]{:S(2)}) collective-permute-start(bf16[32,1024]{1,0:T(8,128)(2,1)} %get-tuple-element.132), channel_id=1, source_target_pairs={{0,2},{2,0},{1,3},{3,1},{4,6},{6,4},{5,7},{7,5},{8,10},{10,8},{9,1... | collective-permute-start | bytes 196616 | tf_op jit(solution)/shard_map/ppermute | solution.py:951
  135.1 11.9 %collective-permute-start.15 = (bf16[32,1024]{1,0:T(8,128)(2,1)}, bf16[32,1024]{1,0:T(8,128)(2,1)}, u32[]{:S(2)}, u32[]{:S(2)}) collective-permute-start(bf16[32,1024]{1,0:T(8,128)(2,1)} %get-tuple-element.133), channel_id=1, source_target_pairs={{0,4},{4,0},{1,5},{5,1},{2,6},{6,2},{3,7},{7,3},{8,12},{12,8},{9,1... | collective-permute-start | bytes 196616 | tf_op jit(solution)/shard_map/ppermute | solution.py:952
  138.1 10.6 %collective-permute-start.16 = (bf16[32,1024]{1,0:T(8,128)(2,1)}, bf16[32,1024]{1,0:T(8,128)(2,1)}, u32[]{:S(2)}, u32[]{:S(2)}) collective-permute-start(bf16[32,1024]{1,0:T(8,128)(2,1)} %get-tuple-element.134), channel_id=1, source_target_pairs={{0,6},{2,4},{4,2},{6,0},{1,7},{3,5},{5,3},{7,1},{8,14},{10,12},{12... | collective-permute-start | bytes 196616 | tf_op jit(solution)/shard_map/ppermute | solution.py:953
  152.7 4.0 %collective-permute-start.18 = (bf16[128,1152]{1,0:T(8,128)(2,1)}, bf16[128,1152]{1,0:T(8,128)(2,1)}, u32[]{:S(2)}, u32[]{:S(2)}) collective-permute-start(bf16[128,1152]{1,0:T(8,128)(2,1)} %get-tuple-element.138.refs_2_), channel_id=1, source_target_pairs={{0,2},{2,0},{1,3},{3,1},{4,6},{6,4},{5,7},{7,5},{8,10},{10,8},{9,1... | collective-permute-start | bytes 884744 | tf_op jit(solution)/shard_map/ppermute | solution.py:969
  153.2 3.5 %collective-permute-start.19 = (f32[1,2304]{1,0:T(1,128)}, f32[1,2304]{1,0:T(1,128)}, u32[]{:S(2)}, u32[]{:S(2)}) collective-permute-start(f32[1,2304]{1,0:T(1,128)} %get-tuple-element.139.refs_4_), channel_id=1, source_target_pairs={{0,2},{2,0},{1,3},{3,1},{4,6},{6,4},{5,7},{7,5},{8,10},{10,8},{9,1... | collective-permute-start | bytes 27656 | tf_op jit(solution)/shard_map/ppermute | solution.py:970
  153.3 3.4 %collective-permute-start.21 = (f32[1,1536]{1,0:T(1,128)}, f32[1,1536]{1,0:T(1,128)}, u32[]{:S(2)}, u32[]{:S(2)}) collective-permute-start(f32[1,1536]{1,0:T(1,128)} %get-tuple-element.140), channel_id=1, source_target_pairs={{0,3},{1,2},{2,1},{3,0},{4,7},{5,6},{6,5},{7,4},{8,11},{9,10},{10,... | collective-permute-start | bytes 18440 | tf_op jit(solution)/shard_map/ppermute | solution.py:972
  153.7 3.0 %collective-permute-start.20 = (f32[1,1536]{1,0:T(1,128)}, f32[1,1536]{1,0:T(1,128)}, u32[]{:S(2)}, u32[]{:S(2)}) collective-permute-start(f32[1,1536]{1,0:T(1,128)} %get-tuple-element.140), channel_id=1, source_target_pairs={{0,1},{1,0},{2,3},{3,2},{4,5},{5,4},{6,7},{7,6},{8,9},{9,8},{10,11... | collective-permute-start | bytes 18440 | tf_op jit(solution)/shard_map/ppermute | solution.py:971
  160.2 25.7 %all-to-all-start.5 = ((bf16[32,128,128]{2,1,0:T(8,128)(2,1)}), bf16[32,128,128]{2,1,0:T(8,128)(2,1)}, u32[]{:S(2)}, u32[]{:S(2)}) async-start(bf16[32,128,128]{2,1,0:T(8,128)(2,1)} %qkv_products.1), calls=%async_computation.5 | async-start | bytes 2097152 | tf_op jit(solution)/shard_map/all_to_all | solution.py:984
  165.7 16.8 %collective-permute-start.22 = (bf16[128,768]{1,0:T(8,128)(2,1)}, bf16[128,768]{1,0:T(8,128)(2,1)}, u32[]{:S(2)}, u32[]{:S(2)}) collective-permute-start(bf16[128,768]{1,0:T(8,128)(2,1)} %get-tuple-element.145.refs_0_), channel_id=1, source_target_pairs={{0,1},{1,0},{2,3},{3,2},{4,5},{5,4},{6,7},{7,6},{8,9},{9,8},{10,11... | collective-permute-start | bytes 589832 | tf_op jit(solution)/shard_map/ppermute | solution.py:974

commit v4 on v3

--- a/solution.py
+++ b/solution.py
@@ -12,6 +12,7 @@
 CTX = ("x", "y", "zh", "core")
 CHIPS = ("x", "y", "zh")
 PLANE = ("x", "y")
+EDGE = ("y", "zh", "core")
 SWAP = ((0, 1), (1, 0))
 CROSS = ((0, 3), (1, 2), (2, 1), (3, 0))
 HALF = 64
@@ -19,7 +20,7 @@
 GROUP = 256
 STREAM = 8192
 ROWS = (BLOCKS + 1) * HALF
-FF_TILE = 512
+FF_TILE = 768
 FAR = 1e9
 SCALING = 1.0 / math.sqrt(HEAD_DIM)
 EXP2_SCALE = SCALING / math.log(2.0)
@@ -103,12 +104,11 @@
             copy.start()
             given[at] = there
             pending.append((there, at, copy))
-        targets = []
+        targets, extra, begun = [], [], []
         for slot, at in enumerate(copied_out):
             made = out_buffers[slot] if len(outs[at][1].shape) > 1 else out_buffers[slot].at[0]
-            copy = pltpu.make_async_copy(made, results[at], out_sems.at[slot])
+            targets.append((out_buffers[slot], made, results[at], out_sems.at[slot]))
             results[at] = out_buffers[slot]
-            targets.append((out_buffers[slot], copy))
 
         def wait(ref):
             for entry in list(pending):
@@ -116,12 +116,18 @@
                     entry[2].wait()
                     pending[:] = [other for other in pending if other is not entry]
 
-        def flush(ref):
-            for entry in list(targets):
-                if entry[0] is ref:
-                    entry[1].start()
-                    flushing.append(entry[1])
-                    targets[:] = [other for other in targets if other is not entry]
+        def flush(ref, begin=None, end=None):
+            for buffer_ref, made, there, sem in targets:
+                if buffer_ref is not ref:
+                    continue
+                if begin is not None:
+                    sem = out_sems.at[len(copied_out) + len(extra)]
+                    extra.append(sem)
+                    made, there = made.at[begin:end], there.at[begin:end]
+                copy = pltpu.make_async_copy(made, there, sem)
+                copy.start()
+                flushing.append(copy)
+                begun.append(ref)
 
         for entry in list(pending):
             if entry[1] not in lazy:
@@ -129,8 +135,9 @@
         kernel(wait, flush, *given, *results, *rest)
         for entry in list(pending):
             wait(entry[0])
-        for entry in list(targets):
-            flush(entry[0])
+        for entry in targets:
+            if not any(ref is entry[0] for ref in begun):
+                flush(entry[0])
         for copy in flushing:
             copy.wait()
 
@@ -144,7 +151,7 @@
         + [buffer(outs[at][1]) for at in copied_out]
         + [
             pltpu.SemaphoreType.DMA((max(1, len(copied_in)),)),
-            pltpu.SemaphoreType.DMA((max(1, len(copied_out)),)),
+            pltpu.SemaphoreType.DMA((len(copied_out) + 4,)),
         ]
         + list(scratch),
         compiler_params=pltpu.CompilerParams(vmem_limit_bytes=VMEM_BYTES),
@@ -292,15 +299,21 @@
         recip = jnp.broadcast_to(1.0 / jnp.where(den == 0.0, 1.0, den), (HALF, 128))
         full = num_ref[rows] * recip
         full_ref[rows] = jnp.where(lane_ids(HALF, 128) < HALF, recip, full)
-        packed = pack_from_high(full).astype(jnp.bfloat16)
-        if block < BLOCKS:
-            place = jnp.where(upper == 1, BLOCKS - 1 - block, block)
-            for copy in range(2):
-                back_ref[pl.ds(2 * place + copy, 1), :32] = packed[None]
-                back_ref[pl.ds(2 * place + copy, 1), 32:] = jnp.zeros((1, 32, 128), jnp.bfloat16)
+    flush(full_ref)
+    for place in range(BLOCKS):
+        block = jnp.where(upper == 1, BLOCKS - 1 - place, place)
+        rows = pl.ds(pl.multiple_of(block * HALF, HALF), HALF)
+        packed = pack_from_high(full_ref[rows]).astype(jnp.bfloat16)
+        if place < BLOCKS - 1:
+            edge = jnp.zeros((32, 128), jnp.bfloat16)
         else:
-            for copy in range(2):
-                back_ref[2 * BLOCKS - 2 + copy, 32:] = packed
+            edge = pack_from_high(full_ref[BLOCKS * HALF :]).astype(jnp.bfloat16)
+        for copy in range(2):
+            back_ref[2 * place + copy, :32] = packed
+            back_ref[2 * place + copy, 32:] = edge
+        if place == BLOCKS // 2 - 1:
+            flush(back_ref, 0, BLOCKS)
+    flush(back_ref, BLOCKS, 2 * BLOCKS)
 
 
 def attend_grad_kernel(
@@ -449,17 +462,14 @@
     wide = lane_ids(HALF, 128) < HALF
     for ref in (q_ref, k_ref, v_ref):
         wait(ref)
+    pay_ref[12:] = jnp.zeros((4, HALF + 48, 128), jnp.bfloat16)
+    flush(pay_ref, 12, 16)
+    all_queries = jnp.dot(low, q_ref[...], preferred_element_type=jnp.float32) + q_bias_ref[...]
+    all_keys = jnp.dot(low, k_ref[...], preferred_element_type=jnp.float32)
+    all_values = jnp.dot(low, v_ref[...], preferred_element_type=jnp.float32) + v_bias_ref[...]
     for pair in range(3):
         columns = slice(pair * 128, (pair + 1) * 128)
-        queries = (
-            jnp.dot(low, q_ref[:, columns], preferred_element_type=jnp.float32)
-            + q_bias_ref[:, columns]
-        )
-        keyset = jnp.dot(low, k_ref[:, columns], preferred_element_type=jnp.float32)
-        values = (
-            jnp.dot(low, v_ref[:, columns], preferred_element_type=jnp.float32)
-            + v_bias_ref[:, columns]
-        )
+        queries, keyset, values = all_queries[:, columns], all_keys[:, columns], all_values[:, columns]
         for half in range(2):
             rows = slice(half * HALF, (half + 1) * HALF)
             for odd in range(2):
@@ -473,7 +483,7 @@
                 pay_ref[index, :HALF] = both.astype(jnp.bfloat16)
                 pay_ref[index, HALF : HALF + 32] = packed.astype(jnp.bfloat16)
                 pay_ref[index, HALF + 32 :] = lines[half]
-    pay_ref[12:] = jnp.zeros((4, HALF + 48, 128), jnp.bfloat16)
+        flush(pay_ref, 4 * pair, 4 * pair + 4)
 
 
 def prepare_kernel(wait, flush, low_ref, send_ref, keep_ref):
@@ -591,14 +601,12 @@
     vec_ref[:, 2304:3072] = jnp.sum(dnormed * unit, axis=0, keepdims=True)
     vec_ref[:, 3072:3840] = jnp.sum(dnormed, axis=0, keepdims=True)
     vec_ref[:, 3840:] = jnp.sum(low.astype(jnp.float32), axis=0, keepdims=True)
+    pay_ref[12:] = jnp.zeros((4, HALF, 128), jnp.bfloat16)
+    flush(pay_ref, 12, 16)
     wait(o_ref)
+    all_heads = lax.dot_general(low, o_ref[...], trans_right, preferred_element_type=jnp.float32)
     for pair in range(3):
-        dheads = lax.dot_general(
-            low,
-            o_ref[pair * 128 : (pair + 1) * 128],
-            trans_right,
-            preferred_element_type=jnp.float32,
-        )
+        dheads = all_heads[:, pair * 128 : (pair + 1) * 128]
         for odd in range(2):
             pack = pack_from_high if odd else pack_from_low
             lower = pack(dheads[:HALF]).astype(jnp.bfloat16)
@@ -608,8 +616,7 @@
             pay_ref[index, 32:] = higher
             pay_ref[index + 1, :32] = higher
             pay_ref[index + 1, 32:] = higher
-    pay_ref[12:] = jnp.zeros((4, HALF, 128), jnp.bfloat16)
-    flush(pay_ref)
+        flush(pay_ref, 4 * pair, 4 * pair + 4)
     both_ref[:, :768] = low
     both_ref[:, 768:] = attn_ref[...]
 
@@ -732,6 +739,8 @@
         )
         out_ref[pl.ds(2 * block + 1 - high, 1), :HALF] = pair.astype(jnp.bfloat16)[None]
         out_ref[pl.ds(2 * block + 1 - high, 1), HALF:] = jnp.zeros((1, 32, 128), jnp.bfloat16)
+        if block % 8 == 7:
+            flush(out_ref, 2 * block - 14, 2 * block + 2)
 
 
 def qkv_products_kernel(
@@ -757,6 +766,8 @@
             rows = slice(12 * half, 12 * half + 12)
             tiles = [block[rows, 128 * tile : 128 * tile + 128] for tile in range(9)]
             out_ref[2 * pair + half] = jnp.concatenate(tiles + [lines], axis=0).astype(jnp.bfloat16)
+        if pair % 8 == 7:
+            flush(out_ref, 2 * pair - 14, 2 * pair + 2)
 
 
 def finish_kernel(
@@ -783,9 +794,8 @@
     me = 2 * lax.axis_index("zh") + lax.axis_index("core")
     parts = [total[12 * index : 12 * index + 12, :1024] for index in range(4)]
     vec = jnp.concatenate([total[row : row + 1, 768:896] for row in range(36)], axis=1)
-    vec = jnp.concatenate([vec, jnp.zeros((1, 512), jnp.float32)], axis=1)
-    lines = [vec[:, 1024 * row : 1024 * (row + 1)] for row in range(5)]
-    lines = jnp.concatenate(lines + [jnp.zeros((3, 1024), jnp.float32)], axis=0)
+    lines = jnp.concatenate([vec[:, 1152 * row : 1152 * (row + 1)] for row in range(4)], axis=0)
+    spare = jnp.zeros((12, 128), jnp.float32)
 
     def part(offset):
         value = parts[offset]
@@ -794,10 +804,8 @@
         return value
 
     for ref, offset in ((here_ref, 0), (core_ref, 1), (high_ref, 2), (cross_ref, 3)):
-        ref[...] = jnp.concatenate(
-            [part(offset), jnp.zeros((4, 1024), jnp.float32), lines, jnp.zeros((8, 1024), jnp.float32)],
-            axis=0,
-        ).astype(ref.dtype)
+        both = jnp.concatenate([part(offset), spare], axis=1)
+        ref[...] = jnp.concatenate([both, lines], axis=0).astype(ref.dtype)
 
 
 def ffn_finish_kernel(
@@ -812,12 +820,12 @@
     up_ref[:, 768:] = jnp.where(first, jnp.where(low, high, here), jnp.where(low, cross, core))
     down_ref[:, :768] = jnp.where(first, jnp.where(low, core, cross), jnp.where(low, here, high))
     down_ref[:, 768:] = jnp.where(first, jnp.where(low, cross, core), jnp.where(low, high, here))
-    mine = alls[0][:, 768:] + alls[2][:, 768:]
-    other = alls[1][:, 768:] + alls[3][:, 768:]
+    mine = alls[0][:, 768:1024] + alls[2][:, 768:1024]
+    other = alls[1][:, 768:1024] + alls[3][:, 768:1024]
     o_ref[:, :256] = jnp.where(first, mine, other)[:12]
     o_ref[:, 256:] = jnp.where(first, other[:, 128:], mine[:, 128:])[:12]
-    vec = jnp.where(first, alls[1][16:24] + alls[3][16:24], alls[0][16:24] + alls[2][16:24])
-    vec = jnp.concatenate([vec[row : row + 1] for row in range(5)], axis=1)
+    vec = jnp.where(first, alls[1][12:] + alls[3][12:], alls[0][12:] + alls[2][12:])
+    vec = jnp.concatenate([vec[row : row + 1] for row in range(4)], axis=1)
     begin = 0
     for ref in (up_bias_out, down_bias_out, gain_out, shift_out, o_bias_out):
         ref[...] = vec[:, begin : begin + ref.shape[1]]
@@ -869,7 +877,7 @@
     own, x_send, o_other = lax.optimization_barrier((own, x_send, o_other))
     pairs = own[:, :HALF]
     one = lax.ppermute(pairs, "core", SWAP)
-    edge = lax.ppermute(own[BLOCKS - 1], "y", ((1, 0), (3, 2)))
+    edge = lax.ppermute(own[BLOCKS - 1], EDGE, ((7, 3), (15, 11)))
     two = lax.ppermute(pairs, "zh", SWAP)
     two, edge = lax.optimization_barrier((two, edge))
     three = lax.ppermute(two, "core", SWAP)
@@ -934,7 +942,7 @@
     ffn_other = lax.ppermute(ffn, "wa", SWAP)
     given, kept, dq, edge_grad = attend_grad(kv, q_rows, start_rows, full_rows, dh)
     given, ffn_other = lax.optimization_barrier((given, ffn_other))
-    edge_got = lax.ppermute(edge_grad, "y", ((0, 1), (2, 3)))
+    edge_got = lax.ppermute(edge_grad, EDGE, ((3, 7), (11, 15)))
     taken = lax.ppermute(given, "core", SWAP)
     merged = call(
         merge_kernel, "merge",
@@ -945,7 +953,7 @@
     grads = lax.all_to_all(merged, CHIPS, 0, 0, tiled=True)
     ffn_core, ffn_high, ffn_cross, ffn_here = call(
         ffn_sums_kernel, "ffn_sums", copied(ffn_blocks),
-        [("v", whole(32, 1024)) for _ in range(3)] + [("v", whole(32, 1024, dtype=f32))],
+        [("v", whole(16, 1152)) for _ in range(3)] + [("v", whole(16, 1152, dtype=f32))],
         cost=0,
     )
     ffn_core = lax.ppermute(ffn_core, "core", SWAP)

time: 190 us -> 189 us (level)
  starting transfers between devices: 66.2 us -> 63.8 us
  waiting for transfers between devices: 48.7 us -> 50.9 us
    ppermute x2, waiting for transfers between devices: 8.28 us -> 2.08 us  [on_device(): ffn_high = lax.ppermute(ffn_high, 'zh', SWAP)]
    ppermute x2, waiting for transfers between devices: 6.59 us -> 12.7 us  [on_device(): ffn_cross = lax.ppermute(ffn_cross, ('zh', 'core'), CROSS)]
    ppermute x2, starting transfers between devices: 4.98 us -> 1.91 us  [the longest x1 1.26 us: on_device(): edge_got = lax.ppermute(edge_grad, EDGE, ((3, 7), (11, 15)))]
    all_to_all x1, starting transfers between devices: 6.91 us -> 9.25 us  [on_device(): grads = lax.all_to_all(merged, CHIPS, 0, 0, tiled=True)]
  transfers between devices with their start and end apart: 29 -> 29, of which waited for: 12 -> 13; matrix products, arithmetic and copies ran while one was open for 0% -> 0% of each run, Pallas kernels for 23% -> 23%
where the time goes in v4:
time: 189 us; the launch traced here: 188 us
  Pallas kernels  69.5 us (37%)
  starting transfers between devices  63.8 us (34%)
  waiting for transfers between devices  50.9 us (27%)
  local copies, waits for them, and re-layouts  2.43 us (1%)
    pallas_call x17, Pallas kernels, call(): pl.pallas_call(body, out_shape=tuple((out for _, out in outs)), in_specs=...  69.5 us
    ppermute x1, waiting for transfers between devices, on_device(): dn_one_other = lax.ppermute(dn_one, 'wa', SWAP)  12.9 us
    ppermute x2, waiting for transfers between devices, on_device(): ffn_cross = lax.ppermute(ffn_cross, ('zh', 'core'), CROSS)  12.7 us
    all_to_all x1, starting transfers between devices, on_device(): grads = lax.all_to_all(merged, CHIPS, 0, 0, tiled=True)  9.25 us
    all_to_all x1, waiting for transfers between devices, on_device(): got = lax.all_to_all(back, ('x', 'y', 'wa'), 0, 0, tiled=True)  7.2 us
    all_to_all x1, starting transfers between devices, on_device(): own = lax.all_to_all(payload, PLANE, 0, 0, tiled=True)  6.8 us
    all_to_all x1, waiting for transfers between devices, on_device(): own = lax.all_to_all(payload, PLANE, 0, 0, tiled=True)  6.04 us
    ppermute x2, starting transfers between devices, on_device(): ffn_high = lax.ppermute(ffn_high, 'zh', SWAP)  5.98 us
  transfers between devices with their start and end apart: 29, of which 13 were waited for; matrix products, arithmetic and copies ran while one was open for 0% of the time, Pallas kernels for 23%

profile of v4, /device:TPU:1, one launch (start us, length us, event | category | flops | bytes accessed | tf_op | source)
XLA Modules:
  0.0 187.7 jit_solution(10543410580620454388)
XLA Ops:
  0.7 3.0 %project.1 = (bf16[16,112,128]{2,1,0:T(8,128)(2,1)}, bf16[128,768]{1,0:T(8,128)(2,1)}) custom-call(bf16[128,768]{1,0:T(8,128)(2,1)} %refs_2_.9, s32[128]{0:T(128)} %refs_1_.5, f32[768]{0:T(1024)} %refs_5_.9, f32[768]{0:T(1024)} %refs_3_.6, f32[384]{0:T(512)} %refs_4_.6, f32[384]{0:T(512)} %refs_5_.5, bf16[768,384]{1,0:T(8,128)(2,1)} %refs_2_.8, ...), custom_call_target="tpu_custom_call" | custom-call | flops 2000000000 | tf_op jit(solution)/shard_map/project/pallas_call | solution.py:145
  3.7 2.5 %collective-permute-start = (bf16[384,768]{1,0:T(8,128)(2,1)}, bf16[384,768]{1,0:T(8,128)(2,1)}, u32[]{:S(2)}, u32[]{:S(2)}) collective-permute-start(bf16[384,768]{1,0:T(8,128)(2,1)} %refs_9_.1), channel_id=1, source_target_pairs={{0,1},{1,0},{2,3},{3,2},{4,5},{5,4},{6,7},{7,6},{8,9},{9,8},{10,11... | collective-permute-start | bytes 1769480 | tf_op jit(solution)/shard_map/ppermute | solution.py:871
  6.2 6.8 %all-to-all-start = ((bf16[16,112,128]{2,1,0:T(8,128)(2,1)}), bf16[16,112,128]{2,1,0:T(8,128)(2,1)}, u32[]{:S(2)}, u32[]{:S(2)}) async-start(bf16[16,112,128]{2,1,0:T(8,128)(2,1)} %get-tuple-element.97), calls=%async_computation | async-start | bytes 917504 | tf_op jit(solution)/shard_map/all_to_all | solution.py:869
  13.0 2.6 %prepare.1 = (bf16[128,384]{1,0:T(8,128)(2,1)}, bf16[128,384]{1,0:T(8,128)(2,1)}) custom-call(bf16[128,768]{1,0:T(8,128)(2,1)} %get-tuple-element.95.refs_0_), custom_call_target="tpu_custom_call" | custom-call | flops 2000000000 | tf_op jit(solution)/shard_map/prepare/pallas_call | solution.py:145
  15.6 6.0 %all-to-all-done.refs_0_ = bf16[16,112,128]{2,1,0:T(8,128)(2,1)} async-done(((bf16[16,112,128]{2,1,0:T(8,128)(2,1)}), bf16[16,112,128]{2,1,0:T(8,128)(2,1)}, u32[]{:S(2)}, u32[]{:S(2)}) %all-to-all-start) | async-done | bytes 458784 | tf_op jit(solution)/shard_map/all_to_all | solution.py:869
  21.7 1.0 slice.6
  22.7 3.4 %collective-permute-start.2 = (bf16[16,64,128]{2,1,0:T(8,128)(2,1)S(1)}, bf16[16,64,128]{2,1,0:T(8,128)(2,1)S(1)}, u32[]{:S(2)}, u32[]{:S(2)}) collective-permute-start(bf16[16,64,128]{2,1,0:T(8,128)(2,1)S(1)} %slice.6), channel_id=1, source_target_pairs={{0,4},{4,0},{1,5},{5,1},{2,6},{6,2},{3,7},{7,3},{8,12},{12,8},{9,1... | collective-permute-start | bytes 786440 | tf_op jit(solution)/shard_map/ppermute | solution.py:881
  26.0 0.8 slice_bitcast_fusion
  27.5 3.5 %collective-permute-start.1 = (bf16[16,64,128]{2,1,0:T(8,128)(2,1)S(1)}, bf16[16,64,128]{2,1,0:T(8,128)(2,1)S(1)}, u32[]{:S(2)}, u32[]{:S(2)}) collective-permute-start(bf16[16,64,128]{2,1,0:T(8,128)(2,1)S(1)} %slice.6), channel_id=1, source_target_pairs={{0,2},{2,0},{1,3},{3,1},{4,6},{6,4},{5,7},{7,5},{8,10},{10,8},{9,1... | collective-permute-start | bytes 786440 | tf_op jit(solution)/shard_map/ppermute | solution.py:879
  31.0 2.8 %collective-permute-start.4 = (bf16[16,64,128]{2,1,0:T(8,128)(2,1)S(1)}, bf16[16,64,128]{2,1,0:T(8,128)(2,1)}, u32[]{:S(2)}, u32[]{:S(2)}) collective-permute-start(bf16[16,64,128]{2,1,0:T(8,128)(2,1)S(1)} %collective-permute-done.2.refs_2_), channel_id=1, source_target_pairs={{0,2},{2,0},{1,3},{3,1},{4,6},{6,4},{5,7},{7,5},{8,10},{10,8},{9,1... | collective-permute-start | bytes 786440 | tf_op jit(solution)/shard_map/ppermute | solution.py:883
  35.1 6.0 %attend.1 = (bf16[32,64,128]{2,1,0:T(8,128)(2,1)}, bf16[17,256,128]{2,1,0:T(8,128)(2,1)}, bf16[1088,128]{1,0:T(8,128)(2,1)}, f32[1088,128]{1,0:T(8,128)}, f32[1088,128]{1,0:T(8,128)}) custom-call(bf16[16,112,128]{2,1,0:T(8,128)(2,1)} %all-to-all-done.refs_0_, bf16[16,64,128]{2,1,0:T(8,128)(2,1)} %copy-done.1, bf16[16,64,128]{2,1,0:T(8,128)(2,1)} %copy-done, ...), custom_call_target="tpu_custom_call" | custom-call | flops 3000000000 | tf_op jit(solution)/shard_map/attend/pallas_call | solution.py:145
  41.1 5.1 %all-to-all-start.1 = ((bf16[32,64,128]{2,1,0:T(8,128)(2,1)}), bf16[32,64,128]{2,1,0:T(8,128)(2,1)}, u32[]{:S(2)}, u32[]{:S(2)}) async-start(bf16[32,64,128]{2,1,0:T(8,128)(2,1)} %get-tuple-element.107), calls=%async_computation.1 | async-start | bytes 1048576 | tf_op jit(solution)/shard_map/all_to_all | solution.py:891
  46.2 3.7 %dhidden.1 = (f32[128,1536]{1,0:T(8,128)}, f32[1,768]{1,0:T(1,128)}) custom-call(bf16[128,768]{1,0:T(8,128)(2,1)} %refs_3_.11, s32[128]{0:T(128)} %refs_4_.11, bf16[1536,768]{1,0:T(8,128)(2,1)} %refs_1_.8), custom_call_target="tpu_custom_call" | custom-call | flops 2000000000 | tf_op jit(solution)/shard_map/dhidden/pallas_call | solution.py:145
  50.0 7.2 %all-to-all-done.1.refs_0_ = bf16[32,64,128]{2,1,0:T(8,128)(2,1)} async-done(((bf16[32,64,128]{2,1,0:T(8,128)(2,1)}), bf16[32,64,128]{2,1,0:T(8,128)(2,1)}, u32[]{:S(2)}, u32[]{:S(2)}) %all-to-all-start.1) | async-done | bytes 524320 | tf_op jit(solution)/shard_map/all_to_all | solution.py:891
  57.2 6.9 %middle.1 = (bf16[128,768]{1,0:T(8,128)(2,1)}, bf16[128,1536]{1,0:T(8,128)(2,1)}, bf16[128,1536]{1,0:T(8,128)(2,1)}, bf16[128,1536]{1,0:T(8,128)(2,1)}, bf16[128...) custom-call(bf16[32,64,128]{2,1,0:T(8,128)(2,1)} %all-to-all-done.1., ...), custom_call_target="tpu_custom_call" | custom-call | flops 2000000000 | tf_op jit(solution)/shard_map/middle/pallas_call | solution.py:145
  64.6 2.2 %collective-permute-start.9 = (bf16[128,1536]{1,0:T(8,128)(2,1)}, bf16[128,1536]{1,0:T(8,128)(2,1)}, u32[]{:S(2)}, u32[]{:S(2)}) collective-permute-start(bf16[128,1536]{1,0:T(8,128)(2,1)} %get-tuple-element.125), channel_id=1, source_target_pairs={{0,2},{2,0},{1,3},{3,1},{4,6},{6,4},{5,7},{7,5},{8,10},{10,8},{9,1... | collective-permute-start | bytes 1179656 | tf_op jit(solution)/shard_map/ppermute | solution.py:916
  66.8 3.3 %collective-permute-start.10 = (bf16[128,1536]{1,0:T(8,128)(2,1)}, bf16[128,1536]{1,0:T(8,128)(2,1)}, u32[]{:S(2)}, u32[]{:S(2)}) collective-permute-start(bf16[128,1536]{1,0:T(8,128)(2,1)} %get-tuple-element.126), channel_id=1, source_target_pairs={{0,4},{4,0},{1,5},{5,1},{2,6},{6,2},{3,7},{7,3},{8,12},{12,8},{9,1... | collective-permute-start | bytes 1179656 | tf_op jit(solution)/shard_map/ppermute | solution.py:914
  70.1 3.0 %ffn.1.refs_0_ = bf16[128,768]{1,0:T(8,128)(2,1)} custom-call(bf16[128,1536]{1,0:T(8,128)(2,1)} %get-tuple-element.111.refs_0_, bf16[1536,768]{1,0:T(8,128)(2,1)} %refs_1_.8), custom_call_target="tpu_custom_call" | custom-call | tf_op jit(solution)/shard_map/ffn/pallas_call | solution.py:145
  73.1 4.6 %dheads.1 = (bf16[16,64,128]{2,1,0:T(8,128)(2,1)}, bf16[128,1152]{1,0:T(8,128)(2,1)}, f32[128,768]{1,0:T(8,128)}, f32[1,4608]{1,0:T(1,128)}) custom-call(bf16[128,768]{1,0:T(8,128)(2,1)} %get-tuple-element.110.refs_0_, bf16[128,768]{1,0:T(8,128)(2,1)} %collective-permute-done.5.refs_1_, f32[128,768]{1,0:T(8,128)} %get-tuple-element.113.refs_2_, ...), custom_call_target="tpu_custom_call" | custom-call | tf_op jit(solution)/shard_map/dheads/pallas_call | solution.py:145
  78.2 4.2 %all-to-all-start.2 = ((bf16[16,64,128]{2,1,0:T(8,128)(2,1)}), bf16[16,64,128]{2,1,0:T(8,128)(2,1)}, u32[]{:S(2)}, u32[]{:S(2)}) async-start(bf16[16,64,128]{2,1,0:T(8,128)(2,1)} %get-tuple-element.117), calls=%async_computation.2 | async-start | bytes 524288 | tf_op jit(solution)/shard_map/all_to_all | solution.py:932
  82.7 1.4 collective-permute-done.13.refs_7_
  84.2 0.8 collective-permute-start.6
  85.0 6.1 %collective-permute-done.11.refs_3_ = bf16[128,1536]{1,0:T(8,128)(2,1)} collective-permute-done((bf16[128,1536]{1,0:T(8,128)(2,1)}, bf16[128,1536]{1,0:T(8,128)(2,1)}, u32[]{:S(2)}, u32[]{:S(2)}) %collective-permute-start.11) | collective-permute-done | bytes 393248 | tf_op jit(solution)/shard_map/ppermute | solution.py:915
  91.1 3.9 %ffn_products.1 = bf16[768,1024]{1,0:T(8,128)(2,1)} custom-call(bf16[128,1536]{1,0:T(8,128)(2,1)} %get-tuple-element.124.refs_0_, bf16[128,1536]{1,0:T(8,128)(2,1)} %collective-permute-done.9.refs_1_, bf16[128,1536]{1,0:T(8,128)(2,1)} %collective-permute-done.10.refs_2_, bf16[128,1536]{1,0:T(8,128)(2,1)} %collective-permute-done.11.refs_3_, ...), custom_call_target="tpu_custom_call" | custom-call | flops 2000000000 | tf_op jit(solution)/shard_map/ffn_products/pallas_call | solution.py:145
  95.0 4.4 %all-to-all-start.3 = ((bf16[16,48,1024]{2,1,0:T(8,128)(2,1)}), bf16[16,48,1024]{2,1,0:T(8,128)(2,1)}, u32[]{:S(2)}, u32[]{:S(2)}) async-start(bf16[16,48,1024]{2,1,0:T(8,128)(2,1)} %bitcast.3), calls=%async_computation.3 | async-start | bytes 3145728 | tf_op jit(solution)/shard_map/all_to_all | solution.py:941
  99.4 13.4 %attend_grad.1 = (bf16[32,64,128]{2,1,0:T(8,128)(2,1)}, bf16[32,64,128]{2,1,0:T(8,128)(2,1)}, bf16[16,32,128]{2,1,0:T(8,128)(2,1)}, bf16[96,128]{1,0:T(8,128)(2,1)}) custom-call(bf16[17,256,128]{2,1,0:T(8,128)(2,1)} %get-tuple-element.103.refs_0_, bf16[1088,128]{1,0:T(8,128)(2,1)} %get-tuple-element.104.refs_1_, f32[1088,128]{1,0:T(8,128)} %get-tuple-element.105.refs_2_, ...), custom_call_target="tpu_custom_call" | custom-call | flops 40000000000 | tf_op jit(solution)/shard_map/attend_grad/pallas_call | solution.py:145
  113.0 1.3 collective-permute-start.8
  114.2 1.0 collective-permute-done.7.refs_1_
  115.2 2.2 %merge.1 = bf16[32,96,128]{2,1,0:T(8,128)(2,1)} custom-call(bf16[32,64,128]{2,1,0:T(8,128)(2,1)} %get-tuple-element.118.refs_0_, bf16[32,64,128]{2,1,0:T(8,128)(2,1)} %collective-permute-done.7.refs_1_, bf16[16,32,128]{2,1,0:T(8,128)(2,1)} %get-tuple-element.122.refs_2_, bf16[96,128]{1,0:T(8,128)(2,1)} %collective-permute-done.8.refs_3_), custom_call_target="tpu_custom_call" | custom-call | flops 2000000000 | tf_op jit(solution)/shard_map/merge/pallas_call | solution.py:145
  117.4 4.1 %all-to-all-done.3.refs_0_ = bf16[16,48,1024]{2,1,0:T(8,128)(2,1)} async-done(((bf16[16,48,1024]{2,1,0:T(8,128)(2,1)}), bf16[16,48,1024]{2,1,0:T(8,128)(2,1)}, u32[]{:S(2)}, u32[]{:S(2)}) %all-to-all-start.3) | async-done | bytes 1572896 | tf_op jit(solution)/shard_map/all_to_all | solution.py:941
  121.6 9.3 %all-to-all-start.4 = ((bf16[32,96,128]{2,1,0:T(8,128)(2,1)}), bf16[32,96,128]{2,1,0:T(8,128)(2,1)}, u32[]{:S(2)}, u32[]{:S(2)}) async-start(bf16[32,96,128]{2,1,0:T(8,128)(2,1)} %merge.1), calls=%async_computation.4 | async-start | bytes 1572864 | tf_op jit(solution)/shard_map/all_to_all | solution.py:953
  130.9 2.4 %ffn_sums.1 = (bf16[16,1152]{1,0:T(8,128)(2,1)}, bf16[16,1152]{1,0:T(8,128)(2,1)}, bf16[16,1152]{1,0:T(8,128)(2,1)}, f32[16,1152]{1,0:T(8,128)}) custom-call(bf16[16,48,1024]{2,1,0:T(8,128)(2,1)} %all-to-all-done.3.refs_0_), custom_call_target="tpu_custom_call" | custom-call | tf_op jit(solution)/shard_map/ffn_sums/pallas_call | solution.py:145
  133.3 0.8 collective-permute-start.14
  134.1 2.7 %collective-permute-start.15 = (bf16[16,1152]{1,0:T(8,128)(2,1)}, bf16[16,1152]{1,0:T(8,128)(2,1)}, u32[]{:S(2)}, u32[]{:S(2)}) collective-permute-start(bf16[16,1152]{1,0:T(8,128)(2,1)} %get-tuple-element.133), channel_id=1, source_target_pairs={{0,4},{4,0},{1,5},{5,1},{2,6},{6,2},{3,7},{7,3},{8,12},{12,8},{9,1... | collective-permute-start | bytes 110600 | tf_op jit(solution)/shard_map/ppermute | solution.py:960
  137.3 2.1 %collective-permute-done.15.refs_2_ = bf16[16,1152]{1,0:T(8,128)(2,1)} collective-permute-done((bf16[16,1152]{1,0:T(8,128)(2,1)}, bf16[16,1152]{1,0:T(8,128)(2,1)}, u32[]{:S(2)}, u32[]{:S(2)}) %collective-permute-start.15) | collective-permute-done | bytes 36896 | tf_op jit(solution)/shard_map/ppermute | solution.py:960
  139.4 6.6 %collective-permute-done.16.refs_3_ = bf16[16,1152]{1,0:T(8,128)(2,1)} collective-permute-done((bf16[16,1152]{1,0:T(8,128)(2,1)}, bf16[16,1152]{1,0:T(8,128)(2,1)}, u32[]{:S(2)}, u32[]{:S(2)}) %collective-permute-start.16) | collective-permute-done | bytes 36896 | tf_op jit(solution)/shard_map/ppermute | solution.py:961
  146.0 0.9 all-to-all-done.4.refs_0_
  146.9 4.1 %dnormed.1 = (bf16[128,1152]{1,0:T(8,128)(2,1)}, f32[1,1536]{1,0:T(1,128)}, f32[1,2304]{1,0:T(1,128)}, bf16[128,768]{1,0:T(8,128)(2,1)}) custom-call(bf16[32,96,128]{2,1,0:T(8,128)(2,1)} %all-to-all-done.4.refs_0_, bf16[128,768]{1,0:T(8,128)(2,1)} %refs_2_.9, bf16[768,384]{1,0:T(8,128)(2,1)} %refs_2_.8, bf16[768,384]{1,0:T(8,128)(2,1)} %refs_3_.9, ...), custom_call_target="tpu_custom_call" | custom-call | tf_op jit(solution)/shard_map/dnormed/pallas_call | solution.py:145
  151.6 0.9 collective-permute-start.21
  152.4 0.9 collective-permute-start.20
  153.3 1.6 collective-permute-done.21.refs_7_
  155.2 3.5 %qkv_products.1 = bf16[32,128,128]{2,1,0:T(8,128)(2,1)} custom-call(bf16[128,384]{1,0:T(8,128)(2,1)} %get-tuple-element.96.refs_0_, bf16[128,384]{1,0:T(8,128)(2,1)} %collective-permute-done.17.refs_1_, bf16[128,1152]{1,0:T(8,128)(2,1)} %get-tuple-element.138.refs_2_, bf16[128,1152]{1,0:T(8,128)(2,1)} %collective-permute-done.18.refs_3_, ...), custom_call_target="tpu_custom_call" | custom-call | tf_op jit(solution)/shard_map/qkv_products/pallas_call | solution.py:145
  158.8 5.5 %all-to-all-start.5 = ((bf16[32,128,128]{2,1,0:T(8,128)(2,1)}), bf16[32,128,128]{2,1,0:T(8,128)(2,1)}, u32[]{:S(2)}, u32[]{:S(2)}) async-start(bf16[32,128,128]{2,1,0:T(8,128)(2,1)} %qkv_products.1), calls=%async_computation.5 | async-start | bytes 2097152 | tf_op jit(solution)/shard_map/all_to_all | solution.py:992
  164.4 2.9 %output.1 = bf16[128,768]{1,0:T(8,128)(2,1)} custom-call(bf16[128,768]{1,0:T(8,128)(2,1)} %ffn.1.refs_0_, bf16[128,768]{1,0:T(8,128)(2,1)} %collective-permute-done.6.refs_1_, f32[128,768]{1,0:T(8,128)} %get-tuple-element.113.refs_2_, bf16[128,768]{1,0:T(8,128)(2,1)} %refs_2_.9, s32[128]{0:T(128)} %refs_4_.11, f32[768]{0:T(1024)} %refs_5_.8), custom_call_target="tpu_custom_call" | custom-call | tf_op jit(solution)/shard_map/output/pallas_call | solution.py:145
  167.4 1.7 ffn_finish.1
  169.1 12.9 %collective-permute-done.22.refs_1_ = bf16[128,768]{1,0:T(8,128)(2,1)} collective-permute-done((bf16[128,768]{1,0:T(8,128)(2,1)}, bf16[128,768]{1,0:T(8,128)(2,1)}, u32[]{:S(2)}, u32[]{:S(2)}) %collective-permute-start.22) | collective-permute-done | bytes 196640 | tf_op jit(solution)/shard_map/ppermute | solution.py:982
  182.0 3.4 %input_grad.1 = f32[128,768]{1,0:T(8,128)} custom-call(bf16[128,768]{1,0:T(8,128)(2,1)} %get-tuple-element.145.refs_0_, bf16[128,768]{1,0:T(8,128)(2,1)} %collective-permute-done.22.refs_1_, bf16[128,768]{1,0:T(8,128)(2,1)} %refs_2_.9, bf16[128,768]{1,0:T(8,128)(2,1)} %refs_3_.11, s32[128]{0:T(128)} %refs_4_.11, f32[768]{0:T(1024)} %refs_5_.9, ...), custom_call_target="tpu_custom_call" | custom-call | tf_op jit(solution)/shard_map/input_grad/pallas_call | solution.py:145
  185.5 2.1 %finish.1 = (f32[12,384]{1,0:T(8,128)}, f32[12,384]{1,0:T(8,128)}, f32[12,384]{1,0:T(8,128)}, f32[768]{0:T(1024)}, f32[768]{0:T(1024)}, /*index=5*/f32[384]{0:T(512)}, f32[384]{0:T(512)}) custom-call(bf16[32,128,128]{2,1,0:T(8,128)(2,1)} %all-to-all-done.5.refs_0_), custom_call_target="tpu_custom_call" | custom-call | flops 2000000000 | tf_op jit(solution)/shard_map/finish/pallas_call | solution.py:145
  (35 shorter events, 5.1 us)
Async XLA Ops:
  3.7 18.0 %collective-permute-start = (bf16[384,768]{1,0:T(8,128)(2,1)}, bf16[384,768]{1,0:T(8,128)(2,1)}, u32[]{:S(2)}, u32[]{:S(2)}) collective-permute-start(bf16[384,768]{1,0:T(8,128)(2,1)} %refs_9_.1), channel_id=1, source_target_pairs={{0,1},{1,0},{2,3},{3,2},{4,5},{5,4},{6,7},{7,6},{8,9},{9,8},{10,11... | collective-permute-start | bytes 1769480 | tf_op jit(solution)/shard_map/ppermute | solution.py:871
  6.2 15.5 %all-to-all-start = ((bf16[16,112,128]{2,1,0:T(8,128)(2,1)}), bf16[16,112,128]{2,1,0:T(8,128)(2,1)}, u32[]{:S(2)}, u32[]{:S(2)}) async-start(bf16[16,112,128]{2,1,0:T(8,128)(2,1)} %get-tuple-element.97), calls=%async_computation | async-start | bytes 917504 | tf_op jit(solution)/shard_map/all_to_all | solution.py:869
  22.7 8.3 %collective-permute-start.2 = (bf16[16,64,128]{2,1,0:T(8,128)(2,1)S(1)}, bf16[16,64,128]{2,1,0:T(8,128)(2,1)S(1)}, u32[]{:S(2)}, u32[]{:S(2)}) collective-permute-start(bf16[16,64,128]{2,1,0:T(8,128)(2,1)S(1)} %slice.6), channel_id=1, source_target_pairs={{0,4},{4,0},{1,5},{5,1},{2,6},{6,2},{3,7},{7,3},{8,12},{12,8},{9,1... | collective-permute-start | bytes 786440 | tf_op jit(solution)/shard_map/ppermute | solution.py:881
  26.8 4.2 %collective-permute-start.3 = (bf16[112,128]{1,0:T(8,128)(2,1)S(1)}, bf16[112,128]{1,0:T(8,128)(2,1)S(1)}, u32[]{:S(2)}, u32[]{:S(2)}) collective-permute-start(bf16[112,128]{1,0:T(8,128)(2,1)S(1)} %slice_bitcast_fusion), channel_id=1, source_target_pairs={{14,6},{30,22},{15,7},{31,23},{46,38},{62,54},{47,39},{63,55},{78,... | collective-permute-start | bytes 86024 | tf_op jit(solution)/shard_map/ppermute | solution.py:880
  27.5 6.4 %collective-permute-start.1 = (bf16[16,64,128]{2,1,0:T(8,128)(2,1)S(1)}, bf16[16,64,128]{2,1,0:T(8,128)(2,1)S(1)}, u32[]{:S(2)}, u32[]{:S(2)}) collective-permute-start(bf16[16,64,128]{2,1,0:T(8,128)(2,1)S(1)} %slice.6), channel_id=1, source_target_pairs={{0,2},{2,0},{1,3},{3,1},{4,6},{6,4},{5,7},{7,5},{8,10},{10,8},{9,1... | collective-permute-start | bytes 786440 | tf_op jit(solution)/shard_map/ppermute | solution.py:879
  31.0 2.9 %copy-start.2 = (bf16[112,128]{1,0:T(8,128)(2,1)}, bf16[112,128]{1,0:T(8,128)(2,1)S(1)}, u32[]{:S(2)}) copy-start(bf16[112,128]{1,0:T(8,128)(2,1)S(1)} %collective-permute-done.3.refs_4_) | copy-start | bytes 86020
  31.0 2.9 %copy-start = (bf16[16,64,128]{2,1,0:T(8,128)(2,1)}, bf16[16,64,128]{2,1,0:T(8,128)(2,1)S(1)}, u32[]{:S(2)}) copy-start(bf16[16,64,128]{2,1,0:T(8,128)(2,1)S(1)} %collective-permute-done.2.refs_2_) | copy-start | bytes 786436
  31.0 4.1 %collective-permute-start.4 = (bf16[16,64,128]{2,1,0:T(8,128)(2,1)S(1)}, bf16[16,64,128]{2,1,0:T(8,128)(2,1)}, u32[]{:S(2)}, u32[]{:S(2)}) collective-permute-start(bf16[16,64,128]{2,1,0:T(8,128)(2,1)S(1)} %collective-permute-done.2.refs_2_), channel_id=1, source_target_pairs={{0,2},{2,0},{1,3},{3,1},{4,6},{6,4},{5,7},{7,5},{8,10},{10,8},{9,1... | collective-permute-start | bytes 786440 | tf_op jit(solution)/shard_map/ppermute | solution.py:883
  33.8 0.7 copy-start.1
  41.1 16.0 %all-to-all-start.1 = ((bf16[32,64,128]{2,1,0:T(8,128)(2,1)}), bf16[32,64,128]{2,1,0:T(8,128)(2,1)}, u32[]{:S(2)}, u32[]{:S(2)}) async-start(bf16[32,64,128]{2,1,0:T(8,128)(2,1)} %get-tuple-element.107), calls=%async_computation.1 | async-start | bytes 1048576 | tf_op jit(solution)/shard_map/all_to_all | solution.py:891
  64.0 9.1 %collective-permute-start.5 = (bf16[128,768]{1,0:T(8,128)(2,1)}, bf16[128,768]{1,0:T(8,128)(2,1)}, u32[]{:S(2)}, u32[]{:S(2)}) collective-permute-start(bf16[128,768]{1,0:T(8,128)(2,1)} %get-tuple-element.110.refs_0_), channel_id=1, source_target_pairs={{0,1},{1,0},{2,3},{3,2},{4,5},{5,4},{6,7},{7,6},{8,9},{9,8},{10,11... | collective-permute-start | bytes 589832 | tf_op jit(solution)/shard_map/ppermute | solution.py:913
  64.6 20.4 %collective-permute-start.9 = (bf16[128,1536]{1,0:T(8,128)(2,1)}, bf16[128,1536]{1,0:T(8,128)(2,1)}, u32[]{:S(2)}, u32[]{:S(2)}) collective-permute-start(bf16[128,1536]{1,0:T(8,128)(2,1)} %get-tuple-element.125), channel_id=1, source_target_pairs={{0,2},{2,0},{1,3},{3,1},{4,6},{6,4},{5,7},{7,5},{8,10},{10,8},{9,1... | collective-permute-start | bytes 1179656 | tf_op jit(solution)/shard_map/ppermute | solution.py:916
  66.8 18.2 %collective-permute-start.10 = (bf16[128,1536]{1,0:T(8,128)(2,1)}, bf16[128,1536]{1,0:T(8,128)(2,1)}, u32[]{:S(2)}, u32[]{:S(2)}) collective-permute-start(bf16[128,1536]{1,0:T(8,128)(2,1)} %get-tuple-element.126), channel_id=1, source_target_pairs={{0,4},{4,0},{1,5},{5,1},{2,6},{6,2},{3,7},{7,3},{8,12},{12,8},{9,1... | collective-permute-start | bytes 1179656 | tf_op jit(solution)/shard_map/ppermute | solution.py:914
  70.1 21.0 %collective-permute-start.11 = (bf16[128,1536]{1,0:T(8,128)(2,1)}, bf16[128,1536]{1,0:T(8,128)(2,1)}, u32[]{:S(2)}, u32[]{:S(2)}) collective-permute-start(bf16[128,1536]{1,0:T(8,128)(2,1)} %get-tuple-element.127), channel_id=1, source_target_pairs={{0,6},{2,4},{4,2},{6,0},{1,7},{3,5},{5,3},{7,1},{8,14},{10,12},{12... | collective-permute-start | bytes 1179656 | tf_op jit(solution)/shard_map/ppermute | solution.py:915
  77.7 13.4 %collective-permute-start.12 = (bf16[128,1152]{1,0:T(8,128)(2,1)}, bf16[128,1152]{1,0:T(8,128)(2,1)}, u32[]{:S(2)}, u32[]{:S(2)}) collective-permute-start(bf16[128,1152]{1,0:T(8,128)(2,1)} %get-tuple-element.128.refs_4_), channel_id=1, source_target_pairs={{0,2},{2,0},{1,3},{3,1},{4,6},{6,4},{5,7},{7,5},{8,10},{10,8},{9,1... | collective-permute-start | bytes 884744 | tf_op jit(solution)/shard_map/ppermute | solution.py:933
  78.2 16.8 %all-to-all-start.2 = ((bf16[16,64,128]{2,1,0:T(8,128)(2,1)}), bf16[16,64,128]{2,1,0:T(8,128)(2,1)}, u32[]{:S(2)}, u32[]{:S(2)}) async-start(bf16[16,64,128]{2,1,0:T(8,128)(2,1)} %get-tuple-element.117), calls=%async_computation.2 | async-start | bytes 524288 | tf_op jit(solution)/shard_map/all_to_all | solution.py:932
  82.4 1.8 collective-permute-start.13
  84.2 28.7 %collective-permute-start.6 = (bf16[128,768]{1,0:T(8,128)(2,1)}, bf16[128,768]{1,0:T(8,128)(2,1)}, u32[]{:S(2)}, u32[]{:S(2)}) collective-permute-start(bf16[128,768]{1,0:T(8,128)(2,1)} %ffn.1.refs_0_), channel_id=1, source_target_pairs={{0,1},{1,0},{2,3},{3,2},{4,5},{5,4},{6,7},{7,6},{8,9},{9,8},{10,11... | collective-permute-start | bytes 589832 | tf_op jit(solution)/shard_map/ppermute | solution.py:942
  95.0 26.6 %all-to-all-start.3 = ((bf16[16,48,1024]{2,1,0:T(8,128)(2,1)}), bf16[16,48,1024]{2,1,0:T(8,128)(2,1)}, u32[]{:S(2)}, u32[]{:S(2)}) async-start(bf16[16,48,1024]{2,1,0:T(8,128)(2,1)} %bitcast.3), calls=%async_computation.3 | async-start | bytes 3145728 | tf_op jit(solution)/shard_map/all_to_all | solution.py:941
  112.9 2.3 %collective-permute-start.7 = (bf16[32,64,128]{2,1,0:T(8,128)(2,1)}, bf16[32,64,128]{2,1,0:T(8,128)(2,1)}, u32[]{:S(2)}, u32[]{:S(2)}) collective-permute-start(bf16[32,64,128]{2,1,0:T(8,128)(2,1)} %get-tuple-element.121), channel_id=1, source_target_pairs={{0,2},{2,0},{1,3},{3,1},{4,6},{6,4},{5,7},{7,5},{8,10},{10,8},{9,1... | collective-permute-start | bytes 1572872 | tf_op jit(solution)/shard_map/ppermute | solution.py:946
  113.0 1.3 collective-permute-start.8
  121.6 25.3 %all-to-all-start.4 = ((bf16[32,96,128]{2,1,0:T(8,128)(2,1)}), bf16[32,96,128]{2,1,0:T(8,128)(2,1)}, u32[]{:S(2)}, u32[]{:S(2)}) async-start(bf16[32,96,128]{2,1,0:T(8,128)(2,1)} %merge.1), calls=%async_computation.4 | async-start | bytes 1572864 | tf_op jit(solution)/shard_map/all_to_all | solution.py:953
  130.8 6.5 %collective-permute-start.17 = (bf16[128,384]{1,0:T(8,128)(2,1)}, bf16[128,384]{1,0:T(8,128)(2,1)}, u32[]{:S(2)}, u32[]{:S(2)}) collective-permute-start(bf16[128,384]{1,0:T(8,128)(2,1)} %get-tuple-element.135), channel_id=1, source_target_pairs={{0,2},{2,0},{1,3},{3,1},{4,6},{6,4},{5,7},{7,5},{8,10},{10,8},{9,1... | collective-permute-start | bytes 294920 | tf_op jit(solution)/shard_map/ppermute | solution.py:884
  133.3 4.0 %collective-permute-start.14 = (bf16[16,1152]{1,0:T(8,128)(2,1)}, bf16[16,1152]{1,0:T(8,128)(2,1)}, u32[]{:S(2)}, u32[]{:S(2)}) collective-permute-start(bf16[16,1152]{1,0:T(8,128)(2,1)} %get-tuple-element.132), channel_id=1, source_target_pairs={{0,2},{2,0},{1,3},{3,1},{4,6},{6,4},{5,7},{7,5},{8,10},{10,8},{9,1... | collective-permute-start | bytes 110600 | tf_op jit(solution)/shard_map/ppermute | solution.py:959
  134.1 5.3 %collective-permute-start.15 = (bf16[16,1152]{1,0:T(8,128)(2,1)}, bf16[16,1152]{1,0:T(8,128)(2,1)}, u32[]{:S(2)}, u32[]{:S(2)}) collective-permute-start(bf16[16,1152]{1,0:T(8,128)(2,1)} %get-tuple-element.133), channel_id=1, source_target_pairs={{0,4},{4,0},{1,5},{5,1},{2,6},{6,2},{3,7},{7,3},{8,12},{12,8},{9,1... | collective-permute-start | bytes 110600 | tf_op jit(solution)/shard_map/ppermute | solution.py:960
  136.8 9.2 %collective-permute-start.16 = (bf16[16,1152]{1,0:T(8,128)(2,1)}, bf16[16,1152]{1,0:T(8,128)(2,1)}, u32[]{:S(2)}, u32[]{:S(2)}) collective-permute-start(bf16[16,1152]{1,0:T(8,128)(2,1)} %get-tuple-element.134), channel_id=1, source_target_pairs={{0,6},{2,4},{4,2},{6,0},{1,7},{3,5},{5,3},{7,1},{8,14},{10,12},{12... | collective-permute-start | bytes 110600 | tf_op jit(solution)/shard_map/ppermute | solution.py:961
  151.0 4.3 %collective-permute-start.18 = (bf16[128,1152]{1,0:T(8,128)(2,1)}, bf16[128,1152]{1,0:T(8,128)(2,1)}, u32[]{:S(2)}, u32[]{:S(2)}) collective-permute-start(bf16[128,1152]{1,0:T(8,128)(2,1)} %get-tuple-element.138.refs_2_), channel_id=1, source_target_pairs={{0,2},{2,0},{1,3},{3,1},{4,6},{6,4},{5,7},{7,5},{8,10},{10,8},{9,1... | collective-permute-start | bytes 884744 | tf_op jit(solution)/shard_map/ppermute | solution.py:977
  151.4 3.8 %collective-permute-start.19 = (f32[1,2304]{1,0:T(1,128)}, f32[1,2304]{1,0:T(1,128)}, u32[]{:S(2)}, u32[]{:S(2)}) collective-permute-start(f32[1,2304]{1,0:T(1,128)} %get-tuple-element.139.refs_4_), channel_id=1, source_target_pairs={{0,2},{2,0},{1,3},{3,1},{4,6},{6,4},{5,7},{7,5},{8,10},{10,8},{9,1... | collective-permute-start | bytes 27656 | tf_op jit(solution)/shard_map/ppermute | solution.py:978
  151.6 3.4 %collective-permute-start.21 = (f32[1,1536]{1,0:T(1,128)}, f32[1,1536]{1,0:T(1,128)}, u32[]{:S(2)}, u32[]{:S(2)}) collective-permute-start(f32[1,1536]{1,0:T(1,128)} %get-tuple-element.140), channel_id=1, source_target_pairs={{0,3},{1,2},{2,1},{3,0},{4,7},{5,6},{6,5},{7,4},{8,11},{9,10},{10,... | collective-permute-start | bytes 18440 | tf_op jit(solution)/shard_map/ppermute | solution.py:980
  152.4 2.8 %collective-permute-start.20 = (f32[1,1536]{1,0:T(1,128)}, f32[1,1536]{1,0:T(1,128)}, u32[]{:S(2)}, u32[]{:S(2)}) collective-permute-start(f32[1,1536]{1,0:T(1,128)} %get-tuple-element.140), channel_id=1, source_target_pairs={{0,1},{1,0},{2,3},{3,2},{4,5},{5,4},{6,7},{7,6},{8,9},{9,8},{10,11... | collective-permute-start | bytes 18440 | tf_op jit(solution)/shard_map/ppermute | solution.py:979
  158.8 26.7 %all-to-all-start.5 = ((bf16[32,128,128]{2,1,0:T(8,128)(2,1)}), bf16[32,128,128]{2,1,0:T(8,128)(2,1)}, u32[]{:S(2)}, u32[]{:S(2)}) async-start(bf16[32,128,128]{2,1,0:T(8,128)(2,1)} %qkv_products.1), calls=%async_computation.5 | async-start | bytes 2097152 | tf_op jit(solution)/shard_map/all_to_all | solution.py:992
  164.3 17.7 %collective-permute-start.22 = (bf16[128,768]{1,0:T(8,128)(2,1)}, bf16[128,768]{1,0:T(8,128)(2,1)}, u32[]{:S(2)}, u32[]{:S(2)}) collective-permute-start(bf16[128,768]{1,0:T(8,128)(2,1)} %get-tuple-element.145.refs_0_), channel_id=1, source_target_pairs={{0,1},{1,0},{2,3},{3,2},{4,5},{5,4},{6,7},{7,6},{8,9},{9,8},{10,11... | collective-permute-start | bytes 589832 | tf_op jit(solution)/shard_map/ppermute | solution.py:982

commit v5 on v4

--- a/solution.py
+++ b/solution.py
@@ -626,27 +626,29 @@
     vec_ref, vec_sent_ref, out_ref,
 ):
     pieces = (here_ref, core_ref, high_ref, cross_ref)
-    lefts = jnp.concatenate([ref[:, :768] for ref in pieces], axis=0)
-    for at in range(0, 768, 384):
-        rights = jnp.concatenate([ref[:, 768 + at : 1152 + at] for ref in pieces], axis=0)
-        out_ref[:, at : at + 384] = lax.dot_general(
-            lefts, rights, trans_left, preferred_element_type=jnp.float32
-        ).astype(jnp.bfloat16)
     first = lax.axis_index("core") == 0
-    both = jnp.concatenate([both_ref[...], sent_ref[...]], axis=0)
-    product = lax.dot_general(
-        both[:, :768],
-        jnp.where(first, both[:, 768:1024], both[:, 896:]),
-        trans_left,
-        preferred_element_type=jnp.float32,
-    )
-    out_ref[:, 896:] = product[:, 128:].astype(jnp.bfloat16)
     vec = vec_ref[...] + vec_sent_ref[...]
     lines = [vec[:, 128 * row : 128 * (row + 1)] for row in range(36)]
     lines = jnp.concatenate(lines + [jnp.zeros((12, 128), jnp.float32)], axis=0)
-    for plane in range(16):
-        rows = slice(48 * plane, 48 * plane + 48)
-        out_ref[rows, 768:896] = jnp.where(first, product[rows, :128], lines).astype(jnp.bfloat16)
+    rights = jnp.concatenate([ref[:, 768:] for ref in pieces], axis=0)
+    both = jnp.concatenate([both_ref[...], sent_ref[...]], axis=0)
+    attn = jnp.where(first, both[:, 768:1024], both[:, 896:])
+    for half in range(2):
+        rows = slice(384 * half, 384 * half + 384)
+        product = lax.dot_general(
+            both[:, rows], attn, trans_left, preferred_element_type=jnp.float32
+        )
+        out_ref[rows, 896:] = product[:, 128:].astype(jnp.bfloat16)
+        for plane in range(8):
+            at = slice(48 * plane, 48 * plane + 48)
+            out_ref[384 * half + 48 * plane : 384 * half + 48 * plane + 48, 768:896] = jnp.where(
+                first, product[at, :128], lines
+            ).astype(jnp.bfloat16)
+        lefts = jnp.concatenate([ref[:, rows] for ref in pieces], axis=0)
+        out_ref[rows, :768] = lax.dot_general(
+            lefts, rights, trans_left, preferred_element_type=jnp.float32
+        ).astype(jnp.bfloat16)
+        flush(out_ref, 384 * half, 384 * half + 384)
 
 
 def ffn_kernel(wait, flush, hidden_ref, down_ref, out_ref):

time: 189 us -> 188 us (level)
  no operation moved by 1% of the time
where the time goes in v5:
time: 188 us; the launch traced here: 187 us
  Pallas kernels  69.1 us (37%)
  starting transfers between devices  62.8 us (33%)
  waiting for transfers between devices  51.3 us (27%)
  local copies, waits for them, and re-layouts  2.43 us (1%)
    pallas_call x17, Pallas kernels, call(): pl.pallas_call(body, out_shape=tuple((out for _, out in outs)), in_specs=...  69.1 us
    ppermute x2, waiting for transfers between devices, on_device(): ffn_cross = lax.ppermute(ffn_cross, ('zh', 'core'), CROSS)  13.1 us
    ppermute x1, waiting for transfers between devices, on_device(): dn_one_other = lax.ppermute(dn_one, 'wa', SWAP)  12.5 us
    all_to_all x1, starting transfers between devices, on_device(): grads = lax.all_to_all(merged, CHIPS, 0, 0, tiled=True)  8.57 us
    all_to_all x1, waiting for transfers between devices, on_device(): got = lax.all_to_all(back, ('x', 'y', 'wa'), 0, 0, tiled=True)  7.2 us
    all_to_all x1, starting transfers between devices, on_device(): own = lax.all_to_all(payload, PLANE, 0, 0, tiled=True)  6.8 us
    all_to_all x1, waiting for transfers between devices, on_device(): own = lax.all_to_all(payload, PLANE, 0, 0, tiled=True)  6.04 us
    ppermute x2, starting transfers between devices, on_device(): ffn_high = lax.ppermute(ffn_high, 'zh', SWAP)  5.97 us
  transfers between devices with their start and end apart: 29, of which 13 were waited for; matrix products, arithmetic and copies ran while one was open for 0% of the time, Pallas kernels for 23%

profile of v5, /device:TPU:1, one launch (start us, length us, event | category | flops | bytes accessed | tf_op | source)
XLA Modules:
  0.0 186.7 jit_solution(17694522187941083081)
XLA Ops:
  0.7 3.0 %project.1 = (bf16[16,112,128]{2,1,0:T(8,128)(2,1)}, bf16[128,768]{1,0:T(8,128)(2,1)}) custom-call(bf16[128,768]{1,0:T(8,128)(2,1)} %refs_2_.9, s32[128]{0:T(128)} %refs_1_.5, f32[768]{0:T(1024)} %refs_5_.9, f32[768]{0:T(1024)} %refs_3_.6, f32[384]{0:T(512)} %refs_4_.6, f32[384]{0:T(512)} %refs_5_.5, bf16[768,384]{1,0:T(8,128)(2,1)} %refs_2_.8, ...), custom_call_target="tpu_custom_call" | custom-call | flops 2000000000 | tf_op jit(solution)/shard_map/project/pallas_call | solution.py:145
  3.7 2.5 %collective-permute-start = (bf16[384,768]{1,0:T(8,128)(2,1)}, bf16[384,768]{1,0:T(8,128)(2,1)}, u32[]{:S(2)}, u32[]{:S(2)}) collective-permute-start(bf16[384,768]{1,0:T(8,128)(2,1)} %refs_9_.1), channel_id=1, source_target_pairs={{0,1},{1,0},{2,3},{3,2},{4,5},{5,4},{6,7},{7,6},{8,9},{9,8},{10,11... | collective-permute-start | bytes 1769480 | tf_op jit(solution)/shard_map/ppermute | solution.py:873
  6.2 6.8 %all-to-all-start = ((bf16[16,112,128]{2,1,0:T(8,128)(2,1)}), bf16[16,112,128]{2,1,0:T(8,128)(2,1)}, u32[]{:S(2)}, u32[]{:S(2)}) async-start(bf16[16,112,128]{2,1,0:T(8,128)(2,1)} %get-tuple-element.97), calls=%async_computation | async-start | bytes 917504 | tf_op jit(solution)/shard_map/all_to_all | solution.py:871
  13.0 2.6 %prepare.1 = (bf16[128,384]{1,0:T(8,128)(2,1)}, bf16[128,384]{1,0:T(8,128)(2,1)}) custom-call(bf16[128,768]{1,0:T(8,128)(2,1)} %get-tuple-element.95.refs_0_), custom_call_target="tpu_custom_call" | custom-call | flops 2000000000 | tf_op jit(solution)/shard_map/prepare/pallas_call | solution.py:145
  15.6 6.0 %all-to-all-done.refs_0_ = bf16[16,112,128]{2,1,0:T(8,128)(2,1)} async-done(((bf16[16,112,128]{2,1,0:T(8,128)(2,1)}), bf16[16,112,128]{2,1,0:T(8,128)(2,1)}, u32[]{:S(2)}, u32[]{:S(2)}) %all-to-all-start) | async-done | bytes 458784 | tf_op jit(solution)/shard_map/all_to_all | solution.py:871
  21.7 1.0 slice.6
  22.7 3.4 %collective-permute-start.2 = (bf16[16,64,128]{2,1,0:T(8,128)(2,1)S(1)}, bf16[16,64,128]{2,1,0:T(8,128)(2,1)S(1)}, u32[]{:S(2)}, u32[]{:S(2)}) collective-permute-start(bf16[16,64,128]{2,1,0:T(8,128)(2,1)S(1)} %slice.6), channel_id=1, source_target_pairs={{0,4},{4,0},{1,5},{5,1},{2,6},{6,2},{3,7},{7,3},{8,12},{12,8},{9,1... | collective-permute-start | bytes 786440 | tf_op jit(solution)/shard_map/ppermute | solution.py:883
  26.0 0.8 slice_bitcast_fusion
  27.5 3.5 %collective-permute-start.1 = (bf16[16,64,128]{2,1,0:T(8,128)(2,1)S(1)}, bf16[16,64,128]{2,1,0:T(8,128)(2,1)S(1)}, u32[]{:S(2)}, u32[]{:S(2)}) collective-permute-start(bf16[16,64,128]{2,1,0:T(8,128)(2,1)S(1)} %slice.6), channel_id=1, source_target_pairs={{0,2},{2,0},{1,3},{3,1},{4,6},{6,4},{5,7},{7,5},{8,10},{10,8},{9,1... | collective-permute-start | bytes 786440 | tf_op jit(solution)/shard_map/ppermute | solution.py:881
  31.0 2.8 %collective-permute-start.4 = (bf16[16,64,128]{2,1,0:T(8,128)(2,1)S(1)}, bf16[16,64,128]{2,1,0:T(8,128)(2,1)}, u32[]{:S(2)}, u32[]{:S(2)}) collective-permute-start(bf16[16,64,128]{2,1,0:T(8,128)(2,1)S(1)} %collective-permute-done.2.refs_2_), channel_id=1, source_target_pairs={{0,2},{2,0},{1,3},{3,1},{4,6},{6,4},{5,7},{7,5},{8,10},{10,8},{9,1... | collective-permute-start | bytes 786440 | tf_op jit(solution)/shard_map/ppermute | solution.py:885
  35.1 6.0 %attend.1 = (bf16[32,64,128]{2,1,0:T(8,128)(2,1)}, bf16[17,256,128]{2,1,0:T(8,128)(2,1)}, bf16[1088,128]{1,0:T(8,128)(2,1)}, f32[1088,128]{1,0:T(8,128)}, f32[1088,128]{1,0:T(8,128)}) custom-call(bf16[16,112,128]{2,1,0:T(8,128)(2,1)} %all-to-all-done.refs_0_, bf16[16,64,128]{2,1,0:T(8,128)(2,1)} %copy-done.1, bf16[16,64,128]{2,1,0:T(8,128)(2,1)} %copy-done, ...), custom_call_target="tpu_custom_call" | custom-call | flops 3000000000 | tf_op jit(solution)/shard_map/attend/pallas_call | solution.py:145
  41.1 5.1 %all-to-all-start.1 = ((bf16[32,64,128]{2,1,0:T(8,128)(2,1)}), bf16[32,64,128]{2,1,0:T(8,128)(2,1)}, u32[]{:S(2)}, u32[]{:S(2)}) async-start(bf16[32,64,128]{2,1,0:T(8,128)(2,1)} %get-tuple-element.107), calls=%async_computation.1 | async-start | bytes 1048576 | tf_op jit(solution)/shard_map/all_to_all | solution.py:893
  46.2 3.7 %dhidden.1 = (f32[128,1536]{1,0:T(8,128)}, f32[1,768]{1,0:T(1,128)}) custom-call(bf16[128,768]{1,0:T(8,128)(2,1)} %refs_3_.11, s32[128]{0:T(128)} %refs_4_.11, bf16[1536,768]{1,0:T(8,128)(2,1)} %refs_1_.8), custom_call_target="tpu_custom_call" | custom-call | flops 2000000000 | tf_op jit(solution)/shard_map/dhidden/pallas_call | solution.py:145
  50.0 7.2 %all-to-all-done.1.refs_0_ = bf16[32,64,128]{2,1,0:T(8,128)(2,1)} async-done(((bf16[32,64,128]{2,1,0:T(8,128)(2,1)}), bf16[32,64,128]{2,1,0:T(8,128)(2,1)}, u32[]{:S(2)}, u32[]{:S(2)}) %all-to-all-start.1) | async-done | bytes 524320 | tf_op jit(solution)/shard_map/all_to_all | solution.py:893
  57.2 6.9 %middle.1 = (bf16[128,768]{1,0:T(8,128)(2,1)}, bf16[128,1536]{1,0:T(8,128)(2,1)}, bf16[128,1536]{1,0:T(8,128)(2,1)}, bf16[128,1536]{1,0:T(8,128)(2,1)}, bf16[128...) custom-call(bf16[32,64,128]{2,1,0:T(8,128)(2,1)} %all-to-all-done.1., ...), custom_call_target="tpu_custom_call" | custom-call | flops 2000000000 | tf_op jit(solution)/shard_map/middle/pallas_call | solution.py:145
  64.6 2.2 %collective-permute-start.9 = (bf16[128,1536]{1,0:T(8,128)(2,1)}, bf16[128,1536]{1,0:T(8,128)(2,1)}, u32[]{:S(2)}, u32[]{:S(2)}) collective-permute-start(bf16[128,1536]{1,0:T(8,128)(2,1)} %get-tuple-element.125), channel_id=1, source_target_pairs={{0,2},{2,0},{1,3},{3,1},{4,6},{6,4},{5,7},{7,5},{8,10},{10,8},{9,1... | collective-permute-start | bytes 1179656 | tf_op jit(solution)/shard_map/ppermute | solution.py:918
  66.8 3.3 %collective-permute-start.10 = (bf16[128,1536]{1,0:T(8,128)(2,1)}, bf16[128,1536]{1,0:T(8,128)(2,1)}, u32[]{:S(2)}, u32[]{:S(2)}) collective-permute-start(bf16[128,1536]{1,0:T(8,128)(2,1)} %get-tuple-element.126), channel_id=1, source_target_pairs={{0,4},{4,0},{1,5},{5,1},{2,6},{6,2},{3,7},{7,3},{8,12},{12,8},{9,1... | collective-permute-start | bytes 1179656 | tf_op jit(solution)/shard_map/ppermute | solution.py:916
  70.1 3.0 %ffn.1.refs_0_ = bf16[128,768]{1,0:T(8,128)(2,1)} custom-call(bf16[128,1536]{1,0:T(8,128)(2,1)} %get-tuple-element.111.refs_0_, bf16[1536,768]{1,0:T(8,128)(2,1)} %refs_1_.8), custom_call_target="tpu_custom_call" | custom-call | tf_op jit(solution)/shard_map/ffn/pallas_call | solution.py:145
  73.1 4.6 %dheads.1 = (bf16[16,64,128]{2,1,0:T(8,128)(2,1)}, bf16[128,1152]{1,0:T(8,128)(2,1)}, f32[128,768]{1,0:T(8,128)}, f32[1,4608]{1,0:T(1,128)}) custom-call(bf16[128,768]{1,0:T(8,128)(2,1)} %get-tuple-element.110.refs_0_, bf16[128,768]{1,0:T(8,128)(2,1)} %collective-permute-done.5.refs_1_, f32[128,768]{1,0:T(8,128)} %get-tuple-element.113.refs_2_, ...), custom_call_target="tpu_custom_call" | custom-call | tf_op jit(solution)/shard_map/dheads/pallas_call | solution.py:145
  78.2 4.2 %all-to-all-start.2 = ((bf16[16,64,128]{2,1,0:T(8,128)(2,1)}), bf16[16,64,128]{2,1,0:T(8,128)(2,1)}, u32[]{:S(2)}, u32[]{:S(2)}) async-start(bf16[16,64,128]{2,1,0:T(8,128)(2,1)} %get-tuple-element.117), calls=%async_computation.2 | async-start | bytes 524288 | tf_op jit(solution)/shard_map/all_to_all | solution.py:934
  82.7 1.4 collective-permute-done.13.refs_7_
  84.2 0.8 collective-permute-start.6
  85.0 6.1 %collective-permute-done.11.refs_3_ = bf16[128,1536]{1,0:T(8,128)(2,1)} collective-permute-done((bf16[128,1536]{1,0:T(8,128)(2,1)}, bf16[128,1536]{1,0:T(8,128)(2,1)}, u32[]{:S(2)}, u32[]{:S(2)}) %collective-permute-start.11) | collective-permute-done | bytes 393248 | tf_op jit(solution)/shard_map/ppermute | solution.py:917
  91.1 3.5 %ffn_products.1 = bf16[768,1024]{1,0:T(8,128)(2,1)} custom-call(bf16[128,1536]{1,0:T(8,128)(2,1)} %get-tuple-element.124.refs_0_, bf16[128,1536]{1,0:T(8,128)(2,1)} %collective-permute-done.9.refs_1_, bf16[128,1536]{1,0:T(8,128)(2,1)} %collective-permute-done.10.refs_2_, bf16[128,1536]{1,0:T(8,128)(2,1)} %collective-permute-done.11.refs_3_, ...), custom_call_target="tpu_custom_call" | custom-call | flops 2000000000 | tf_op jit(solution)/shard_map/ffn_products/pallas_call | solution.py:145
  94.6 4.4 %all-to-all-start.3 = ((bf16[16,48,1024]{2,1,0:T(8,128)(2,1)}), bf16[16,48,1024]{2,1,0:T(8,128)(2,1)}, u32[]{:S(2)}, u32[]{:S(2)}) async-start(bf16[16,48,1024]{2,1,0:T(8,128)(2,1)} %bitcast.3), calls=%async_computation.3 | async-start | bytes 3145728 | tf_op jit(solution)/shard_map/all_to_all | solution.py:943
  99.0 13.4 %attend_grad.1 = (bf16[32,64,128]{2,1,0:T(8,128)(2,1)}, bf16[32,64,128]{2,1,0:T(8,128)(2,1)}, bf16[16,32,128]{2,1,0:T(8,128)(2,1)}, bf16[96,128]{1,0:T(8,128)(2,1)}) custom-call(bf16[17,256,128]{2,1,0:T(8,128)(2,1)} %get-tuple-element.103.refs_0_, bf16[1088,128]{1,0:T(8,128)(2,1)} %get-tuple-element.104.refs_1_, f32[1088,128]{1,0:T(8,128)} %get-tuple-element.105.refs_2_, ...), custom_call_target="tpu_custom_call" | custom-call | flops 40000000000 | tf_op jit(solution)/shard_map/attend_grad/pallas_call | solution.py:145
  112.6 1.3 collective-permute-start.8
  113.8 1.0 collective-permute-done.7.refs_1_
  114.8 2.2 %merge.1 = bf16[32,96,128]{2,1,0:T(8,128)(2,1)} custom-call(bf16[32,64,128]{2,1,0:T(8,128)(2,1)} %get-tuple-element.118.refs_0_, bf16[32,64,128]{2,1,0:T(8,128)(2,1)} %collective-permute-done.7.refs_1_, bf16[16,32,128]{2,1,0:T(8,128)(2,1)} %get-tuple-element.122.refs_2_, bf16[96,128]{1,0:T(8,128)(2,1)} %collective-permute-done.8.refs_3_), custom_call_target="tpu_custom_call" | custom-call | flops 2000000000 | tf_op jit(solution)/shard_map/merge/pallas_call | solution.py:145
  117.0 4.1 %all-to-all-done.3.refs_0_ = bf16[16,48,1024]{2,1,0:T(8,128)(2,1)} async-done(((bf16[16,48,1024]{2,1,0:T(8,128)(2,1)}), bf16[16,48,1024]{2,1,0:T(8,128)(2,1)}, u32[]{:S(2)}, u32[]{:S(2)}) %all-to-all-start.3) | async-done | bytes 1572896 | tf_op jit(solution)/shard_map/all_to_all | solution.py:943
  121.2 8.6 %all-to-all-start.4 = ((bf16[32,96,128]{2,1,0:T(8,128)(2,1)}), bf16[32,96,128]{2,1,0:T(8,128)(2,1)}, u32[]{:S(2)}, u32[]{:S(2)}) async-start(bf16[32,96,128]{2,1,0:T(8,128)(2,1)} %merge.1), calls=%async_computation.4 | async-start | bytes 1572864 | tf_op jit(solution)/shard_map/all_to_all | solution.py:955
  129.9 2.4 %ffn_sums.1 = (bf16[16,1152]{1,0:T(8,128)(2,1)}, bf16[16,1152]{1,0:T(8,128)(2,1)}, bf16[16,1152]{1,0:T(8,128)(2,1)}, f32[16,1152]{1,0:T(8,128)}) custom-call(bf16[16,48,1024]{2,1,0:T(8,128)(2,1)} %all-to-all-done.3.refs_0_), custom_call_target="tpu_custom_call" | custom-call | tf_op jit(solution)/shard_map/ffn_sums/pallas_call | solution.py:145
  132.8 2.7 %collective-permute-start.15 = (bf16[16,1152]{1,0:T(8,128)(2,1)}, bf16[16,1152]{1,0:T(8,128)(2,1)}, u32[]{:S(2)}, u32[]{:S(2)}) collective-permute-start(bf16[16,1152]{1,0:T(8,128)(2,1)} %get-tuple-element.133), channel_id=1, source_target_pairs={{0,4},{4,0},{1,5},{5,1},{2,6},{6,2},{3,7},{7,3},{8,12},{12,8},{9,1... | collective-permute-start | bytes 110600 | tf_op jit(solution)/shard_map/ppermute | solution.py:962
  135.5 0.8 collective-permute-start.16
  136.3 1.6 collective-permute-done.15.refs_2_
  137.8 7.0 %collective-permute-done.16.refs_3_ = bf16[16,1152]{1,0:T(8,128)(2,1)} collective-permute-done((bf16[16,1152]{1,0:T(8,128)(2,1)}, bf16[16,1152]{1,0:T(8,128)(2,1)}, u32[]{:S(2)}, u32[]{:S(2)}) %collective-permute-start.16) | collective-permute-done | bytes 36896 | tf_op jit(solution)/shard_map/ppermute | solution.py:963
  144.8 0.9 all-to-all-done.4.refs_0_
  145.8 4.1 %dnormed.1 = (bf16[128,1152]{1,0:T(8,128)(2,1)}, f32[1,1536]{1,0:T(1,128)}, f32[1,2304]{1,0:T(1,128)}, bf16[128,768]{1,0:T(8,128)(2,1)}) custom-call(bf16[32,96,128]{2,1,0:T(8,128)(2,1)} %all-to-all-done.4.refs_0_, bf16[128,768]{1,0:T(8,128)(2,1)} %refs_2_.9, bf16[768,384]{1,0:T(8,128)(2,1)} %refs_2_.8, bf16[768,384]{1,0:T(8,128)(2,1)} %refs_3_.9, ...), custom_call_target="tpu_custom_call" | custom-call | tf_op jit(solution)/shard_map/dnormed/pallas_call | solution.py:145
  150.5 1.6 collective-permute-start.21
  152.2 1.7 collective-permute-done.21.refs_7_
  153.8 1.0 collective-permute-done.20.refs_6_
  154.9 3.5 %qkv_products.1 = bf16[32,128,128]{2,1,0:T(8,128)(2,1)} custom-call(bf16[128,384]{1,0:T(8,128)(2,1)} %get-tuple-element.96.refs_0_, bf16[128,384]{1,0:T(8,128)(2,1)} %collective-permute-done.17.refs_1_, bf16[128,1152]{1,0:T(8,128)(2,1)} %get-tuple-element.138.refs_2_, bf16[128,1152]{1,0:T(8,128)(2,1)} %collective-permute-done.18.refs_3_, ...), custom_call_target="tpu_custom_call" | custom-call | tf_op jit(solution)/shard_map/qkv_products/pallas_call | solution.py:145
  158.4 5.3 %all-to-all-start.5 = ((bf16[32,128,128]{2,1,0:T(8,128)(2,1)}), bf16[32,128,128]{2,1,0:T(8,128)(2,1)}, u32[]{:S(2)}, u32[]{:S(2)}) async-start(bf16[32,128,128]{2,1,0:T(8,128)(2,1)} %qkv_products.1), calls=%async_computation.5 | async-start | bytes 2097152 | tf_op jit(solution)/shard_map/all_to_all | solution.py:994
  163.8 2.9 %output.1 = bf16[128,768]{1,0:T(8,128)(2,1)} custom-call(bf16[128,768]{1,0:T(8,128)(2,1)} %ffn.1.refs_0_, bf16[128,768]{1,0:T(8,128)(2,1)} %collective-permute-done.6.refs_1_, f32[128,768]{1,0:T(8,128)} %get-tuple-element.113.refs_2_, bf16[128,768]{1,0:T(8,128)(2,1)} %refs_2_.9, s32[128]{0:T(128)} %refs_4_.11, f32[768]{0:T(1024)} %refs_5_.8), custom_call_target="tpu_custom_call" | custom-call | tf_op jit(solution)/shard_map/output/pallas_call | solution.py:145
  166.7 1.7 ffn_finish.1
  168.5 12.5 %collective-permute-done.22.refs_1_ = bf16[128,768]{1,0:T(8,128)(2,1)} collective-permute-done((bf16[128,768]{1,0:T(8,128)(2,1)}, bf16[128,768]{1,0:T(8,128)(2,1)}, u32[]{:S(2)}, u32[]{:S(2)}) %collective-permute-start.22) | collective-permute-done | bytes 196640 | tf_op jit(solution)/shard_map/ppermute | solution.py:984
  181.0 3.4 %input_grad.1 = f32[128,768]{1,0:T(8,128)} custom-call(bf16[128,768]{1,0:T(8,128)(2,1)} %get-tuple-element.145.refs_0_, bf16[128,768]{1,0:T(8,128)(2,1)} %collective-permute-done.22.refs_1_, bf16[128,768]{1,0:T(8,128)(2,1)} %refs_2_.9, bf16[128,768]{1,0:T(8,128)(2,1)} %refs_3_.11, s32[128]{0:T(128)} %refs_4_.11, f32[768]{0:T(1024)} %refs_5_.9, ...), custom_call_target="tpu_custom_call" | custom-call | tf_op jit(solution)/shard_map/input_grad/pallas_call | solution.py:145
  184.5 2.1 %finish.1 = (f32[12,384]{1,0:T(8,128)}, f32[12,384]{1,0:T(8,128)}, f32[12,384]{1,0:T(8,128)}, f32[768]{0:T(1024)}, f32[768]{0:T(1024)}, /*index=5*/f32[384]{0:T(512)}, f32[384]{0:T(512)}) custom-call(bf16[32,128,128]{2,1,0:T(8,128)(2,1)} %all-to-all-done.5.refs_0_), custom_call_target="tpu_custom_call" | custom-call | flops 2000000000 | tf_op jit(solution)/shard_map/finish/pallas_call | solution.py:145
  (35 shorter events, 4.9 us)
Async XLA Ops:
  3.7 18.0 %collective-permute-start = (bf16[384,768]{1,0:T(8,128)(2,1)}, bf16[384,768]{1,0:T(8,128)(2,1)}, u32[]{:S(2)}, u32[]{:S(2)}) collective-permute-start(bf16[384,768]{1,0:T(8,128)(2,1)} %refs_9_.1), channel_id=1, source_target_pairs={{0,1},{1,0},{2,3},{3,2},{4,5},{5,4},{6,7},{7,6},{8,9},{9,8},{10,11... | collective-permute-start | bytes 1769480 | tf_op jit(solution)/shard_map/ppermute | solution.py:873
  6.2 15.5 %all-to-all-start = ((bf16[16,112,128]{2,1,0:T(8,128)(2,1)}), bf16[16,112,128]{2,1,0:T(8,128)(2,1)}, u32[]{:S(2)}, u32[]{:S(2)}) async-start(bf16[16,112,128]{2,1,0:T(8,128)(2,1)} %get-tuple-element.97), calls=%async_computation | async-start | bytes 917504 | tf_op jit(solution)/shard_map/all_to_all | solution.py:871
  22.7 8.3 %collective-permute-start.2 = (bf16[16,64,128]{2,1,0:T(8,128)(2,1)S(1)}, bf16[16,64,128]{2,1,0:T(8,128)(2,1)S(1)}, u32[]{:S(2)}, u32[]{:S(2)}) collective-permute-start(bf16[16,64,128]{2,1,0:T(8,128)(2,1)S(1)} %slice.6), channel_id=1, source_target_pairs={{0,4},{4,0},{1,5},{5,1},{2,6},{6,2},{3,7},{7,3},{8,12},{12,8},{9,1... | collective-permute-start | bytes 786440 | tf_op jit(solution)/shard_map/ppermute | solution.py:883
  26.8 4.2 %collective-permute-start.3 = (bf16[112,128]{1,0:T(8,128)(2,1)S(1)}, bf16[112,128]{1,0:T(8,128)(2,1)S(1)}, u32[]{:S(2)}, u32[]{:S(2)}) collective-permute-start(bf16[112,128]{1,0:T(8,128)(2,1)S(1)} %slice_bitcast_fusion), channel_id=1, source_target_pairs={{14,6},{30,22},{15,7},{31,23},{46,38},{62,54},{47,39},{63,55},{78,... | collective-permute-start | bytes 86024 | tf_op jit(solution)/shard_map/ppermute | solution.py:882
  27.5 6.4 %collective-permute-start.1 = (bf16[16,64,128]{2,1,0:T(8,128)(2,1)S(1)}, bf16[16,64,128]{2,1,0:T(8,128)(2,1)S(1)}, u32[]{:S(2)}, u32[]{:S(2)}) collective-permute-start(bf16[16,64,128]{2,1,0:T(8,128)(2,1)S(1)} %slice.6), channel_id=1, source_target_pairs={{0,2},{2,0},{1,3},{3,1},{4,6},{6,4},{5,7},{7,5},{8,10},{10,8},{9,1... | collective-permute-start | bytes 786440 | tf_op jit(solution)/shard_map/ppermute | solution.py:881
  31.0 2.9 %copy-start.2 = (bf16[112,128]{1,0:T(8,128)(2,1)}, bf16[112,128]{1,0:T(8,128)(2,1)S(1)}, u32[]{:S(2)}) copy-start(bf16[112,128]{1,0:T(8,128)(2,1)S(1)} %collective-permute-done.3.refs_4_) | copy-start | bytes 86020
  31.0 2.9 %copy-start = (bf16[16,64,128]{2,1,0:T(8,128)(2,1)}, bf16[16,64,128]{2,1,0:T(8,128)(2,1)S(1)}, u32[]{:S(2)}) copy-start(bf16[16,64,128]{2,1,0:T(8,128)(2,1)S(1)} %collective-permute-done.2.refs_2_) | copy-start | bytes 786436
  31.0 4.1 %collective-permute-start.4 = (bf16[16,64,128]{2,1,0:T(8,128)(2,1)S(1)}, bf16[16,64,128]{2,1,0:T(8,128)(2,1)}, u32[]{:S(2)}, u32[]{:S(2)}) collective-permute-start(bf16[16,64,128]{2,1,0:T(8,128)(2,1)S(1)} %collective-permute-done.2.refs_2_), channel_id=1, source_target_pairs={{0,2},{2,0},{1,3},{3,1},{4,6},{6,4},{5,7},{7,5},{8,10},{10,8},{9,1... | collective-permute-start | bytes 786440 | tf_op jit(solution)/shard_map/ppermute | solution.py:885
  33.8 0.7 copy-start.1
  41.1 16.0 %all-to-all-start.1 = ((bf16[32,64,128]{2,1,0:T(8,128)(2,1)}), bf16[32,64,128]{2,1,0:T(8,128)(2,1)}, u32[]{:S(2)}, u32[]{:S(2)}) async-start(bf16[32,64,128]{2,1,0:T(8,128)(2,1)} %get-tuple-element.107), calls=%async_computation.1 | async-start | bytes 1048576 | tf_op jit(solution)/shard_map/all_to_all | solution.py:893
  64.0 9.1 %collective-permute-start.5 = (bf16[128,768]{1,0:T(8,128)(2,1)}, bf16[128,768]{1,0:T(8,128)(2,1)}, u32[]{:S(2)}, u32[]{:S(2)}) collective-permute-start(bf16[128,768]{1,0:T(8,128)(2,1)} %get-tuple-element.110.refs_0_), channel_id=1, source_target_pairs={{0,1},{1,0},{2,3},{3,2},{4,5},{5,4},{6,7},{7,6},{8,9},{9,8},{10,11... | collective-permute-start | bytes 589832 | tf_op jit(solution)/shard_map/ppermute | solution.py:915
  64.6 20.4 %collective-permute-start.9 = (bf16[128,1536]{1,0:T(8,128)(2,1)}, bf16[128,1536]{1,0:T(8,128)(2,1)}, u32[]{:S(2)}, u32[]{:S(2)}) collective-permute-start(bf16[128,1536]{1,0:T(8,128)(2,1)} %get-tuple-element.125), channel_id=1, source_target_pairs={{0,2},{2,0},{1,3},{3,1},{4,6},{6,4},{5,7},{7,5},{8,10},{10,8},{9,1... | collective-permute-start | bytes 1179656 | tf_op jit(solution)/shard_map/ppermute | solution.py:918
  66.8 18.2 %collective-permute-start.10 = (bf16[128,1536]{1,0:T(8,128)(2,1)}, bf16[128,1536]{1,0:T(8,128)(2,1)}, u32[]{:S(2)}, u32[]{:S(2)}) collective-permute-start(bf16[128,1536]{1,0:T(8,128)(2,1)} %get-tuple-element.126), channel_id=1, source_target_pairs={{0,4},{4,0},{1,5},{5,1},{2,6},{6,2},{3,7},{7,3},{8,12},{12,8},{9,1... | collective-permute-start | bytes 1179656 | tf_op jit(solution)/shard_map/ppermute | solution.py:916
  70.1 21.0 %collective-permute-start.11 = (bf16[128,1536]{1,0:T(8,128)(2,1)}, bf16[128,1536]{1,0:T(8,128)(2,1)}, u32[]{:S(2)}, u32[]{:S(2)}) collective-permute-start(bf16[128,1536]{1,0:T(8,128)(2,1)} %get-tuple-element.127), channel_id=1, source_target_pairs={{0,6},{2,4},{4,2},{6,0},{1,7},{3,5},{5,3},{7,1},{8,14},{10,12},{12... | collective-permute-start | bytes 1179656 | tf_op jit(solution)/shard_map/ppermute | solution.py:917
  77.7 13.4 %collective-permute-start.12 = (bf16[128,1152]{1,0:T(8,128)(2,1)}, bf16[128,1152]{1,0:T(8,128)(2,1)}, u32[]{:S(2)}, u32[]{:S(2)}) collective-permute-start(bf16[128,1152]{1,0:T(8,128)(2,1)} %get-tuple-element.128.refs_4_), channel_id=1, source_target_pairs={{0,2},{2,0},{1,3},{3,1},{4,6},{6,4},{5,7},{7,5},{8,10},{10,8},{9,1... | collective-permute-start | bytes 884744 | tf_op jit(solution)/shard_map/ppermute | solution.py:935
  78.2 16.4 %all-to-all-start.2 = ((bf16[16,64,128]{2,1,0:T(8,128)(2,1)}), bf16[16,64,128]{2,1,0:T(8,128)(2,1)}, u32[]{:S(2)}, u32[]{:S(2)}) async-start(bf16[16,64,128]{2,1,0:T(8,128)(2,1)} %get-tuple-element.117), calls=%async_computation.2 | async-start | bytes 524288 | tf_op jit(solution)/shard_map/all_to_all | solution.py:934
  82.4 1.8 collective-permute-start.13
  84.2 28.3 %collective-permute-start.6 = (bf16[128,768]{1,0:T(8,128)(2,1)}, bf16[128,768]{1,0:T(8,128)(2,1)}, u32[]{:S(2)}, u32[]{:S(2)}) collective-permute-start(bf16[128,768]{1,0:T(8,128)(2,1)} %ffn.1.refs_0_), channel_id=1, source_target_pairs={{0,1},{1,0},{2,3},{3,2},{4,5},{5,4},{6,7},{7,6},{8,9},{9,8},{10,11... | collective-permute-start | bytes 589832 | tf_op jit(solution)/shard_map/ppermute | solution.py:944
  94.6 26.6 %all-to-all-start.3 = ((bf16[16,48,1024]{2,1,0:T(8,128)(2,1)}), bf16[16,48,1024]{2,1,0:T(8,128)(2,1)}, u32[]{:S(2)}, u32[]{:S(2)}) async-start(bf16[16,48,1024]{2,1,0:T(8,128)(2,1)} %bitcast.3), calls=%async_computation.3 | async-start | bytes 3145728 | tf_op jit(solution)/shard_map/all_to_all | solution.py:943
  112.5 2.3 %collective-permute-start.7 = (bf16[32,64,128]{2,1,0:T(8,128)(2,1)}, bf16[32,64,128]{2,1,0:T(8,128)(2,1)}, u32[]{:S(2)}, u32[]{:S(2)}) collective-permute-start(bf16[32,64,128]{2,1,0:T(8,128)(2,1)} %get-tuple-element.121), channel_id=1, source_target_pairs={{0,2},{2,0},{1,3},{3,1},{4,6},{6,4},{5,7},{7,5},{8,10},{10,8},{9,1... | collective-permute-start | bytes 1572872 | tf_op jit(solution)/shard_map/ppermute | solution.py:948
  112.6 1.3 collective-permute-start.8
  121.2 24.6 %all-to-all-start.4 = ((bf16[32,96,128]{2,1,0:T(8,128)(2,1)}), bf16[32,96,128]{2,1,0:T(8,128)(2,1)}, u32[]{:S(2)}, u32[]{:S(2)}) async-start(bf16[32,96,128]{2,1,0:T(8,128)(2,1)} %merge.1), calls=%async_computation.4 | async-start | bytes 1572864 | tf_op jit(solution)/shard_map/all_to_all | solution.py:955
  129.8 6.5 %collective-permute-start.17 = (bf16[128,384]{1,0:T(8,128)(2,1)}, bf16[128,384]{1,0:T(8,128)(2,1)}, u32[]{:S(2)}, u32[]{:S(2)}) collective-permute-start(bf16[128,384]{1,0:T(8,128)(2,1)} %get-tuple-element.135), channel_id=1, source_target_pairs={{0,2},{2,0},{1,3},{3,1},{4,6},{6,4},{5,7},{7,5},{8,10},{10,8},{9,1... | collective-permute-start | bytes 294920 | tf_op jit(solution)/shard_map/ppermute | solution.py:886
  132.2 4.0 %collective-permute-start.14 = (bf16[16,1152]{1,0:T(8,128)(2,1)}, bf16[16,1152]{1,0:T(8,128)(2,1)}, u32[]{:S(2)}, u32[]{:S(2)}) collective-permute-start(bf16[16,1152]{1,0:T(8,128)(2,1)} %get-tuple-element.132), channel_id=1, source_target_pairs={{0,2},{2,0},{1,3},{3,1},{4,6},{6,4},{5,7},{7,5},{8,10},{10,8},{9,1... | collective-permute-start | bytes 110600 | tf_op jit(solution)/shard_map/ppermute | solution.py:961
  132.8 5.0 %collective-permute-start.15 = (bf16[16,1152]{1,0:T(8,128)(2,1)}, bf16[16,1152]{1,0:T(8,128)(2,1)}, u32[]{:S(2)}, u32[]{:S(2)}) collective-permute-start(bf16[16,1152]{1,0:T(8,128)(2,1)} %get-tuple-element.133), channel_id=1, source_target_pairs={{0,4},{4,0},{1,5},{5,1},{2,6},{6,2},{3,7},{7,3},{8,12},{12,8},{9,1... | collective-permute-start | bytes 110600 | tf_op jit(solution)/shard_map/ppermute | solution.py:962
  135.5 9.4 %collective-permute-start.16 = (bf16[16,1152]{1,0:T(8,128)(2,1)}, bf16[16,1152]{1,0:T(8,128)(2,1)}, u32[]{:S(2)}, u32[]{:S(2)}) collective-permute-start(bf16[16,1152]{1,0:T(8,128)(2,1)} %get-tuple-element.134), channel_id=1, source_target_pairs={{0,6},{2,4},{4,2},{6,0},{1,7},{3,5},{5,3},{7,1},{8,14},{10,12},{12... | collective-permute-start | bytes 110600 | tf_op jit(solution)/shard_map/ppermute | solution.py:963
  149.9 5.0 %collective-permute-start.18 = (bf16[128,1152]{1,0:T(8,128)(2,1)}, bf16[128,1152]{1,0:T(8,128)(2,1)}, u32[]{:S(2)}, u32[]{:S(2)}) collective-permute-start(bf16[128,1152]{1,0:T(8,128)(2,1)} %get-tuple-element.138.refs_2_), channel_id=1, source_target_pairs={{0,2},{2,0},{1,3},{3,1},{4,6},{6,4},{5,7},{7,5},{8,10},{10,8},{9,1... | collective-permute-start | bytes 884744 | tf_op jit(solution)/shard_map/ppermute | solution.py:979
  150.3 4.5 %collective-permute-start.19 = (f32[1,2304]{1,0:T(1,128)}, f32[1,2304]{1,0:T(1,128)}, u32[]{:S(2)}, u32[]{:S(2)}) collective-permute-start(f32[1,2304]{1,0:T(1,128)} %get-tuple-element.139.refs_4_), channel_id=1, source_target_pairs={{0,2},{2,0},{1,3},{3,1},{4,6},{6,4},{5,7},{7,5},{8,10},{10,8},{9,1... | collective-permute-start | bytes 27656 | tf_op jit(solution)/shard_map/ppermute | solution.py:980
  150.5 3.4 %collective-permute-start.21 = (f32[1,1536]{1,0:T(1,128)}, f32[1,1536]{1,0:T(1,128)}, u32[]{:S(2)}, u32[]{:S(2)}) collective-permute-start(f32[1,1536]{1,0:T(1,128)} %get-tuple-element.140), channel_id=1, source_target_pairs={{0,3},{1,2},{2,1},{3,0},{4,7},{5,6},{6,5},{7,4},{8,11},{9,10},{10,... | collective-permute-start | bytes 18440 | tf_op jit(solution)/shard_map/ppermute | solution.py:982
  152.1 2.8 %collective-permute-start.20 = (f32[1,1536]{1,0:T(1,128)}, f32[1,1536]{1,0:T(1,128)}, u32[]{:S(2)}, u32[]{:S(2)}) collective-permute-start(f32[1,1536]{1,0:T(1,128)} %get-tuple-element.140), channel_id=1, source_target_pairs={{0,1},{1,0},{2,3},{3,2},{4,5},{5,4},{6,7},{7,6},{8,9},{9,8},{10,11... | collective-permute-start | bytes 18440 | tf_op jit(solution)/shard_map/ppermute | solution.py:981
  158.4 26.1 %all-to-all-start.5 = ((bf16[32,128,128]{2,1,0:T(8,128)(2,1)}), bf16[32,128,128]{2,1,0:T(8,128)(2,1)}, u32[]{:S(2)}, u32[]{:S(2)}) async-start(bf16[32,128,128]{2,1,0:T(8,128)(2,1)} %qkv_products.1), calls=%async_computation.5 | async-start | bytes 2097152 | tf_op jit(solution)/shard_map/all_to_all | solution.py:994
  163.7 17.3 %collective-permute-start.22 = (bf16[128,768]{1,0:T(8,128)(2,1)}, bf16[128,768]{1,0:T(8,128)(2,1)}, u32[]{:S(2)}, u32[]{:S(2)}) collective-permute-start(bf16[128,768]{1,0:T(8,128)(2,1)} %get-tuple-element.145.refs_0_), channel_id=1, source_target_pairs={{0,1},{1,0},{2,3},{3,2},{4,5},{5,4},{6,7},{7,6},{8,9},{9,8},{10,11... | collective-permute-start | bytes 589832 | tf_op jit(solution)/shard_map/ppermute | solution.py:984

commit v6 on v5

--- a/solution.py
+++ b/solution.py
@@ -596,11 +596,6 @@
     dmid_ref[...] = dmiddle
     flush(dmid_ref)
     low = dmiddle.astype(jnp.bfloat16)
-    vec_ref[:, :1536] = up_ref[...]
-    vec_ref[:, 1536:2304] = down_ref[...]
-    vec_ref[:, 2304:3072] = jnp.sum(dnormed * unit, axis=0, keepdims=True)
-    vec_ref[:, 3072:3840] = jnp.sum(dnormed, axis=0, keepdims=True)
-    vec_ref[:, 3840:] = jnp.sum(low.astype(jnp.float32), axis=0, keepdims=True)
     pay_ref[12:] = jnp.zeros((4, HALF, 128), jnp.bfloat16)
     flush(pay_ref, 12, 16)
     wait(o_ref)
@@ -617,6 +612,11 @@
             pay_ref[index + 1, :32] = higher
             pay_ref[index + 1, 32:] = higher
         flush(pay_ref, 4 * pair, 4 * pair + 4)
+    vec_ref[:, :1536] = up_ref[...]
+    vec_ref[:, 1536:2304] = down_ref[...]
+    vec_ref[:, 2304:3072] = jnp.sum(dnormed * unit, axis=0, keepdims=True)
+    vec_ref[:, 3072:3840] = jnp.sum(dnormed, axis=0, keepdims=True)
+    vec_ref[:, 3840:] = jnp.sum(low.astype(jnp.float32), axis=0, keepdims=True)
     both_ref[:, :768] = low
     both_ref[:, 768:] = attn_ref[...]
 
@@ -750,19 +750,19 @@
     vec_ref, vec_sent_ref, wa_ref, cross_ref, out_ref,
     product_ref,
 ):
-    lefts = jnp.concatenate([keep_ref[...], sent_ref[...]], axis=0)
-    for at in range(0, 1152, 384):
-        columns = slice(at, at + 384)
-        rights = jnp.concatenate([grads_ref[:, columns], grads_sent_ref[:, columns]], axis=0)
-        product_ref[:, columns] = lax.dot_general(
-            lefts, rights, trans_left, preferred_element_type=jnp.float32
-        )
     vec = vec_ref[...] + vec_sent_ref[...]
     norms = vec[:, :1536] + (wa_ref[...] + cross_ref[...])
     vec = jnp.concatenate([norms, vec[:, 1536:]], axis=1)
     lines = [vec[:, 128 * row : 128 * (row + 1)] for row in range(18)]
     lines = jnp.concatenate(lines + [jnp.zeros((2, 128), jnp.float32)], axis=0)
+    rights = jnp.concatenate([grads_ref[...], grads_sent_ref[...]], axis=0)
     for pair in range(16):
+        if pair % 8 == 0:
+            features = slice(24 * pair, 24 * pair + 192)
+            lefts = jnp.concatenate([keep_ref[:, features], sent_ref[:, features]], axis=0)
+            product_ref[features] = lax.dot_general(
+                lefts, rights, trans_left, preferred_element_type=jnp.float32
+            )
         block = product_ref[24 * pair : 24 * pair + 24]
         for half in range(2):
             rows = slice(12 * half, 12 * half + 12)

time: 188 us -> 188 us (level)
  no operation moved by 1% of the time
where the time goes in v6:
time: 188 us; the launch traced here: 187 us
  Pallas kernels  69 us (37%)
  starting transfers between devices  62.8 us (33%)
  waiting for transfers between devices  51.3 us (27%)
  local copies, waits for them, and re-layouts  2.43 us (1%)
    pallas_call x17, Pallas kernels, call(): pl.pallas_call(body, out_shape=tuple((out for _, out in outs)), in_specs=...  69 us
    ppermute x2, waiting for transfers between devices, on_device(): ffn_cross = lax.ppermute(ffn_cross, ('zh', 'core'), CROSS)  13.4 us
    ppermute x1, waiting for transfers between devices, on_device(): dn_one_other = lax.ppermute(dn_one, 'wa', SWAP)  12.5 us
    all_to_all x1, starting transfers between devices, on_device(): grads = lax.all_to_all(merged, CHIPS, 0, 0, tiled=True)  8.58 us
    all_to_all x1, waiting for transfers between devices, on_device(): got = lax.all_to_all(back, ('x', 'y', 'wa'), 0, 0, tiled=True)  7.2 us
    all_to_all x1, starting transfers between devices, on_device(): own = lax.all_to_all(payload, PLANE, 0, 0, tiled=True)  6.8 us
    all_to_all x1, waiting for transfers between devices, on_device(): own = lax.all_to_all(payload, PLANE, 0, 0, tiled=True)  6.04 us
    ppermute x2, starting transfers between devices, on_device(): ffn_high = lax.ppermute(ffn_high, 'zh', SWAP)  5.97 us
  transfers between devices with their start and end apart: 29, of which 13 were waited for; matrix products, arithmetic and copies ran while one was open for 0% of the time, Pallas kernels for 23%

profile of v6, /device:TPU:1, one launch (start us, length us, event | category | flops | bytes accessed | tf_op | source)
XLA Modules:
  0.0 186.6 jit_solution(1663301850908685456)
XLA Ops:
  0.7 3.0 %project.1 = (bf16[16,112,128]{2,1,0:T(8,128)(2,1)}, bf16[128,768]{1,0:T(8,128)(2,1)}) custom-call(bf16[128,768]{1,0:T(8,128)(2,1)} %refs_2_.9, s32[128]{0:T(128)} %refs_1_.5, f32[768]{0:T(1024)} %refs_5_.9, f32[768]{0:T(1024)} %refs_3_.6, f32[384]{0:T(512)} %refs_4_.6, f32[384]{0:T(512)} %refs_5_.5, bf16[768,384]{1,0:T(8,128)(2,1)} %refs_2_.8, ...), custom_call_target="tpu_custom_call" | custom-call | flops 2000000000 | tf_op jit(solution)/shard_map/project/pallas_call | solution.py:145
  3.7 2.5 %collective-permute-start = (bf16[384,768]{1,0:T(8,128)(2,1)}, bf16[384,768]{1,0:T(8,128)(2,1)}, u32[]{:S(2)}, u32[]{:S(2)}) collective-permute-start(bf16[384,768]{1,0:T(8,128)(2,1)} %refs_9_.1), channel_id=1, source_target_pairs={{0,1},{1,0},{2,3},{3,2},{4,5},{5,4},{6,7},{7,6},{8,9},{9,8},{10,11... | collective-permute-start | bytes 1769480 | tf_op jit(solution)/shard_map/ppermute | solution.py:873
  6.2 6.8 %all-to-all-start = ((bf16[16,112,128]{2,1,0:T(8,128)(2,1)}), bf16[16,112,128]{2,1,0:T(8,128)(2,1)}, u32[]{:S(2)}, u32[]{:S(2)}) async-start(bf16[16,112,128]{2,1,0:T(8,128)(2,1)} %get-tuple-element.97), calls=%async_computation | async-start | bytes 917504 | tf_op jit(solution)/shard_map/all_to_all | solution.py:871
  13.0 2.6 %prepare.1 = (bf16[128,384]{1,0:T(8,128)(2,1)}, bf16[128,384]{1,0:T(8,128)(2,1)}) custom-call(bf16[128,768]{1,0:T(8,128)(2,1)} %get-tuple-element.95.refs_0_), custom_call_target="tpu_custom_call" | custom-call | flops 2000000000 | tf_op jit(solution)/shard_map/prepare/pallas_call | solution.py:145
  15.6 6.0 %all-to-all-done.refs_0_ = bf16[16,112,128]{2,1,0:T(8,128)(2,1)} async-done(((bf16[16,112,128]{2,1,0:T(8,128)(2,1)}), bf16[16,112,128]{2,1,0:T(8,128)(2,1)}, u32[]{:S(2)}, u32[]{:S(2)}) %all-to-all-start) | async-done | bytes 458784 | tf_op jit(solution)/shard_map/all_to_all | solution.py:871
  21.7 1.0 slice.6
  22.7 3.4 %collective-permute-start.2 = (bf16[16,64,128]{2,1,0:T(8,128)(2,1)S(1)}, bf16[16,64,128]{2,1,0:T(8,128)(2,1)S(1)}, u32[]{:S(2)}, u32[]{:S(2)}) collective-permute-start(bf16[16,64,128]{2,1,0:T(8,128)(2,1)S(1)} %slice.6), channel_id=1, source_target_pairs={{0,4},{4,0},{1,5},{5,1},{2,6},{6,2},{3,7},{7,3},{8,12},{12,8},{9,1... | collective-permute-start | bytes 786440 | tf_op jit(solution)/shard_map/ppermute | solution.py:883
  26.0 0.8 slice_bitcast_fusion
  27.5 3.5 %collective-permute-start.1 = (bf16[16,64,128]{2,1,0:T(8,128)(2,1)S(1)}, bf16[16,64,128]{2,1,0:T(8,128)(2,1)S(1)}, u32[]{:S(2)}, u32[]{:S(2)}) collective-permute-start(bf16[16,64,128]{2,1,0:T(8,128)(2,1)S(1)} %slice.6), channel_id=1, source_target_pairs={{0,2},{2,0},{1,3},{3,1},{4,6},{6,4},{5,7},{7,5},{8,10},{10,8},{9,1... | collective-permute-start | bytes 786440 | tf_op jit(solution)/shard_map/ppermute | solution.py:881
  31.0 2.8 %collective-permute-start.4 = (bf16[16,64,128]{2,1,0:T(8,128)(2,1)S(1)}, bf16[16,64,128]{2,1,0:T(8,128)(2,1)}, u32[]{:S(2)}, u32[]{:S(2)}) collective-permute-start(bf16[16,64,128]{2,1,0:T(8,128)(2,1)S(1)} %collective-permute-done.2.refs_2_), channel_id=1, source_target_pairs={{0,2},{2,0},{1,3},{3,1},{4,6},{6,4},{5,7},{7,5},{8,10},{10,8},{9,1... | collective-permute-start | bytes 786440 | tf_op jit(solution)/shard_map/ppermute | solution.py:885
  35.1 6.0 %attend.1 = (bf16[32,64,128]{2,1,0:T(8,128)(2,1)}, bf16[17,256,128]{2,1,0:T(8,128)(2,1)}, bf16[1088,128]{1,0:T(8,128)(2,1)}, f32[1088,128]{1,0:T(8,128)}, f32[1088,128]{1,0:T(8,128)}) custom-call(bf16[16,112,128]{2,1,0:T(8,128)(2,1)} %all-to-all-done.refs_0_, bf16[16,64,128]{2,1,0:T(8,128)(2,1)} %copy-done.1, bf16[16,64,128]{2,1,0:T(8,128)(2,1)} %copy-done, ...), custom_call_target="tpu_custom_call" | custom-call | flops 3000000000 | tf_op jit(solution)/shard_map/attend/pallas_call | solution.py:145
  41.1 5.1 %all-to-all-start.1 = ((bf16[32,64,128]{2,1,0:T(8,128)(2,1)}), bf16[32,64,128]{2,1,0:T(8,128)(2,1)}, u32[]{:S(2)}, u32[]{:S(2)}) async-start(bf16[32,64,128]{2,1,0:T(8,128)(2,1)} %get-tuple-element.107), calls=%async_computation.1 | async-start | bytes 1048576 | tf_op jit(solution)/shard_map/all_to_all | solution.py:893
  46.2 3.7 %dhidden.1 = (f32[128,1536]{1,0:T(8,128)}, f32[1,768]{1,0:T(1,128)}) custom-call(bf16[128,768]{1,0:T(8,128)(2,1)} %refs_3_.11, s32[128]{0:T(128)} %refs_4_.11, bf16[1536,768]{1,0:T(8,128)(2,1)} %refs_1_.8), custom_call_target="tpu_custom_call" | custom-call | flops 2000000000 | tf_op jit(solution)/shard_map/dhidden/pallas_call | solution.py:145
  50.0 7.2 %all-to-all-done.1.refs_0_ = bf16[32,64,128]{2,1,0:T(8,128)(2,1)} async-done(((bf16[32,64,128]{2,1,0:T(8,128)(2,1)}), bf16[32,64,128]{2,1,0:T(8,128)(2,1)}, u32[]{:S(2)}, u32[]{:S(2)}) %all-to-all-start.1) | async-done | bytes 524320 | tf_op jit(solution)/shard_map/all_to_all | solution.py:893
  57.2 6.9 %middle.1 = (bf16[128,768]{1,0:T(8,128)(2,1)}, bf16[128,1536]{1,0:T(8,128)(2,1)}, bf16[128,1536]{1,0:T(8,128)(2,1)}, bf16[128,1536]{1,0:T(8,128)(2,1)}, bf16[128...) custom-call(bf16[32,64,128]{2,1,0:T(8,128)(2,1)} %all-to-all-done.1., ...), custom_call_target="tpu_custom_call" | custom-call | flops 2000000000 | tf_op jit(solution)/shard_map/middle/pallas_call | solution.py:145
  64.6 2.2 %collective-permute-start.9 = (bf16[128,1536]{1,0:T(8,128)(2,1)}, bf16[128,1536]{1,0:T(8,128)(2,1)}, u32[]{:S(2)}, u32[]{:S(2)}) collective-permute-start(bf16[128,1536]{1,0:T(8,128)(2,1)} %get-tuple-element.125), channel_id=1, source_target_pairs={{0,2},{2,0},{1,3},{3,1},{4,6},{6,4},{5,7},{7,5},{8,10},{10,8},{9,1... | collective-permute-start | bytes 1179656 | tf_op jit(solution)/shard_map/ppermute | solution.py:918
  66.8 3.3 %collective-permute-start.10 = (bf16[128,1536]{1,0:T(8,128)(2,1)}, bf16[128,1536]{1,0:T(8,128)(2,1)}, u32[]{:S(2)}, u32[]{:S(2)}) collective-permute-start(bf16[128,1536]{1,0:T(8,128)(2,1)} %get-tuple-element.126), channel_id=1, source_target_pairs={{0,4},{4,0},{1,5},{5,1},{2,6},{6,2},{3,7},{7,3},{8,12},{12,8},{9,1... | collective-permute-start | bytes 1179656 | tf_op jit(solution)/shard_map/ppermute | solution.py:916
  70.1 3.0 %ffn.1.refs_0_ = bf16[128,768]{1,0:T(8,128)(2,1)} custom-call(bf16[128,1536]{1,0:T(8,128)(2,1)} %get-tuple-element.111.refs_0_, bf16[1536,768]{1,0:T(8,128)(2,1)} %refs_1_.8), custom_call_target="tpu_custom_call" | custom-call | tf_op jit(solution)/shard_map/ffn/pallas_call | solution.py:145
  73.1 4.5 %dheads.1 = (bf16[16,64,128]{2,1,0:T(8,128)(2,1)}, bf16[128,1152]{1,0:T(8,128)(2,1)}, f32[128,768]{1,0:T(8,128)}, f32[1,4608]{1,0:T(1,128)}) custom-call(bf16[128,768]{1,0:T(8,128)(2,1)} %get-tuple-element.110.refs_0_, bf16[128,768]{1,0:T(8,128)(2,1)} %collective-permute-done.5.refs_1_, f32[128,768]{1,0:T(8,128)} %get-tuple-element.113.refs_2_, ...), custom_call_target="tpu_custom_call" | custom-call | tf_op jit(solution)/shard_map/dheads/pallas_call | solution.py:145
  78.1 4.2 %all-to-all-start.2 = ((bf16[16,64,128]{2,1,0:T(8,128)(2,1)}), bf16[16,64,128]{2,1,0:T(8,128)(2,1)}, u32[]{:S(2)}, u32[]{:S(2)}) async-start(bf16[16,64,128]{2,1,0:T(8,128)(2,1)} %get-tuple-element.117), calls=%async_computation.2 | async-start | bytes 524288 | tf_op jit(solution)/shard_map/all_to_all | solution.py:934
  82.7 1.4 collective-permute-done.13.refs_7_
  84.1 0.8 collective-permute-start.6
  84.9 6.2 %collective-permute-done.11.refs_3_ = bf16[128,1536]{1,0:T(8,128)(2,1)} collective-permute-done((bf16[128,1536]{1,0:T(8,128)(2,1)}, bf16[128,1536]{1,0:T(8,128)(2,1)}, u32[]{:S(2)}, u32[]{:S(2)}) %collective-permute-start.11) | collective-permute-done | bytes 393248 | tf_op jit(solution)/shard_map/ppermute | solution.py:917
  91.1 3.5 %ffn_products.1 = bf16[768,1024]{1,0:T(8,128)(2,1)} custom-call(bf16[128,1536]{1,0:T(8,128)(2,1)} %get-tuple-element.124.refs_0_, bf16[128,1536]{1,0:T(8,128)(2,1)} %collective-permute-done.9.refs_1_, bf16[128,1536]{1,0:T(8,128)(2,1)} %collective-permute-done.10.refs_2_, bf16[128,1536]{1,0:T(8,128)(2,1)} %collective-permute-done.11.refs_3_, ...), custom_call_target="tpu_custom_call" | custom-call | flops 2000000000 | tf_op jit(solution)/shard_map/ffn_products/pallas_call | solution.py:145
  94.6 4.4 %all-to-all-start.3 = ((bf16[16,48,1024]{2,1,0:T(8,128)(2,1)}), bf16[16,48,1024]{2,1,0:T(8,128)(2,1)}, u32[]{:S(2)}, u32[]{:S(2)}) async-start(bf16[16,48,1024]{2,1,0:T(8,128)(2,1)} %bitcast.3), calls=%async_computation.3 | async-start | bytes 3145728 | tf_op jit(solution)/shard_map/all_to_all | solution.py:943
  99.1 13.4 %attend_grad.1 = (bf16[32,64,128]{2,1,0:T(8,128)(2,1)}, bf16[32,64,128]{2,1,0:T(8,128)(2,1)}, bf16[16,32,128]{2,1,0:T(8,128)(2,1)}, bf16[96,128]{1,0:T(8,128)(2,1)}) custom-call(bf16[17,256,128]{2,1,0:T(8,128)(2,1)} %get-tuple-element.103.refs_0_, bf16[1088,128]{1,0:T(8,128)(2,1)} %get-tuple-element.104.refs_1_, f32[1088,128]{1,0:T(8,128)} %get-tuple-element.105.refs_2_, ...), custom_call_target="tpu_custom_call" | custom-call | flops 40000000000 | tf_op jit(solution)/shard_map/attend_grad/pallas_call | solution.py:145
  112.6 1.3 collective-permute-start.8
  113.9 1.0 collective-permute-done.7.refs_1_
  114.9 2.2 %merge.1 = bf16[32,96,128]{2,1,0:T(8,128)(2,1)} custom-call(bf16[32,64,128]{2,1,0:T(8,128)(2,1)} %get-tuple-element.118.refs_0_, bf16[32,64,128]{2,1,0:T(8,128)(2,1)} %collective-permute-done.7.refs_1_, bf16[16,32,128]{2,1,0:T(8,128)(2,1)} %get-tuple-element.122.refs_2_, bf16[96,128]{1,0:T(8,128)(2,1)} %collective-permute-done.8.refs_3_), custom_call_target="tpu_custom_call" | custom-call | flops 2000000000 | tf_op jit(solution)/shard_map/merge/pallas_call | solution.py:145
  117.1 4.1 %all-to-all-done.3.refs_0_ = bf16[16,48,1024]{2,1,0:T(8,128)(2,1)} async-done(((bf16[16,48,1024]{2,1,0:T(8,128)(2,1)}), bf16[16,48,1024]{2,1,0:T(8,128)(2,1)}, u32[]{:S(2)}, u32[]{:S(2)}) %all-to-all-start.3) | async-done | bytes 1572896 | tf_op jit(solution)/shard_map/all_to_all | solution.py:943
  121.2 8.6 %all-to-all-start.4 = ((bf16[32,96,128]{2,1,0:T(8,128)(2,1)}), bf16[32,96,128]{2,1,0:T(8,128)(2,1)}, u32[]{:S(2)}, u32[]{:S(2)}) async-start(bf16[32,96,128]{2,1,0:T(8,128)(2,1)} %merge.1), calls=%async_computation.4 | async-start | bytes 1572864 | tf_op jit(solution)/shard_map/all_to_all | solution.py:955
  129.9 2.4 %ffn_sums.1 = (bf16[16,1152]{1,0:T(8,128)(2,1)}, bf16[16,1152]{1,0:T(8,128)(2,1)}, bf16[16,1152]{1,0:T(8,128)(2,1)}, f32[16,1152]{1,0:T(8,128)}) custom-call(bf16[16,48,1024]{2,1,0:T(8,128)(2,1)} %all-to-all-done.3.refs_0_), custom_call_target="tpu_custom_call" | custom-call | tf_op jit(solution)/shard_map/ffn_sums/pallas_call | solution.py:145
  132.8 2.7 %collective-permute-start.15 = (bf16[16,1152]{1,0:T(8,128)(2,1)}, bf16[16,1152]{1,0:T(8,128)(2,1)}, u32[]{:S(2)}, u32[]{:S(2)}) collective-permute-start(bf16[16,1152]{1,0:T(8,128)(2,1)} %get-tuple-element.133), channel_id=1, source_target_pairs={{0,4},{4,0},{1,5},{5,1},{2,6},{6,2},{3,7},{7,3},{8,12},{12,8},{9,1... | collective-permute-start | bytes 110600 | tf_op jit(solution)/shard_map/ppermute | solution.py:962
  135.5 0.8 collective-permute-start.16
  136.3 1.5 collective-permute-done.15.refs_2_
  137.7 7.2 %collective-permute-done.16.refs_3_ = bf16[16,1152]{1,0:T(8,128)(2,1)} collective-permute-done((bf16[16,1152]{1,0:T(8,128)(2,1)}, bf16[16,1152]{1,0:T(8,128)(2,1)}, u32[]{:S(2)}, u32[]{:S(2)}) %collective-permute-start.16) | collective-permute-done | bytes 36896 | tf_op jit(solution)/shard_map/ppermute | solution.py:963
  145.0 1.0 all-to-all-done.4.refs_0_
  146.0 4.1 %dnormed.1 = (bf16[128,1152]{1,0:T(8,128)(2,1)}, f32[1,1536]{1,0:T(1,128)}, f32[1,2304]{1,0:T(1,128)}, bf16[128,768]{1,0:T(8,128)(2,1)}) custom-call(bf16[32,96,128]{2,1,0:T(8,128)(2,1)} %all-to-all-done.4.refs_0_, bf16[128,768]{1,0:T(8,128)(2,1)} %refs_2_.9, bf16[768,384]{1,0:T(8,128)(2,1)} %refs_2_.8, bf16[768,384]{1,0:T(8,128)(2,1)} %refs_3_.9, ...), custom_call_target="tpu_custom_call" | custom-call | tf_op jit(solution)/shard_map/dnormed/pallas_call | solution.py:145
  150.7 1.4 collective-permute-start.21
  152.4 1.6 collective-permute-done.21.refs_7_
  154.0 0.8 collective-permute-done.20.refs_6_
  154.9 3.4 %qkv_products.1 = bf16[32,128,128]{2,1,0:T(8,128)(2,1)} custom-call(bf16[128,384]{1,0:T(8,128)(2,1)} %get-tuple-element.96.refs_0_, bf16[128,384]{1,0:T(8,128)(2,1)} %collective-permute-done.17.refs_1_, bf16[128,1152]{1,0:T(8,128)(2,1)} %get-tuple-element.138.refs_2_, bf16[128,1152]{1,0:T(8,128)(2,1)} %collective-permute-done.18.refs_3_, ...), custom_call_target="tpu_custom_call" | custom-call | tf_op jit(solution)/shard_map/qkv_products/pallas_call | solution.py:145
  158.3 5.3 %all-to-all-start.5 = ((bf16[32,128,128]{2,1,0:T(8,128)(2,1)}), bf16[32,128,128]{2,1,0:T(8,128)(2,1)}, u32[]{:S(2)}, u32[]{:S(2)}) async-start(bf16[32,128,128]{2,1,0:T(8,128)(2,1)} %qkv_products.1), calls=%async_computation.5 | async-start | bytes 2097152 | tf_op jit(solution)/shard_map/all_to_all | solution.py:994
  163.7 2.9 %output.1 = bf16[128,768]{1,0:T(8,128)(2,1)} custom-call(bf16[128,768]{1,0:T(8,128)(2,1)} %ffn.1.refs_0_, bf16[128,768]{1,0:T(8,128)(2,1)} %collective-permute-done.6.refs_1_, f32[128,768]{1,0:T(8,128)} %get-tuple-element.113.refs_2_, bf16[128,768]{1,0:T(8,128)(2,1)} %refs_2_.9, s32[128]{0:T(128)} %refs_4_.11, f32[768]{0:T(1024)} %refs_5_.8), custom_call_target="tpu_custom_call" | custom-call | tf_op jit(solution)/shard_map/output/pallas_call | solution.py:145
  166.6 1.7 ffn_finish.1
  168.4 12.5 %collective-permute-done.22.refs_1_ = bf16[128,768]{1,0:T(8,128)(2,1)} collective-permute-done((bf16[128,768]{1,0:T(8,128)(2,1)}, bf16[128,768]{1,0:T(8,128)(2,1)}, u32[]{:S(2)}, u32[]{:S(2)}) %collective-permute-start.22) | collective-permute-done | bytes 196640 | tf_op jit(solution)/shard_map/ppermute | solution.py:984
  180.9 3.4 %input_grad.1 = f32[128,768]{1,0:T(8,128)} custom-call(bf16[128,768]{1,0:T(8,128)(2,1)} %get-tuple-element.145.refs_0_, bf16[128,768]{1,0:T(8,128)(2,1)} %collective-permute-done.22.refs_1_, bf16[128,768]{1,0:T(8,128)(2,1)} %refs_2_.9, bf16[128,768]{1,0:T(8,128)(2,1)} %refs_3_.11, s32[128]{0:T(128)} %refs_4_.11, f32[768]{0:T(1024)} %refs_5_.9, ...), custom_call_target="tpu_custom_call" | custom-call | tf_op jit(solution)/shard_map/input_grad/pallas_call | solution.py:145
  184.4 2.1 %finish.1 = (f32[12,384]{1,0:T(8,128)}, f32[12,384]{1,0:T(8,128)}, f32[12,384]{1,0:T(8,128)}, f32[768]{0:T(1024)}, f32[768]{0:T(1024)}, /*index=5*/f32[384]{0:T(512)}, f32[384]{0:T(512)}) custom-call(bf16[32,128,128]{2,1,0:T(8,128)(2,1)} %all-to-all-done.5.refs_0_), custom_call_target="tpu_custom_call" | custom-call | flops 2000000000 | tf_op jit(solution)/shard_map/finish/pallas_call | solution.py:145
  (35 shorter events, 5.1 us)
Async XLA Ops:
  3.7 18.0 %collective-permute-start = (bf16[384,768]{1,0:T(8,128)(2,1)}, bf16[384,768]{1,0:T(8,128)(2,1)}, u32[]{:S(2)}, u32[]{:S(2)}) collective-permute-start(bf16[384,768]{1,0:T(8,128)(2,1)} %refs_9_.1), channel_id=1, source_target_pairs={{0,1},{1,0},{2,3},{3,2},{4,5},{5,4},{6,7},{7,6},{8,9},{9,8},{10,11... | collective-permute-start | bytes 1769480 | tf_op jit(solution)/shard_map/ppermute | solution.py:873
  6.2 15.5 %all-to-all-start = ((bf16[16,112,128]{2,1,0:T(8,128)(2,1)}), bf16[16,112,128]{2,1,0:T(8,128)(2,1)}, u32[]{:S(2)}, u32[]{:S(2)}) async-start(bf16[16,112,128]{2,1,0:T(8,128)(2,1)} %get-tuple-element.97), calls=%async_computation | async-start | bytes 917504 | tf_op jit(solution)/shard_map/all_to_all | solution.py:871
  22.7 8.3 %collective-permute-start.2 = (bf16[16,64,128]{2,1,0:T(8,128)(2,1)S(1)}, bf16[16,64,128]{2,1,0:T(8,128)(2,1)S(1)}, u32[]{:S(2)}, u32[]{:S(2)}) collective-permute-start(bf16[16,64,128]{2,1,0:T(8,128)(2,1)S(1)} %slice.6), channel_id=1, source_target_pairs={{0,4},{4,0},{1,5},{5,1},{2,6},{6,2},{3,7},{7,3},{8,12},{12,8},{9,1... | collective-permute-start | bytes 786440 | tf_op jit(solution)/shard_map/ppermute | solution.py:883
  26.8 4.2 %collective-permute-start.3 = (bf16[112,128]{1,0:T(8,128)(2,1)S(1)}, bf16[112,128]{1,0:T(8,128)(2,1)S(1)}, u32[]{:S(2)}, u32[]{:S(2)}) collective-permute-start(bf16[112,128]{1,0:T(8,128)(2,1)S(1)} %slice_bitcast_fusion), channel_id=1, source_target_pairs={{14,6},{30,22},{15,7},{31,23},{46,38},{62,54},{47,39},{63,55},{78,... | collective-permute-start | bytes 86024 | tf_op jit(solution)/shard_map/ppermute | solution.py:882
  27.5 6.4 %collective-permute-start.1 = (bf16[16,64,128]{2,1,0:T(8,128)(2,1)S(1)}, bf16[16,64,128]{2,1,0:T(8,128)(2,1)S(1)}, u32[]{:S(2)}, u32[]{:S(2)}) collective-permute-start(bf16[16,64,128]{2,1,0:T(8,128)(2,1)S(1)} %slice.6), channel_id=1, source_target_pairs={{0,2},{2,0},{1,3},{3,1},{4,6},{6,4},{5,7},{7,5},{8,10},{10,8},{9,1... | collective-permute-start | bytes 786440 | tf_op jit(solution)/shard_map/ppermute | solution.py:881
  31.0 2.9 %copy-start.2 = (bf16[112,128]{1,0:T(8,128)(2,1)}, bf16[112,128]{1,0:T(8,128)(2,1)S(1)}, u32[]{:S(2)}) copy-start(bf16[112,128]{1,0:T(8,128)(2,1)S(1)} %collective-permute-done.3.refs_4_) | copy-start | bytes 86020
  31.0 2.9 %copy-start = (bf16[16,64,128]{2,1,0:T(8,128)(2,1)}, bf16[16,64,128]{2,1,0:T(8,128)(2,1)S(1)}, u32[]{:S(2)}) copy-start(bf16[16,64,128]{2,1,0:T(8,128)(2,1)S(1)} %collective-permute-done.2.refs_2_) | copy-start | bytes 786436
  31.0 4.1 %collective-permute-start.4 = (bf16[16,64,128]{2,1,0:T(8,128)(2,1)S(1)}, bf16[16,64,128]{2,1,0:T(8,128)(2,1)}, u32[]{:S(2)}, u32[]{:S(2)}) collective-permute-start(bf16[16,64,128]{2,1,0:T(8,128)(2,1)S(1)} %collective-permute-done.2.refs_2_), channel_id=1, source_target_pairs={{0,2},{2,0},{1,3},{3,1},{4,6},{6,4},{5,7},{7,5},{8,10},{10,8},{9,1... | collective-permute-start | bytes 786440 | tf_op jit(solution)/shard_map/ppermute | solution.py:885
  33.8 0.7 copy-start.1
  41.1 16.0 %all-to-all-start.1 = ((bf16[32,64,128]{2,1,0:T(8,128)(2,1)}), bf16[32,64,128]{2,1,0:T(8,128)(2,1)}, u32[]{:S(2)}, u32[]{:S(2)}) async-start(bf16[32,64,128]{2,1,0:T(8,128)(2,1)} %get-tuple-element.107), calls=%async_computation.1 | async-start | bytes 1048576 | tf_op jit(solution)/shard_map/all_to_all | solution.py:893
  64.0 9.1 %collective-permute-start.5 = (bf16[128,768]{1,0:T(8,128)(2,1)}, bf16[128,768]{1,0:T(8,128)(2,1)}, u32[]{:S(2)}, u32[]{:S(2)}) collective-permute-start(bf16[128,768]{1,0:T(8,128)(2,1)} %get-tuple-element.110.refs_0_), channel_id=1, source_target_pairs={{0,1},{1,0},{2,3},{3,2},{4,5},{5,4},{6,7},{7,6},{8,9},{9,8},{10,11... | collective-permute-start | bytes 589832 | tf_op jit(solution)/shard_map/ppermute | solution.py:915
  64.6 20.3 %collective-permute-start.9 = (bf16[128,1536]{1,0:T(8,128)(2,1)}, bf16[128,1536]{1,0:T(8,128)(2,1)}, u32[]{:S(2)}, u32[]{:S(2)}) collective-permute-start(bf16[128,1536]{1,0:T(8,128)(2,1)} %get-tuple-element.125), channel_id=1, source_target_pairs={{0,2},{2,0},{1,3},{3,1},{4,6},{6,4},{5,7},{7,5},{8,10},{10,8},{9,1... | collective-permute-start | bytes 1179656 | tf_op jit(solution)/shard_map/ppermute | solution.py:918
  66.8 18.1 %collective-permute-start.10 = (bf16[128,1536]{1,0:T(8,128)(2,1)}, bf16[128,1536]{1,0:T(8,128)(2,1)}, u32[]{:S(2)}, u32[]{:S(2)}) collective-permute-start(bf16[128,1536]{1,0:T(8,128)(2,1)} %get-tuple-element.126), channel_id=1, source_target_pairs={{0,4},{4,0},{1,5},{5,1},{2,6},{6,2},{3,7},{7,3},{8,12},{12,8},{9,1... | collective-permute-start | bytes 1179656 | tf_op jit(solution)/shard_map/ppermute | solution.py:916
  70.1 21.0 %collective-permute-start.11 = (bf16[128,1536]{1,0:T(8,128)(2,1)}, bf16[128,1536]{1,0:T(8,128)(2,1)}, u32[]{:S(2)}, u32[]{:S(2)}) collective-permute-start(bf16[128,1536]{1,0:T(8,128)(2,1)} %get-tuple-element.127), channel_id=1, source_target_pairs={{0,6},{2,4},{4,2},{6,0},{1,7},{3,5},{5,3},{7,1},{8,14},{10,12},{12... | collective-permute-start | bytes 1179656 | tf_op jit(solution)/shard_map/ppermute | solution.py:917
  77.6 13.5 %collective-permute-start.12 = (bf16[128,1152]{1,0:T(8,128)(2,1)}, bf16[128,1152]{1,0:T(8,128)(2,1)}, u32[]{:S(2)}, u32[]{:S(2)}) collective-permute-start(bf16[128,1152]{1,0:T(8,128)(2,1)} %get-tuple-element.128.refs_4_), channel_id=1, source_target_pairs={{0,2},{2,0},{1,3},{3,1},{4,6},{6,4},{5,7},{7,5},{8,10},{10,8},{9,1... | collective-permute-start | bytes 884744 | tf_op jit(solution)/shard_map/ppermute | solution.py:935
  78.1 16.5 %all-to-all-start.2 = ((bf16[16,64,128]{2,1,0:T(8,128)(2,1)}), bf16[16,64,128]{2,1,0:T(8,128)(2,1)}, u32[]{:S(2)}, u32[]{:S(2)}) async-start(bf16[16,64,128]{2,1,0:T(8,128)(2,1)} %get-tuple-element.117), calls=%async_computation.2 | async-start | bytes 524288 | tf_op jit(solution)/shard_map/all_to_all | solution.py:934
  82.3 1.8 collective-permute-start.13
  84.1 28.4 %collective-permute-start.6 = (bf16[128,768]{1,0:T(8,128)(2,1)}, bf16[128,768]{1,0:T(8,128)(2,1)}, u32[]{:S(2)}, u32[]{:S(2)}) collective-permute-start(bf16[128,768]{1,0:T(8,128)(2,1)} %ffn.1.refs_0_), channel_id=1, source_target_pairs={{0,1},{1,0},{2,3},{3,2},{4,5},{5,4},{6,7},{7,6},{8,9},{9,8},{10,11... | collective-permute-start | bytes 589832 | tf_op jit(solution)/shard_map/ppermute | solution.py:944
  94.6 26.5 %all-to-all-start.3 = ((bf16[16,48,1024]{2,1,0:T(8,128)(2,1)}), bf16[16,48,1024]{2,1,0:T(8,128)(2,1)}, u32[]{:S(2)}, u32[]{:S(2)}) async-start(bf16[16,48,1024]{2,1,0:T(8,128)(2,1)} %bitcast.3), calls=%async_computation.3 | async-start | bytes 3145728 | tf_op jit(solution)/shard_map/all_to_all | solution.py:943
  112.5 2.3 %collective-permute-start.7 = (bf16[32,64,128]{2,1,0:T(8,128)(2,1)}, bf16[32,64,128]{2,1,0:T(8,128)(2,1)}, u32[]{:S(2)}, u32[]{:S(2)}) collective-permute-start(bf16[32,64,128]{2,1,0:T(8,128)(2,1)} %get-tuple-element.121), channel_id=1, source_target_pairs={{0,2},{2,0},{1,3},{3,1},{4,6},{6,4},{5,7},{7,5},{8,10},{10,8},{9,1... | collective-permute-start | bytes 1572872 | tf_op jit(solution)/shard_map/ppermute | solution.py:948
  112.6 1.3 collective-permute-start.8
  121.2 24.8 %all-to-all-start.4 = ((bf16[32,96,128]{2,1,0:T(8,128)(2,1)}), bf16[32,96,128]{2,1,0:T(8,128)(2,1)}, u32[]{:S(2)}, u32[]{:S(2)}) async-start(bf16[32,96,128]{2,1,0:T(8,128)(2,1)} %merge.1), calls=%async_computation.4 | async-start | bytes 1572864 | tf_op jit(solution)/shard_map/all_to_all | solution.py:955
  129.8 6.5 %collective-permute-start.17 = (bf16[128,384]{1,0:T(8,128)(2,1)}, bf16[128,384]{1,0:T(8,128)(2,1)}, u32[]{:S(2)}, u32[]{:S(2)}) collective-permute-start(bf16[128,384]{1,0:T(8,128)(2,1)} %get-tuple-element.135), channel_id=1, source_target_pairs={{0,2},{2,0},{1,3},{3,1},{4,6},{6,4},{5,7},{7,5},{8,10},{10,8},{9,1... | collective-permute-start | bytes 294920 | tf_op jit(solution)/shard_map/ppermute | solution.py:886
  132.2 4.0 %collective-permute-start.14 = (bf16[16,1152]{1,0:T(8,128)(2,1)}, bf16[16,1152]{1,0:T(8,128)(2,1)}, u32[]{:S(2)}, u32[]{:S(2)}) collective-permute-start(bf16[16,1152]{1,0:T(8,128)(2,1)} %get-tuple-element.132), channel_id=1, source_target_pairs={{0,2},{2,0},{1,3},{3,1},{4,6},{6,4},{5,7},{7,5},{8,10},{10,8},{9,1... | collective-permute-start | bytes 110600 | tf_op jit(solution)/shard_map/ppermute | solution.py:961
  132.8 4.9 %collective-permute-start.15 = (bf16[16,1152]{1,0:T(8,128)(2,1)}, bf16[16,1152]{1,0:T(8,128)(2,1)}, u32[]{:S(2)}, u32[]{:S(2)}) collective-permute-start(bf16[16,1152]{1,0:T(8,128)(2,1)} %get-tuple-element.133), channel_id=1, source_target_pairs={{0,4},{4,0},{1,5},{5,1},{2,6},{6,2},{3,7},{7,3},{8,12},{12,8},{9,1... | collective-permute-start | bytes 110600 | tf_op jit(solution)/shard_map/ppermute | solution.py:962
  135.5 9.5 %collective-permute-start.16 = (bf16[16,1152]{1,0:T(8,128)(2,1)}, bf16[16,1152]{1,0:T(8,128)(2,1)}, u32[]{:S(2)}, u32[]{:S(2)}) collective-permute-start(bf16[16,1152]{1,0:T(8,128)(2,1)} %get-tuple-element.134), channel_id=1, source_target_pairs={{0,6},{2,4},{4,2},{6,0},{1,7},{3,5},{5,3},{7,1},{8,14},{10,12},{12... | collective-permute-start | bytes 110600 | tf_op jit(solution)/shard_map/ppermute | solution.py:963
  150.1 4.8 %collective-permute-start.18 = (bf16[128,1152]{1,0:T(8,128)(2,1)}, bf16[128,1152]{1,0:T(8,128)(2,1)}, u32[]{:S(2)}, u32[]{:S(2)}) collective-permute-start(bf16[128,1152]{1,0:T(8,128)(2,1)} %get-tuple-element.138.refs_2_), channel_id=1, source_target_pairs={{0,2},{2,0},{1,3},{3,1},{4,6},{6,4},{5,7},{7,5},{8,10},{10,8},{9,1... | collective-permute-start | bytes 884744 | tf_op jit(solution)/shard_map/ppermute | solution.py:979
  150.5 4.3 %collective-permute-start.19 = (f32[1,2304]{1,0:T(1,128)}, f32[1,2304]{1,0:T(1,128)}, u32[]{:S(2)}, u32[]{:S(2)}) collective-permute-start(f32[1,2304]{1,0:T(1,128)} %get-tuple-element.139.refs_4_), channel_id=1, source_target_pairs={{0,2},{2,0},{1,3},{3,1},{4,6},{6,4},{5,7},{7,5},{8,10},{10,8},{9,1... | collective-permute-start | bytes 27656 | tf_op jit(solution)/shard_map/ppermute | solution.py:980
  150.7 3.4 %collective-permute-start.21 = (f32[1,1536]{1,0:T(1,128)}, f32[1,1536]{1,0:T(1,128)}, u32[]{:S(2)}, u32[]{:S(2)}) collective-permute-start(f32[1,1536]{1,0:T(1,128)} %get-tuple-element.140), channel_id=1, source_target_pairs={{0,3},{1,2},{2,1},{3,0},{4,7},{5,6},{6,5},{7,4},{8,11},{9,10},{10,... | collective-permute-start | bytes 18440 | tf_op jit(solution)/shard_map/ppermute | solution.py:982
  152.1 2.8 %collective-permute-start.20 = (f32[1,1536]{1,0:T(1,128)}, f32[1,1536]{1,0:T(1,128)}, u32[]{:S(2)}, u32[]{:S(2)}) collective-permute-start(f32[1,1536]{1,0:T(1,128)} %get-tuple-element.140), channel_id=1, source_target_pairs={{0,1},{1,0},{2,3},{3,2},{4,5},{5,4},{6,7},{7,6},{8,9},{9,8},{10,11... | collective-permute-start | bytes 18440 | tf_op jit(solution)/shard_map/ppermute | solution.py:981
  158.3 26.1 %all-to-all-start.5 = ((bf16[32,128,128]{2,1,0:T(8,128)(2,1)}), bf16[32,128,128]{2,1,0:T(8,128)(2,1)}, u32[]{:S(2)}, u32[]{:S(2)}) async-start(bf16[32,128,128]{2,1,0:T(8,128)(2,1)} %qkv_products.1), calls=%async_computation.5 | async-start | bytes 2097152 | tf_op jit(solution)/shard_map/all_to_all | solution.py:994
  163.6 17.3 %collective-permute-start.22 = (bf16[128,768]{1,0:T(8,128)(2,1)}, bf16[128,768]{1,0:T(8,128)(2,1)}, u32[]{:S(2)}, u32[]{:S(2)}) collective-permute-start(bf16[128,768]{1,0:T(8,128)(2,1)} %get-tuple-element.145.refs_0_), channel_id=1, source_target_pairs={{0,1},{1,0},{2,3},{3,2},{4,5},{5,4},{6,7},{7,6},{8,9},{9,8},{10,11... | collective-permute-start | bytes 589832 | tf_op jit(solution)/shard_map/ppermute | solution.py:984
